TPU v7x, 32 devices: a whole 2x2x4 slice. The times are simulated.
32 devices in a mesh: gx: 4 (over y, x), gy: 2 (over core), gz: 4 (over z).
Axes of the slice: x: 2, y: 2, z: 4, core: 2. Of those that a mesh axis runs over, the one named last changes fastest.
Arguments:
- features: bfloat16 [64, 32, 48, 512], P('gx', 'gy', 'gz'), may hold values from -6 to 6
- cotangent: bfloat16 [64, 32, 48, 512], P('gx', 'gy', 'gz'), may hold values from -6 to 6
- reduce_weight: bfloat16 [512, 128], replicated, may hold values from -0.25 to 0.25
- project_weight: bfloat16 [512, 64], replicated, may hold values from -0.25 to 0.25
- expand_weight: bfloat16 [512, 128], replicated, may hold values from -0.5 to 0.5
- adjacency: float32 [64, 64], replicated, may hold values from -0.75 to 0.75
- node_weight: float32 [128, 128], replicated, may hold values from -0.5 to 0.5
Outputs:
- grad_features: bfloat16 [64, 32, 48, 512], P('gx', 'gy', 'gz')
- grad_reduce: float32 [512, 128], P(('gx', 'gy', 'gz'))
- grad_project: float32 [512, 64], P(('gx', 'gy', 'gz'))
- grad_expand: float32 [512, 128], P(('gx', 'gy', 'gz'))
- grad_adjacency: float32 [64, 64], replicated
- grad_node: float32 [128, 128], replicated
All inputs are finite; a program needn't handle non-finite values.
Results may differ from a plain program's by a relative error of at most 0.0064.
Values sent between devices are 32-bit elements; how exact they have to be, the bound alone decides.
No kernel may reach another device: no remote copies, remote signals or barrier semaphores. Data moves between devices by JAX's collectives and lax.ppermute only.
A program may use at most 64 MiB of HBM per device.

v0:
```python
import math

import jax
import jax.numpy as jnp
from jax import lax
from jax.sharding import PartitionSpec as P


def exact(a, b):
    return jnp.dot(a, b, precision=lax.Precision.HIGHEST)


def inner(left, right):
    return lax.dot_general(
        left, right, (((0,), (0,)), ((), ())), preferred_element_type=jnp.float32
    )


def outer(left, right):
    return lax.dot_general(
        left, right, (((1,), (1,)), ((), ())), preferred_element_type=jnp.float32
    )


def on_device(
    features, cotangent, reduce_weight, project_weight, expand_weight, adjacency, node_weight
):
    size_x, size_y, size_z, chan = features.shape
    local = size_x * size_y * size_z
    devcount = lax.axis_size("gx") * lax.axis_size("gy") * lax.axis_size("gz")
    total = local * devcount
    scale = 1.0 / math.sqrt(total)
    flat_x = features.reshape(local, chan)
    flat_g = cotangent.reshape(local, chan)
    reduced = jnp.dot(flat_x, reduce_weight, preferred_element_type=jnp.float32).astype(
        jnp.bfloat16
    )
    projection = jnp.dot(flat_x, project_weight, preferred_element_type=jnp.float32).astype(
        jnp.bfloat16
    )
    d_mapped = jnp.dot(flat_g, expand_weight, preferred_element_type=jnp.float32).astype(
        jnp.bfloat16
    )
    node_term = inner(projection, reduced)
    grad_term = inner(projection, d_mapped)
    node_total, d_node_out = lax.psum((node_term, grad_term), ("gx", "gy", "gz"))
    nodes = scale * node_total
    hidden = nodes - exact(adjacency, nodes)
    pre = exact(hidden, node_weight)
    node_out = jnp.maximum(pre, 0.0).astype(jnp.bfloat16)
    d_pre = jnp.where(pre > 0.0, d_node_out, jnp.float32(0.0))
    grad_node = scale * exact(hidden.T, d_pre)
    d_hidden = exact(d_pre, node_weight.T)
    grad_adjacency = -scale * exact(d_hidden, nodes.T)
    d_nodes = d_hidden - exact(adjacency.T, d_hidden)
    d_nodes_b = d_nodes.astype(jnp.bfloat16)
    d_projection = (outer(d_mapped, node_out) + scale * outer(reduced, d_nodes_b)).astype(
        jnp.bfloat16
    )
    d_reduced = (scale * jnp.dot(projection, d_nodes_b, preferred_element_type=jnp.float32)).astype(
        jnp.bfloat16
    )
    grad_flat = (
        flat_g.astype(jnp.float32)
        + outer(d_reduced, reduce_weight)
        + outer(d_projection, project_weight)
    )
    grad_features = grad_flat.astype(jnp.bfloat16).reshape(features.shape)
    node_f = node_out.astype(jnp.float32)
    dn_f = d_nodes_b.astype(jnp.float32)
    project_term = exact(inner(flat_x, d_mapped), node_f.T) + scale * exact(
        inner(flat_x, reduced), dn_f.T
    )
    expand_term = exact(inner(flat_g, projection), node_f)
    cross_rows, project_rows, expand_rows = (
        lax.psum_scatter(
            inner(flat_x, projection), ("gx", "gy", "gz"), scatter_dimension=0, tiled=True
        ),
        lax.psum_scatter(project_term, ("gx", "gy", "gz"), scatter_dimension=0, tiled=True),
        lax.psum_scatter(expand_term, ("gx", "gy", "gz"), scatter_dimension=0, tiled=True),
    )
    grad_project = scale * project_rows
    grad_expand = scale * expand_rows
    grad_reduce = scale * scale * exact(cross_rows, dn_f)
    return (grad_features, grad_reduce, grad_project, grad_expand, grad_adjacency, grad_node)


def solution(mesh):
    return jax.shard_map(
        on_device,
        mesh=mesh,
        in_specs=(P("gx", "gy", "gz", None), P("gx", "gy", "gz", None), P(), P(), P(), P(), P()),
        out_specs=(
            P("gx", "gy", "gz", None),
            P(("gx", "gy", "gz"), None),
            P(("gx", "gy", "gz"), None),
            P(("gx", "gy", "gz"), None),
            P(),
            P(),
        ),
        check_vma=False,
    )
```

profile of v0, /device:TPU:0, one launch (start us, length us, event | category | flops | bytes accessed | tf_op | source)
XLA Modules:
  0.0 570.3 jit_solution(10960139762587282496)
XLA Ops:
  7.2 6.2 %copy.19 = bf16[16,16,12,512]{3,2,1,0:T(8,128)(2,1)} copy(bf16[16,16,12,512]{3,1,2,0:T(8,128)(2,1)} %param.7) | data formatting | bytes 6291456 | tf_op args[0]
  13.4 4.8 reshape.22
  18.2 1.9 convolution_convert_fusion.2
  20.1 1.9 convolution_convert_fusion.1
  22.0 4.3 copy.18
  26.3 6.2 %reshape.21 = bf16[3072,512]{1,0:T(8,128)(2,1)} reshape(bf16[16,16,12,512]{3,2,1,0:T(8,128)(2,1)} %copy.18) | data formatting | bytes 6291456 | tf_op jit(solution)/shard_map/reshape | solution.py:34
  32.6 2.1 fusion.20
  34.7 2.9 convolution_convert_fusion
  39.5 1.6 convolution_bitcast_fusion
  42.3 2.6 fusion.24
  45.5 1.3 fusion.23
  46.9 113.5 %all-reduce.3.cloned.1.call-done = (f32[64,128]{1,0:T(8,128)}, f32[64,128]{1,0:T(8,128)}) async-done(((f32[64,128]{1,0:T(8,128)}, f32[64,128]{1,0:T(8,128)}), (f32[64,128]{1,0:T(8,128)}, f32[64,128]{1,0:T(8,128)})) %all-reduce.3.cloned.1.call-update) | async-done | bytes 65552 | tf_op jit(solution)/shard_map/psum | solution.py:46
  162.4 2.1 fusion.19
  167.0 5.0 fusion.2
  172.9 2.1 fusion.3
  175.1 2.5 convolution_multiply_fusion.1
  177.7 6.2 %add_convert_fusion = bf16[3072,512]{1,0:T(8,128)(2,1)} fusion(f32[3072,512]{1,0:T(8,128)} %fusion.2, bf16[3072,512]{1,0:T(8,128)(2,1)S(1)} %copy-done.2, bf16[512,64]{0,1:T(8,128)(2,1)S(1)} %copy-done.9, f32[3072,64]{0,1:T(8,128)} %convolution_multiply_fusion.1, bf16[3072,128]{1,0:T(8,128)(2,1)} %copy-done.5, f32[64,128]{1,0:T(8,128)S(1)} %fusion.21), kind=kOutput, calls=%fused_computation | convolution fusion | flops 258359296 | bytes 14254080 | tf_op jit(solution)/shard_map/dot_general | solution.py:20
  184.7 6.2 %reshape.23 = bf16[16,16,12,512]{3,2,1,0:T(8,128)(2,1)} reshape(bf16[3072,512]{1,0:T(8,128)(2,1)} %add_convert_fusion) | data formatting | bytes 6291456 | tf_op jit(solution)/shard_map/reshape | solution.py:68
  190.9 5.9 %copy.20 = bf16[16,16,12,512]{3,1,2,0:T(8,128)(2,1)} copy(bf16[16,16,12,512]{3,2,1,0:T(8,128)(2,1)} %reshape.23) | data formatting | bytes 6291456
  196.8 100.9 %reduce-scatter.10.cloned.1.call-done = f32[16,64]{1,0:T(8,128)} async-done(((f32[512,64]{1,0:T(8,128)}), f32[16,64]{1,0:T(8,128)}) %reduce-scatter.10.cloned.1.call-update) | async-done | bytes 4112
  297.7 1.4 convolution_multiply_fusion.5
  299.1 131.1 %reduce-scatter.6.cloned.1.call-done = f32[16,64]{1,0:T(8,128)} async-done(((f32[512,64]{1,0:T(8,128)}), f32[16,64]{1,0:T(8,128)}) %reduce-scatter.6.cloned.1.call-update) | async-done | bytes 4112 | tf_op jit(solution)/shard_map/reduce_scatter | solution.py:79
  430.2 1.3 broadcast_multiply_fusion.1
  431.5 131.0 %reduce-scatter.8.cloned.1.call-done = f32[16,128]{1,0:T(8,128)} async-done(((f32[512,128]{1,0:T(8,128)}), f32[16,128]{1,0:T(8,128)}) %reduce-scatter.8.cloned.1.call-update) | async-done | bytes 8208 | tf_op jit(solution)/shard_map/reduce_scatter | solution.py:80
  (47 shorter events, 11.2 us)
Async XLA Ops:
  7.2 12.9 %copy-start = (bf16[512,128]{1,0:T(8,128)(2,1)S(1)}, bf16[512,128]{1,0:T(8,128)(2,1)}, u32[]{:S(2)}) copy-start(bf16[512,128]{1,0:T(8,128)(2,1)} %param.9) | copy-start | bytes 393220
  7.2 153.2 %all-reduce.3.cloned.1.call-start = ((), (), s32[]{:S(2)}) async-start(), calls=%async_computation.6 | async-start | bytes 131072 | tf_op jit(solution)/shard_map/psum | solution.py:46
  13.4 4.8 copy-start.8
  20.1 1.9 copy-start.7
  26.3 8.4 %copy-start.10 = (bf16[512,128]{1,0:T(8,128)(2,1)S(1)}, bf16[512,128]{1,0:T(8,128)(2,1)}, u32[]{:S(2)}) copy-start(bf16[512,128]{1,0:T(8,128)(2,1)} %param.11) | copy-start | bytes 393220
  34.7 3.8 copy-start.3
  37.6 0.9 copy-start.5
  39.4 258.3 %reduce-scatter.10.cloned.1.call-start = ((), (), s32[]{:S(2)}) async-start(), calls=%async_computation.5 | async-start | bytes 270336
  42.0 388.2 %reduce-scatter.6.cloned.1.call-start = ((), (), s32[]{:S(2)}) async-start(), calls=%async_computation.3 | async-start | bytes 270336 | tf_op jit(solution)/shard_map/reduce_scatter | solution.py:79
  42.2 2.6 copy-start.1
  42.2 2.6 copy-start.4
  42.2 3.3 copy-start.6
  44.9 115.5 %copy-start.13 = (f32[64,64]{1,0:T(8,128)S(1)}, f32[64,64]{1,0:T(8,128)}, u32[]{:S(2)}) copy-start(f32[64,64]{1,0:T(8,128)} %param.12) | copy-start | bytes 49156
  167.0 5.1 copy-start.12
  167.0 10.7 %copy-start.2 = (bf16[3072,512]{1,0:T(8,128)(2,1)S(1)}, bf16[3072,512]{1,0:T(8,128)(2,1)}, u32[]{:S(2)}) copy-start(bf16[3072,512]{1,0:T(8,128)(2,1)} %reshape.21) | copy-start | bytes 9437188
  167.0 10.7 %copy-start.9 = (bf16[512,64]{0,1:T(8,128)(2,1)S(1)}, bf16[512,64]{0,1:T(8,128)(2,1)}, u32[]{:S(2)}) copy-start(bf16[512,64]{0,1:T(8,128)(2,1)} %param.10) | copy-start | bytes 196612
  175.1 387.3 %reduce-scatter.8.cloned.1.call-start = ((), (), s32[]{:S(2)}) async-start(), calls=%async_computation.4 | async-start | bytes 270336 | tf_op jit(solution)/shard_map/reduce_scatter | solution.py:80
  177.7 6.2 %copy-start.11 = (f32[64,128]{1,0:T(8,128)S(1)}, f32[64,128]{1,0:T(8,128)}, u32[]{:S(2)}) copy-start(f32[64,128]{1,0:T(8,128)} %get-tuple-element.25) | copy-start | bytes 98308
Sparse Core Ops, SparseCore 0:
  39.5 120.8 all-reduce.2
  162.6 134.9 reduce-scatter.9
  300.0 130.1 reduce-scatter.5
  432.3 130.1 reduce-scatter.7
where the time goes:
time: 571 us; the launch traced here: 570 us
  waiting for transfers between devices  476 us (83%)
  matrix products  41.5 us (7%)
  local copies, waits for them, and re-layouts  35.5 us (6%)
  between operations  13.9 us (2%)
    reduce_scatter x1, waiting for transfers between devices, on_device(): lax.psum_scatter(project_term, ('gx', 'gy', 'gz'), scatter_dimension=0, t...  131 us
    reduce_scatter x1, waiting for transfers between devices, on_device(): lax.psum_scatter(expand_term, ('gx', 'gy', 'gz'), scatter_dimension=0, ti...  131 us
    psum x1, waiting for transfers between devices, on_device(): lax.psum((node_term, grad_term), ('gx', 'gy', 'gz'))  114 us
    unnamed x5, waiting for transfers between devices  101 us
    unnamed x32, local copies, waits for them, and re-layouts  18.3 us
    dot_general x3, matrix products, outer(): lax.dot_general(left, right, (((1,), (1,)), ((), ())), preferred_element_...  13.7 us
    dot_general x10, matrix products, exact(): return jnp.dot(a, b, precision=lax.Precision.HIGHEST)  11.8 us
  transfers between devices with their start and end apart: 4, of which 4 were waited for; matrix products, arithmetic and copies ran while one was open for 8% of the time, Pallas kernels for 0%

commit v1 on v0

v1 whole, which is shorter than its diff:
```python
import functools
import math

import jax
import jax.numpy as jnp
from jax import lax
from jax.experimental import pallas as pl
from jax.experimental.pallas import tpu as pltpu
from jax.sharding import PartitionSpec as P

AXES = ("gx", "gy", "gz")
RING = ("gy", "gx", "gz")
F32 = jnp.float32
BF16 = jnp.bfloat16
VMEM_LIMIT = 40 * 1024 * 1024


def exact(a, b, dims=((1,), (0,))):
    return lax.dot_general(
        a, b, (dims, ((), ())), precision=lax.Precision.HIGHEST, preferred_element_type=F32
    )


def mxu(a, b, dims=((1,), (0,))):
    return lax.dot_general(a, b, (dims, ((), ())), preferred_element_type=F32)


def params():
    return pltpu.CompilerParams(vmem_limit_bytes=VMEM_LIMIT)


def cost(flops, nbytes):
    return pl.CostEstimate(flops=flops, bytes_accessed=nbytes, transcendentals=0)


def whole(shape):
    return pl.BlockSpec(shape, lambda *_: (0,) * len(shape))


def row_block(total):
    for size in (512, 384, 256, 128, 64, 32, 16):
        if total % size == 0:
            return size
    return total


def project_kernel(x_ref, g_ref, wr_ref, wpt_ref, we_ref, rd_ref, p_ref, term_ref, wcat_ref):
    cr = wr_ref.shape[1]
    nodes = wpt_ref.shape[0]

    @pl.when(pl.program_id(0) == 0)
    def _():
        wcat_ref[:, :cr] = wr_ref[...]
        padded = jnp.concatenate([wpt_ref[...], jnp.zeros_like(wpt_ref)], axis=0)
        wcat_ref[:, cr:] = padded.T
        term_ref[...] = jnp.zeros_like(term_ref)

    both = mxu(x_ref[...], wcat_ref[...]).astype(BF16)
    mapped = mxu(g_ref[...], we_ref[...]).astype(BF16)
    rd = jnp.concatenate([both[:, :cr], mapped], axis=1)
    proj = both[:, cr:]
    rd_ref[...] = rd
    p_ref[...] = proj
    term_ref[...] += mxu(proj, rd, ((0,), (0,)))[:nodes]


def project(x, g, wr, wpt, we):
    rows, chan = x.shape
    cr, nodes = wr.shape[1], wpt.shape[0]
    step = row_block(rows)
    rowspec = lambda width: pl.BlockSpec((step, width), lambda i: (i, 0))
    return pl.pallas_call(
        project_kernel,
        grid=(rows // step,),
        in_specs=[rowspec(chan), rowspec(chan), whole(wr.shape), whole(wpt.shape), whole(we.shape)],
        out_specs=[
            rowspec(2 * cr),
            rowspec(2 * nodes),
            whole((nodes, 2 * cr)),
            whole((chan, cr + 2 * nodes)),
        ],
        out_shape=[
            jax.ShapeDtypeStruct((rows, 2 * cr), BF16),
            jax.ShapeDtypeStruct((rows, 2 * nodes), BF16),
            jax.ShapeDtypeStruct((nodes, 2 * cr), F32),
            jax.ShapeDtypeStruct((chan, cr + 2 * nodes), BF16),
        ],
        compiler_params=params(),
        cost_estimate=cost(2 * rows * chan * 512, rows * chan * 4 + rows * 768),
        name="project",
    )(x, g, wr, wpt, we)


def weight_kernel(count, index_ref, x_ref, g_ref, rd_ref, p_ref, *rest):
    outs, sums_ref = rest[:count], rest[count]
    step = pl.program_id(0)
    nodes = p_ref.shape[1] // 2
    wide = rd_ref.shape[1]

    @pl.when(step == 0)
    def _():
        sums_ref[...] = jnp.zeros_like(sums_ref)

    proj = p_ref[...][:, :nodes]
    x = x_ref[...]
    sums_ref[:wide] += mxu(rd_ref[...], x, ((0,), (0,)))
    sums_ref[wide : wide + nodes] += mxu(proj, x, ((0,), (0,)))
    sums_ref[wide + nodes :] += mxu(proj, g_ref[...], ((0,), (0,)))

    @pl.when(step == pl.num_programs(0) - 1)
    def _():
        first, _, third, width = outs[0].shape[0], count, outs[0].shape[1], outs[0].shape[2]
        total = sums_ref[...].T.reshape(first, count, third, width)
        scatter(total, 1, count, index_ref, outs)


def scatter(total, axis, count, index_ref, outs):
    me = index_ref[0]
    for peer in range(count):
        for block in range(count):
            @pl.when(lax.bitwise_xor(me, peer) == block)
            def _():
                if axis == 1:
                    outs[peer][...] = total[:, block]
                else:
                    outs[peer][...] = total[block]


def weight_terms(x, g, rd, p, index, sizes):
    rows, chan = x.shape
    step = row_block(rows)
    gx, gy, gz = sizes
    width = rd.shape[1] + p.shape[1]
    part = (gx, chan // (gx * gy), width)
    rowspec = lambda wide: pl.BlockSpec((step, wide), lambda i: (i, 0))
    return pl.pallas_call(
        functools.partial(weight_kernel, gy),
        grid=(rows // step,),
        in_specs=[
            pl.BlockSpec(memory_space=pltpu.SMEM),
            rowspec(chan),
            rowspec(chan),
            rowspec(rd.shape[1]),
            rowspec(p.shape[1]),
        ],
        out_specs=[whole(part)] * gy,
        out_shape=[jax.ShapeDtypeStruct(part, F32)] * gy,
        scratch_shapes=[pltpu.VMEM((width, chan), F32)],
        compiler_params=params(),
        cost_estimate=cost(2 * rows * chan * 512, rows * chan * 4 + rows * 768 + width * chan * 4),
        name="weight_terms",
    )(index, x, g, rd, p)


def split_kernel(ins, count, index_ref, *refs):
    total = refs[0][...]
    for ref in refs[1:ins]:
        total = total + ref[...]
    scatter(total, 0, count, index_ref, refs[ins:])


def split(parts, count, index):
    first, third, width = parts[0].shape
    if first != count:
        parts = [p.reshape(count, third // count, width) for p in parts]
    shape = parts[0].shape
    return pl.pallas_call(
        functools.partial(split_kernel, len(parts), count),
        in_specs=[pl.BlockSpec(memory_space=pltpu.SMEM)] + [pl.BlockSpec(memory_space=pltpu.VMEM)] * len(parts),
        out_specs=[pl.BlockSpec(memory_space=pltpu.VMEM)] * count,
        out_shape=[jax.ShapeDtypeStruct(shape[1:], F32)] * count,
        compiler_params=params(),
        cost_estimate=cost(0, 8 * math.prod(shape) * len(parts)),
        name="split",
    )(index, *parts)


def swap(value, axis, peer):
    size = lax.axis_size(axis)
    return lax.ppermute(value, axis, [(i, i ^ peer) for i in range(size)])


def feature_kernel(
    ins, scale, *refs
):
    terms = refs[:ins]
    (adj_ref, nw_ref, wcat_ref, g_ref, rd_ref, p_ref) = refs[ins : ins + 6]
    (out_ref, ga_ref, gn_ref, no_ref, dn_ref, mix_ref, dnb_ref) = refs[ins + 6 :]
    nodes_n, cr = no_ref.shape

    @pl.when(pl.program_id(0) == 0)
    def _():
        total = terms[0][...]
        for ref in terms[1:]:
            total = total + ref[...]
        adj, nw = adj_ref[...], nw_ref[...]
        nodes = scale * total[:, :cr]
        d_node_out = total[:, cr:]
        hidden = nodes - exact(adj, nodes)
        pre = exact(hidden, nw)
        node_out = jnp.maximum(pre, 0.0).astype(BF16)
        d_pre = jnp.where(pre > 0.0, d_node_out, 0.0)
        gn_ref[...] = scale * exact(hidden, d_pre, ((0,), (0,)))
        d_hidden = exact(d_pre, nw, ((1,), (1,)))
        ga_ref[...] = -scale * exact(d_hidden, nodes, ((1,), (1,)))
        d_nodes = d_hidden - exact(adj, d_hidden, ((0,), (0,)))
        dn = d_nodes.astype(BF16)
        no_ref[...] = node_out.astype(F32)
        dn_ref[...] = dn.astype(F32)
        dnb_ref[:nodes_n] = dn
        dnb_ref[nodes_n:] = jnp.zeros((nodes_n, cr), BF16)
        blank = jnp.zeros((cr, cr), BF16)
        zero = jnp.zeros((nodes_n, cr), F32)
        dn_t = jnp.concatenate([dn.astype(F32), zero], axis=0).T.astype(BF16)
        no_t = jnp.concatenate([node_out.astype(F32), zero], axis=0).T.astype(BF16)
        mix_ref[:cr, :cr] = dn_t
        mix_ref[cr:, :cr] = blank
        mix_ref[:cr, cr:] = blank
        mix_ref[cr:, cr:] = no_t

    mixed = mxu(rd_ref[...], mix_ref[...])
    d_proj = (mixed[:, cr:] + scale * mixed[:, :cr]).astype(BF16)
    d_red = (scale * mxu(p_ref[...], dnb_ref[...])).astype(BF16)
    both = jnp.concatenate([d_red, d_proj], axis=1)
    out = g_ref[...].astype(F32) + mxu(both, wcat_ref[...], ((1,), (1,)))
    out_ref[...] = out.astype(BF16)


def feature_grads(terms, adjacency, node_weight, wcat, g, rd, p, scale):
    rows, chan = g.shape
    nodes, cr = adjacency.shape[0], node_weight.shape[0]
    step = row_block(rows)
    rowspec = lambda width: pl.BlockSpec((step, width), lambda i: (i, 0))
    return pl.pallas_call(
        functools.partial(feature_kernel, len(terms), scale),
        grid=(rows // step,),
        in_specs=[whole(t.shape) for t in terms]
        + [
            whole(adjacency.shape),
            whole(node_weight.shape),
            whole(wcat.shape),
            rowspec(chan),
            rowspec(rd.shape[1]),
            rowspec(p.shape[1]),
        ],
        out_specs=[
            rowspec(chan),
            whole((nodes, nodes)),
            whole((cr, cr)),
            whole((nodes, cr)),
            whole((nodes, cr)),
        ],
        out_shape=[
            jax.ShapeDtypeStruct((rows, chan), BF16),
            jax.ShapeDtypeStruct((nodes, nodes), F32),
            jax.ShapeDtypeStruct((cr, cr), F32),
            jax.ShapeDtypeStruct((nodes, cr), F32),
            jax.ShapeDtypeStruct((nodes, cr), F32),
        ],
        scratch_shapes=[pltpu.VMEM((2 * cr, 2 * cr), BF16), pltpu.VMEM((2 * nodes, cr), BF16)],
        compiler_params=params(),
        cost_estimate=cost(2 * rows * 4 * 65536, rows * chan * 4 + rows * 768),
        name="feature_grads",
    )(*terms, adjacency, node_weight, wcat, g, rd, p)


def finish_kernel(ins, scale, *refs):
    total = refs[0][...]
    for ref in refs[1:ins]:
        total = total + ref[...]
    no_ref, dn_ref, gr_ref, gp_ref, ge_ref = refs[ins:]
    nodes, cr = no_ref.shape
    no, dn = no_ref[...], dn_ref[...]
    x_red, x_dm = total[:, :cr], total[:, cr : 2 * cr]
    cross = total[:, 2 * cr : 2 * cr + nodes]
    g_proj = total[:, 2 * cr + nodes :]
    gr_ref[...] = scale * scale * exact(cross, dn)
    gp_ref[...] = scale * exact(x_dm, no, ((1,), (1,))) + scale * scale * exact(
        x_red, dn, ((1,), (1,))
    )
    ge_ref[...] = scale * exact(g_proj, no)


def finish(parts, no, dn, scale):
    rows = parts[0].shape[0]
    nodes, cr = no.shape
    vmem = pl.BlockSpec(memory_space=pltpu.VMEM)
    return pl.pallas_call(
        functools.partial(finish_kernel, len(parts), scale),
        in_specs=[vmem] * (len(parts) + 2),
        out_specs=[vmem] * 3,
        out_shape=[
            jax.ShapeDtypeStruct((rows, cr), F32),
            jax.ShapeDtypeStruct((rows, nodes), F32),
            jax.ShapeDtypeStruct((rows, cr), F32),
        ],
        compiler_params=params(),
        cost_estimate=cost(0, rows * 4096),
        name="finish",
    )(*parts, no, dn)


def on_device(
    features, cotangent, reduce_weight, project_weight, expand_weight, adjacency, node_weight
):
    size_x, size_y, size_z, chan = features.shape
    local = size_x * size_y * size_z
    sizes = tuple(lax.axis_size(axis) for axis in AXES)
    total = local * math.prod(sizes)
    scale = 1.0 / math.sqrt(total)
    flat_x = features.transpose(0, 2, 1, 3).reshape(local, chan)
    flat_g = cotangent.transpose(0, 2, 1, 3).reshape(local, chan)
    where = {axis: lax.axis_index(axis).reshape(1).astype(jnp.int32) for axis in AXES}

    rd, p, term, wcat = project(flat_x, flat_g, reduce_weight, project_weight.T, expand_weight)

    terms = [term]
    for axis in RING:
        held = terms[0] if len(terms) == 1 else functools.reduce(jnp.add, terms)
        terms = [held] + [swap(held, axis, k) for k in range(1, lax.axis_size(axis))]

    parts = weight_terms(flat_x, flat_g, rd, p, where["gy"], sizes)
    parts = [parts[0]] + [swap(part, "gy", k) for k, part in enumerate(parts) if k]
    for axis in ("gx", "gz"):
        parts = split(parts, lax.axis_size(axis), where[axis])
        parts = [parts[0]] + [swap(part, axis, k) for k, part in enumerate(parts) if k]
        if axis == "gx":
            parts = [part[None] for part in parts]

    flat_out, grad_adjacency, grad_node, no, dn = feature_grads(
        terms, adjacency, node_weight, wcat, flat_g, rd, p, scale
    )
    grad_reduce, grad_project, grad_expand = finish(parts, no, dn, scale)
    grad_features = flat_out.reshape(size_x, size_z, size_y, chan).transpose(0, 2, 1, 3)
    return (grad_features, grad_reduce, grad_project, grad_expand, grad_adjacency, grad_node)


def solution(mesh):
    return jax.shard_map(
        on_device,
        mesh=mesh,
        in_specs=(P("gx", "gy", "gz", None), P("gx", "gy", "gz", None), P(), P(), P(), P(), P()),
        out_specs=(
            P("gx", "gy", "gz", None),
            P(AXES, None),
            P(AXES, None),
            P(AXES, None),
            P(),
            P(),
        ),
        check_vma=False,
    )
```

time: 571 us -> 52.3 us (0.09)
  waiting for transfers between devices: 476 us -> 1.41 us
  matrix products: 41.5 us -> 0 us
  local copies, waits for them, and re-layouts: 35.5 us -> 13.1 us
  starting transfers between devices: 0.34 us -> 18.1 us
  Pallas kernels: 0 us -> 16.8 us
  between operations: 13.9 us -> 0.73 us
    reduce_scatter x2 -> x0, waiting for transfers between devices: 262 us -> none  [the longest x1 131 us: on_device(): lax.psum_scatter(project_term, ('gx', 'gy', 'gz'), scatter_dimension=0, t...]
    psum x1 -> x0, waiting for transfers between devices: 114 us -> none  [on_device(): lax.psum((node_term, grad_term), ('gx', 'gy', 'gz'))]
    unnamed x5 -> x0, waiting for transfers between devices: 101 us -> none
    dot_general x22 -> x0, matrix products: 41.5 us -> none  [the longest x3 13.7 us: outer(): lax.dot_general(left, right, (((1,), (1,)), ((), ())), preferred_element_...]
    ppermute x0 -> x14, starting transfers between devices: none -> 18.1 us  [swap(): return lax.ppermute(value, axis, [(i, i ^ peer) for i in range(size)])]
    reshape x3 -> x0, local copies, waits for them, and re-layouts: 17.2 us -> none  [the longest x1 6.25 us: on_device(): flat_g = cotangent.reshape(local, chan)]
    pallas_call x0 -> x6, Pallas kernels: none -> 16.8 us  [the longest x1 6.18 us: feature_grads(): pl.pallas_call(functools.partial(feature_kernel, len(terms), scale), grid...]
  transfers between devices with their start and end apart: 4 -> 14, of which waited for: 4 -> 1; matrix products, arithmetic and copies ran while one was open for 8% -> 3% of each run, Pallas kernels for 0% -> 16%
where the time goes in v1:
time: 52.3 us; the launch traced here: 51.7 us
  starting transfers between devices  18.1 us (35%)
  Pallas kernels  16.8 us (32%)
  local copies, waits for them, and re-layouts  13.1 us (25%)
  other arithmetic  1.59 us (3%)
  waiting for transfers between devices  1.41 us (3%)
  between operations  0.73 us (1%)
    ppermute x14, starting transfers between devices, swap(): return lax.ppermute(value, axis, [(i, i ^ peer) for i in range(size)])  18.1 us
    unnamed x32, local copies, waits for them, and re-layouts  13.1 us
    pallas_call x1, Pallas kernels, feature_grads(): pl.pallas_call(functools.partial(feature_kernel, len(terms), scale), grid...  6.18 us
    pallas_call x1, Pallas kernels, weight_terms(): pl.pallas_call(functools.partial(weight_kernel, gy), grid=(rows // step,)...  3.99 us
    pallas_call x1, Pallas kernels, project(): pl.pallas_call(project_kernel, grid=(rows // step,), in_specs=[rowspec(ch...  3.87 us
    pallas_call x2, Pallas kernels, split(): pl.pallas_call(functools.partial(split_kernel, len(parts), count), in_spe...  1.86 us
    add x2, other arithmetic, on_device(): held = terms[0] if len(terms) == 1 else functools.reduce(jnp.add, terms)  1.59 us
    ppermute x14, waiting for transfers between devices, swap(): return lax.ppermute(value, axis, [(i, i ^ peer) for i in range(size)])  1.41 us
  transfers between devices with their start and end apart: 14, of which 1 were waited for; matrix products, arithmetic and copies ran while one was open for 3% of the time, Pallas kernels for 16%

profile of v1, /device:TPU:0, one launch (start us, length us, event | category | flops | bytes accessed | tf_op | source)
XLA Modules:
  0.0 51.7 jit_solution(10900623345902218762)
XLA Ops:
  0.6 1.9 %copy-done = bf16[16,16,12,512]{3,1,2,0:T(8,128)(2,1)S(1)} copy-done((bf16[16,16,12,512]{3,1,2,0:T(8,128)(2,1)S(1)}, bf16[16,16,12,512]{3,1,2,0:T(8,128)(2,1)}, u32[]{:S(2)}) %copy-start) | copy-done | bytes 3145752
  2.5 1.9 %copy-done.2 = bf16[16,16,12,512]{3,1,2,0:T(8,128)(2,1)S(1)} copy-done((bf16[16,16,12,512]{3,1,2,0:T(8,128)(2,1)S(1)}, bf16[16,16,12,512]{3,1,2,0:T(8,128)(2,1)}, u32[]{:S(2)}) %copy-start.2) | copy-done | bytes 3145752
  4.4 0.9 %copy-done.9 = bf16[512,128]{1,0:T(8,128)(2,1)S(1)} copy-done((bf16[512,128]{1,0:T(8,128)(2,1)S(1)}, bf16[512,128]{1,0:T(8,128)(2,1)}, u32[]{:S(2)}) %copy-start.9) | copy-done | bytes 131096
  5.3 0.9 %copy-done.10 = bf16[512,128]{1,0:T(8,128)(2,1)S(1)} copy-done((bf16[512,128]{1,0:T(8,128)(2,1)S(1)}, bf16[512,128]{1,0:T(8,128)(2,1)}, u32[]{:S(2)}) %copy-start.10) | copy-done | bytes 131096
  6.2 0.8 %copy-done.13 = bf16[512,64]{0,1:T(8,128)(2,1)S(1)} copy-done((bf16[512,64]{0,1:T(8,128)(2,1)S(1)}, bf16[512,64]{0,1:T(8,128)(2,1)}, u32[]{:S(2)}) %copy-start.13) | copy-done | bytes 65560
  7.1 3.9 %project.1 = (bf16[3072,256]{1,0:T(8,128)(2,1)S(1)}, bf16[3072,128]{1,0:T(8,128)(2,1)S(1)}, f32[64,256]{1,0:T(8,128)S(1)}, bf16[512,256]{1,0:T(8,128)(2,1)S(1)}) custom-call(bf16[3072,512]{1,0:T(8,128)(2,1)S(1)} %bitcast.20, bf16[3072,512]{1,0:T(8,128)(2,1)S(1)} %bitcast.17, bf16[512,128]{1,0:T(8,128)(2,1)S(1)} %copy-done.9, bf16[64,512]{1,0:T(8,128)(2,1)S(1)} %bitcast.26, ...), custom_call_target="tpu_custom_call" | custom-call | flops 1610612736 | bytes 8650752 | tf_op jit(solution)/shard_map/project/pallas_call | solution.py:72
  11.7 4.0 %weight_terms.1 = (f32[4,64,384]{2,1,0:T(8,128)S(1)}, f32[4,64,384]{2,1,0:T(8,128)}) custom-call(s32[1]{0:T(128)} %bitcast.9.index_ref, bf16[3072,512]{1,0:T(8,128)(2,1)S(1)} %bitcast.21, bf16[3072,512]{1,0:T(8,128)(2,1)S(1)} %bitcast.18, bf16[3072,256]{1,0:T(8,128)(2,1)S(1)} %get-tuple-element.30.refs_8_.rd_ref, ...), custom_call_target="tpu_custom_call" | custom-call | flops 1610612736 | bytes 9437184 | tf_op jit(solution)/shard_map/weight_terms/pallas_call | solution.py:136
  16.2 1.4 %collective-permute-done = f32[64,256]{1,0:T(8,128)S(1)} collective-permute-done((f32[64,256]{1,0:T(8,128)S(1)}, f32[64,256]{1,0:T(8,128)S(1)}, u32[]{:S(2)}, u32[]{:S(2)}) %collective-permute-start) | collective-permute-done | bytes 65568 | tf_op jit(solution)/shard_map/ppermute | solution.py:180
  18.3 3.8 %collective-permute-start.3 = (f32[64,256]{1,0:T(8,128)}, f32[64,256]{1,0:T(8,128)}, u32[]{:S(2)}, u32[]{:S(2)}) collective-permute-start(f32[64,256]{1,0:T(8,128)} %add.12), channel_id=1, source_target_pairs={{0,24},{8,16},{16,8},{24,0},{1,25},{9,17},{17,9},{25,1},{2,26},{10... | collective-permute-start | bytes 196616 | tf_op jit(solution)/shard_map/ppermute | solution.py:180
  22.6 1.8 %split.2 = (f32[64,384]{1,0:T(8,128)S(1)}, f32[64,384]{1,0:T(8,128)S(1)}, f32[64,384]{1,0:T(8,128)}, f32[64,384]{1,0:T(8,128)}) custom-call(s32[1]{0:T(128)} %bitcast.8.index_ref, f32[4,64,384]{2,1,0:T(8,128)S(1)} %get-tuple-element.33.refs_0_, f32[4,64,384]{2,1,0:T(8,128)} %collective-permute-done.7.refs_1_), custom_call_target="tpu_custom_call" | custom-call | bytes 1572864 | tf_op jit(solution)/shard_map/split/pallas_call | solution.py:167
  24.4 2.0 %collective-permute-start.8 = (f32[64,384]{1,0:T(8,128)S(1)}, f32[64,384]{1,0:T(8,128)S(1)}, u32[]{:S(2)}, u32[]{:S(2)}) collective-permute-start(f32[64,384]{1,0:T(8,128)S(1)} %get-tuple-element.36), channel_id=1, source_target_pairs={{0,8},{8,0},{16,24},{24,16},{1,9},{9,1},{17,25},{25,17},{2,10},{10... | collective-permute-start | bytes 294920 | tf_op jit(solution)/shard_map/ppermute | solution.py:180
  26.4 1.5 %collective-permute-start.9 = (f32[64,384]{1,0:T(8,128)}, f32[64,384]{1,0:T(8,128)S(1)}, u32[]{:S(2)}, u32[]{:S(2)}) collective-permute-start(f32[64,384]{1,0:T(8,128)} %get-tuple-element.37), channel_id=1, source_target_pairs={{0,16},{8,24},{16,0},{24,8},{1,17},{9,25},{17,1},{25,9},{2,18},{10... | collective-permute-start | bytes 294920 | tf_op jit(solution)/shard_map/ppermute | solution.py:180
  28.1 1.0 %add_add_fusion.refs_0_ = f32[64,256]{1,0:T(8,128)S(1)} fusion(f32[64,256]{1,0:T(8,128)} %collective-permute-done.3, f32[64,256]{1,0:T(8,128)} %collective-permute-done.2, f32[64,256]{1,0:T(8,128)} %add.12, f32[64,256]{1,0:T(8,128)} %collective-permute-done.1), kind=kLoop, calls=%fused_computation | loop fusion | flops 49152 | bytes 327680 | tf_op jit(solution)/shard_map/add | solution.py:319
  29.1 3.9 %collective-permute-start.6 = (f32[64,256]{1,0:T(8,128)S(1)}, f32[64,256]{1,0:T(8,128)}, u32[]{:S(2)}, u32[]{:S(2)}) collective-permute-start(f32[64,256]{1,0:T(8,128)S(1)} %add_add_fusion.refs_0_), channel_id=1, source_target_pairs={{0,3},{1,2},{2,1},{3,0},{4,7},{5,6},{6,5},{7,4},{8,11},{9,10},{10,... | collective-permute-start | bytes 196616 | tf_op jit(solution)/shard_map/ppermute | solution.py:180
  33.7 0.9 %copy-done.12 = f32[64,384]{1,0:T(8,128)S(1)} copy-done((f32[64,384]{1,0:T(8,128)S(1)}, f32[64,384]{1,0:T(8,128)}, u32[]{:S(2)}) %copy-start.12) | copy-done | bytes 98328
  34.6 1.6 %collective-permute-start.11 = (f32[16,384]{1,0:T(8,128)S(1)}, f32[16,384]{1,0:T(8,128)S(1)}, u32[]{:S(2)}, u32[]{:S(2)}) collective-permute-start(f32[16,384]{1,0:T(8,128)S(1)} %get-tuple-element.40), channel_id=1, source_target_pairs={{0,1},{1,0},{2,3},{3,2},{4,5},{5,4},{6,7},{7,6},{8,9},{9,8},{10,11... | collective-permute-start | bytes 73736 | tf_op jit(solution)/shard_map/ppermute | solution.py:180
  36.2 2.8 %collective-permute-start.12 = (f32[16,384]{1,0:T(8,128)S(1)}, f32[16,384]{1,0:T(8,128)S(1)}, u32[]{:S(2)}, u32[]{:S(2)}) collective-permute-start(f32[16,384]{1,0:T(8,128)S(1)} %get-tuple-element.41), channel_id=1, source_target_pairs={{0,2},{1,3},{2,0},{3,1},{4,6},{5,7},{6,4},{7,5},{8,10},{9,11},{10,... | collective-permute-start | bytes 73736 | tf_op jit(solution)/shard_map/ppermute | solution.py:180
  39.5 1.4 %copy-done.4 = bf16[3072,256]{1,0:T(8,128)(2,1)S(1)} copy-done((bf16[3072,256]{1,0:T(8,128)(2,1)S(1)}, bf16[3072,256]{1,0:T(8,128)(2,1)}, u32[]{:S(2)}) %copy-start.4) | copy-done | bytes 1572888
  40.9 1.1 %copy-done.6 = bf16[3072,128]{1,0:T(8,128)(2,1)S(1)} copy-done((bf16[3072,128]{1,0:T(8,128)(2,1)S(1)}, bf16[3072,128]{1,0:T(8,128)(2,1)}, u32[]{:S(2)}) %copy-start.6) | copy-done | bytes 786456
  42.1 0.9 %copy-done.8 = bf16[512,256]{1,0:T(8,128)(2,1)S(1)} copy-done((bf16[512,256]{1,0:T(8,128)(2,1)S(1)}, bf16[512,256]{1,0:T(8,128)(2,1)}, u32[]{:S(2)}) %copy-start.8) | copy-done | bytes 262168
  43.0 0.8 %copy-done.14 = f32[128,128]{1,0:T(8,128)S(1)} copy-done((f32[128,128]{1,0:T(8,128)S(1)}, f32[128,128]{1,0:T(8,128)}, u32[]{:S(2)}) %copy-start.14) | copy-done | bytes 65560
  43.8 0.8 %copy-done.15 = f32[64,64]{1,0:T(8,128)S(1)} copy-done((f32[64,64]{1,0:T(8,128)S(1)}, f32[64,64]{1,0:T(8,128)}, u32[]{:S(2)}) %copy-start.15) | copy-done | bytes 16408
  44.6 6.2 %feature_grads.1 = (bf16[3072,512]{1,0:T(8,128)(2,1)}, f32[64,64]{1,0:T(8,128)}, f32[128,128]{1,0:T(8,128)}, f32[64,128]{1,0:T(8,128)S(1)}, f32[64,128]{1,0:T(8,128)S(1)}) custom-call(f32[64,256]{1,0:T(8,128)S(1)} %add_add_fusion.refs_0_, f32[64,256]{1,0:T(8,128)} %collective-permute-done.4.refs_1_, f32[64,256]{1,0:T(8,128)} %collective-permute-done.5.refs_2_, ...), custom_call_target="tpu_custom_call" | custom-call | flops 1610612736 | bytes 8650752 | tf_op jit(solution)/shard_map/feature_grads/pallas_call | solution.py:234
  50.8 0.9 %finish.1 = (f32[16,128]{1,0:T(8,128)}, f32[16,64]{1,0:T(8,128)}, f32[16,128]{1,0:T(8,128)}) custom-call(f32[16,384]{1,0:T(8,128)S(1)} %get-tuple-element.39.refs_0_, f32[16,384]{1,0:T(8,128)S(1)} %collective-permute-done.11.refs_1_, f32[16,384]{1,0:T(8,128)S(1)} %collective-permute-done.12.refs_2_, f32[16,384]{1,0:T(8,128)S(1)} %collective-permute-done.13.refs_3_, ...), custom_call_target="tpu_custom_call" | custom-call | bytes 65536 | tf_op jit(solution)/shard_map/finish/pallas_call | solution.py:288
  (44 shorter events, 4.0 us)
Async XLA Ops:
  0.6 1.9 %copy-start = (bf16[16,16,12,512]{3,1,2,0:T(8,128)(2,1)S(1)}, bf16[16,16,12,512]{3,1,2,0:T(8,128)(2,1)}, u32[]{:S(2)}) copy-start(bf16[16,16,12,512]{3,1,2,0:T(8,128)(2,1)} %param.8) | copy-start | bytes 9437188
  2.5 1.9 %copy-start.2 = (bf16[16,16,12,512]{3,1,2,0:T(8,128)(2,1)S(1)}, bf16[16,16,12,512]{3,1,2,0:T(8,128)(2,1)}, u32[]{:S(2)}) copy-start(bf16[16,16,12,512]{3,1,2,0:T(8,128)(2,1)} %param.7) | copy-start | bytes 9437188
  4.4 0.9 %copy-start.9 = (bf16[512,128]{1,0:T(8,128)(2,1)S(1)}, bf16[512,128]{1,0:T(8,128)(2,1)}, u32[]{:S(2)}) copy-start(bf16[512,128]{1,0:T(8,128)(2,1)} %wr_ref.1) | copy-start | bytes 393220
  11.7 4.0 %copy-start.3 = (bf16[3072,256]{1,0:T(8,128)(2,1)}, bf16[3072,256]{1,0:T(8,128)(2,1)S(1)}, u32[]{:S(2)}) copy-start(bf16[3072,256]{1,0:T(8,128)(2,1)S(1)} %get-tuple-element.30.refs_8_.rd_ref) | copy-start | bytes 4718596
  11.7 4.0 %copy-start.5 = (bf16[3072,128]{1,0:T(8,128)(2,1)}, bf16[3072,128]{1,0:T(8,128)(2,1)S(1)}, u32[]{:S(2)}) copy-start(bf16[3072,128]{1,0:T(8,128)(2,1)S(1)} %get-tuple-element.31.refs_9_.p_ref) | copy-start | bytes 2359300
  11.7 27.8 %copy-start.1 = (bf16[16,16,12,512]{3,1,2,0:T(8,128)(2,1)S(1)}, bf16[16,16,12,512]{3,1,2,0:T(8,128)(2,1)}, u32[]{:S(2)}) copy-start(bf16[16,16,12,512]{3,1,2,0:T(8,128)(2,1)} %param.8) | copy-start | bytes 9437188
  15.7 7.0 %collective-permute-start.7 = (f32[4,64,384]{2,1,0:T(8,128)}, f32[4,64,384]{2,1,0:T(8,128)}, u32[]{:S(2)}, u32[]{:S(2)}) collective-permute-start(f32[4,64,384]{2,1,0:T(8,128)} %get-tuple-element.34), channel_id=1, source_target_pairs={{0,4},{4,0},{1,5},{5,1},{2,6},{6,2},{3,7},{7,3},{8,12},{12,8},{9,1... | collective-permute-start | bytes 1179656 | tf_op jit(solution)/shard_map/ppermute | solution.py:180
  16.2 1.4 %collective-permute-start = (f32[64,256]{1,0:T(8,128)S(1)}, f32[64,256]{1,0:T(8,128)S(1)}, u32[]{:S(2)}, u32[]{:S(2)}) collective-permute-start(f32[64,256]{1,0:T(8,128)S(1)} %get-tuple-element.28), channel_id=1, source_target_pairs={{0,4},{4,0},{1,5},{5,1},{2,6},{6,2},{3,7},{7,3},{8,12},{12,8},{9,1... | collective-permute-start | bytes 196616 | tf_op jit(solution)/shard_map/ppermute | solution.py:180
  18.3 9.6 %collective-permute-start.3 = (f32[64,256]{1,0:T(8,128)}, f32[64,256]{1,0:T(8,128)}, u32[]{:S(2)}, u32[]{:S(2)}) collective-permute-start(f32[64,256]{1,0:T(8,128)} %add.12), channel_id=1, source_target_pairs={{0,24},{8,16},{16,8},{24,0},{1,25},{9,17},{17,9},{25,1},{2,26},{10... | collective-permute-start | bytes 196616 | tf_op jit(solution)/shard_map/ppermute | solution.py:180
  22.0 6.1 %collective-permute-start.2 = (f32[64,256]{1,0:T(8,128)}, f32[64,256]{1,0:T(8,128)}, u32[]{:S(2)}, u32[]{:S(2)}) collective-permute-start(f32[64,256]{1,0:T(8,128)} %add.12), channel_id=1, source_target_pairs={{0,16},{8,24},{16,0},{24,8},{1,17},{9,25},{17,1},{25,9},{2,18},{10... | collective-permute-start | bytes 196616 | tf_op jit(solution)/shard_map/ppermute | solution.py:180
  22.6 5.5 %collective-permute-start.1 = (f32[64,256]{1,0:T(8,128)}, f32[64,256]{1,0:T(8,128)}, u32[]{:S(2)}, u32[]{:S(2)}) collective-permute-start(f32[64,256]{1,0:T(8,128)} %add.12), channel_id=1, source_target_pairs={{0,8},{8,0},{16,24},{24,16},{1,9},{9,1},{17,25},{25,17},{2,10},{10... | collective-permute-start | bytes 196616 | tf_op jit(solution)/shard_map/ppermute | solution.py:180
  24.4 8.6 %copy-start.11 = (f32[64,384]{1,0:T(8,128)}, f32[64,384]{1,0:T(8,128)S(1)}, u32[]{:S(2)}) copy-start(f32[64,384]{1,0:T(8,128)S(1)} %get-tuple-element.35) | copy-start | bytes 294916
  24.4 8.6 %collective-permute-start.8 = (f32[64,384]{1,0:T(8,128)S(1)}, f32[64,384]{1,0:T(8,128)S(1)}, u32[]{:S(2)}, u32[]{:S(2)}) collective-permute-start(f32[64,384]{1,0:T(8,128)S(1)} %get-tuple-element.36), channel_id=1, source_target_pairs={{0,8},{8,0},{16,24},{24,16},{1,9},{9,1},{17,25},{25,17},{2,10},{10... | collective-permute-start | bytes 294920 | tf_op jit(solution)/shard_map/ppermute | solution.py:180
  26.4 7.3 %collective-permute-start.9 = (f32[64,384]{1,0:T(8,128)}, f32[64,384]{1,0:T(8,128)S(1)}, u32[]{:S(2)}, u32[]{:S(2)}) collective-permute-start(f32[64,384]{1,0:T(8,128)} %get-tuple-element.37), channel_id=1, source_target_pairs={{0,16},{8,24},{16,0},{24,8},{1,17},{9,25},{17,1},{25,9},{2,18},{10... | collective-permute-start | bytes 294920 | tf_op jit(solution)/shard_map/ppermute | solution.py:180
  27.9 5.8 %collective-permute-start.10 = (f32[64,384]{1,0:T(8,128)}, f32[64,384]{1,0:T(8,128)S(1)}, u32[]{:S(2)}, u32[]{:S(2)}) collective-permute-start(f32[64,384]{1,0:T(8,128)} %get-tuple-element.38), channel_id=1, source_target_pairs={{0,24},{8,16},{16,8},{24,0},{1,25},{9,17},{17,9},{25,1},{2,26},{10... | collective-permute-start | bytes 294920 | tf_op jit(solution)/shard_map/ppermute | solution.py:180
  29.1 9.9 %collective-permute-start.6 = (f32[64,256]{1,0:T(8,128)S(1)}, f32[64,256]{1,0:T(8,128)}, u32[]{:S(2)}, u32[]{:S(2)}) collective-permute-start(f32[64,256]{1,0:T(8,128)S(1)} %add_add_fusion.refs_0_), channel_id=1, source_target_pairs={{0,3},{1,2},{2,1},{3,0},{4,7},{5,6},{6,5},{7,4},{8,11},{9,10},{10,... | collective-permute-start | bytes 196616 | tf_op jit(solution)/shard_map/ppermute | solution.py:180
  33.0 6.5 %collective-permute-start.5 = (f32[64,256]{1,0:T(8,128)S(1)}, f32[64,256]{1,0:T(8,128)}, u32[]{:S(2)}, u32[]{:S(2)}) collective-permute-start(f32[64,256]{1,0:T(8,128)S(1)} %add_add_fusion.refs_0_), channel_id=1, source_target_pairs={{0,2},{1,3},{2,0},{3,1},{4,6},{5,7},{6,4},{7,5},{8,10},{9,11},{10,... | collective-permute-start | bytes 196616 | tf_op jit(solution)/shard_map/ppermute | solution.py:180
  33.0 6.5 %collective-permute-start.4 = (f32[64,256]{1,0:T(8,128)S(1)}, f32[64,256]{1,0:T(8,128)}, u32[]{:S(2)}, u32[]{:S(2)}) collective-permute-start(f32[64,256]{1,0:T(8,128)S(1)} %add_add_fusion.refs_0_), channel_id=1, source_target_pairs={{0,1},{1,0},{2,3},{3,2},{4,5},{5,4},{6,7},{7,6},{8,9},{9,8},{10,11... | collective-permute-start | bytes 196616 | tf_op jit(solution)/shard_map/ppermute | solution.py:180
  34.6 16.2 %collective-permute-start.11 = (f32[16,384]{1,0:T(8,128)S(1)}, f32[16,384]{1,0:T(8,128)S(1)}, u32[]{:S(2)}, u32[]{:S(2)}) collective-permute-start(f32[16,384]{1,0:T(8,128)S(1)} %get-tuple-element.40), channel_id=1, source_target_pairs={{0,1},{1,0},{2,3},{3,2},{4,5},{5,4},{6,7},{7,6},{8,9},{9,8},{10,11... | collective-permute-start | bytes 73736 | tf_op jit(solution)/shard_map/ppermute | solution.py:180
  36.2 14.6 %collective-permute-start.12 = (f32[16,384]{1,0:T(8,128)S(1)}, f32[16,384]{1,0:T(8,128)S(1)}, u32[]{:S(2)}, u32[]{:S(2)}) collective-permute-start(f32[16,384]{1,0:T(8,128)S(1)} %get-tuple-element.41), channel_id=1, source_target_pairs={{0,2},{1,3},{2,0},{3,1},{4,6},{5,7},{6,4},{7,5},{8,10},{9,11},{10,... | collective-permute-start | bytes 73736 | tf_op jit(solution)/shard_map/ppermute | solution.py:180
  39.0 11.8 %collective-permute-start.13 = (f32[16,384]{1,0:T(8,128)S(1)}, f32[16,384]{1,0:T(8,128)S(1)}, u32[]{:S(2)}, u32[]{:S(2)}) collective-permute-start(f32[16,384]{1,0:T(8,128)S(1)} %get-tuple-element.42), channel_id=1, source_target_pairs={{0,3},{1,2},{2,1},{3,0},{4,7},{5,6},{6,5},{7,4},{8,11},{9,10},{10,... | collective-permute-start | bytes 73736 | tf_op jit(solution)/shard_map/ppermute | solution.py:180
  39.5 1.4 %copy-start.4 = (bf16[3072,256]{1,0:T(8,128)(2,1)S(1)}, bf16[3072,256]{1,0:T(8,128)(2,1)}, u32[]{:S(2)}) copy-start(bf16[3072,256]{1,0:T(8,128)(2,1)} %copy-done.3) | copy-start | bytes 4718596
  40.9 1.1 %copy-start.6 = (bf16[3072,128]{1,0:T(8,128)(2,1)S(1)}, bf16[3072,128]{1,0:T(8,128)(2,1)}, u32[]{:S(2)}) copy-start(bf16[3072,128]{1,0:T(8,128)(2,1)} %copy-done.5) | copy-start | bytes 2359300
  42.1 0.9 %copy-start.8 = (bf16[512,256]{1,0:T(8,128)(2,1)S(1)}, bf16[512,256]{1,0:T(8,128)(2,1)}, u32[]{:S(2)}) copy-start(bf16[512,256]{1,0:T(8,128)(2,1)} %copy-done.7) | copy-start | bytes 786436
  (6 other events, 5.0 us)

commit v2 on v1

v2 whole, which is shorter than its diff:
```python
import functools
import math

import jax
import jax.numpy as jnp
from jax import lax
from jax.experimental import pallas as pl
from jax.experimental.pallas import tpu as pltpu
from jax.sharding import PartitionSpec as P

AXES = ("gx", "gy", "gz")
F32 = jnp.float32
BF16 = jnp.bfloat16
HBM = pl.BlockSpec(memory_space=pltpu.HBM)
VMEM = pl.BlockSpec(memory_space=pltpu.VMEM)
SMEM = pl.BlockSpec(memory_space=pltpu.SMEM)
VMEM_LIMIT = 24 * 1024 * 1024


def exact(a, b, dims=((1,), (0,))):
    return lax.dot_general(
        a, b, (dims, ((), ())), precision=lax.Precision.HIGHEST, preferred_element_type=F32
    )


def mxu(a, b, dims=((1,), (0,))):
    return lax.dot_general(a, b, (dims, ((), ())), preferred_element_type=F32)


def held(shape, kind):
    return pltpu.VMEM(shape, kind)


def params():
    return pltpu.CompilerParams(vmem_limit_bytes=VMEM_LIMIT)


def cost(flops, nbytes):
    return pl.CostEstimate(flops=flops, bytes_accessed=nbytes, transcendentals=0)


def row_block(total):
    for size in (512, 384, 256, 128, 64, 32, 16):
        if total % size == 0:
            return size
    return total


def project_kernel(
    step, x_hbm, g_hbm, wr_hbm, wpt_hbm, we_hbm, adj_hbm, nw_hbm,
    x_ref, g_ref, rd_ref, p_ref, term_ref, wcat_ref, adj_ref, nw_ref, wpt_ref, we_ref, sems, xsem, gsem,
):
    rows = x_ref.shape[0]
    nodes = wpt_ref.shape[0]
    cr = we_ref.shape[1]
    chunks = [pl.ds(start, step) for start in range(0, rows, step)]
    load = lambda src, dst, sem: pltpu.make_async_copy(src, dst, sem)
    small = [
        load(wr_hbm, wcat_ref.at[:, pl.ds(0, cr)], sems.at[0]),
        load(wpt_hbm, wpt_ref, sems.at[1]),
        load(we_hbm, we_ref, sems.at[2]),
        load(adj_hbm, adj_ref, sems.at[3]),
        load(nw_hbm, nw_ref, sems.at[4]),
    ]
    xs = [load(x_hbm.at[c], x_ref.at[c], xsem.at[i]) for i, c in enumerate(chunks)]
    gs = [load(g_hbm.at[c], g_ref.at[c], gsem.at[i]) for i, c in enumerate(chunks)]
    for copy in small[:3]:
        copy.start()
    for x_copy, g_copy in zip(xs, gs):
        x_copy.start()
        g_copy.start()
    for copy in small[3:]:
        copy.start()
    for copy in small[:3]:
        copy.wait()
    padded = jnp.concatenate([wpt_ref[...], jnp.zeros_like(wpt_ref)], axis=0)
    wcat_ref[:, cr:] = padded.T
    for i, c in enumerate(chunks):
        xs[i].wait()
        both = mxu(x_ref[c], wcat_ref[...]).astype(BF16)
        gs[i].wait()
        mapped = mxu(g_ref[c], we_ref[...]).astype(BF16)
        rd = jnp.concatenate([both[:, :cr], mapped], axis=1)
        proj = both[:, cr:]
        rd_ref[c] = rd
        p_ref[c] = proj
        part = mxu(proj, rd, ((0,), (0,)))[:nodes]
        if i == 0:
            term_ref[:nodes] = part[:, :cr]
            term_ref[nodes:] = part[:, cr:]
        else:
            term_ref[:nodes] += part[:, :cr]
            term_ref[nodes:] += part[:, cr:]
    for copy in small[3:]:
        copy.wait()


def project(x, g, wr, wpt, we, adjacency, node_weight):
    rows, chan = x.shape
    cr, nodes = wr.shape[1], wpt.shape[0]
    step = row_block(rows)
    return pl.pallas_call(
        functools.partial(project_kernel, step),
        in_specs=[HBM] * 7,
        out_specs=[VMEM] * 8,
        out_shape=[
            held((rows, chan), BF16),
            held((rows, chan), BF16),
            held((rows, 2 * cr), BF16),
            held((rows, 2 * nodes), BF16),
            held((2 * nodes, cr), F32),
            held((chan, cr + 2 * nodes), BF16),
            held(adjacency.shape, F32),
            held(node_weight.shape, F32),
        ],
        scratch_shapes=[
            pltpu.VMEM(wpt.shape, BF16),
            pltpu.VMEM(we.shape, BF16),
            pltpu.SemaphoreType.DMA((5,)),
            pltpu.SemaphoreType.DMA((rows // step,)),
            pltpu.SemaphoreType.DMA((rows // step,)),
        ],
        compiler_params=params(),
        cost_estimate=cost(2 * rows * chan * 512, rows * chan * 4 + rows * 768),
        name="project",
    )(*(pltpu.with_memory_space_constraint(v, pltpu.HBM) for v in (x, g, wr, wpt, we, adjacency, node_weight)))


def weight_kernel(step, count, index_ref, x_ref, g_ref, rd_ref, p_ref, *rest):
    outs, (sums_ref, turned_ref) = rest[:count], rest[count:]
    rows = x_ref.shape[0]
    nodes = p_ref.shape[1] // 2
    wide = rd_ref.shape[1]
    for start in range(0, rows, step):
        c = pl.ds(start, step)
        proj = p_ref[c][:, :nodes]
        x = x_ref[c]
        pieces = (
            mxu(rd_ref[c], x, ((0,), (0,))),
            mxu(proj, x, ((0,), (0,))),
            mxu(proj, g_ref[c], ((0,), (0,))),
        )
        at = 0
        for piece in pieces:
            span = pl.ds(at, piece.shape[0])
            at += piece.shape[0]
            if start == 0:
                sums_ref[span] = piece
            else:
                sums_ref[span] += piece
    turned_ref[...] = sums_ref[...].T.reshape(turned_ref.shape)
    me = index_ref[0]
    for peer in range(count):
        outs[peer][...] = turned_ref[:, lax.bitwise_xor(me, peer)]


def weight_terms(x, g, rd, p, index, sizes):
    rows, chan = x.shape
    step = row_block(rows)
    gx, gy, gz = sizes
    width = rd.shape[1] + p.shape[1]
    part = (gx, chan // (gx * gy), width)
    return pl.pallas_call(
        functools.partial(weight_kernel, step, gy),
        in_specs=[SMEM] + [VMEM] * 4,
        out_specs=[VMEM] * gy,
        out_shape=[held(part, F32)] * gy,
        scratch_shapes=[
            pltpu.VMEM((width, chan), F32),
            pltpu.VMEM((gx, gy, chan // (gx * gy), width), F32),
        ],
        compiler_params=params(),
        cost_estimate=cost(2 * rows * chan * 512, rows * chan * 4 + rows * 768 + width * chan * 4),
        name="weight_terms",
    )(index, x, g, rd, p)


def split_kernel(ins, count, index_ref, *refs):
    outs, total_ref = refs[ins:-1], refs[-1]
    total = refs[0][...]
    for ref in refs[1:ins]:
        total = total + ref[...]
    total_ref[...] = total
    me = index_ref[0]
    for peer in range(count):
        outs[peer][...] = total_ref[lax.bitwise_xor(me, peer)]


def split(parts, count, index):
    first, third, width = parts[0].shape
    if first != count:
        parts = [p.reshape(count, third // count, width) for p in parts]
    shape = parts[0].shape
    return pl.pallas_call(
        functools.partial(split_kernel, len(parts), count),
        in_specs=[SMEM] + [VMEM] * len(parts),
        out_specs=[VMEM] * count,
        out_shape=[held(shape[1:], F32)] * count,
        scratch_shapes=[pltpu.VMEM(shape, F32)],
        compiler_params=params(),
        cost_estimate=cost(0, 8 * math.prod(shape) * len(parts)),
        name="split",
    )(index, *parts)


def share_kernel(in_ref, out_ref):
    total = jnp.sum(in_ref[...], axis=0, keepdims=True)
    out_ref[...] = jnp.broadcast_to(total, out_ref.shape)


def share(value):
    return pl.pallas_call(
        share_kernel,
        in_specs=[VMEM],
        out_specs=VMEM,
        out_shape=held(value.shape, F32),
        compiler_params=params(),
        name="share",
    )(value)


def node_sum(term):
    devices = math.prod(lax.axis_size(axis) for axis in AXES)
    shape = term.shape
    if term.size % (devices * 128):
        return lax.psum(term, AXES)
    lanes = min(128, term.size // devices)
    parts = term.reshape(devices, -1, lanes)
    got = lax.all_to_all(parts, AXES, 0, 0, tiled=True)
    return lax.all_to_all(share(got), AXES, 0, 0, tiled=True).reshape(shape)


def swap(value, axis, peer):
    size = lax.axis_size(axis)
    return lax.ppermute(value, axis, [(i, i ^ peer) for i in range(size)])


def feature_kernel(
    step, scale, total_ref, adj_ref, nw_ref, wcat_ref, g_ref, rd_ref, p_ref,
    out_hbm, ga_ref, gn_ref, no_ref, dn_ref, out_ref, mix_ref, dnb_ref, sems,
):
    nodes_n, cr = no_ref.shape
    rows = g_ref.shape[0]
    adj, nw = adj_ref[...], nw_ref[...]
    nodes = scale * total_ref[:nodes_n]
    d_node_out = total_ref[nodes_n:]
    hidden = nodes - exact(adj, nodes)
    pre = exact(hidden, nw)
    node_out = jnp.maximum(pre, 0.0).astype(BF16)
    d_pre = jnp.where(pre > 0.0, d_node_out, 0.0)
    d_hidden = exact(d_pre, nw, ((1,), (1,)))
    d_nodes = d_hidden - exact(adj, d_hidden, ((0,), (0,)))
    dn = d_nodes.astype(BF16)
    no_ref[...] = node_out.astype(F32)
    dn_ref[...] = dn.astype(F32)
    dnb_ref[:nodes_n] = dn
    dnb_ref[nodes_n:] = jnp.zeros((nodes_n, cr), BF16)
    blank = jnp.zeros((cr, cr), BF16)
    zero = jnp.zeros((nodes_n, cr), F32)
    mix_ref[:cr, :cr] = jnp.concatenate([dn.astype(F32), zero], axis=0).T.astype(BF16)
    mix_ref[cr:, :cr] = blank
    mix_ref[:cr, cr:] = blank
    mix_ref[cr:, cr:] = jnp.concatenate([node_out.astype(F32), zero], axis=0).T.astype(BF16)
    copies = []
    for i, start in enumerate(range(0, rows, step)):
        c = pl.ds(start, step)
        mixed = mxu(rd_ref[c], mix_ref[...])
        d_proj = (mixed[:, cr:] + scale * mixed[:, :cr]).astype(BF16)
        d_red = (scale * mxu(p_ref[c], dnb_ref[...])).astype(BF16)
        both = jnp.concatenate([d_red, d_proj], axis=1)
        out = g_ref[c].astype(F32) + mxu(both, wcat_ref[...], ((1,), (1,)))
        out_ref[c] = out.astype(BF16)
        copies.append(pltpu.make_async_copy(out_ref.at[c], out_hbm.at[c], sems.at[i]))
        copies[-1].start()
    gn_ref[...] = scale * exact(hidden, d_pre, ((0,), (0,)))
    ga_ref[...] = -scale * exact(d_hidden, nodes, ((1,), (1,)))
    for copy in copies:
        copy.wait()


def feature_grads(total, adjacency, node_weight, wcat, g, rd, p, scale):
    rows, chan = g.shape
    nodes, cr = adjacency.shape[0], node_weight.shape[0]
    step = row_block(rows)
    return pl.pallas_call(
        functools.partial(feature_kernel, step, scale),
        in_specs=[VMEM] * 7,
        out_specs=[HBM] + [VMEM] * 4,
        out_shape=[
            pltpu.HBM((rows, chan), BF16),
            held((nodes, nodes), F32),
            held((cr, cr), F32),
            held((nodes, cr), F32),
            held((nodes, cr), F32),
        ],
        scratch_shapes=[
            pltpu.VMEM((rows, chan), BF16),
            pltpu.VMEM((2 * cr, 2 * cr), BF16),
            pltpu.VMEM((2 * nodes, cr), BF16),
            pltpu.SemaphoreType.DMA((rows // step,)),
        ],
        compiler_params=params(),
        cost_estimate=cost(2 * rows * 4 * 65536, rows * chan * 4 + rows * 768),
        name="feature_grads",
    )(total, adjacency, node_weight, wcat, g, rd, p)


def finish_kernel(ins, scale, *refs):
    total = refs[0][...]
    for ref in refs[1:ins]:
        total = total + ref[...]
    no_ref, dn_ref, gr_ref, gp_ref, ge_ref = refs[ins:]
    nodes, cr = no_ref.shape
    no, dn = no_ref[...], dn_ref[...]
    x_red, x_dm = total[:, :cr], total[:, cr : 2 * cr]
    cross = total[:, 2 * cr : 2 * cr + nodes]
    g_proj = total[:, 2 * cr + nodes :]
    gr_ref[...] = scale * scale * exact(cross, dn)
    gp_ref[...] = scale * exact(x_dm, no, ((1,), (1,))) + scale * scale * exact(
        x_red, dn, ((1,), (1,))
    )
    ge_ref[...] = scale * exact(g_proj, no)


def finish(parts, no, dn, scale):
    rows = parts[0].shape[0]
    nodes, cr = no.shape
    return pl.pallas_call(
        functools.partial(finish_kernel, len(parts), scale),
        in_specs=[VMEM] * (len(parts) + 2),
        out_specs=[VMEM] * 3,
        out_shape=[
            held((rows, cr), F32),
            held((rows, nodes), F32),
            held((rows, cr), F32),
        ],
        compiler_params=params(),
        cost_estimate=cost(0, rows * 4096),
        name="finish",
    )(*parts, no, dn)


def on_device(
    features, cotangent, reduce_weight, project_weight, expand_weight, adjacency, node_weight
):
    size_x, size_y, size_z, chan = features.shape
    local = size_x * size_y * size_z
    sizes = tuple(lax.axis_size(axis) for axis in AXES)
    total = local * math.prod(sizes)
    scale = 1.0 / math.sqrt(total)
    flat_x = features.transpose(0, 2, 1, 3).reshape(local, chan)
    flat_g = cotangent.transpose(0, 2, 1, 3).reshape(local, chan)
    where = {axis: lax.axis_index(axis).reshape(1).astype(jnp.int32) for axis in AXES}

    x, g, rd, p, term, wcat, adj, nw = project(
        flat_x, flat_g, reduce_weight, project_weight.T, expand_weight, adjacency, node_weight
    )
    total_term = node_sum(term)

    parts = weight_terms(x, g, rd, p, where["gy"], sizes)
    parts = [parts[0]] + [swap(part, "gy", k) for k, part in enumerate(parts) if k]
    for axis in ("gx", "gz"):
        parts = split(parts, lax.axis_size(axis), where[axis])
        parts = [parts[0]] + [swap(part, axis, k) for k, part in enumerate(parts) if k]
        if axis == "gx":
            parts = [part[None] for part in parts]

    flat_out, grad_adjacency, grad_node, no, dn = feature_grads(
        total_term, adj, nw, wcat, g, rd, p, scale
    )
    grad_reduce, grad_project, grad_expand = finish(parts, no, dn, scale)
    grad_features = flat_out.reshape(size_x, size_z, size_y, chan).transpose(0, 2, 1, 3)
    return (grad_features, grad_reduce, grad_project, grad_expand, grad_adjacency, grad_node)


def solution(mesh):
    return jax.shard_map(
        on_device,
        mesh=mesh,
        in_specs=(P("gx", "gy", "gz", None), P("gx", "gy", "gz", None), P(), P(), P(), P(), P()),
        out_specs=(
            P("gx", "gy", "gz", None),
            P(AXES, None),
            P(AXES, None),
            P(AXES, None),
            P(),
            P(),
        ),
        check_vma=False,
    )
```

time: 52.3 us -> 62.3 us (1.19)
  blocking collectives: 0 us -> 14.3 us
  starting transfers between devices: 18.1 us -> 11.7 us
  waiting for transfers between devices: 1.41 us -> 5.31 us
  other arithmetic: 1.59 us -> 0 us
  local copies, waits for them, and re-layouts: 13.1 us -> 12.2 us
  Pallas kernels: 16.8 us -> 17.6 us
    all_to_all x0 -> x1, blocking collectives: none -> 14.3 us  [node_sum(): got = lax.all_to_all(parts, AXES, 0, 0, tiled=True)]
    ppermute x14 -> x7, starting transfers between devices: 18.1 us -> 8.39 us  [swap(): return lax.ppermute(value, axis, [(i, i ^ peer) for i in range(size)])]
    ppermute x14 -> x7, waiting for transfers between devices: 1.41 us -> 5.31 us  [swap(): return lax.ppermute(value, axis, [(i, i ^ peer) for i in range(size)])]
    all_to_all x0 -> x1, starting transfers between devices: none -> 3.29 us  [node_sum(): return lax.all_to_all(share(got), AXES, 0, 0, tiled=True).reshape(shape)]
    add x2 -> x0, other arithmetic: 1.59 us -> none  [on_device(): held = terms[0] if len(terms) == 1 else functools.reduce(jnp.add, terms)]
    pallas_call x3 -> x4, Pallas kernels: 14 us -> 15.5 us  [the longest x1 8.05 us: project(): pl.pallas_call(functools.partial(project_kernel, step), in_specs=[HBM] *...]
    unnamed x32 -> x31, local copies, waits for them, and re-layouts: 13.1 us -> 12.2 us
  transfers between devices with their start and end apart: 14 -> 8, of which waited for: 1 -> 3; matrix products, arithmetic and copies ran while one was open for 3% -> 2% of each run, Pallas kernels for 16% -> 10%
where the time goes in v2:
time: 62.3 us; the launch traced here: 61.8 us
  Pallas kernels  17.6 us (28%)
  blocking collectives  14.3 us (23%)
  local copies, waits for them, and re-layouts  12.2 us (20%)
  starting transfers between devices  11.7 us (19%)
  waiting for transfers between devices  5.31 us (9%)
  between operations  0.72 us (1%)
    all_to_all x1, blocking collectives, node_sum(): got = lax.all_to_all(parts, AXES, 0, 0, tiled=True)  14.3 us
    unnamed x31, local copies, waits for them, and re-layouts  12.2 us
    ppermute x7, starting transfers between devices, swap(): return lax.ppermute(value, axis, [(i, i ^ peer) for i in range(size)])  8.39 us
    pallas_call x1, Pallas kernels, project(): pl.pallas_call(functools.partial(project_kernel, step), in_specs=[HBM] *...  8.05 us
    ppermute x7, waiting for transfers between devices, swap(): return lax.ppermute(value, axis, [(i, i ^ peer) for i in range(size)])  5.31 us
    pallas_call x1, Pallas kernels, feature_grads(): pl.pallas_call(functools.partial(feature_kernel, step, scale), in_specs=[...  4.4 us
    all_to_all x1, starting transfers between devices, node_sum(): return lax.all_to_all(share(got), AXES, 0, 0, tiled=True).reshape(shape)  3.29 us
    pallas_call x1, Pallas kernels, weight_terms(): pl.pallas_call(functools.partial(weight_kernel, step, gy), in_specs=[SMEM...  3.03 us
  transfers between devices with their start and end apart: 8, of which 3 were waited for; matrix products, arithmetic and copies ran while one was open for 2% of the time, Pallas kernels for 10%

profile of v2, /device:TPU:0, one launch (start us, length us, event | category | flops | bytes accessed | tf_op | source)
XLA Modules:
  0.0 61.8 jit_solution(1041200157545904363)
XLA Ops:
  0.6 8.1 %project.1 = (bf16[3072,512]{1,0:T(8,128)(2,1)S(1)}, bf16[3072,512]{1,0:T(8,128)(2,1)S(1)}, bf16[3072,256]{1,0:T(8,128)(2,1)S(1)}, bf16[3072,128]{1,0:T(8,128)(2...) custom-call(bf16[3072,512]{1,0:T(8,128)(2,1)} %bitcast.24, ...), custom_call_target="tpu_custom_call" | custom-call | flops 1610612736 | bytes 8650752 | tf_op jit(solution)/shard_map/project/pallas_call | solution.py:102
  8.7 0.7 %copy-done.7 = bf16[512,256]{1,0:T(8,128)(2,1)} copy-done((bf16[512,256]{1,0:T(8,128)(2,1)}, bf16[512,256]{1,0:T(8,128)(2,1)S(1)}, u32[]{:S(2)}) %copy-start.7) | copy-done | bytes 262168
  9.4 0.6 copy-done.9
  10.7 3.0 %weight_terms.1 = (f32[4,64,384]{2,1,0:T(8,128)S(1)}, f32[4,64,384]{2,1,0:T(8,128)}) custom-call(s32[1]{0:T(128)} %bitcast.11.index_ref, bf16[3072,512]{1,0:T(8,128)(2,1)S(1)} %get-tuple-element.40.x_ref, bf16[3072,512]{1,0:T(8,128)(2,1)S(1)} %get-tuple-element.36.g_ref, bf16[3072,256]{1,0:T(8,128)(2,1)S(1)} %get-tuple-element.37.rd_ref, ...), custom_call_target="tpu_custom_call" | custom-call | flops 1610612736 | bytes 9437184 | tf_op jit(solution)/shard_map/weight_terms/pallas_call | solution.py:163
  14.1 14.3 %all_to_all.10.in_ref = f32[32,4,128]{2,1,0:T(4,128)S(1)} all-to-all(f32[32,4,128]{2,1,0:T(4,128)S(1)} %bitcast.23), channel_id=1, replica_groups=mesh['gx'=4,'gy'=2,'gz'=4] {'gx','gy','gz'}, dimensions={0} | all-to-all | bytes 131072 | tf_op jit(solution)/shard_map/all_to_all | solution.py:229
  28.5 0.6 %copy-done.4 = f32[32,4,128]{2,1,0:T(4,128)} copy-done((f32[32,4,128]{2,1,0:T(4,128)}, f32[32,4,128]{2,1,0:T(4,128)S(1)}, u32[]{:S(2)}) %copy-start.4) | copy-done | bytes 65560
  29.1 3.3 %all-to-all-start.1 = ((f32[32,4,128]{2,1,0:T(4,128)}), f32[32,4,128]{2,1,0:T(4,128)}, u32[]{:S(2)}, u32[]{:S(2)}) async-start(f32[32,4,128]{2,1,0:T(4,128)} %copy-done.4), calls=%async_computation.1 | async-start | bytes 131072 | tf_op jit(solution)/shard_map/all_to_all | solution.py:230
  32.4 1.7 %split.2 = (f32[64,384]{1,0:T(8,128)S(1)}, f32[64,384]{1,0:T(8,128)}, f32[64,384]{1,0:T(8,128)}, f32[64,384]{1,0:T(8,128)}) custom-call(s32[1]{0:T(128)} %bitcast.10.index_ref, f32[4,64,384]{2,1,0:T(8,128)S(1)} %get-tuple-element.41.refs_0_, f32[4,64,384]{2,1,0:T(8,128)} %collective-permute-done.refs_1_), custom_call_target="tpu_custom_call" | custom-call | bytes 1572864 | tf_op jit(solution)/shard_map/split/pallas_call | solution.py:194
  34.1 0.6 %copy-done.5 = f32[64,384]{1,0:T(8,128)} copy-done((f32[64,384]{1,0:T(8,128)}, f32[64,384]{1,0:T(8,128)S(1)}, u32[]{:S(2)}) %copy-start.5) | copy-done | bytes 98328
  34.8 1.6 %collective-permute-start.1 = (f32[64,384]{1,0:T(8,128)}, f32[64,384]{1,0:T(8,128)S(1)}, u32[]{:S(2)}, u32[]{:S(2)}) collective-permute-start(f32[64,384]{1,0:T(8,128)} %get-tuple-element.44), channel_id=1, source_target_pairs={{0,8},{8,0},{16,24},{24,16},{1,9},{9,1},{17,25},{25,17},{2,10},{10... | collective-permute-start | bytes 294920 | tf_op jit(solution)/shard_map/ppermute | solution.py:235
  36.3 1.5 %collective-permute-start.2 = (f32[64,384]{1,0:T(8,128)}, f32[64,384]{1,0:T(8,128)S(1)}, u32[]{:S(2)}, u32[]{:S(2)}) collective-permute-start(f32[64,384]{1,0:T(8,128)} %get-tuple-element.45), channel_id=1, source_target_pairs={{0,16},{8,24},{16,0},{24,8},{1,17},{9,25},{17,1},{25,9},{2,18},{10... | collective-permute-start | bytes 294920 | tf_op jit(solution)/shard_map/ppermute | solution.py:235
  38.3 1.7 %collective-permute-done.1 = f32[64,384]{1,0:T(8,128)S(1)} collective-permute-done((f32[64,384]{1,0:T(8,128)}, f32[64,384]{1,0:T(8,128)S(1)}, u32[]{:S(2)}, u32[]{:S(2)}) %collective-permute-start.1) | collective-permute-done | bytes 98336 | tf_op jit(solution)/shard_map/ppermute | solution.py:235
  39.9 2.4 %collective-permute-done.2 = f32[64,384]{1,0:T(8,128)S(1)} collective-permute-done((f32[64,384]{1,0:T(8,128)}, f32[64,384]{1,0:T(8,128)S(1)}, u32[]{:S(2)}, u32[]{:S(2)}) %collective-permute-start.2) | collective-permute-done | bytes 98336 | tf_op jit(solution)/shard_map/ppermute | solution.py:235
  42.4 1.2 %collective-permute-done.3 = f32[64,384]{1,0:T(8,128)S(1)} collective-permute-done((f32[64,384]{1,0:T(8,128)}, f32[64,384]{1,0:T(8,128)S(1)}, u32[]{:S(2)}, u32[]{:S(2)}) %collective-permute-start.3) | collective-permute-done | bytes 98336 | tf_op jit(solution)/shard_map/ppermute | solution.py:235
  43.6 0.9 %copy-done.6 = f32[64,384]{1,0:T(8,128)S(1)} copy-done((f32[64,384]{1,0:T(8,128)S(1)}, f32[64,384]{1,0:T(8,128)}, u32[]{:S(2)}) %copy-start.6) | copy-done | bytes 98328
  44.5 1.6 %collective-permute-start.4 = (f32[16,384]{1,0:T(8,128)S(1)}, f32[16,384]{1,0:T(8,128)S(1)}, u32[]{:S(2)}, u32[]{:S(2)}) collective-permute-start(f32[16,384]{1,0:T(8,128)S(1)} %get-tuple-element.48), channel_id=1, source_target_pairs={{0,1},{1,0},{2,3},{3,2},{4,5},{5,4},{6,7},{7,6},{8,9},{9,8},{10,11... | collective-permute-start | bytes 73736 | tf_op jit(solution)/shard_map/ppermute | solution.py:235
  46.1 2.5 %collective-permute-start.5 = (f32[16,384]{1,0:T(8,128)S(1)}, f32[16,384]{1,0:T(8,128)S(1)}, u32[]{:S(2)}, u32[]{:S(2)}) collective-permute-start(f32[16,384]{1,0:T(8,128)S(1)} %get-tuple-element.49), channel_id=1, source_target_pairs={{0,2},{1,3},{2,0},{3,1},{4,6},{5,7},{6,4},{7,5},{8,10},{9,11},{10,... | collective-permute-start | bytes 73736 | tf_op jit(solution)/shard_map/ppermute | solution.py:235
  48.9 1.4 %copy-done.1 = bf16[3072,256]{1,0:T(8,128)(2,1)S(1)} copy-done((bf16[3072,256]{1,0:T(8,128)(2,1)S(1)}, bf16[3072,256]{1,0:T(8,128)(2,1)}, u32[]{:S(2)}) %copy-start.1) | copy-done | bytes 1572888
  50.4 1.1 %copy-done.3 = bf16[3072,128]{1,0:T(8,128)(2,1)S(1)} copy-done((bf16[3072,128]{1,0:T(8,128)(2,1)S(1)}, bf16[3072,128]{1,0:T(8,128)(2,1)}, u32[]{:S(2)}) %copy-start.3) | copy-done | bytes 786456
  51.5 0.9 %copy-done.8 = bf16[512,256]{1,0:T(8,128)(2,1)S(1)} copy-done((bf16[512,256]{1,0:T(8,128)(2,1)S(1)}, bf16[512,256]{1,0:T(8,128)(2,1)}, u32[]{:S(2)}) %copy-start.8) | copy-done | bytes 262168
  52.4 0.8 %copy-done.10 = f32[128,128]{1,0:T(8,128)S(1)} copy-done((f32[128,128]{1,0:T(8,128)S(1)}, f32[128,128]{1,0:T(8,128)}, u32[]{:S(2)}) %copy-start.10) | copy-done | bytes 65560
  53.3 0.8 %copy-done.12 = f32[64,64]{1,0:T(8,128)S(1)} copy-done((f32[64,64]{1,0:T(8,128)S(1)}, f32[64,64]{1,0:T(8,128)}, u32[]{:S(2)}) %copy-start.12) | copy-done | bytes 16408
  54.0 4.4 %feature_grads.1 = (bf16[3072,512]{1,0:T(8,128)(2,1)}, f32[64,64]{1,0:T(8,128)S(1)}, f32[128,128]{1,0:T(8,128)S(1)}, f32[64,128]{1,0:T(8,128)S(1)}, f32[64,128]{1,0:T(8,128)S(1)}) custom-call(f32[128,128]{1,0:T(8,128)} %bitcast.6.total_ref, f32[64,64]{1,0:T(8,128)S(1)} %copy-done.12, f32[128,128]{1,0:T(8,128)S(1)} %copy-done.10, ...), custom_call_target="tpu_custom_call" | custom-call | flops 1610612736 | bytes 8650752 | tf_op jit(solution)/shard_map/feature_grads/pallas_call | solution.py:285
  58.4 0.6 %copy.17 = f32[128,128]{1,0:T(8,128)} copy(f32[128,128]{1,0:T(8,128)S(1)} %get-tuple-element.63) | data formatting | bytes 131072
  (31 shorter events, 4.7 us)
Async XLA Ops:
  8.7 0.7 %copy-start.7 = (bf16[512,256]{1,0:T(8,128)(2,1)}, bf16[512,256]{1,0:T(8,128)(2,1)S(1)}, u32[]{:S(2)}) copy-start(bf16[512,256]{1,0:T(8,128)(2,1)S(1)} %get-tuple-element.35.wcat_ref) | copy-start | bytes 786436
  9.4 0.6 %copy-start.9 = (f32[128,128]{1,0:T(8,128)}, f32[128,128]{1,0:T(8,128)S(1)}, u32[]{:S(2)}) copy-start(f32[128,128]{1,0:T(8,128)S(1)} %get-tuple-element.34.nw_ref) | copy-start | bytes 196612
  10.0 0.6 copy-start.11
  10.7 3.0 %copy-start = (bf16[3072,256]{1,0:T(8,128)(2,1)}, bf16[3072,256]{1,0:T(8,128)(2,1)S(1)}, u32[]{:S(2)}) copy-start(bf16[3072,256]{1,0:T(8,128)(2,1)S(1)} %get-tuple-element.37.rd_ref) | copy-start | bytes 4718596
  10.7 3.0 %copy-start.2 = (bf16[3072,128]{1,0:T(8,128)(2,1)}, bf16[3072,128]{1,0:T(8,128)(2,1)S(1)}, u32[]{:S(2)}) copy-start(bf16[3072,128]{1,0:T(8,128)(2,1)S(1)} %get-tuple-element.38.p_ref) | copy-start | bytes 2359300
  13.7 18.7 %collective-permute-start = (f32[4,64,384]{2,1,0:T(8,128)}, f32[4,64,384]{2,1,0:T(8,128)}, u32[]{:S(2)}, u32[]{:S(2)}) collective-permute-start(f32[4,64,384]{2,1,0:T(8,128)} %get-tuple-element.42), channel_id=1, source_target_pairs={{0,4},{4,0},{1,5},{5,1},{2,6},{6,2},{3,7},{7,3},{8,12},{12,8},{9,1... | collective-permute-start | bytes 1179656 | tf_op jit(solution)/shard_map/ppermute | solution.py:235
  28.4 0.6 %copy-start.4 = (f32[32,4,128]{2,1,0:T(4,128)}, f32[32,4,128]{2,1,0:T(4,128)S(1)}, u32[]{:S(2)}) copy-start(f32[32,4,128]{2,1,0:T(4,128)S(1)} %share.1) | copy-start | bytes 196612
  29.1 19.9 %all-to-all-start.1 = ((f32[32,4,128]{2,1,0:T(4,128)}), f32[32,4,128]{2,1,0:T(4,128)}, u32[]{:S(2)}, u32[]{:S(2)}) async-start(f32[32,4,128]{2,1,0:T(4,128)} %copy-done.4), calls=%async_computation.1 | async-start | bytes 131072 | tf_op jit(solution)/shard_map/all_to_all | solution.py:230
  34.1 0.6 %copy-start.5 = (f32[64,384]{1,0:T(8,128)}, f32[64,384]{1,0:T(8,128)S(1)}, u32[]{:S(2)}) copy-start(f32[64,384]{1,0:T(8,128)S(1)} %get-tuple-element.43) | copy-start | bytes 294916
  34.8 5.2 %collective-permute-start.1 = (f32[64,384]{1,0:T(8,128)}, f32[64,384]{1,0:T(8,128)S(1)}, u32[]{:S(2)}, u32[]{:S(2)}) collective-permute-start(f32[64,384]{1,0:T(8,128)} %get-tuple-element.44), channel_id=1, source_target_pairs={{0,8},{8,0},{16,24},{24,16},{1,9},{9,1},{17,25},{25,17},{2,10},{10... | collective-permute-start | bytes 294920 | tf_op jit(solution)/shard_map/ppermute | solution.py:235
  36.3 6.1 %collective-permute-start.2 = (f32[64,384]{1,0:T(8,128)}, f32[64,384]{1,0:T(8,128)S(1)}, u32[]{:S(2)}, u32[]{:S(2)}) collective-permute-start(f32[64,384]{1,0:T(8,128)} %get-tuple-element.45), channel_id=1, source_target_pairs={{0,16},{8,24},{16,0},{24,8},{1,17},{9,25},{17,1},{25,9},{2,18},{10... | collective-permute-start | bytes 294920 | tf_op jit(solution)/shard_map/ppermute | solution.py:235
  37.8 5.7 %collective-permute-start.3 = (f32[64,384]{1,0:T(8,128)}, f32[64,384]{1,0:T(8,128)S(1)}, u32[]{:S(2)}, u32[]{:S(2)}) collective-permute-start(f32[64,384]{1,0:T(8,128)} %get-tuple-element.46), channel_id=1, source_target_pairs={{0,24},{8,16},{16,8},{24,0},{1,25},{9,17},{17,9},{25,1},{2,26},{10... | collective-permute-start | bytes 294920 | tf_op jit(solution)/shard_map/ppermute | solution.py:235
  43.6 0.9 %copy-start.6 = (f32[64,384]{1,0:T(8,128)S(1)}, f32[64,384]{1,0:T(8,128)}, u32[]{:S(2)}) copy-start(f32[64,384]{1,0:T(8,128)} %copy-done.5) | copy-start | bytes 294916
  44.5 15.2 %collective-permute-start.4 = (f32[16,384]{1,0:T(8,128)S(1)}, f32[16,384]{1,0:T(8,128)S(1)}, u32[]{:S(2)}, u32[]{:S(2)}) collective-permute-start(f32[16,384]{1,0:T(8,128)S(1)} %get-tuple-element.48), channel_id=1, source_target_pairs={{0,1},{1,0},{2,3},{3,2},{4,5},{5,4},{6,7},{7,6},{8,9},{9,8},{10,11... | collective-permute-start | bytes 73736 | tf_op jit(solution)/shard_map/ppermute | solution.py:235
  46.1 13.6 %collective-permute-start.5 = (f32[16,384]{1,0:T(8,128)S(1)}, f32[16,384]{1,0:T(8,128)S(1)}, u32[]{:S(2)}, u32[]{:S(2)}) collective-permute-start(f32[16,384]{1,0:T(8,128)S(1)} %get-tuple-element.49), channel_id=1, source_target_pairs={{0,2},{1,3},{2,0},{3,1},{4,6},{5,7},{6,4},{7,5},{8,10},{9,11},{10,... | collective-permute-start | bytes 73736 | tf_op jit(solution)/shard_map/ppermute | solution.py:235
  48.6 11.1 %collective-permute-start.6 = (f32[16,384]{1,0:T(8,128)S(1)}, f32[16,384]{1,0:T(8,128)S(1)}, u32[]{:S(2)}, u32[]{:S(2)}) collective-permute-start(f32[16,384]{1,0:T(8,128)S(1)} %get-tuple-element.50), channel_id=1, source_target_pairs={{0,3},{1,2},{2,1},{3,0},{4,7},{5,6},{6,5},{7,4},{8,11},{9,10},{10,... | collective-permute-start | bytes 73736 | tf_op jit(solution)/shard_map/ppermute | solution.py:235
  48.9 1.4 %copy-start.1 = (bf16[3072,256]{1,0:T(8,128)(2,1)S(1)}, bf16[3072,256]{1,0:T(8,128)(2,1)}, u32[]{:S(2)}) copy-start(bf16[3072,256]{1,0:T(8,128)(2,1)} %copy-done) | copy-start | bytes 4718596
  50.3 1.1 %copy-start.3 = (bf16[3072,128]{1,0:T(8,128)(2,1)S(1)}, bf16[3072,128]{1,0:T(8,128)(2,1)}, u32[]{:S(2)}) copy-start(bf16[3072,128]{1,0:T(8,128)(2,1)} %copy-done.2) | copy-start | bytes 2359300
  51.5 0.9 %copy-start.8 = (bf16[512,256]{1,0:T(8,128)(2,1)S(1)}, bf16[512,256]{1,0:T(8,128)(2,1)}, u32[]{:S(2)}) copy-start(bf16[512,256]{1,0:T(8,128)(2,1)} %copy-done.7) | copy-start | bytes 786436
  52.4 0.8 %copy-start.10 = (f32[128,128]{1,0:T(8,128)S(1)}, f32[128,128]{1,0:T(8,128)}, u32[]{:S(2)}) copy-start(f32[128,128]{1,0:T(8,128)} %copy-done.9) | copy-start | bytes 196612
  53.3 0.8 %copy-start.12 = (f32[64,64]{1,0:T(8,128)S(1)}, f32[64,64]{1,0:T(8,128)}, u32[]{:S(2)}) copy-start(f32[64,64]{1,0:T(8,128)} %copy-done.11) | copy-start | bytes 49156

commit v3 on v2

v3 whole, which is shorter than its diff:
```python
import functools
import math

import jax
import jax.numpy as jnp
from jax import lax
from jax.experimental import pallas as pl
from jax.experimental.pallas import tpu as pltpu
from jax.sharding import PartitionSpec as P

AXES = ("gx", "gy", "gz")
F32 = jnp.float32
BF16 = jnp.bfloat16
HBM = pl.BlockSpec(memory_space=pltpu.HBM)
VMEM = pl.BlockSpec(memory_space=pltpu.VMEM)
SMEM = pl.BlockSpec(memory_space=pltpu.SMEM)
VMEM_LIMIT = 24 * 1024 * 1024
AHEAD = 2


def exact(a, b, dims=((1,), (0,))):
    return lax.dot_general(
        a, b, (dims, ((), ())), precision=lax.Precision.HIGHEST, preferred_element_type=F32
    )


def mxu(a, b, dims=((1,), (0,))):
    return lax.dot_general(a, b, (dims, ((), ())), preferred_element_type=F32)


def held(shape, kind):
    return pltpu.VMEM(shape, kind)


def params():
    return pltpu.CompilerParams(vmem_limit_bytes=VMEM_LIMIT)


def cost(flops, nbytes):
    return pl.CostEstimate(flops=flops, bytes_accessed=nbytes, transcendentals=0)


def row_block(total):
    for size in (512, 384, 256, 128, 64, 32, 16):
        if total % size == 0:
            return size
    return total


def project_kernel(
    step, x_hbm, g_hbm, wr_hbm, wpt_hbm, we_hbm,
    x_ref, g_ref, rd_ref, p_ref, term_ref, rd_hbm, p_hbm, wcat_hbm,
    wcat_ref, wpt_ref, we_ref, small_sem, in_sem, out_sem,
):
    rows = x_ref.shape[0]
    nodes = wpt_ref.shape[0]
    cr = we_ref.shape[1]
    chunks = [pl.ds(start, step) for start in range(0, rows, step)]
    move = pltpu.make_async_copy
    loads = [
        (
            move(x_hbm.at[c], x_ref.at[c], in_sem.at[0, i]),
            move(g_hbm.at[c], g_ref.at[c], in_sem.at[1, i]),
        )
        for i, c in enumerate(chunks)
    ]
    small = [
        move(wr_hbm, wcat_ref.at[:, pl.ds(0, cr)], small_sem.at[0]),
        move(wpt_hbm, wpt_ref, small_sem.at[1]),
        move(we_hbm, we_ref, small_sem.at[2]),
    ]
    for copy in small:
        copy.start()
    for pair in loads[:AHEAD]:
        for copy in pair:
            copy.start()
    small[0].wait()
    small[1].wait()
    padded = jnp.concatenate([wpt_ref[...], jnp.zeros_like(wpt_ref)], axis=0)
    wcat_ref[:, cr:] = padded.T
    small[2].wait()
    stores = [move(wcat_ref, wcat_hbm, small_sem.at[3])]
    stores[0].start()
    for i, c in enumerate(chunks):
        loads[i][0].wait()
        both = mxu(x_ref[c], wcat_ref[...]).astype(BF16)
        loads[i][1].wait()
        if i + AHEAD < len(loads):
            for copy in loads[i + AHEAD]:
                copy.start()
        mapped = mxu(g_ref[c], we_ref[...]).astype(BF16)
        rd = jnp.concatenate([both[:, :cr], mapped], axis=1)
        proj = both[:, cr:]
        rd_ref[c] = rd
        p_ref[c] = proj
        pair = [
            move(rd_ref.at[c], rd_hbm.at[c], out_sem.at[0, i]),
            move(p_ref.at[c], p_hbm.at[c], out_sem.at[1, i]),
        ]
        for copy in pair:
            copy.start()
        stores += pair
        part = mxu(proj, rd, ((0,), (0,)))[:nodes]
        if i == 0:
            term_ref[:nodes] = part[:, :cr]
            term_ref[nodes:] = part[:, cr:]
        else:
            term_ref[:nodes] += part[:, :cr]
            term_ref[nodes:] += part[:, cr:]
    for copy in stores:
        copy.wait()


def from_hbm(*values):
    return [pltpu.with_memory_space_constraint(value, pltpu.HBM) for value in values]


def project(x, g, wr, wpt, we):
    rows, chan = x.shape
    cr, nodes = wr.shape[1], wpt.shape[0]
    step = row_block(rows)
    count = rows // step
    return pl.pallas_call(
        functools.partial(project_kernel, step),
        in_specs=[HBM] * 5,
        out_specs=[VMEM] * 5 + [HBM] * 3,
        out_shape=[
            held((rows, chan), BF16),
            held((rows, chan), BF16),
            held((rows, 2 * cr), BF16),
            held((rows, 2 * nodes), BF16),
            held((2 * nodes, cr), F32),
            pltpu.HBM((rows, 2 * cr), BF16),
            pltpu.HBM((rows, 2 * nodes), BF16),
            pltpu.HBM((chan, cr + 2 * nodes), BF16),
        ],
        scratch_shapes=[
            pltpu.VMEM((chan, cr + 2 * nodes), BF16),
            pltpu.VMEM(wpt.shape, BF16),
            pltpu.VMEM(we.shape, BF16),
            pltpu.SemaphoreType.DMA((4,)),
            pltpu.SemaphoreType.DMA((2, count)),
            pltpu.SemaphoreType.DMA((2, count)),
        ],
        compiler_params=params(),
        cost_estimate=cost(2 * rows * chan * 512, rows * chan * 4 + rows * 768),
        name="project",
    )(*from_hbm(x, g, wr, wpt, we))


def weight_kernel(step, x_ref, g_ref, rd_ref, p_ref, out_ref, sums_ref):
    rows = x_ref.shape[0]
    nodes = p_ref.shape[1] // 2
    for start in range(0, rows, step):
        c = pl.ds(start, step)
        proj = p_ref[c][:, :nodes]
        x = x_ref[c]
        pieces = (
            mxu(rd_ref[c], x, ((0,), (0,))),
            mxu(proj, x, ((0,), (0,))),
            mxu(proj, g_ref[c], ((0,), (0,))),
        )
        at = 0
        for piece in pieces:
            span = pl.ds(at, piece.shape[0])
            at += piece.shape[0]
            if start == 0:
                sums_ref[span] = piece
            else:
                sums_ref[span] += piece
    turned = sums_ref[...].T
    gy, gx, size, _ = out_ref.shape
    for i in range(gx):
        for j in range(gy):
            at = (i * gy + j) * size
            out_ref[j, i] = turned[at : at + size]


def weight_terms(x, g, rd, p, sizes):
    rows, chan = x.shape
    step = row_block(rows)
    gx, gy, gz = sizes
    width = rd.shape[1] + p.shape[1]
    return pl.pallas_call(
        functools.partial(weight_kernel, step),
        in_specs=[VMEM] * 4,
        out_specs=VMEM,
        out_shape=held((gy, gx, chan // (gx * gy), width), F32),
        scratch_shapes=[pltpu.VMEM((width, chan), F32)],
        compiler_params=params(),
        cost_estimate=cost(2 * rows * chan * 512, rows * chan * 4 + rows * 768 + width * chan * 4),
        name="weight_terms",
    )(x, g, rd, p)


def add_kernel(in_ref, out_ref):
    total = in_ref[0]
    for i in range(1, in_ref.shape[0]):
        total = total + in_ref[i]
    out_ref[...] = jnp.broadcast_to(total[None], out_ref.shape)


def add(value, repeats):
    return pl.pallas_call(
        add_kernel,
        in_specs=[VMEM],
        out_specs=VMEM,
        out_shape=held((repeats, *value.shape[1:]), F32),
        compiler_params=params(),
        cost_estimate=cost(0, 8 * value.size),
        name="add",
    )(value)


def exchange(value, axis):
    return lax.all_to_all(value, axis, 0, 0, tiled=True)


def node_sum(term):
    size = {axis: lax.axis_size(axis) for axis in AXES}
    parts = term.reshape(size["gy"], -1, term.shape[1])
    parts = exchange(parts, "gy")
    for axis in ("gx", "gz"):
        parts = exchange(add(parts, size[axis]), axis)
    return exchange(add(parts, size["gy"]), "gy").reshape(term.shape)


def weight_sums(parts):
    size = {axis: lax.axis_size(axis) for axis in AXES}
    parts = add(exchange(parts, "gy"), 1)[0]
    parts = add(exchange(parts, "gx"), 1)[0]
    return exchange(parts.reshape(size["gz"], -1, parts.shape[1]), "gz")


def feature_kernel(
    step, scale, total_ref, adj_hbm, nw_hbm, wcat_hbm, g_hbm, rd_hbm, p_hbm,
    out_hbm, ga_ref, gn_ref, no_ref, dn_ref,
    adj_ref, nw_ref, wcat_ref, g_ref, rd_ref, p_ref, out_ref, mix_ref, dnb_ref,
    small_sem, in_sem, out_sem,
):
    nodes_n, cr = no_ref.shape
    rows = g_ref.shape[0]
    chunks = [pl.ds(start, step) for start in range(0, rows, step)]
    move = pltpu.make_async_copy
    small = [
        move(adj_hbm, adj_ref, small_sem.at[0]),
        move(nw_hbm, nw_ref, small_sem.at[1]),
        move(wcat_hbm, wcat_ref, small_sem.at[2]),
    ]
    loads = [
        [
            move(src.at[c], dst.at[c], in_sem.at[k, i])
            for k, (src, dst) in enumerate(((rd_hbm, rd_ref), (p_hbm, p_ref), (g_hbm, g_ref)))
        ]
        for i, c in enumerate(chunks)
    ]
    for copy in small:
        copy.start()
    for group in loads[:AHEAD]:
        for copy in group:
            copy.start()
    small[0].wait()
    small[1].wait()
    adj, nw = adj_ref[...], nw_ref[...]
    nodes = scale * total_ref[:nodes_n]
    d_node_out = total_ref[nodes_n:]
    hidden = nodes - exact(adj, nodes)
    pre = exact(hidden, nw)
    node_out = jnp.maximum(pre, 0.0).astype(BF16)
    d_pre = jnp.where(pre > 0.0, d_node_out, 0.0)
    d_hidden = exact(d_pre, nw, ((1,), (1,)))
    d_nodes = d_hidden - exact(adj, d_hidden, ((0,), (0,)))
    dn = d_nodes.astype(BF16)
    no_ref[...] = node_out.astype(F32)
    dn_ref[...] = dn.astype(F32)
    dnb_ref[:nodes_n] = dn
    dnb_ref[nodes_n:] = jnp.zeros((nodes_n, cr), BF16)
    blank = jnp.zeros((cr, cr), BF16)
    zero = jnp.zeros((nodes_n, cr), F32)
    mix_ref[:cr, :cr] = jnp.concatenate([dn.astype(F32), zero], axis=0).T.astype(BF16)
    mix_ref[cr:, :cr] = blank
    mix_ref[:cr, cr:] = blank
    mix_ref[cr:, cr:] = jnp.concatenate([node_out.astype(F32), zero], axis=0).T.astype(BF16)
    small[2].wait()
    copies = []
    for i, c in enumerate(chunks):
        for copy in loads[i]:
            copy.wait()
        if i + AHEAD < len(loads):
            for copy in loads[i + AHEAD]:
                copy.start()
        mixed = mxu(rd_ref[c], mix_ref[...])
        d_proj = (mixed[:, cr:] + scale * mixed[:, :cr]).astype(BF16)
        d_red = (scale * mxu(p_ref[c], dnb_ref[...])).astype(BF16)
        both = jnp.concatenate([d_red, d_proj], axis=1)
        out = g_ref[c].astype(F32) + mxu(both, wcat_ref[...], ((1,), (1,)))
        out_ref[c] = out.astype(BF16)
        copies.append(move(out_ref.at[c], out_hbm.at[c], out_sem.at[i]))
        copies[-1].start()
    gn_ref[...] = scale * exact(hidden, d_pre, ((0,), (0,)))
    ga_ref[...] = -scale * exact(d_hidden, nodes, ((1,), (1,)))
    for copy in copies:
        copy.wait()


def feature_grads(total, adjacency, node_weight, wcat, g, rd, p, scale):
    rows, chan = g.shape
    nodes, cr = adjacency.shape[0], node_weight.shape[0]
    step = row_block(rows)
    count = rows // step
    loaded = (adjacency, node_weight, wcat, g, rd, p)
    return pl.pallas_call(
        functools.partial(feature_kernel, step, scale),
        in_specs=[VMEM] + [HBM] * 6,
        out_specs=[HBM] + [VMEM] * 4,
        out_shape=[
            pltpu.HBM((rows, chan), BF16),
            jax.ShapeDtypeStruct((nodes, nodes), F32),
            jax.ShapeDtypeStruct((cr, cr), F32),
            held((nodes, cr), F32),
            held((nodes, cr), F32),
        ],
        scratch_shapes=[pltpu.VMEM(value.shape, value.dtype) for value in loaded]
        + [
            pltpu.VMEM((rows, chan), BF16),
            pltpu.VMEM((2 * cr, 2 * cr), BF16),
            pltpu.VMEM((2 * nodes, cr), BF16),
            pltpu.SemaphoreType.DMA((3,)),
            pltpu.SemaphoreType.DMA((3, count)),
            pltpu.SemaphoreType.DMA((count,)),
        ],
        compiler_params=params(),
        cost_estimate=cost(2 * rows * 4 * 65536, rows * chan * 4 + rows * 768),
        name="feature_grads",
    )(total, *from_hbm(*loaded))


def finish_kernel(scale, parts_ref, no_ref, dn_ref, gr_ref, gp_ref, ge_ref):
    total = parts_ref[0]
    for i in range(1, parts_ref.shape[0]):
        total = total + parts_ref[i]
    nodes, cr = no_ref.shape
    no, dn = no_ref[...], dn_ref[...]
    x_red, x_dm = total[:, :cr], total[:, cr : 2 * cr]
    cross = total[:, 2 * cr : 2 * cr + nodes]
    g_proj = total[:, 2 * cr + nodes :]
    gr_ref[...] = scale * scale * exact(cross, dn)
    gp_ref[...] = scale * exact(x_dm, no, ((1,), (1,))) + scale * scale * exact(
        x_red, dn, ((1,), (1,))
    )
    ge_ref[...] = scale * exact(g_proj, no)


def finish(parts, no, dn, scale):
    rows = parts.shape[1]
    nodes, cr = no.shape
    return pl.pallas_call(
        functools.partial(finish_kernel, scale),
        in_specs=[VMEM] * 3,
        out_specs=[VMEM] * 3,
        out_shape=[
            jax.ShapeDtypeStruct((rows, cr), F32),
            jax.ShapeDtypeStruct((rows, nodes), F32),
            jax.ShapeDtypeStruct((rows, cr), F32),
        ],
        compiler_params=params(),
        cost_estimate=cost(0, rows * 4096),
        name="finish",
    )(parts, no, dn)


def on_device(
    features, cotangent, reduce_weight, project_weight, expand_weight, adjacency, node_weight
):
    size_x, size_y, size_z, chan = features.shape
    local = size_x * size_y * size_z
    sizes = tuple(lax.axis_size(axis) for axis in AXES)
    total = local * math.prod(sizes)
    scale = 1.0 / math.sqrt(total)
    flat_x = features.transpose(0, 2, 1, 3).reshape(local, chan)
    flat_g = cotangent.transpose(0, 2, 1, 3).reshape(local, chan)

    x, g, rd, p, term, rd_far, p_far, wcat = project(
        flat_x, flat_g, reduce_weight, project_weight.T, expand_weight
    )
    node_total = node_sum(term)
    parts = weight_sums(weight_terms(x, g, rd, p, sizes))

    flat_out, grad_adjacency, grad_node, no, dn = feature_grads(
        node_total, adjacency, node_weight, wcat, flat_g, rd_far, p_far, scale
    )
    grad_reduce, grad_project, grad_expand = finish(parts, no, dn, scale)
    grad_features = flat_out.reshape(size_x, size_z, size_y, chan).transpose(0, 2, 1, 3)
    return (grad_features, grad_reduce, grad_project, grad_expand, grad_adjacency, grad_node)


def solution(mesh):
    return jax.shard_map(
        on_device,
        mesh=mesh,
        in_specs=(P("gx", "gy", "gz", None), P("gx", "gy", "gz", None), P(), P(), P(), P(), P()),
        out_specs=(
            P("gx", "gy", "gz", None),
            P(AXES, None),
            P(AXES, None),
            P(AXES, None),
            P(),
            P(),
        ),
        check_vma=False,
    )
```

time: 62.3 us -> 73.5 us (1.18)
  starting transfers between devices: 11.7 us -> 24.4 us
  blocking collectives: 14.3 us -> 3.78 us
  waiting for transfers between devices: 5.31 us -> 12.7 us
  Pallas kernels: 17.6 us -> 23 us
  local copies, waits for them, and re-layouts: 12.2 us -> 8.12 us
    all_to_all x1 -> x6, starting transfers between devices: 3.29 us -> 24.4 us  [exchange(): return lax.all_to_all(value, axis, 0, 0, tiled=True)]
    all_to_all x1 -> x6, waiting for transfers between devices: 0.01 us -> 12.7 us  [exchange(): return lax.all_to_all(value, axis, 0, 0, tiled=True)]
    all_to_all x1, blocking collectives: 14.3 us -> 3.78 us  [exchange(): return lax.all_to_all(value, axis, 0, 0, tiled=True)]
    ppermute x7 -> x0, starting transfers between devices: 8.39 us -> none  [swap(): return lax.ppermute(value, axis, [(i, i ^ peer) for i in range(size)])]
    ppermute x7 -> x0, waiting for transfers between devices: 5.31 us -> none  [swap(): return lax.ppermute(value, axis, [(i, i ^ peer) for i in range(size)])]
    unnamed x31 -> x12, local copies, waits for them, and re-layouts: 12.2 us -> 8.12 us
    pallas_call x1, Pallas kernels: 4.4 us -> 7.38 us  [feature_grads(): pl.pallas_call(functools.partial(feature_kernel, step, scale), in_specs=[...]
    pallas_call x5 -> x7, Pallas kernels: 5.11 us -> 7.38 us  [the longest x5 3.4 us: add(): pl.pallas_call(add_kernel, in_specs=[VMEM], out_specs=VMEM, out_shape=hel...]
  transfers between devices with their start and end apart: 8 -> 6, of which waited for: 3 -> 4; matrix products, arithmetic and copies ran while one was open for 2% -> 0% of each run, Pallas kernels for 10% -> 18%
where the time goes in v3:
time: 73.5 us; the launch traced here: 72.6 us
  starting transfers between devices  24.4 us (33%)
  Pallas kernels  23 us (31%)
  waiting for transfers between devices  12.7 us (17%)
  local copies, waits for them, and re-layouts  8.12 us (11%)
  blocking collectives  3.78 us (5%)
    all_to_all x6, starting transfers between devices, exchange(): return lax.all_to_all(value, axis, 0, 0, tiled=True)  24.4 us
    all_to_all x6, waiting for transfers between devices, exchange(): return lax.all_to_all(value, axis, 0, 0, tiled=True)  12.7 us
    pallas_call x1, Pallas kernels, project(): pl.pallas_call(functools.partial(project_kernel, step), in_specs=[HBM] *...  8.2 us
    unnamed x12, local copies, waits for them, and re-layouts  8.12 us
    pallas_call x1, Pallas kernels, feature_grads(): pl.pallas_call(functools.partial(feature_kernel, step, scale), in_specs=[...  7.38 us
    all_to_all x1, blocking collectives, exchange(): return lax.all_to_all(value, axis, 0, 0, tiled=True)  3.78 us
    pallas_call x5, Pallas kernels, add(): pl.pallas_call(add_kernel, in_specs=[VMEM], out_specs=VMEM, out_shape=hel...  3.4 us
    pallas_call x1, Pallas kernels, weight_terms(): pl.pallas_call(functools.partial(weight_kernel, step), in_specs=[VMEM] *...  3.11 us
  transfers between devices with their start and end apart: 6, of which 4 were waited for; matrix products, arithmetic and copies ran while one was open for 0% of the time, Pallas kernels for 18%

profile of v3, /device:TPU:0, one launch (start us, length us, event | category | flops | bytes accessed | tf_op | source)
XLA Modules:
  0.0 72.6 jit_solution(12188294153865448322)
XLA Ops:
  0.6 8.2 %project.1 = (bf16[3072,512]{1,0:T(8,128)(2,1)S(1)}, bf16[3072,512]{1,0:T(8,128)(2,1)S(1)}, bf16[3072,256]{1,0:T(8,128)(2,1)S(1)}, bf16[3072,128]{1,0:T(8,128)(2...) custom-call(bf16[3072,512]{1,0:T(8,128)(2,1)} %bitcast.16, ...), custom_call_target="tpu_custom_call" | custom-call | flops 1610612736 | bytes 8650752 | tf_op jit(solution)/shard_map/project/pallas_call | solution.py:123
  8.8 1.7 %copy-done = bf16[3072,512]{1,0:T(8,128)(2,1)} copy-done((bf16[3072,512]{1,0:T(8,128)(2,1)}, bf16[3072,512]{1,0:T(8,128)(2,1)S(1)}, u32[]{:S(2)}) %copy-start) | copy-done | bytes 3145752
  10.5 1.1 %copy-done.2 = bf16[3072,256]{1,0:T(8,128)(2,1)} copy-done((bf16[3072,256]{1,0:T(8,128)(2,1)}, bf16[3072,256]{1,0:T(8,128)(2,1)S(1)}, u32[]{:S(2)}) %copy-start.2) | copy-done | bytes 1572888
  11.6 0.9 %copy-done.4 = bf16[3072,128]{1,0:T(8,128)(2,1)} copy-done((bf16[3072,128]{1,0:T(8,128)(2,1)}, bf16[3072,128]{1,0:T(8,128)(2,1)S(1)}, u32[]{:S(2)}) %copy-start.4) | copy-done | bytes 786456
  12.5 3.8 %all_to_all.35.in_ref = f32[2,64,128]{2,1,0:T(8,128)S(1)} all-to-all(f32[2,64,128]{2,1,0:T(8,128)S(1)} %bitcast.15), channel_id=1, replica_groups=mesh['gx'=4,'gy'=2,'gz'=4] {'gy'}, dimensions={0} | all-to-all | bytes 131072 | tf_op jit(solution)/shard_map/all_to_all | solution.py:216
  16.3 0.7 add.5
  17.0 5.2 %all-to-all-start.1 = ((f32[4,64,128]{2,1,0:T(8,128)}), f32[4,64,128]{2,1,0:T(8,128)S(1)}, u32[]{:S(2)}, u32[]{:S(2)}) async-start(f32[4,64,128]{2,1,0:T(8,128)} %add.5), calls=%async_computation.1 | async-start | bytes 262144 | tf_op jit(solution)/shard_map/all_to_all | solution.py:216
  22.1 1.9 %copy-done.1 = bf16[3072,512]{1,0:T(8,128)(2,1)S(1)} copy-done((bf16[3072,512]{1,0:T(8,128)(2,1)S(1)}, bf16[3072,512]{1,0:T(8,128)(2,1)}, u32[]{:S(2)}) %copy-start.1) | copy-done | bytes 3145752
  24.0 1.4 %copy-done.3 = bf16[3072,256]{1,0:T(8,128)(2,1)S(1)} copy-done((bf16[3072,256]{1,0:T(8,128)(2,1)S(1)}, bf16[3072,256]{1,0:T(8,128)(2,1)}, u32[]{:S(2)}) %copy-start.3) | copy-done | bytes 1572888
  25.4 1.1 %copy-done.5 = bf16[3072,128]{1,0:T(8,128)(2,1)S(1)} copy-done((bf16[3072,128]{1,0:T(8,128)(2,1)S(1)}, bf16[3072,128]{1,0:T(8,128)(2,1)}, u32[]{:S(2)}) %copy-start.5) | copy-done | bytes 786456
  26.6 3.1 %weight_terms.1 = f32[2,4,64,384]{3,2,1,0:T(8,128)} custom-call(bf16[3072,512]{1,0:T(8,128)(2,1)S(1)} %get-tuple-element.27.x_ref, bf16[3072,512]{1,0:T(8,128)(2,1)S(1)} %copy-done.1, bf16[3072,256]{1,0:T(8,128)(2,1)S(1)} %copy-done.3, bf16[3072,128]{1,0:T(8,128)(2,1)S(1)} %copy-done.5), custom_call_target="tpu_custom_call" | custom-call | flops 1610612736 | bytes 9437184 | tf_op jit(solution)/shard_map/weight_terms/pallas_call | solution.py:184
  29.7 3.5 %all-to-all-start.4 = ((f32[2,4,64,384]{3,2,1,0:T(8,128)}), f32[2,4,64,384]{3,2,1,0:T(8,128)S(1)}, u32[]{:S(2)}, u32[]{:S(2)}) async-start(f32[2,4,64,384]{3,2,1,0:T(8,128)} %weight_terms.1), calls=%async_computation.4 | async-start | bytes 1572864 | tf_op jit(solution)/shard_map/all_to_all | solution.py:216
  33.2 0.7 add.6
  33.9 1.3 %all-to-all-done.4.in_ref = f32[2,4,64,384]{3,2,1,0:T(8,128)S(1)} async-done(((f32[2,4,64,384]{3,2,1,0:T(8,128)}), f32[2,4,64,384]{3,2,1,0:T(8,128)S(1)}, u32[]{:S(2)}, u32[]{:S(2)}) %all-to-all-start.4) | async-done | bytes 786464 | tf_op jit(solution)/shard_map/all_to_all | solution.py:216
  35.1 4.9 %all-to-all-start.2 = ((f32[4,64,128]{2,1,0:T(8,128)}), f32[4,64,128]{2,1,0:T(8,128)S(1)}, u32[]{:S(2)}, u32[]{:S(2)}) async-start(f32[4,64,128]{2,1,0:T(8,128)} %add.6), calls=%async_computation.2 | async-start | bytes 262144 | tf_op jit(solution)/shard_map/all_to_all | solution.py:216
  40.0 0.8 %add.8 = f32[1,4,64,384]{3,2,1,0:T(8,128)} custom-call(f32[2,4,64,384]{3,2,1,0:T(8,128)S(1)} %all-to-all-done.4.in_ref), custom_call_target="tpu_custom_call" | custom-call | bytes 1572864 | tf_op jit(solution)/shard_map/add/pallas_call | solution.py:204
  40.8 5.4 %all-to-all-done.2.in_ref = f32[4,64,128]{2,1,0:T(8,128)S(1)} async-done(((f32[4,64,128]{2,1,0:T(8,128)}), f32[4,64,128]{2,1,0:T(8,128)S(1)}, u32[]{:S(2)}, u32[]{:S(2)}) %all-to-all-start.2) | async-done | bytes 131104 | tf_op jit(solution)/shard_map/all_to_all | solution.py:216
  46.2 4.2 %all-to-all-start.5 = ((f32[4,64,384]{2,1,0:T(8,128)}), f32[4,64,384]{2,1,0:T(8,128)S(1)}, u32[]{:S(2)}, u32[]{:S(2)}) async-start(f32[4,64,384]{2,1,0:T(8,128)} %bitcast.9), calls=%async_computation.5 | async-start | bytes 786432 | tf_op jit(solution)/shard_map/all_to_all | solution.py:216
  51.0 5.2 %all-to-all-done.5.in_ref = f32[4,64,384]{2,1,0:T(8,128)S(1)} async-done(((f32[4,64,384]{2,1,0:T(8,128)}), f32[4,64,384]{2,1,0:T(8,128)S(1)}, u32[]{:S(2)}, u32[]{:S(2)}) %all-to-all-start.5) | async-done | bytes 393248 | tf_op jit(solution)/shard_map/all_to_all | solution.py:216
  56.3 3.3 %all-to-all-start.3 = ((f32[2,64,128]{2,1,0:T(8,128)}), f32[2,64,128]{2,1,0:T(8,128)S(1)}, u32[]{:S(2)}, u32[]{:S(2)}) async-start(f32[2,64,128]{2,1,0:T(8,128)} %add.7), calls=%async_computation.3 | async-start | bytes 131072 | tf_op jit(solution)/shard_map/all_to_all | solution.py:216
  60.2 0.7 %all-to-all-done.3 = f32[2,64,128]{2,1,0:T(8,128)S(1)} async-done(((f32[2,64,128]{2,1,0:T(8,128)}), f32[2,64,128]{2,1,0:T(8,128)S(1)}, u32[]{:S(2)}, u32[]{:S(2)}) %all-to-all-start.3) | async-done | bytes 65568 | tf_op jit(solution)/shard_map/all_to_all | solution.py:216
  61.0 3.3 %all-to-all-start.6 = ((f32[4,16,384]{2,1,0:T(8,128)}), f32[4,16,384]{2,1,0:T(8,128)S(1)}, u32[]{:S(2)}, u32[]{:S(2)}) async-start(f32[4,16,384]{2,1,0:T(8,128)} %bitcast.10), calls=%async_computation.6 | async-start | bytes 196608 | tf_op jit(solution)/shard_map/all_to_all | solution.py:216
  64.3 7.4 %feature_grads.1 = (bf16[3072,512]{1,0:T(8,128)(2,1)}, f32[64,64]{1,0:T(8,128)}, f32[128,128]{1,0:T(8,128)}, f32[64,128]{1,0:T(8,128)S(1)}, f32[64,128]{1,0:T(8,128)S(1)}) custom-call(f32[128,128]{1,0:T(8,128)S(1)} %bitcast.14, f32[64,64]{1,0:T(8,128)} %adj_hbm.1, f32[128,128]{1,0:T(8,128)} %nw_hbm.1, bf16[512,256]{1,0:T(8,128)(2,1)} %get-tuple-element.23.wcat_hbm, ...), custom_call_target="tpu_custom_call" | custom-call | flops 1610612736 | bytes 8650752 | tf_op jit(solution)/shard_map/feature_grads/pallas_call | solution.py:312
  71.7 0.9 %finish.1 = (f32[16,128]{1,0:T(8,128)}, f32[16,64]{1,0:T(8,128)}, f32[16,128]{1,0:T(8,128)}) custom-call(f32[4,16,384]{2,1,0:T(8,128)S(1)} %all-to-all-done.6.parts_ref, f32[64,128]{1,0:T(8,128)S(1)} %get-tuple-element.31.no_ref, f32[64,128]{1,0:T(8,128)S(1)} %get-tuple-element.32.dn_ref), custom_call_target="tpu_custom_call" | custom-call | bytes 65536 | tf_op jit(solution)/shard_map/finish/pallas_call | solution.py:357
  (10 shorter events, 1.3 us)
Async XLA Ops:
  8.8 1.7 %copy-start = (bf16[3072,512]{1,0:T(8,128)(2,1)}, bf16[3072,512]{1,0:T(8,128)(2,1)S(1)}, u32[]{:S(2)}) copy-start(bf16[3072,512]{1,0:T(8,128)(2,1)S(1)} %get-tuple-element.28.g_ref) | copy-start | bytes 9437188
  10.5 1.1 %copy-start.2 = (bf16[3072,256]{1,0:T(8,128)(2,1)}, bf16[3072,256]{1,0:T(8,128)(2,1)S(1)}, u32[]{:S(2)}) copy-start(bf16[3072,256]{1,0:T(8,128)(2,1)S(1)} %get-tuple-element.29.rd_ref) | copy-start | bytes 4718596
  11.6 0.9 %copy-start.4 = (bf16[3072,128]{1,0:T(8,128)(2,1)}, bf16[3072,128]{1,0:T(8,128)(2,1)S(1)}, u32[]{:S(2)}) copy-start(bf16[3072,128]{1,0:T(8,128)(2,1)S(1)} %get-tuple-element.30.p_ref) | copy-start | bytes 2359300
  17.0 12.7 %all-to-all-start.1 = ((f32[4,64,128]{2,1,0:T(8,128)}), f32[4,64,128]{2,1,0:T(8,128)S(1)}, u32[]{:S(2)}, u32[]{:S(2)}) async-start(f32[4,64,128]{2,1,0:T(8,128)} %add.5), calls=%async_computation.1 | async-start | bytes 262144 | tf_op jit(solution)/shard_map/all_to_all | solution.py:216
  22.1 1.9 %copy-start.1 = (bf16[3072,512]{1,0:T(8,128)(2,1)S(1)}, bf16[3072,512]{1,0:T(8,128)(2,1)}, u32[]{:S(2)}) copy-start(bf16[3072,512]{1,0:T(8,128)(2,1)} %copy-done) | copy-start | bytes 9437188
  24.0 1.4 %copy-start.3 = (bf16[3072,256]{1,0:T(8,128)(2,1)S(1)}, bf16[3072,256]{1,0:T(8,128)(2,1)}, u32[]{:S(2)}) copy-start(bf16[3072,256]{1,0:T(8,128)(2,1)} %copy-done.2) | copy-start | bytes 4718596
  25.4 1.1 %copy-start.5 = (bf16[3072,128]{1,0:T(8,128)(2,1)S(1)}, bf16[3072,128]{1,0:T(8,128)(2,1)}, u32[]{:S(2)}) copy-start(bf16[3072,128]{1,0:T(8,128)(2,1)} %copy-done.4) | copy-start | bytes 2359300
  29.7 5.5 %all-to-all-start.4 = ((f32[2,4,64,384]{3,2,1,0:T(8,128)}), f32[2,4,64,384]{3,2,1,0:T(8,128)S(1)}, u32[]{:S(2)}, u32[]{:S(2)}) async-start(f32[2,4,64,384]{3,2,1,0:T(8,128)} %weight_terms.1), calls=%async_computation.4 | async-start | bytes 1572864 | tf_op jit(solution)/shard_map/all_to_all | solution.py:216
  35.1 11.1 %all-to-all-start.2 = ((f32[4,64,128]{2,1,0:T(8,128)}), f32[4,64,128]{2,1,0:T(8,128)S(1)}, u32[]{:S(2)}, u32[]{:S(2)}) async-start(f32[4,64,128]{2,1,0:T(8,128)} %add.6), calls=%async_computation.2 | async-start | bytes 262144 | tf_op jit(solution)/shard_map/all_to_all | solution.py:216
  46.2 10.1 %all-to-all-start.5 = ((f32[4,64,384]{2,1,0:T(8,128)}), f32[4,64,384]{2,1,0:T(8,128)S(1)}, u32[]{:S(2)}, u32[]{:S(2)}) async-start(f32[4,64,384]{2,1,0:T(8,128)} %bitcast.9), calls=%async_computation.5 | async-start | bytes 786432 | tf_op jit(solution)/shard_map/all_to_all | solution.py:216
  56.3 4.7 %all-to-all-start.3 = ((f32[2,64,128]{2,1,0:T(8,128)}), f32[2,64,128]{2,1,0:T(8,128)S(1)}, u32[]{:S(2)}, u32[]{:S(2)}) async-start(f32[2,64,128]{2,1,0:T(8,128)} %add.7), calls=%async_computation.3 | async-start | bytes 131072 | tf_op jit(solution)/shard_map/all_to_all | solution.py:216
  61.0 10.7 %all-to-all-start.6 = ((f32[4,16,384]{2,1,0:T(8,128)}), f32[4,16,384]{2,1,0:T(8,128)S(1)}, u32[]{:S(2)}, u32[]{:S(2)}) async-start(f32[4,16,384]{2,1,0:T(8,128)} %bitcast.10), calls=%async_computation.6 | async-start | bytes 196608 | tf_op jit(solution)/shard_map/all_to_all | solution.py:216

commit v4 on v3

v4 whole, which is shorter than its diff:
```python
import functools
import math

import jax
import jax.numpy as jnp
from jax import lax
from jax.experimental import pallas as pl
from jax.experimental.pallas import tpu as pltpu
from jax.sharding import PartitionSpec as P

AXES = ("gx", "gy", "gz")
F32 = jnp.float32
BF16 = jnp.bfloat16
HBM = pl.BlockSpec(memory_space=pltpu.HBM)
VMEM = pl.BlockSpec(memory_space=pltpu.VMEM)
SMEM = pl.BlockSpec(memory_space=pltpu.SMEM)
VMEM_LIMIT = 24 * 1024 * 1024


def exact(a, b, dims=((1,), (0,))):
    return lax.dot_general(
        a, b, (dims, ((), ())), precision=lax.Precision.HIGHEST, preferred_element_type=F32
    )


def mxu(a, b, dims=((1,), (0,))):
    return lax.dot_general(a, b, (dims, ((), ())), preferred_element_type=F32)


def params():
    return pltpu.CompilerParams(vmem_limit_bytes=VMEM_LIMIT)


def cost(flops, nbytes):
    return pl.CostEstimate(flops=flops, bytes_accessed=nbytes, transcendentals=0)


def whole(shape):
    return pl.BlockSpec(shape, lambda *_: (0,) * len(shape))


def in_hbm(*values):
    return [pltpu.with_memory_space_constraint(value, pltpu.HBM) for value in values]


def row_block(total):
    for size in (512, 384, 256, 128, 64, 32, 16):
        if total % size == 0:
            return size
    return total


class Cube:
    def __init__(self, mesh):
        self.size = {axis: mesh.shape[axis] for axis in AXES}
        self.count = math.prod(self.size.values())
        stride = {"gx": self.size["gy"] * self.size["gz"], "gy": self.size["gz"], "gz": 1}
        bits = {
            axis: [stride[axis] << k for k in range(self.size[axis].bit_length() - 1)] for axis in AXES
        }
        self.core = bits["gy"][0]
        rest = bits["gx"] + bits["gy"][1:] + bits["gz"]
        self.orders = [rest, rest]
        if len(bits["gx"]) == 2:
            self.orders = [rest, [rest[1], rest[0]] + rest[2:]]
        self.rounds = len(rest)

    def side(self, device):
        return 1 if device & self.core else 0

    def traced_side(self, device):
        return lax.bitwise_and(lax.div(device, jnp.int32(self.core)), jnp.int32(1))

    def swap(self, value, level):
        masks = [self.core] * 2 if level < 0 else [order[level] for order in self.orders]
        pairs = [(d, d ^ masks[self.side(d)]) for d in range(self.count)]
        return lax.ppermute(value, AXES, pairs)

    def masks(self, side):
        order = self.orders[side]
        last = len(order) - 1
        return [
            sum(order[level] for level in range(len(order)) if j >> (last - level) & 1)
            for j in range(1 << len(order))
        ]


def thirds(value, weight):
    rows = value.shape[0]
    high = value.astype(BF16)
    rest = value - high.astype(F32)
    middle = rest.astype(BF16)
    low = (rest - middle.astype(F32)).astype(BF16)
    out = mxu(jnp.concatenate([high, middle, low], axis=0), weight)
    return (out[2 * rows :] + out[rows : 2 * rows]) + out[:rows]


def gather_kernel(
    cube, where_ref, x_ref, g_ref, wr_ref, wpt_ref, we_ref,
    rd_ref, p_ref, wcat_ref, keep_ref, send_ref, *rest,
):
    sorted_here = len(rest) == 6
    if sorted_here:
        kept_ref, sent_ref, sums_ref, turned_ref, term_ref, cat_ref = rest
    else:
        turned_ref, sums_ref, term_ref, cat_ref = rest
    cr = wr_ref.shape[1]
    nodes = wpt_ref.shape[0]
    wide = 2 * cr

    @pl.when(pl.program_id(0) == 0)
    def _():
        cat_ref[:, :cr] = wr_ref[...]
        padded = jnp.concatenate([wpt_ref[...], jnp.zeros_like(wpt_ref)], axis=0)
        cat_ref[:, cr:] = padded.T
        wcat_ref[...] = cat_ref[...]
        sums_ref[...] = jnp.zeros_like(sums_ref)

    x, g = x_ref[...], g_ref[...]
    both = mxu(x, cat_ref[...]).astype(BF16)
    mapped = mxu(g, we_ref[...]).astype(BF16)
    rd = jnp.concatenate([both[:, :cr], mapped], axis=1)
    rd_ref[...] = rd
    p_ref[...] = both[:, cr:]
    proj = both[:, cr : cr + nodes]
    sums_ref[:wide] += mxu(rd, x, ((0,), (0,)))
    sums_ref[wide : wide + nodes] += mxu(proj, x, ((0,), (0,)))
    sums_ref[wide + nodes :] += mxu(proj, g, ((0,), (0,)))

    @pl.when(pl.program_id(0) == pl.num_programs(0) - 1)
    def _():
        term_ref[0] = thirds(sums_ref[wide : wide + nodes], wr_ref[...])
        term_ref[1] = thirds(sums_ref[wide + nodes :], we_ref[...])
        me = where_ref[0]
        side = cube.traced_side(me)
        keep_ref[...] = term_ref[side]
        send_ref[...] = term_ref[1 - side]
        turned_ref[...] = sums_ref[...].T
        if sorted_here:
            size = kept_ref.shape[1]
            mine = [jnp.where(side == 0, a, b) for a, b in zip(cube.masks(0), cube.masks(1))]
            other = [jnp.where(side == 0, b, a) for a, b in zip(cube.masks(0), cube.masks(1))]
            for masks, base, out_ref in ((mine, me, kept_ref), (other, me ^ cube.core, sent_ref)):
                for j, mask in enumerate(masks):
                    at = pl.multiple_of((base ^ mask) * size, size)
                    out_ref[j] = turned_ref[pl.ds(at, size), :]


def gather(cube, where, x, g, wr, wpt, we):
    rows, chan = x.shape
    cr, nodes = wr.shape[1], wpt.shape[0]
    step = row_block(rows)
    width = 2 * cr + 2 * nodes
    half = cube.count // 2
    size = chan // cube.count
    sorted_here = size % 8 == 0
    rowspec = lambda wide: pl.BlockSpec((step, wide), lambda i: (i, 0))
    outs = [
        (rowspec(2 * cr), pltpu.HBM((rows, 2 * cr), BF16)),
        (rowspec(2 * nodes), pltpu.HBM((rows, 2 * nodes), BF16)),
        (whole((chan, cr + 2 * nodes)), pltpu.HBM((chan, cr + 2 * nodes), BF16)),
        (VMEM, pltpu.VMEM((nodes, cr), F32)),
        (VMEM, pltpu.VMEM((nodes, cr), F32)),
    ]
    scratch = [pltpu.VMEM((width, chan), F32)]
    if sorted_here:
        outs += [(VMEM, pltpu.VMEM((half, size, width), F32))] * 2
        scratch += [pltpu.VMEM((chan, width), F32)]
    else:
        outs += [(VMEM, jax.ShapeDtypeStruct((chan, width), F32))]
    scratch += [pltpu.VMEM((2, nodes, cr), F32), pltpu.VMEM((chan, cr + 2 * nodes), BF16)]
    rd, p, wcat, keep, send, *blocks = pl.pallas_call(
        functools.partial(gather_kernel, cube),
        grid=(rows // step,),
        in_specs=[SMEM, rowspec(chan), rowspec(chan), whole(wr.shape), whole(wpt.shape), whole(we.shape)],
        out_specs=[spec for spec, _ in outs],
        out_shape=[shape for _, shape in outs],
        scratch_shapes=scratch,
        compiler_params=params(),
        cost_estimate=cost(2 * rows * chan * 1024, rows * chan * 4 + rows * 768),
        name="gather",
    )(where, *in_hbm(x, g, wr, wpt, we))
    if not sorted_here:
        me = where[0]
        side = cube.traced_side(me)
        table = jnp.array([cube.masks(0), cube.masks(1)], jnp.int32)
        cut = blocks[0].reshape(cube.count, size, width)
        blocks = [cut[me ^ table[side]], cut[me ^ cube.core ^ table[1 - side]]]
    return rd, p, wcat, keep, send, blocks[0], blocks[1]


def add_kernel(a_ref, b_ref, out_ref):
    out_ref[...] = a_ref[...] + b_ref[...]


def add(a, b):
    return pl.pallas_call(
        add_kernel,
        in_specs=[VMEM] * 2,
        out_specs=VMEM,
        out_shape=pltpu.VMEM(a.shape, F32),
        compiler_params=params(),
        cost_estimate=cost(a.size, 12 * a.size),
        name="add",
    )(a, b)


def halve_kernel(a_ref, b_ref, keep_ref, send_ref):
    half = keep_ref.shape[0]
    keep_ref[...] = a_ref[:half] + b_ref[:half]
    send_ref[...] = a_ref[half:] + b_ref[half:]


def halve(a, b):
    shape = (a.shape[0] // 2, *a.shape[1:])
    return pl.pallas_call(
        halve_kernel,
        in_specs=[VMEM] * 2,
        out_specs=[VMEM] * 2,
        out_shape=[pltpu.VMEM(shape, F32)] * 2,
        compiler_params=params(),
        cost_estimate=cost(a.size, 12 * a.size),
        name="halve",
    )(a, b)


def feature_kernel(
    step, scale, cube, where_ref, mine_ref, other_ref, adj_hbm, nw_hbm, wcat_hbm, rd_hbm, p_hbm, g_hbm,
    out_hbm, ga_ref, gn_ref, no_ref, dn_ref,
    adj_ref, nw_ref, wcat_ref, rd_ref, p_ref, g_ref, out_ref, mix_ref, dnb_ref,
    small_sem, in_sem, out_sem,
):
    nodes_n, cr = no_ref.shape
    rows = g_ref.shape[0]
    chunks = [pl.ds(start, step) for start in range(0, rows, step)]
    move = pltpu.make_async_copy
    small = [
        move(adj_hbm, adj_ref, small_sem.at[0]),
        move(nw_hbm, nw_ref, small_sem.at[1]),
        move(wcat_hbm, wcat_ref, small_sem.at[2]),
    ]
    loads = [
        [
            move(src.at[c], dst.at[c], in_sem.at[k, i])
            for k, (src, dst) in enumerate(((rd_hbm, rd_ref), (p_hbm, p_ref), (g_hbm, g_ref)))
        ]
        for i, c in enumerate(chunks)
    ]
    for copy in small:
        copy.start()
    for group in loads:
        for copy in group:
            copy.start()
    first = cube.traced_side(where_ref[0]) == 0
    mine, other = mine_ref[...], other_ref[...]
    nodes = scale * jnp.where(first, mine, other)
    d_node_out = jnp.where(first, other, mine)
    small[0].wait()
    small[1].wait()
    adj, nw = adj_ref[...], nw_ref[...]
    hidden = nodes - exact(adj, nodes)
    pre = exact(hidden, nw)
    node_out = jnp.maximum(pre, 0.0).astype(BF16)
    d_pre = jnp.where(pre > 0.0, d_node_out, 0.0)
    d_hidden = exact(d_pre, nw, ((1,), (1,)))
    d_nodes = d_hidden - exact(adj, d_hidden, ((0,), (0,)))
    dn = d_nodes.astype(BF16)
    no_ref[...] = node_out.astype(F32)
    dn_ref[...] = dn.astype(F32)
    dnb_ref[:nodes_n] = dn
    dnb_ref[nodes_n:] = jnp.zeros((nodes_n, cr), BF16)
    blank = jnp.zeros((cr, cr), BF16)
    zero = jnp.zeros((nodes_n, cr), F32)
    mix_ref[:cr, :cr] = jnp.concatenate([dn.astype(F32), zero], axis=0).T.astype(BF16)
    mix_ref[cr:, :cr] = blank
    mix_ref[:cr, cr:] = blank
    mix_ref[cr:, cr:] = jnp.concatenate([node_out.astype(F32), zero], axis=0).T.astype(BF16)
    small[2].wait()
    copies = []
    for i, c in enumerate(chunks):
        for copy in loads[i]:
            copy.wait()
        mixed = mxu(rd_ref[c], mix_ref[...])
        d_proj = (mixed[:, cr:] + scale * mixed[:, :cr]).astype(BF16)
        d_red = (scale * mxu(p_ref[c], dnb_ref[...])).astype(BF16)
        both = jnp.concatenate([d_red, d_proj], axis=1)
        out = g_ref[c].astype(F32) + mxu(both, wcat_ref[...], ((1,), (1,)))
        out_ref[c] = out.astype(BF16)
        copies.append(move(out_ref.at[c], out_hbm.at[c], out_sem.at[i]))
        copies[-1].start()
    gn_ref[...] = scale * exact(hidden, d_pre, ((0,), (0,)))
    ga_ref[...] = -scale * exact(d_hidden, nodes, ((1,), (1,)))
    for copy in copies:
        copy.wait()


def feature_grads(cube, where, mine, other, adjacency, node_weight, wcat, rd, p, g, scale):
    rows, chan = g.shape
    nodes, cr = adjacency.shape[0], node_weight.shape[0]
    step = row_block(rows)
    count = rows // step
    loaded = (adjacency, node_weight, wcat, rd, p, g)
    return pl.pallas_call(
        functools.partial(feature_kernel, step, scale, cube),
        in_specs=[SMEM, VMEM, VMEM] + [HBM] * 6,
        out_specs=[HBM] + [VMEM] * 4,
        out_shape=[
            pltpu.HBM((rows, chan), BF16),
            jax.ShapeDtypeStruct((nodes, nodes), F32),
            jax.ShapeDtypeStruct((cr, cr), F32),
            pltpu.VMEM((nodes, cr), F32),
            pltpu.VMEM((nodes, cr), F32),
        ],
        scratch_shapes=[pltpu.VMEM(value.shape, value.dtype) for value in loaded]
        + [
            pltpu.VMEM((rows, chan), BF16),
            pltpu.VMEM((2 * cr, 2 * cr), BF16),
            pltpu.VMEM((2 * nodes, cr), BF16),
            pltpu.SemaphoreType.DMA((3,)),
            pltpu.SemaphoreType.DMA((3, count)),
            pltpu.SemaphoreType.DMA((count,)),
        ],
        compiler_params=params(),
        cost_estimate=cost(2 * rows * 4 * 65536, rows * chan * 4 + rows * 768),
        name="feature_grads",
    )(where, mine, other, *in_hbm(*loaded))


def finish_kernel(scale, kept_ref, got_ref, no_ref, dn_ref, gr_ref, gp_ref, ge_ref):
    total = kept_ref[0] + got_ref[0]
    nodes, cr = no_ref.shape
    no, dn = no_ref[...], dn_ref[...]
    x_red, x_dm = total[:, :cr], total[:, cr : 2 * cr]
    cross = total[:, 2 * cr : 2 * cr + nodes]
    g_proj = total[:, 2 * cr + nodes :]
    gr_ref[...] = scale * scale * exact(cross, dn)
    gp_ref[...] = scale * exact(x_dm, no, ((1,), (1,))) + scale * scale * exact(
        x_red, dn, ((1,), (1,))
    )
    ge_ref[...] = scale * exact(g_proj, no)


def finish(kept, got, no, dn, scale):
    rows = kept.shape[1]
    nodes, cr = no.shape
    return pl.pallas_call(
        functools.partial(finish_kernel, scale),
        in_specs=[VMEM] * 4,
        out_specs=[VMEM] * 3,
        out_shape=[
            jax.ShapeDtypeStruct((rows, cr), F32),
            jax.ShapeDtypeStruct((rows, nodes), F32),
            jax.ShapeDtypeStruct((rows, cr), F32),
        ],
        compiler_params=params(),
        cost_estimate=cost(0, rows * 4096),
        name="finish",
    )(kept, got, no, dn)


def on_device(
    cube, features, cotangent, reduce_weight, project_weight, expand_weight, adjacency, node_weight
):
    size_x, size_y, size_z, chan = features.shape
    local = size_x * size_y * size_z
    scale = 1.0 / math.sqrt(local * cube.count)
    flat_x = features.transpose(0, 2, 1, 3).reshape(local, chan)
    flat_g = cotangent.transpose(0, 2, 1, 3).reshape(local, chan)
    me = lax.axis_index(AXES).astype(jnp.int32)
    where = me.reshape(1)

    rd, p, wcat, keep, send, kept, sent = gather(
        cube, where, flat_x, flat_g, reduce_weight, project_weight.T, expand_weight
    )
    mine = add(keep, cube.swap(send, -1))
    got = cube.swap(sent, -1)
    for level in range(cube.rounds):
        mine_got = cube.swap(mine, level)
        kept, sent = halve(kept, got)
        got = cube.swap(sent, level)
        mine = add(mine, mine_got)
    other = cube.swap(mine, -1)

    flat_out, grad_adjacency, grad_node, no, dn = feature_grads(
        cube, where, mine, other, adjacency, node_weight, wcat, rd, p, flat_g, scale
    )
    grad_reduce, grad_project, grad_expand = finish(kept, got, no, dn, scale)
    grad_features = flat_out.reshape(size_x, size_z, size_y, chan).transpose(0, 2, 1, 3)
    return (grad_features, grad_reduce, grad_project, grad_expand, grad_adjacency, grad_node)


def solution(mesh):
    return jax.shard_map(
        functools.partial(on_device, Cube(mesh)),
        mesh=mesh,
        in_specs=(P("gx", "gy", "gz", None), P("gx", "gy", "gz", None), P(), P(), P(), P(), P()),
        out_specs=(
            P("gx", "gy", "gz", None),
            P(AXES, None),
            P(AXES, None),
            P(AXES, None),
            P(),
            P(),
        ),
        check_vma=False,
    )
```

time: 73.5 us -> 44.7 us (0.61)
  starting transfers between devices: 24.4 us -> 14.2 us
  local copies, waits for them, and re-layouts: 8.12 us -> 0 us
  Pallas kernels: 23 us -> 17.5 us
  blocking collectives: 3.78 us -> 0 us
    all_to_all x6 -> x0, starting transfers between devices: 24.4 us -> none  [exchange(): return lax.all_to_all(value, axis, 0, 0, tiled=True)]
    ppermute x0 -> x11, starting transfers between devices: none -> 14.2 us  [swap(): return lax.ppermute(value, AXES, pairs)]
    all_to_all x6 -> x0, waiting for transfers between devices: 12.7 us -> none  [exchange(): return lax.all_to_all(value, axis, 0, 0, tiled=True)]
    ppermute x0 -> x11, waiting for transfers between devices: none -> 12 us  [swap(): return lax.ppermute(value, AXES, pairs)]
    unnamed x12 -> x0, local copies, waits for them, and re-layouts: 8.12 us -> none
    pallas_call x8 -> x11, Pallas kernels: 22.1 us -> 16.6 us  [the longest x1 8.91 us: gather(): pl.pallas_call(functools.partial(gather_kernel, cube), grid=(rows // step...]
    all_to_all x1 -> x0, blocking collectives: 3.78 us -> none  [exchange(): return lax.all_to_all(value, axis, 0, 0, tiled=True)]
  transfers between devices with their start and end apart: 6 -> 11, of which waited for: 4 -> 7; matrix products, arithmetic and copies ran while one was open for 0% -> 0% of each run, Pallas kernels for 18% -> 17%
where the time goes in v4:
time: 44.7 us; the launch traced here: 44.4 us
  Pallas kernels  17.5 us (39%)
  starting transfers between devices  14.2 us (32%)
  waiting for transfers between devices  12 us (27%)
  between operations  0.69 us (2%)
    ppermute x11, starting transfers between devices, swap(): return lax.ppermute(value, AXES, pairs)  14.2 us
    ppermute x11, waiting for transfers between devices, swap(): return lax.ppermute(value, AXES, pairs)  12 us
    pallas_call x1, Pallas kernels, gather(): pl.pallas_call(functools.partial(gather_kernel, cube), grid=(rows // step...  8.91 us
    pallas_call x1, Pallas kernels, feature_grads(): pl.pallas_call(functools.partial(feature_kernel, step, scale, cube), in_s...  7.62 us
  transfers between devices with their start and end apart: 11, of which 7 were waited for; matrix products, arithmetic and copies ran while one was open for 0% of the time, Pallas kernels for 17%

profile of v4, /device:TPU:0, one launch (start us, length us, event | category | flops | bytes accessed | tf_op | source)
XLA Modules:
  0.0 44.4 jit_solution(7377316217936378026)
XLA Ops:
  0.6 8.9 %gather.1 = (bf16[3072,256]{1,0:T(8,128)(2,1)}, bf16[3072,128]{1,0:T(8,128)(2,1)}, bf16[512,256]{1,0:T(8,128)(2,1)}, f32[64,128]{1,0:T(8,128)S(1)}, f32[64,128]{...) custom-call(s32[1]{0:T(128)} %bitcast.where_ref, bf16[3072,512]{1,0:T(8,128)(2,1)} %bitcast.11, ...), custom_call_target="tpu_custom_call" | custom-call | flops 3221225472 | bytes 8650752 | tf_op jit(solution)/shard_map/gather/pallas_call | solution.py:172
  9.6 0.5 %collective-permute-start.6 = (f32[16,16,384]{2,1,0:T(8,128)S(1)}, f32[16,16,384]{2,1,0:T(8,128)S(1)}, u32[]{:S(2)}, u32[]{:S(2)}) collective-permute-start(f32[16,16,384]{2,1,0:T(8,128)S(1)} %get-tuple-element.36), channel_id=1, source_target_pairs={{0,4},{1,5},{2,6},{3,7},{4,0},{5,1},{6,2},{7,3},{8,12},{9,13},{10,... | collective-permute-start | bytes 1179656 | tf_op jit(solution)/shard_map/ppermute | solution.py:77
  10.1 1.3 %collective-permute-done.6.b_ref = f32[16,16,384]{2,1,0:T(8,128)S(1)} collective-permute-done((f32[16,16,384]{2,1,0:T(8,128)S(1)}, f32[16,16,384]{2,1,0:T(8,128)S(1)}, u32[]{:S(2)}, u32[]{:S(2)}) %collective-permute-start.6) | collective-permute-done | bytes 393248 | tf_op jit(solution)/shard_map/ppermute | solution.py:77
  11.4 2.9 %collective-permute-start.7 = (f32[8,16,384]{2,1,0:T(8,128)S(1)}, f32[8,16,384]{2,1,0:T(8,128)S(1)}, u32[]{:S(2)}, u32[]{:S(2)}) collective-permute-start(f32[8,16,384]{2,1,0:T(8,128)S(1)} %get-tuple-element.38), channel_id=1, source_target_pairs={{0,8},{1,9},{2,10},{3,11},{4,20},{5,21},{6,22},{7,23},{8,0},{9,1},... | collective-permute-start | bytes 589832 | tf_op jit(solution)/shard_map/ppermute | solution.py:77
  14.4 0.0 collective-permute-start
  14.4 1.2 %collective-permute-done.b_ref = f32[64,128]{1,0:T(8,128)S(1)} collective-permute-done((f32[64,128]{1,0:T(8,128)S(1)}, f32[64,128]{1,0:T(8,128)S(1)}, u32[]{:S(2)}, u32[]{:S(2)}) %collective-permute-start) | collective-permute-done | bytes 32800 | tf_op jit(solution)/shard_map/ppermute | solution.py:77
  15.6 1.0 %collective-permute-start.1 = (f32[64,128]{1,0:T(8,128)S(1)}, f32[64,128]{1,0:T(8,128)S(1)}, u32[]{:S(2)}, u32[]{:S(2)}) collective-permute-start(f32[64,128]{1,0:T(8,128)S(1)} %add.13.a_ref), channel_id=1, source_target_pairs={{0,8},{1,9},{2,10},{3,11},{4,20},{5,21},{6,22},{7,23},{8,0},{9,1},... | collective-permute-start | bytes 98312 | tf_op jit(solution)/shard_map/ppermute | solution.py:77
  16.6 1.4 %collective-permute-done.7.b_ref = f32[8,16,384]{2,1,0:T(8,128)S(1)} collective-permute-done((f32[8,16,384]{2,1,0:T(8,128)S(1)}, f32[8,16,384]{2,1,0:T(8,128)S(1)}, u32[]{:S(2)}, u32[]{:S(2)}) %collective-permute-start.7) | collective-permute-done | bytes 196640 | tf_op jit(solution)/shard_map/ppermute | solution.py:77
  18.1 2.1 %collective-permute-start.8 = (f32[4,16,384]{2,1,0:T(8,128)S(1)}, f32[4,16,384]{2,1,0:T(8,128)S(1)}, u32[]{:S(2)}, u32[]{:S(2)}) collective-permute-start(f32[4,16,384]{2,1,0:T(8,128)S(1)} %get-tuple-element.40), channel_id=1, source_target_pairs={{0,16},{1,17},{2,18},{3,19},{4,12},{5,13},{6,14},{7,15},{8,24},{9,... | collective-permute-start | bytes 294920 | tf_op jit(solution)/shard_map/ppermute | solution.py:77
  20.2 0.0 collective-permute-done.1.b_ref
  20.2 0.8 %collective-permute-start.2 = (f32[64,128]{1,0:T(8,128)S(1)}, f32[64,128]{1,0:T(8,128)S(1)}, u32[]{:S(2)}, u32[]{:S(2)}) collective-permute-start(f32[64,128]{1,0:T(8,128)S(1)} %add.14.a_ref), channel_id=1, source_target_pairs={{0,16},{1,17},{2,18},{3,19},{4,12},{5,13},{6,14},{7,15},{8,24},{9,... | collective-permute-start | bytes 98312 | tf_op jit(solution)/shard_map/ppermute | solution.py:77
  21.0 3.1 %collective-permute-done.2.b_ref = f32[64,128]{1,0:T(8,128)S(1)} collective-permute-done((f32[64,128]{1,0:T(8,128)S(1)}, f32[64,128]{1,0:T(8,128)S(1)}, u32[]{:S(2)}, u32[]{:S(2)}) %collective-permute-start.2) | collective-permute-done | bytes 32800 | tf_op jit(solution)/shard_map/ppermute | solution.py:77
  24.2 1.6 %collective-permute-start.3 = (f32[64,128]{1,0:T(8,128)S(1)}, f32[64,128]{1,0:T(8,128)S(1)}, u32[]{:S(2)}, u32[]{:S(2)}) collective-permute-start(f32[64,128]{1,0:T(8,128)S(1)} %add.15.a_ref), channel_id=1, source_target_pairs={{0,1},{1,0},{2,3},{3,2},{4,5},{5,4},{6,7},{7,6},{8,9},{9,8},{10,11... | collective-permute-start | bytes 98312 | tf_op jit(solution)/shard_map/ppermute | solution.py:77
  25.7 2.4 %collective-permute-done.3.b_ref = f32[64,128]{1,0:T(8,128)S(1)} collective-permute-done((f32[64,128]{1,0:T(8,128)S(1)}, f32[64,128]{1,0:T(8,128)S(1)}, u32[]{:S(2)}, u32[]{:S(2)}) %collective-permute-start.3) | collective-permute-done | bytes 32800 | tf_op jit(solution)/shard_map/ppermute | solution.py:77
  28.1 2.8 %collective-permute-start.4 = (f32[64,128]{1,0:T(8,128)S(1)}, f32[64,128]{1,0:T(8,128)S(1)}, u32[]{:S(2)}, u32[]{:S(2)}) collective-permute-start(f32[64,128]{1,0:T(8,128)S(1)} %add.16.a_ref), channel_id=1, source_target_pairs={{0,2},{1,3},{2,0},{3,1},{4,6},{5,7},{6,4},{7,5},{8,10},{9,11},{10,... | collective-permute-start | bytes 98312 | tf_op jit(solution)/shard_map/ppermute | solution.py:77
  30.9 0.0 collective-permute-done.8.b_ref
  31.0 1.7 %collective-permute-start.9 = (f32[2,16,384]{2,1,0:T(8,128)S(1)}, f32[2,16,384]{2,1,0:T(8,128)S(1)}, u32[]{:S(2)}, u32[]{:S(2)}) collective-permute-start(f32[2,16,384]{2,1,0:T(8,128)S(1)} %get-tuple-element.42), channel_id=1, source_target_pairs={{0,1},{1,0},{2,3},{3,2},{4,5},{5,4},{6,7},{7,6},{8,9},{9,8},{10,11... | collective-permute-start | bytes 147464 | tf_op jit(solution)/shard_map/ppermute | solution.py:77
  32.7 0.3 collective-permute-done.4.b_ref
  32.9 0.0 collective-permute-start.5
  32.9 2.2 %collective-permute-done.9.b_ref = f32[2,16,384]{2,1,0:T(8,128)S(1)} collective-permute-done((f32[2,16,384]{2,1,0:T(8,128)S(1)}, f32[2,16,384]{2,1,0:T(8,128)S(1)}, u32[]{:S(2)}, u32[]{:S(2)}) %collective-permute-start.9) | collective-permute-done | bytes 49184 | tf_op jit(solution)/shard_map/ppermute | solution.py:77
  35.1 0.8 %collective-permute-start.10 = (f32[1,16,384]{2,1,0:T(8,128)S(1)}, f32[1,16,384]{2,1,0:T(8,128)S(1)}, u32[]{:S(2)}, u32[]{:S(2)}) collective-permute-start(f32[1,16,384]{2,1,0:T(8,128)S(1)} %get-tuple-element.44), channel_id=1, source_target_pairs={{0,2},{1,3},{2,0},{3,1},{4,6},{5,7},{6,4},{7,5},{8,10},{9,11},{10,... | collective-permute-start | bytes 73736 | tf_op jit(solution)/shard_map/ppermute | solution.py:77
  35.9 7.6 %feature_grads.1 = (bf16[3072,512]{1,0:T(8,128)(2,1)}, f32[64,64]{1,0:T(8,128)}, f32[128,128]{1,0:T(8,128)}, f32[64,128]{1,0:T(8,128)S(1)}, f32[64,128]{1,0:T(8,128)S(1)}) custom-call(s32[1]{0:T(128)} %bitcast.where_ref, f32[64,128]{1,0:T(8,128)S(1)} %add.17.mine_ref, f32[64,128]{1,0:T(8,128)S(1)} %collective-permute-done.5.other_ref, f32[64,64]{1,0:T(8,128)} %adj_hbm.1, ...), custom_call_target="tpu_custom_call" | custom-call | flops 1610612736 | bytes 8650752 | tf_op jit(solution)/shard_map/feature_grads/pallas_call | solution.py:303
  43.5 0.0 collective-permute-done.10.got_ref
  43.5 0.9 %finish.1 = (f32[16,128]{1,0:T(8,128)}, f32[16,64]{1,0:T(8,128)}, f32[16,128]{1,0:T(8,128)}) custom-call(f32[1,16,384]{2,1,0:T(8,128)S(1)} %get-tuple-element.43.kept_ref, f32[1,16,384]{2,1,0:T(8,128)S(1)} %collective-permute-done.10.got_ref, f32[64,128]{1,0:T(8,128)S(1)} %get-tuple-element.45.no_ref, f32[64,128]{1,0:T(8,128)S(1)} %get-tuple-element.46.dn_ref), custom_call_target="tpu_custom_call" | custom-call | bytes 65536 | tf_op jit(solution)/shard_map/finish/pallas_call | solution.py:346
  (10 shorter events, 0.1 us)
Async XLA Ops:
  9.6 1.8 %collective-permute-start.6 = (f32[16,16,384]{2,1,0:T(8,128)S(1)}, f32[16,16,384]{2,1,0:T(8,128)S(1)}, u32[]{:S(2)}, u32[]{:S(2)}) collective-permute-start(f32[16,16,384]{2,1,0:T(8,128)S(1)} %get-tuple-element.36), channel_id=1, source_target_pairs={{0,4},{1,5},{2,6},{3,7},{4,0},{5,1},{6,2},{7,3},{8,12},{9,13},{10,... | collective-permute-start | bytes 1179656 | tf_op jit(solution)/shard_map/ppermute | solution.py:77
  11.4 6.6 %collective-permute-start.7 = (f32[8,16,384]{2,1,0:T(8,128)S(1)}, f32[8,16,384]{2,1,0:T(8,128)S(1)}, u32[]{:S(2)}, u32[]{:S(2)}) collective-permute-start(f32[8,16,384]{2,1,0:T(8,128)S(1)} %get-tuple-element.38), channel_id=1, source_target_pairs={{0,8},{1,9},{2,10},{3,11},{4,20},{5,21},{6,22},{7,23},{8,0},{9,1},... | collective-permute-start | bytes 589832 | tf_op jit(solution)/shard_map/ppermute | solution.py:77
  14.4 1.2 %collective-permute-start = (f32[64,128]{1,0:T(8,128)S(1)}, f32[64,128]{1,0:T(8,128)S(1)}, u32[]{:S(2)}, u32[]{:S(2)}) collective-permute-start(f32[64,128]{1,0:T(8,128)S(1)} %get-tuple-element.30), channel_id=1, source_target_pairs={{0,4},{1,5},{2,6},{3,7},{4,0},{5,1},{6,2},{7,3},{8,12},{9,13},{10,... | collective-permute-start | bytes 98312 | tf_op jit(solution)/shard_map/ppermute | solution.py:77
  15.6 4.6 %collective-permute-start.1 = (f32[64,128]{1,0:T(8,128)S(1)}, f32[64,128]{1,0:T(8,128)S(1)}, u32[]{:S(2)}, u32[]{:S(2)}) collective-permute-start(f32[64,128]{1,0:T(8,128)S(1)} %add.13.a_ref), channel_id=1, source_target_pairs={{0,8},{1,9},{2,10},{3,11},{4,20},{5,21},{6,22},{7,23},{8,0},{9,1},... | collective-permute-start | bytes 98312 | tf_op jit(solution)/shard_map/ppermute | solution.py:77
  18.1 12.9 %collective-permute-start.8 = (f32[4,16,384]{2,1,0:T(8,128)S(1)}, f32[4,16,384]{2,1,0:T(8,128)S(1)}, u32[]{:S(2)}, u32[]{:S(2)}) collective-permute-start(f32[4,16,384]{2,1,0:T(8,128)S(1)} %get-tuple-element.40), channel_id=1, source_target_pairs={{0,16},{1,17},{2,18},{3,19},{4,12},{5,13},{6,14},{7,15},{8,24},{9,... | collective-permute-start | bytes 294920 | tf_op jit(solution)/shard_map/ppermute | solution.py:77
  20.2 4.0 %collective-permute-start.2 = (f32[64,128]{1,0:T(8,128)S(1)}, f32[64,128]{1,0:T(8,128)S(1)}, u32[]{:S(2)}, u32[]{:S(2)}) collective-permute-start(f32[64,128]{1,0:T(8,128)S(1)} %add.14.a_ref), channel_id=1, source_target_pairs={{0,16},{1,17},{2,18},{3,19},{4,12},{5,13},{6,14},{7,15},{8,24},{9,... | collective-permute-start | bytes 98312 | tf_op jit(solution)/shard_map/ppermute | solution.py:77
  24.2 3.9 %collective-permute-start.3 = (f32[64,128]{1,0:T(8,128)S(1)}, f32[64,128]{1,0:T(8,128)S(1)}, u32[]{:S(2)}, u32[]{:S(2)}) collective-permute-start(f32[64,128]{1,0:T(8,128)S(1)} %add.15.a_ref), channel_id=1, source_target_pairs={{0,1},{1,0},{2,3},{3,2},{4,5},{5,4},{6,7},{7,6},{8,9},{9,8},{10,11... | collective-permute-start | bytes 98312 | tf_op jit(solution)/shard_map/ppermute | solution.py:77
  28.1 4.8 %collective-permute-start.4 = (f32[64,128]{1,0:T(8,128)S(1)}, f32[64,128]{1,0:T(8,128)S(1)}, u32[]{:S(2)}, u32[]{:S(2)}) collective-permute-start(f32[64,128]{1,0:T(8,128)S(1)} %add.16.a_ref), channel_id=1, source_target_pairs={{0,2},{1,3},{2,0},{3,1},{4,6},{5,7},{6,4},{7,5},{8,10},{9,11},{10,... | collective-permute-start | bytes 98312 | tf_op jit(solution)/shard_map/ppermute | solution.py:77
  31.0 4.2 %collective-permute-start.9 = (f32[2,16,384]{2,1,0:T(8,128)S(1)}, f32[2,16,384]{2,1,0:T(8,128)S(1)}, u32[]{:S(2)}, u32[]{:S(2)}) collective-permute-start(f32[2,16,384]{2,1,0:T(8,128)S(1)} %get-tuple-element.42), channel_id=1, source_target_pairs={{0,1},{1,0},{2,3},{3,2},{4,5},{5,4},{6,7},{7,6},{8,9},{9,8},{10,11... | collective-permute-start | bytes 147464 | tf_op jit(solution)/shard_map/ppermute | solution.py:77
  32.9 3.0 %collective-permute-start.5 = (f32[64,128]{1,0:T(8,128)S(1)}, f32[64,128]{1,0:T(8,128)S(1)}, u32[]{:S(2)}, u32[]{:S(2)}) collective-permute-start(f32[64,128]{1,0:T(8,128)S(1)} %add.17.mine_ref), channel_id=1, source_target_pairs={{0,4},{1,5},{2,6},{3,7},{4,0},{5,1},{6,2},{7,3},{8,12},{9,13},{10,... | collective-permute-start | bytes 98312 | tf_op jit(solution)/shard_map/ppermute | solution.py:77
  35.1 8.4 %collective-permute-start.10 = (f32[1,16,384]{2,1,0:T(8,128)S(1)}, f32[1,16,384]{2,1,0:T(8,128)S(1)}, u32[]{:S(2)}, u32[]{:S(2)}) collective-permute-start(f32[1,16,384]{2,1,0:T(8,128)S(1)} %get-tuple-element.44), channel_id=1, source_target_pairs={{0,2},{1,3},{2,0},{3,1},{4,6},{5,7},{6,4},{7,5},{8,10},{9,11},{10,... | collective-permute-start | bytes 73736 | tf_op jit(solution)/shard_map/ppermute | solution.py:77

commit v5 on v4

--- a/solution.py
+++ b/solution.py
@@ -43,9 +43,9 @@
     return [pltpu.with_memory_space_constraint(value, pltpu.HBM) for value in values]
 
 
-def row_block(total):
-    for size in (512, 384, 256, 128, 64, 32, 16):
-        if total % size == 0:
+def row_block(total, largest):
+    for size in (768, 512, 384, 256, 128, 64, 32, 16):
+        if size <= largest and total % size == 0:
             return size
     return total
 
@@ -85,25 +85,13 @@
         ]
 
 
-def thirds(value, weight):
-    rows = value.shape[0]
-    high = value.astype(BF16)
-    rest = value - high.astype(F32)
-    middle = rest.astype(BF16)
-    low = (rest - middle.astype(F32)).astype(BF16)
-    out = mxu(jnp.concatenate([high, middle, low], axis=0), weight)
-    return (out[2 * rows :] + out[rows : 2 * rows]) + out[:rows]
-
-
 def gather_kernel(
-    cube, where_ref, x_ref, g_ref, wr_ref, wpt_ref, we_ref,
-    rd_ref, p_ref, wcat_ref, keep_ref, send_ref, *rest,
+    cube, sorted_here, where_ref, x_ref, g_ref, wr_ref, wpt_ref, we_ref, rd_ref, p_ref, wcat_ref, *rest
 ):
-    sorted_here = len(rest) == 6
     if sorted_here:
         kept_ref, sent_ref, sums_ref, turned_ref, term_ref, cat_ref = rest
     else:
-        turned_ref, sums_ref, term_ref, cat_ref = rest
+        keep_ref, send_ref, turned_ref, sums_ref, term_ref, cat_ref = rest
     cr = wr_ref.shape[1]
     nodes = wpt_ref.shape[0]
     wide = 2 * cr
@@ -115,6 +103,7 @@
         cat_ref[:, cr:] = padded.T
         wcat_ref[...] = cat_ref[...]
         sums_ref[...] = jnp.zeros_like(sums_ref)
+        term_ref[...] = jnp.zeros_like(term_ref)
 
     x, g = x_ref[...], g_ref[...]
     both = mxu(x, cat_ref[...]).astype(BF16)
@@ -122,34 +111,42 @@
     rd = jnp.concatenate([both[:, :cr], mapped], axis=1)
     rd_ref[...] = rd
     p_ref[...] = both[:, cr:]
-    proj = both[:, cr : cr + nodes]
-    sums_ref[:wide] += mxu(rd, x, ((0,), (0,)))
-    sums_ref[wide : wide + nodes] += mxu(proj, x, ((0,), (0,)))
-    sums_ref[wide + nodes :] += mxu(proj, g, ((0,), (0,)))
+    turned = jnp.concatenate([rd, both[:, cr:]], axis=1).T
+    proj = turned[wide : wide + nodes]
+    sums_ref[: wide + nodes] += mxu(turned[: wide + nodes], x)
+    sums_ref[wide + nodes :] += mxu(proj, g)
+    term = mxu(proj, rd)
+    term_ref[0] += term[:, :cr]
+    term_ref[1] += term[:, cr:]
 
     @pl.when(pl.program_id(0) == pl.num_programs(0) - 1)
     def _():
-        term_ref[0] = thirds(sums_ref[wide : wide + nodes], wr_ref[...])
-        term_ref[1] = thirds(sums_ref[wide + nodes :], we_ref[...])
         me = where_ref[0]
         side = cube.traced_side(me)
-        keep_ref[...] = term_ref[side]
-        send_ref[...] = term_ref[1 - side]
         turned_ref[...] = sums_ref[...].T
-        if sorted_here:
-            size = kept_ref.shape[1]
+        if not sorted_here:
+            keep_ref[...] = term_ref[side]
+            send_ref[...] = term_ref[1 - side]
+        else:
+            kept_ref[:nodes] = term_ref[side]
+            sent_ref[:nodes] = term_ref[1 - side]
+            size = turned_ref.shape[0] // cube.count
             mine = [jnp.where(side == 0, a, b) for a, b in zip(cube.masks(0), cube.masks(1))]
             other = [jnp.where(side == 0, b, a) for a, b in zip(cube.masks(0), cube.masks(1))]
             for masks, base, out_ref in ((mine, me, kept_ref), (other, me ^ cube.core, sent_ref)):
-                for j, mask in enumerate(masks):
+                to = nodes
+                for mask in masks:
                     at = pl.multiple_of((base ^ mask) * size, size)
-                    out_ref[j] = turned_ref[pl.ds(at, size), :]
+                    block = turned_ref[pl.ds(at, size), :]
+                    for lane in range(0, block.shape[1], cr):
+                        out_ref[to : to + size] = block[:, lane : lane + cr]
+                        to += size
 
 
 def gather(cube, where, x, g, wr, wpt, we):
     rows, chan = x.shape
     cr, nodes = wr.shape[1], wpt.shape[0]
-    step = row_block(rows)
+    step = row_block(rows, 768)
     width = 2 * cr + 2 * nodes
     half = cube.count // 2
     size = chan // cube.count
@@ -159,18 +156,17 @@
         (rowspec(2 * cr), pltpu.HBM((rows, 2 * cr), BF16)),
         (rowspec(2 * nodes), pltpu.HBM((rows, 2 * nodes), BF16)),
         (whole((chan, cr + 2 * nodes)), pltpu.HBM((chan, cr + 2 * nodes), BF16)),
-        (VMEM, pltpu.VMEM((nodes, cr), F32)),
-        (VMEM, pltpu.VMEM((nodes, cr), F32)),
     ]
     scratch = [pltpu.VMEM((width, chan), F32)]
     if sorted_here:
-        outs += [(VMEM, pltpu.VMEM((half, size, width), F32))] * 2
+        outs += [(VMEM, pltpu.VMEM((nodes + half * size * width // cr, cr), F32))] * 2
         scratch += [pltpu.VMEM((chan, width), F32)]
     else:
+        outs += [(VMEM, jax.ShapeDtypeStruct((nodes, cr), F32))] * 2
         outs += [(VMEM, jax.ShapeDtypeStruct((chan, width), F32))]
     scratch += [pltpu.VMEM((2, nodes, cr), F32), pltpu.VMEM((chan, cr + 2 * nodes), BF16)]
-    rd, p, wcat, keep, send, *blocks = pl.pallas_call(
-        functools.partial(gather_kernel, cube),
+    rd, p, wcat, kept, sent, *sums = pl.pallas_call(
+        functools.partial(gather_kernel, cube, sorted_here),
         grid=(rows // step,),
         in_specs=[SMEM, rowspec(chan), rowspec(chan), whole(wr.shape), whole(wpt.shape), whole(we.shape)],
         out_specs=[spec for spec, _ in outs],
@@ -181,56 +177,49 @@
         name="gather",
     )(where, *in_hbm(x, g, wr, wpt, we))
     if not sorted_here:
-        me = where[0]
-        side = cube.traced_side(me)
+        side = cube.traced_side(where[0])
         table = jnp.array([cube.masks(0), cube.masks(1)], jnp.int32)
-        cut = blocks[0].reshape(cube.count, size, width)
-        blocks = [cut[me ^ table[side]], cut[me ^ cube.core ^ table[1 - side]]]
-    return rd, p, wcat, keep, send, blocks[0], blocks[1]
-
-
-def add_kernel(a_ref, b_ref, out_ref):
-    out_ref[...] = a_ref[...] + b_ref[...]
-
-
-def add(a, b):
+        cut = sums[0].reshape(cube.count, size, width // cr, cr).transpose(0, 2, 1, 3)
+        lay = lambda head, index: jnp.concatenate([head, cut[index].reshape(-1, cr)])
+        kept = lay(kept, where[0] ^ table[side])
+        sent = lay(sent, where[0] ^ cube.core ^ table[1 - side])
+    return rd, p, wcat, kept, sent
+
+
+def step_kernel(head, a_ref, b_ref, keep_ref, send_ref):
+    half = send_ref.shape[0] - head
+    nodes = a_ref[:head] + b_ref[:head]
+    send_ref[:head] = nodes
+    if half:
+        keep_ref[:head] = nodes
+        keep_ref[head:] = a_ref[head : head + half] + b_ref[head : head + half]
+        send_ref[head:] = a_ref[head + half :] + b_ref[head + half :]
+    else:
+        keep_ref[...] = a_ref[head:] + b_ref[head:]
+
+
+def step(head, last, a, b):
+    rest, lanes = a.shape[0] - head, a.shape[1]
+    shapes = (rest, head) if last else (head + rest // 2,) * 2
     return pl.pallas_call(
-        add_kernel,
+        functools.partial(step_kernel, head),
         in_specs=[VMEM] * 2,
-        out_specs=VMEM,
-        out_shape=pltpu.VMEM(a.shape, F32),
+        out_specs=[VMEM] * 2,
+        out_shape=[pltpu.VMEM((size, lanes), F32) for size in shapes],
         compiler_params=params(),
         cost_estimate=cost(a.size, 12 * a.size),
-        name="add",
+        name="step",
     )(a, b)
 
 
-def halve_kernel(a_ref, b_ref, keep_ref, send_ref):
-    half = keep_ref.shape[0]
-    keep_ref[...] = a_ref[:half] + b_ref[:half]
-    send_ref[...] = a_ref[half:] + b_ref[half:]
-
-
-def halve(a, b):
-    shape = (a.shape[0] // 2, *a.shape[1:])
-    return pl.pallas_call(
-        halve_kernel,
-        in_specs=[VMEM] * 2,
-        out_specs=[VMEM] * 2,
-        out_shape=[pltpu.VMEM(shape, F32)] * 2,
-        compiler_params=params(),
-        cost_estimate=cost(a.size, 12 * a.size),
-        name="halve",
-    )(a, b)
-
-
 def feature_kernel(
-    step, scale, cube, where_ref, mine_ref, other_ref, adj_hbm, nw_hbm, wcat_hbm, rd_hbm, p_hbm, g_hbm,
-    out_hbm, ga_ref, gn_ref, no_ref, dn_ref,
+    step, scale, cube, where_ref, mine_ref, other_ref, sums_ref,
+    adj_hbm, nw_hbm, wcat_hbm, rd_hbm, p_hbm, g_hbm,
+    out_hbm, gr_ref, gp_ref, ge_ref, ga_ref, gn_ref,
     adj_ref, nw_ref, wcat_ref, rd_ref, p_ref, g_ref, out_ref, mix_ref, dnb_ref,
     small_sem, in_sem, out_sem,
 ):
-    nodes_n, cr = no_ref.shape
+    nodes_n, cr = mine_ref.shape
     rows = g_ref.shape[0]
     chunks = [pl.ds(start, step) for start in range(0, rows, step)]
     move = pltpu.make_async_copy
@@ -265,8 +254,6 @@
     d_hidden = exact(d_pre, nw, ((1,), (1,)))
     d_nodes = d_hidden - exact(adj, d_hidden, ((0,), (0,)))
     dn = d_nodes.astype(BF16)
-    no_ref[...] = node_out.astype(F32)
-    dn_ref[...] = dn.astype(F32)
     dnb_ref[:nodes_n] = dn
     dnb_ref[nodes_n:] = jnp.zeros((nodes_n, cr), BF16)
     blank = jnp.zeros((cr, cr), BF16)
@@ -290,26 +277,36 @@
         copies[-1].start()
     gn_ref[...] = scale * exact(hidden, d_pre, ((0,), (0,)))
     ga_ref[...] = -scale * exact(d_hidden, nodes, ((1,), (1,)))
+    no_f, dn_f = node_out.astype(F32), dn.astype(F32)
+    size = gr_ref.shape[0]
+    x_red, x_dm, with_proj = (sums_ref[k * size : (k + 1) * size] for k in range(3))
+    gr_ref[...] = scale * scale * exact(with_proj[:, :nodes_n], dn_f)
+    gp_ref[...] = scale * exact(x_dm, no_f, ((1,), (1,))) + scale * scale * exact(
+        x_red, dn_f, ((1,), (1,))
+    )
+    ge_ref[...] = scale * exact(with_proj[:, nodes_n:], no_f)
     for copy in copies:
         copy.wait()
 
 
-def feature_grads(cube, where, mine, other, adjacency, node_weight, wcat, rd, p, g, scale):
+def feature_grads(cube, where, mine, other, sums, adjacency, node_weight, wcat, rd, p, g, scale):
     rows, chan = g.shape
     nodes, cr = adjacency.shape[0], node_weight.shape[0]
-    step = row_block(rows)
+    step = row_block(rows, 512)
     count = rows // step
+    size = chan // cube.count
     loaded = (adjacency, node_weight, wcat, rd, p, g)
     return pl.pallas_call(
         functools.partial(feature_kernel, step, scale, cube),
-        in_specs=[SMEM, VMEM, VMEM] + [HBM] * 6,
-        out_specs=[HBM] + [VMEM] * 4,
+        in_specs=[SMEM, VMEM, VMEM, VMEM] + [HBM] * 6,
+        out_specs=[HBM] + [VMEM] * 5,
         out_shape=[
             pltpu.HBM((rows, chan), BF16),
+            jax.ShapeDtypeStruct((size, cr), F32),
+            jax.ShapeDtypeStruct((size, nodes), F32),
+            jax.ShapeDtypeStruct((size, cr), F32),
             jax.ShapeDtypeStruct((nodes, nodes), F32),
             jax.ShapeDtypeStruct((cr, cr), F32),
-            pltpu.VMEM((nodes, cr), F32),
-            pltpu.VMEM((nodes, cr), F32),
         ],
         scratch_shapes=[pltpu.VMEM(value.shape, value.dtype) for value in loaded]
         + [
@@ -323,39 +320,7 @@
         compiler_params=params(),
         cost_estimate=cost(2 * rows * 4 * 65536, rows * chan * 4 + rows * 768),
         name="feature_grads",
-    )(where, mine, other, *in_hbm(*loaded))
-
-
-def finish_kernel(scale, kept_ref, got_ref, no_ref, dn_ref, gr_ref, gp_ref, ge_ref):
-    total = kept_ref[0] + got_ref[0]
-    nodes, cr = no_ref.shape
-    no, dn = no_ref[...], dn_ref[...]
-    x_red, x_dm = total[:, :cr], total[:, cr : 2 * cr]
-    cross = total[:, 2 * cr : 2 * cr + nodes]
-    g_proj = total[:, 2 * cr + nodes :]
-    gr_ref[...] = scale * scale * exact(cross, dn)
-    gp_ref[...] = scale * exact(x_dm, no, ((1,), (1,))) + scale * scale * exact(
-        x_red, dn, ((1,), (1,))
-    )
-    ge_ref[...] = scale * exact(g_proj, no)
-
-
-def finish(kept, got, no, dn, scale):
-    rows = kept.shape[1]
-    nodes, cr = no.shape
-    return pl.pallas_call(
-        functools.partial(finish_kernel, scale),
-        in_specs=[VMEM] * 4,
-        out_specs=[VMEM] * 3,
-        out_shape=[
-            jax.ShapeDtypeStruct((rows, cr), F32),
-            jax.ShapeDtypeStruct((rows, nodes), F32),
-            jax.ShapeDtypeStruct((rows, cr), F32),
-        ],
-        compiler_params=params(),
-        cost_estimate=cost(0, rows * 4096),
-        name="finish",
-    )(kept, got, no, dn)
+    )(where, mine, other, sums, *in_hbm(*loaded))
 
 
 def on_device(
@@ -369,22 +334,17 @@
     me = lax.axis_index(AXES).astype(jnp.int32)
     where = me.reshape(1)
 
-    rd, p, wcat, keep, send, kept, sent = gather(
+    rd, p, wcat, kept, sent = gather(
         cube, where, flat_x, flat_g, reduce_weight, project_weight.T, expand_weight
     )
-    mine = add(keep, cube.swap(send, -1))
-    got = cube.swap(sent, -1)
-    for level in range(cube.rounds):
-        mine_got = cube.swap(mine, level)
-        kept, sent = halve(kept, got)
-        got = cube.swap(sent, level)
-        mine = add(mine, mine_got)
-    other = cube.swap(mine, -1)
-
-    flat_out, grad_adjacency, grad_node, no, dn = feature_grads(
-        cube, where, mine, other, adjacency, node_weight, wcat, rd, p, flat_g, scale
-    )
-    grad_reduce, grad_project, grad_expand = finish(kept, got, no, dn, scale)
+    nodes = adjacency.shape[0]
+    for level in range(-1, cube.rounds):
+        kept, sent = step(nodes, level == cube.rounds - 1, kept, cube.swap(sent, level))
+    other = cube.swap(sent, -1)
+
+    flat_out, grad_reduce, grad_project, grad_expand, grad_adjacency, grad_node = feature_grads(
+        cube, where, sent, other, kept, adjacency, node_weight, wcat, rd, p, flat_g, scale
+    )
     grad_features = flat_out.reshape(size_x, size_z, size_y, chan).transpose(0, 2, 1, 3)
     return (grad_features, grad_reduce, grad_project, grad_expand, grad_adjacency, grad_node)
 

time: 44.7 us -> 41.9 us (0.937)
  starting transfers between devices: 14.2 us -> 11.4 us
  waiting for transfers between devices: 12 us -> 14.1 us
  Pallas kernels: 17.5 us -> 15.5 us
    ppermute x11 -> x6, starting transfers between devices: 14.2 us -> 11.4 us  [swap(): return lax.ppermute(value, AXES, pairs)]
    ppermute x11 -> x6, waiting for transfers between devices: 12 us -> 14.1 us  [swap(): return lax.ppermute(value, AXES, pairs)]
    pallas_call x11 -> x6, Pallas kernels: 9.89 us -> 7.89 us  [the longest x1 7.78 us: gather(): pl.pallas_call(functools.partial(gather_kernel, cube, sorted_here), grid=...]
  transfers between devices with their start and end apart: 11 -> 6, of which waited for: 7 -> 6; matrix products, arithmetic and copies ran while one was open for 0% -> 0% of each run, Pallas kernels for 17% -> 0%
where the time goes in v5:
time: 41.9 us; the launch traced here: 41.7 us
  Pallas kernels  15.5 us (37%)
  waiting for transfers between devices  14.1 us (34%)
  starting transfers between devices  11.4 us (27%)
  between operations  0.67 us (2%)
    ppermute x6, waiting for transfers between devices, swap(): return lax.ppermute(value, AXES, pairs)  14.1 us
    ppermute x6, starting transfers between devices, swap(): return lax.ppermute(value, AXES, pairs)  11.4 us
    pallas_call x1, Pallas kernels, gather(): pl.pallas_call(functools.partial(gather_kernel, cube, sorted_here), grid=...  7.78 us
    pallas_call x1, Pallas kernels, feature_grads(): pl.pallas_call(functools.partial(feature_kernel, step, scale, cube), in_s...  7.66 us
  transfers between devices with their start and end apart: 6, of which 6 were waited for; matrix products, arithmetic and copies ran while one was open for 0% of the time, Pallas kernels for 0%

profile of v5, /device:TPU:0, one launch (start us, length us, event | category | flops | bytes accessed | tf_op | source)
XLA Modules:
  0.0 41.7 jit_solution(2848021991395331242)
XLA Ops:
  0.6 7.8 %gather.1 = (bf16[3072,256]{1,0:T(8,128)(2,1)}, bf16[3072,128]{1,0:T(8,128)(2,1)}, bf16[512,256]{1,0:T(8,128)(2,1)}, f32[832,128]{1,0:T(8,128)S(1)}, f32[832,128]{1,0:T(8,128)S(1)}) custom-call(s32[1]{0:T(128)} %bitcast.where_ref, bf16[3072,512]{1,0:T(8,128)(2,1)} %bitcast.11, bf16[3072,512]{1,0:T(8,128)(2,1)} %bitcast.12, bf16[512,128]{1,0:T(8,128)(2,1)} %wr_ref.1, ...), custom_call_target="tpu_custom_call" | custom-call | flops 3221225472 | bytes 8650752 | tf_op jit(solution)/shard_map/gather/pallas_call | solution.py:168
  8.4 0.5 %collective-permute-start = (f32[832,128]{1,0:T(8,128)S(1)}, f32[832,128]{1,0:T(8,128)S(1)}, u32[]{:S(2)}, u32[]{:S(2)}) collective-permute-start(f32[832,128]{1,0:T(8,128)S(1)} %get-tuple-element.28), channel_id=1, source_target_pairs={{0,4},{1,5},{2,6},{3,7},{4,0},{5,1},{6,2},{7,3},{8,12},{9,13},{10,... | collective-permute-start | bytes 1277960 | tf_op jit(solution)/shard_map/ppermute | solution.py:77
  8.9 1.4 %collective-permute-done.b_ref = f32[832,128]{1,0:T(8,128)S(1)} collective-permute-done((f32[832,128]{1,0:T(8,128)S(1)}, f32[832,128]{1,0:T(8,128)S(1)}, u32[]{:S(2)}, u32[]{:S(2)}) %collective-permute-start) | collective-permute-done | bytes 426016 | tf_op jit(solution)/shard_map/ppermute | solution.py:77
  10.4 2.9 %collective-permute-start.1 = (f32[448,128]{1,0:T(8,128)S(1)}, f32[448,128]{1,0:T(8,128)S(1)}, u32[]{:S(2)}, u32[]{:S(2)}) collective-permute-start(f32[448,128]{1,0:T(8,128)S(1)} %get-tuple-element.30), channel_id=1, source_target_pairs={{0,8},{1,9},{2,10},{3,11},{4,20},{5,21},{6,22},{7,23},{8,0},{9,1},... | collective-permute-start | bytes 688136 | tf_op jit(solution)/shard_map/ppermute | solution.py:77
  13.3 4.0 %collective-permute-done.1.b_ref = f32[448,128]{1,0:T(8,128)S(1)} collective-permute-done((f32[448,128]{1,0:T(8,128)S(1)}, f32[448,128]{1,0:T(8,128)S(1)}, u32[]{:S(2)}, u32[]{:S(2)}) %collective-permute-start.1) | collective-permute-done | bytes 229408 | tf_op jit(solution)/shard_map/ppermute | solution.py:77
  17.3 2.1 %collective-permute-start.2 = (f32[256,128]{1,0:T(8,128)S(1)}, f32[256,128]{1,0:T(8,128)S(1)}, u32[]{:S(2)}, u32[]{:S(2)}) collective-permute-start(f32[256,128]{1,0:T(8,128)S(1)} %get-tuple-element.32), channel_id=1, source_target_pairs={{0,16},{1,17},{2,18},{3,19},{4,12},{5,13},{6,14},{7,15},{8,24},{9,... | collective-permute-start | bytes 393224 | tf_op jit(solution)/shard_map/ppermute | solution.py:77
  19.5 2.9 %collective-permute-done.2.b_ref = f32[256,128]{1,0:T(8,128)S(1)} collective-permute-done((f32[256,128]{1,0:T(8,128)S(1)}, f32[256,128]{1,0:T(8,128)S(1)}, u32[]{:S(2)}, u32[]{:S(2)}) %collective-permute-start.2) | collective-permute-done | bytes 131104 | tf_op jit(solution)/shard_map/ppermute | solution.py:77
  22.4 2.1 %collective-permute-start.3 = (f32[160,128]{1,0:T(8,128)S(1)}, f32[160,128]{1,0:T(8,128)S(1)}, u32[]{:S(2)}, u32[]{:S(2)}) collective-permute-start(f32[160,128]{1,0:T(8,128)S(1)} %get-tuple-element.34), channel_id=1, source_target_pairs={{0,1},{1,0},{2,3},{3,2},{4,5},{5,4},{6,7},{7,6},{8,9},{9,8},{10,11... | collective-permute-start | bytes 245768 | tf_op jit(solution)/shard_map/ppermute | solution.py:77
  24.6 2.4 %collective-permute-done.3.b_ref = f32[160,128]{1,0:T(8,128)S(1)} collective-permute-done((f32[160,128]{1,0:T(8,128)S(1)}, f32[160,128]{1,0:T(8,128)S(1)}, u32[]{:S(2)}, u32[]{:S(2)}) %collective-permute-start.3) | collective-permute-done | bytes 81952 | tf_op jit(solution)/shard_map/ppermute | solution.py:77
  27.0 3.6 %collective-permute-start.4 = (f32[112,128]{1,0:T(8,128)S(1)}, f32[112,128]{1,0:T(8,128)S(1)}, u32[]{:S(2)}, u32[]{:S(2)}) collective-permute-start(f32[112,128]{1,0:T(8,128)S(1)} %get-tuple-element.36), channel_id=1, source_target_pairs={{0,2},{1,3},{2,0},{3,1},{4,6},{5,7},{6,4},{7,5},{8,10},{9,11},{10,... | collective-permute-start | bytes 172040 | tf_op jit(solution)/shard_map/ppermute | solution.py:77
  30.6 2.2 %collective-permute-done.4.b_ref = f32[112,128]{1,0:T(8,128)S(1)} collective-permute-done((f32[112,128]{1,0:T(8,128)S(1)}, f32[112,128]{1,0:T(8,128)S(1)}, u32[]{:S(2)}, u32[]{:S(2)}) %collective-permute-start.4) | collective-permute-done | bytes 57376 | tf_op jit(solution)/shard_map/ppermute | solution.py:77
  32.8 0.1 collective-permute-start.5
  32.9 1.2 %collective-permute-done.5.other_ref = f32[64,128]{1,0:T(8,128)S(1)} collective-permute-done((f32[64,128]{1,0:T(8,128)S(1)}, f32[64,128]{1,0:T(8,128)S(1)}, u32[]{:S(2)}, u32[]{:S(2)}) %collective-permute-start.5) | collective-permute-done | bytes 32800 | tf_op jit(solution)/shard_map/ppermute | solution.py:77
  34.1 7.7 %feature_grads.1 = (bf16[3072,512]{1,0:T(8,128)(2,1)}, f32[16,128]{1,0:T(8,128)}, f32[16,64]{1,0:T(8,128)}, f32[16,128]{1,0:T(8,128)}, f32[64,64]{1,0:T(8,128)}, /*index=5*/f32[128,128]{1,0:T(8,128)}) custom-call(s32[1]{0:T(128)} %bitcast.where_ref, f32[64,128]{1,0:T(8,128)S(1)} %get-tuple-element.37.mine_ref, ...), custom_call_target="tpu_custom_call" | custom-call | flops 1610612736 | bytes 8650752 | tf_op jit(solution)/shard_map/feature_grads/pallas_call | solution.py:299
  (5 shorter events, 0.1 us)
Async XLA Ops:
  8.4 1.9 %collective-permute-start = (f32[832,128]{1,0:T(8,128)S(1)}, f32[832,128]{1,0:T(8,128)S(1)}, u32[]{:S(2)}, u32[]{:S(2)}) collective-permute-start(f32[832,128]{1,0:T(8,128)S(1)} %get-tuple-element.28), channel_id=1, source_target_pairs={{0,4},{1,5},{2,6},{3,7},{4,0},{5,1},{6,2},{7,3},{8,12},{9,13},{10,... | collective-permute-start | bytes 1277960 | tf_op jit(solution)/shard_map/ppermute | solution.py:77
  10.4 6.9 %collective-permute-start.1 = (f32[448,128]{1,0:T(8,128)S(1)}, f32[448,128]{1,0:T(8,128)S(1)}, u32[]{:S(2)}, u32[]{:S(2)}) collective-permute-start(f32[448,128]{1,0:T(8,128)S(1)} %get-tuple-element.30), channel_id=1, source_target_pairs={{0,8},{1,9},{2,10},{3,11},{4,20},{5,21},{6,22},{7,23},{8,0},{9,1},... | collective-permute-start | bytes 688136 | tf_op jit(solution)/shard_map/ppermute | solution.py:77
  17.3 5.1 %collective-permute-start.2 = (f32[256,128]{1,0:T(8,128)S(1)}, f32[256,128]{1,0:T(8,128)S(1)}, u32[]{:S(2)}, u32[]{:S(2)}) collective-permute-start(f32[256,128]{1,0:T(8,128)S(1)} %get-tuple-element.32), channel_id=1, source_target_pairs={{0,16},{1,17},{2,18},{3,19},{4,12},{5,13},{6,14},{7,15},{8,24},{9,... | collective-permute-start | bytes 393224 | tf_op jit(solution)/shard_map/ppermute | solution.py:77
  22.4 4.6 %collective-permute-start.3 = (f32[160,128]{1,0:T(8,128)S(1)}, f32[160,128]{1,0:T(8,128)S(1)}, u32[]{:S(2)}, u32[]{:S(2)}) collective-permute-start(f32[160,128]{1,0:T(8,128)S(1)} %get-tuple-element.34), channel_id=1, source_target_pairs={{0,1},{1,0},{2,3},{3,2},{4,5},{5,4},{6,7},{7,6},{8,9},{9,8},{10,11... | collective-permute-start | bytes 245768 | tf_op jit(solution)/shard_map/ppermute | solution.py:77
  27.0 5.8 %collective-permute-start.4 = (f32[112,128]{1,0:T(8,128)S(1)}, f32[112,128]{1,0:T(8,128)S(1)}, u32[]{:S(2)}, u32[]{:S(2)}) collective-permute-start(f32[112,128]{1,0:T(8,128)S(1)} %get-tuple-element.36), channel_id=1, source_target_pairs={{0,2},{1,3},{2,0},{3,1},{4,6},{5,7},{6,4},{7,5},{8,10},{9,11},{10,... | collective-permute-start | bytes 172040 | tf_op jit(solution)/shard_map/ppermute | solution.py:77
  32.8 1.3 %collective-permute-start.5 = (f32[64,128]{1,0:T(8,128)S(1)}, f32[64,128]{1,0:T(8,128)S(1)}, u32[]{:S(2)}, u32[]{:S(2)}) collective-permute-start(f32[64,128]{1,0:T(8,128)S(1)} %get-tuple-element.37.mine_ref), channel_id=1, source_target_pairs={{0,4},{1,5},{2,6},{3,7},{4,0},{5,1},{6,2},{7,3},{8,12},{9,13},{10,... | collective-permute-start | bytes 98312 | tf_op jit(solution)/shard_map/ppermute | solution.py:77

commit v6 on v4

v6 whole, which is shorter than its diff:
```python
import functools
import math

import jax
import jax.numpy as jnp
from jax import lax
from jax.experimental import pallas as pl
from jax.experimental.pallas import tpu as pltpu
from jax.sharding import PartitionSpec as P

AXES = ("gx", "gy", "gz")
F32 = jnp.float32
BF16 = jnp.bfloat16
HBM = pl.BlockSpec(memory_space=pltpu.HBM)
VMEM = pl.BlockSpec(memory_space=pltpu.VMEM)
SMEM = pl.BlockSpec(memory_space=pltpu.SMEM)
VMEM_LIMIT = 24 * 1024 * 1024


def exact(a, b, dims=((1,), (0,))):
    return lax.dot_general(
        a, b, (dims, ((), ())), precision=lax.Precision.HIGHEST, preferred_element_type=F32
    )


def mxu(a, b, dims=((1,), (0,))):
    return lax.dot_general(a, b, (dims, ((), ())), preferred_element_type=F32)


def params():
    return pltpu.CompilerParams(vmem_limit_bytes=VMEM_LIMIT)


def cost(flops, nbytes):
    return pl.CostEstimate(flops=flops, bytes_accessed=nbytes, transcendentals=0)


def in_hbm(*values):
    return [pltpu.with_memory_space_constraint(value, pltpu.HBM) for value in values]


def row_block(total):
    for size in (768, 512, 384, 256, 128, 64, 32, 16):
        if total % size == 0:
            return size
    return total


class Cube:
    def __init__(self, mesh):
        self.size = {axis: mesh.shape[axis] for axis in AXES}
        self.count = math.prod(self.size.values())
        stride = {"gx": self.size["gy"] * self.size["gz"], "gy": self.size["gz"], "gz": 1}
        bits = {
            axis: [stride[axis] << k for k in range(self.size[axis].bit_length() - 1)] for axis in AXES
        }
        self.core = bits["gy"][0]
        rest = bits["gx"] + bits["gy"][1:] + bits["gz"]
        self.orders = [rest, rest]
        if len(bits["gx"]) == 2:
            self.orders = [rest, [rest[1], rest[0]] + rest[2:]]
        self.rounds = len(rest)

    def side(self, device):
        return 1 if device & self.core else 0

    def traced_side(self, device):
        return lax.bitwise_and(lax.div(device, jnp.int32(self.core)), jnp.int32(1))

    def swap(self, value, level):
        masks = [self.core] * 2 if level < 0 else [order[level] for order in self.orders]
        pairs = [(d, d ^ masks[self.side(d)]) for d in range(self.count)]
        return lax.ppermute(value, AXES, pairs)

    def masks(self, side):
        order = self.orders[side]
        last = len(order) - 1
        return [
            sum(order[level] for level in range(len(order)) if j >> (last - level) & 1)
            for j in range(1 << len(order))
        ]


def gather_kernel(
    cube, step, sorted_here, where_ref, x_hbm, g_hbm, wr_hbm, wpt_hbm, we_hbm, rdp_hbm, wcat_hbm, *rest
):
    if sorted_here:
        kept_ref, sent_ref, turned_ref, *rest = rest
    else:
        keep_ref, send_ref, turned_ref, *rest = rest
    x_ref, g_ref, rdp_ref, cat_ref, wpt_ref, we_ref, sums_ref, term_ref, small_sem, in_sem, out_sem = rest
    rows = x_ref.shape[0]
    cr = we_ref.shape[1]
    nodes = wpt_ref.shape[0]
    wide = 2 * cr
    count = rows // step
    move = pltpu.make_async_copy
    small = [
        move(wr_hbm, cat_ref.at[:, pl.ds(0, cr)], small_sem.at[0]),
        move(wpt_hbm, wpt_ref, small_sem.at[1]),
        move(we_hbm, we_ref, small_sem.at[2]),
    ]
    load_cuts = sorted({0, min(1, count), min(2, count), count})
    store_cuts = sorted({0, max(count - 2, 0), max(count - 1, 0), count})
    span = lambda cuts, i: pl.ds(cuts[i] * step, (cuts[i + 1] - cuts[i]) * step)
    loads = [
        (
            move(x_hbm.at[span(load_cuts, i)], x_ref.at[span(load_cuts, i)], in_sem.at[0, i]),
            move(g_hbm.at[span(load_cuts, i)], g_ref.at[span(load_cuts, i)], in_sem.at[1, i]),
        )
        for i in range(len(load_cuts) - 1)
    ]
    stores = [
        move(rdp_ref.at[span(store_cuts, i)], rdp_hbm.at[span(store_cuts, i)], out_sem.at[i])
        for i in range(len(store_cuts) - 1)
    ]
    for copy in (*small, *loads[0]):
        copy.start()
    sums_ref[...] = jnp.zeros_like(sums_ref)
    term_ref[...] = jnp.zeros_like(term_ref)
    small[0].wait()
    small[1].wait()
    padded = jnp.concatenate([wpt_ref[...], jnp.zeros_like(wpt_ref)], axis=0)
    cat_ref[:, cr:] = padded.T
    keep_weights = move(cat_ref, wcat_hbm, small_sem.at[3])
    keep_weights.start()
    small[2].wait()

    @pl.loop(0, count)
    def _(i):
        for k, pair in enumerate(loads):
            @pl.when(i == load_cuts[k])
            def _():
                for copy in pair:
                    copy.wait()
                if k + 1 < len(loads):
                    for copy in loads[k + 1]:
                        copy.start()

        c = pl.ds(pl.multiple_of(i * step, step), step)
        x, g = x_ref[c], g_ref[c]
        both = mxu(x, cat_ref[...]).astype(BF16)
        mapped = mxu(g, we_ref[...]).astype(BF16)
        rdp = jnp.concatenate([both[:, :cr], mapped, both[:, cr:]], axis=1)
        rdp_ref[c] = rdp
        turned = rdp.T
        proj = turned[wide : wide + nodes]
        sums_ref[: wide + nodes] += mxu(turned[: wide + nodes], x)
        sums_ref[wide + nodes :] += mxu(proj, g)
        term = mxu(proj, rdp[:, :wide])
        term_ref[0] += term[:, :cr]
        term_ref[1] += term[:, cr:]
        for k, copy in enumerate(stores):
            pl.when(i == store_cuts[k + 1] - 1)(copy.start)

    me = where_ref[0]
    side = cube.traced_side(me)
    turned_ref[...] = sums_ref[...].T
    if not sorted_here:
        keep_ref[...] = term_ref[side]
        send_ref[...] = term_ref[1 - side]
    else:
        kept_ref[:nodes] = term_ref[side]
        sent_ref[:nodes] = term_ref[1 - side]
        size = turned_ref.shape[0] // cube.count
        mine = [jnp.where(side == 0, a, b) for a, b in zip(cube.masks(0), cube.masks(1))]
        other = [jnp.where(side == 0, b, a) for a, b in zip(cube.masks(0), cube.masks(1))]
        for masks, base, out_ref in ((mine, me, kept_ref), (other, me ^ cube.core, sent_ref)):
            to = nodes
            for mask in masks:
                at = pl.multiple_of((base ^ mask) * size, size)
                block = turned_ref[pl.ds(at, size), :]
                for lane in range(0, block.shape[1], cr):
                    out_ref[to : to + size] = block[:, lane : lane + cr]
                    to += size
    for copy in (keep_weights, *stores):
        copy.wait()


def gather(cube, where, x, g, wr, wpt, we):
    rows, chan = x.shape
    cr, nodes = wr.shape[1], wpt.shape[0]
    step = row_block(rows)
    width = 2 * cr + 2 * nodes
    half = cube.count // 2
    size = chan // cube.count
    sorted_here = size % 8 == 0
    outs = [
        (HBM, pltpu.HBM((rows, width), BF16)),
        (HBM, pltpu.HBM((chan, cr + 2 * nodes), BF16)),
    ]
    scratch = []
    if sorted_here:
        outs += [(VMEM, pltpu.VMEM((nodes + half * size * width // cr, cr), F32))] * 2
        scratch += [pltpu.VMEM((chan, width), F32)]
    else:
        outs += [(VMEM, jax.ShapeDtypeStruct((nodes, cr), F32))] * 2
        outs += [(VMEM, jax.ShapeDtypeStruct((chan, width), F32))]
    scratch += [
        pltpu.VMEM((rows, chan), BF16),
        pltpu.VMEM((rows, chan), BF16),
        pltpu.VMEM((rows, width), BF16),
        pltpu.VMEM((chan, cr + 2 * nodes), BF16),
        pltpu.VMEM(wpt.shape, BF16),
        pltpu.VMEM(we.shape, BF16),
        pltpu.VMEM((width, chan), F32),
        pltpu.VMEM((2, nodes, cr), F32),
        pltpu.SemaphoreType.DMA((4,)),
        pltpu.SemaphoreType.DMA((2, 3)),
        pltpu.SemaphoreType.DMA((3,)),
    ]
    rdp, wcat, kept, sent, *sums = pl.pallas_call(
        functools.partial(gather_kernel, cube, step, sorted_here),
        in_specs=[SMEM] + [HBM] * 5,
        out_specs=[spec for spec, _ in outs],
        out_shape=[shape for _, shape in outs],
        scratch_shapes=scratch,
        compiler_params=params(),
        cost_estimate=cost(2 * rows * chan * 1024, rows * chan * 4 + rows * 768),
        name="gather",
    )(where, *in_hbm(x, g, wr, wpt, we))
    if not sorted_here:
        side = cube.traced_side(where[0])
        table = jnp.array([cube.masks(0), cube.masks(1)], jnp.int32)
        cut = sums[0].reshape(cube.count, size, width // cr, cr).transpose(0, 2, 1, 3)
        lay = lambda head, index: jnp.concatenate([head, cut[index].reshape(-1, cr)])
        kept = lay(kept, where[0] ^ table[side])
        sent = lay(sent, where[0] ^ cube.core ^ table[1 - side])
    return rdp, wcat, kept, sent


def add_kernel(a_ref, b_ref, out_ref):
    rows = out_ref.shape[0]
    out_ref[...] = a_ref[:rows] + b_ref[:rows]


def add(a, b, rows):
    return pl.pallas_call(
        add_kernel,
        in_specs=[VMEM] * 2,
        out_specs=VMEM,
        out_shape=pltpu.VMEM((rows, a.shape[1]), F32),
        compiler_params=params(),
        cost_estimate=cost(rows * a.shape[1], 12 * rows * a.shape[1]),
        name="add",
    )(a, b)


def halve_kernel(skip, a_ref, b_ref, _, keep_ref, send_ref):
    half = keep_ref.shape[0]
    keep_ref[...] = a_ref[skip : skip + half] + b_ref[skip : skip + half]
    send_ref[...] = a_ref[skip + half :] + b_ref[skip + half :]


def halve(a, b, skip, after):
    shape = ((a.shape[0] - skip) // 2, a.shape[1])
    return pl.pallas_call(
        functools.partial(halve_kernel, skip),
        in_specs=[VMEM] * 2 + [pl.BlockSpec(memory_space=pl.ANY)],
        out_specs=[VMEM] * 2,
        out_shape=[pltpu.VMEM(shape, F32)] * 2,
        compiler_params=params(),
        cost_estimate=cost(a.size, 12 * a.size),
        name="halve",
    )(a, b, after)


def feature_kernel(
    step, scale, cube, where_ref, mine_ref, other_ref, adj_hbm, nw_hbm, wcat_hbm, rdp_hbm, g_hbm,
    out_hbm, ga_ref, gn_ref, no_ref, dn_ref,
    adj_ref, nw_ref, wcat_ref, rdp_ref, g_ref, out_ref, mix_ref, dnb_ref, in_sem, out_sem,
):
    nodes_n, cr = mine_ref.shape
    rows = g_ref.shape[0]
    wide = 2 * cr
    move = pltpu.make_async_copy
    pairs = (
        (adj_hbm, adj_ref), (nw_hbm, nw_ref), (rdp_hbm, rdp_ref), (wcat_hbm, wcat_ref), (g_hbm, g_ref)
    )
    loads = [move(src, dst, in_sem.at[k]) for k, (src, dst) in enumerate(pairs)]
    for copy in loads:
        copy.start()
    first = cube.traced_side(where_ref[0]) == 0
    mine, other = mine_ref[...], other_ref[...]
    nodes = scale * jnp.where(first, mine, other)
    d_node_out = jnp.where(first, other, mine)
    loads[0].wait()
    loads[1].wait()
    adj, nw = adj_ref[...], nw_ref[...]
    hidden = nodes - exact(adj, nodes)
    pre = exact(hidden, nw)
    node_out = jnp.maximum(pre, 0.0).astype(BF16)
    d_pre = jnp.where(pre > 0.0, d_node_out, 0.0)
    d_hidden = exact(d_pre, nw, ((1,), (1,)))
    d_nodes = d_hidden - exact(adj, d_hidden, ((0,), (0,)))
    dn = d_nodes.astype(BF16)
    no_f, dn_f = node_out.astype(F32), dn.astype(F32)
    no_ref[...] = no_f
    dn_ref[...] = dn_f
    dnb_ref[:nodes_n] = dn
    dnb_ref[nodes_n:] = jnp.zeros((nodes_n, cr), BF16)
    blank = jnp.zeros((cr, cr), BF16)
    zero = jnp.zeros((nodes_n, cr), F32)
    mix_ref[:cr, :cr] = jnp.concatenate([dn_f, zero], axis=0).T.astype(BF16)
    mix_ref[cr:, :cr] = blank
    mix_ref[:cr, cr:] = blank
    mix_ref[cr:, cr:] = jnp.concatenate([no_f, zero], axis=0).T.astype(BF16)
    for copy in loads[2:]:
        copy.wait()
    copies = []
    for i, start in enumerate(range(0, rows, step)):
        c = pl.ds(start, step)
        rdp = rdp_ref[c]
        mixed = mxu(rdp[:, :wide], mix_ref[...])
        d_proj = (mixed[:, cr:] + scale * mixed[:, :cr]).astype(BF16)
        d_red = (scale * mxu(rdp[:, wide:], dnb_ref[...])).astype(BF16)
        both = jnp.concatenate([d_red, d_proj], axis=1)
        out = g_ref[c].astype(F32) + mxu(both, wcat_ref[...], ((1,), (1,)))
        out_ref[c] = out.astype(BF16)
        copies.append(move(out_ref.at[c], out_hbm.at[c], out_sem.at[i]))
        copies[-1].start()
    gn_ref[...] = scale * exact(hidden, d_pre, ((0,), (0,)))
    ga_ref[...] = -scale * exact(d_hidden, nodes, ((1,), (1,)))
    for copy in copies:
        copy.wait()


def feature_grads(cube, where, mine, other, adjacency, node_weight, wcat, rdp, g, scale):
    rows, chan = g.shape
    nodes, cr = adjacency.shape[0], node_weight.shape[0]
    step = row_block(rows)
    loaded = (adjacency, node_weight, rdp, wcat, g)
    order = (adjacency, node_weight, wcat, rdp, g)
    return pl.pallas_call(
        functools.partial(feature_kernel, step, scale, cube),
        in_specs=[SMEM, VMEM, VMEM] + [HBM] * len(loaded),
        out_specs=[HBM] + [VMEM] * 4,
        out_shape=[
            pltpu.HBM((rows, chan), BF16),
            jax.ShapeDtypeStruct((nodes, nodes), F32),
            jax.ShapeDtypeStruct((cr, cr), F32),
            pltpu.VMEM((nodes, cr), F32),
            pltpu.VMEM((nodes, cr), F32),
        ],
        scratch_shapes=[pltpu.VMEM(value.shape, value.dtype) for value in order]
        + [
            pltpu.VMEM((rows, chan), BF16),
            pltpu.VMEM((2 * cr, 2 * cr), BF16),
            pltpu.VMEM((2 * nodes, cr), BF16),
            pltpu.SemaphoreType.DMA((len(loaded),)),
            pltpu.SemaphoreType.DMA((rows // step,)),
        ],
        compiler_params=params(),
        cost_estimate=cost(2 * rows * 4 * 65536, rows * chan * 4 + rows * 768),
        name="feature_grads",
    )(where, mine, other, *in_hbm(*order))


def finish_kernel(scale, kept_ref, got_ref, no_ref, dn_ref, gr_ref, gp_ref, ge_ref):
    total = kept_ref[...] + got_ref[...]
    nodes = no_ref.shape[0]
    no, dn = no_ref[...], dn_ref[...]
    size = gr_ref.shape[0]
    x_red, x_dm, with_proj = (total[k * size : (k + 1) * size] for k in range(3))
    gr_ref[...] = scale * scale * exact(with_proj[:, :nodes], dn)
    gp_ref[...] = scale * exact(x_dm, no, ((1,), (1,))) + scale * scale * exact(
        x_red, dn, ((1,), (1,))
    )
    ge_ref[...] = scale * exact(with_proj[:, nodes:], no)


def finish(kept, got, no, dn, size, scale):
    nodes, cr = no.shape
    return pl.pallas_call(
        functools.partial(finish_kernel, scale),
        in_specs=[VMEM] * 4,
        out_specs=[VMEM] * 3,
        out_shape=[
            jax.ShapeDtypeStruct((size, cr), F32),
            jax.ShapeDtypeStruct((size, nodes), F32),
            jax.ShapeDtypeStruct((size, cr), F32),
        ],
        compiler_params=params(),
        cost_estimate=cost(0, size * 4096),
        name="finish",
    )(kept, got, no, dn)


def on_device(
    cube, features, cotangent, reduce_weight, project_weight, expand_weight, adjacency, node_weight
):
    size_x, size_y, size_z, chan = features.shape
    local = size_x * size_y * size_z
    scale = 1.0 / math.sqrt(local * cube.count)
    flat_x = features.transpose(0, 2, 1, 3).reshape(local, chan)
    flat_g = cotangent.transpose(0, 2, 1, 3).reshape(local, chan)
    me = lax.axis_index(AXES).astype(jnp.int32)
    where = me.reshape(1)

    rdp, wcat, kept, sent = gather(
        cube, where, flat_x, flat_g, reduce_weight, project_weight.T, expand_weight
    )
    nodes = adjacency.shape[0]
    got = cube.swap(sent, -1)
    sums = [add(kept, got, nodes)]
    for level in range(cube.rounds):
        sums.append(add(sums[-1], cube.swap(sums[-1], level), nodes))
    mine = sums[-1]
    other = cube.swap(mine, -1)
    for level in range(cube.rounds):
        after = sums[min(level + 1, cube.rounds)] if level else sums[0]
        kept, sent = halve(kept, got, 0 if level else nodes, after)
        got = cube.swap(sent, level)

    flat_out, grad_adjacency, grad_node, no, dn = feature_grads(
        cube, where, mine, other, adjacency, node_weight, wcat, rdp, flat_g, scale
    )
    grad_reduce, grad_project, grad_expand = finish(
        kept, got, no, dn, chan // cube.count, scale
    )
    grad_features = flat_out.reshape(size_x, size_z, size_y, chan).transpose(0, 2, 1, 3)
    return (grad_features, grad_reduce, grad_project, grad_expand, grad_adjacency, grad_node)


def solution(mesh):
    return jax.shard_map(
        functools.partial(on_device, Cube(mesh)),
        mesh=mesh,
        in_specs=(P("gx", "gy", "gz", None), P("gx", "gy", "gz", None), P(), P(), P(), P(), P()),
        out_specs=(
            P("gx", "gy", "gz", None),
            P(AXES, None),
            P(AXES, None),
            P(AXES, None),
            P(),
            P(),
        ),
        check_vma=False,
    )
```

time: 44.7 us -> 42.3 us (0.946)
  Pallas kernels: 17.5 us -> 14.9 us
    pallas_call x1, Pallas kernels: 7.62 us -> 6.03 us  [feature_grads(): pl.pallas_call(functools.partial(feature_kernel, step, scale, cube), in_s...]
    pallas_call x5, Pallas kernels: 8.99 us -> 7.92 us  [the longest x1 7.84 us: gather(): pl.pallas_call(functools.partial(gather_kernel, cube, step, sorted_here),...]
    ppermute x11 -> x10, starting transfers between devices: 14.2 us -> 14.5 us  [swap(): return lax.ppermute(value, AXES, pairs)]
    ppermute x11 -> x10, waiting for transfers between devices: 12 us -> 12 us  [swap(): return lax.ppermute(value, AXES, pairs)]
  transfers between devices with their start and end apart: 11 -> 10, of which waited for: 7 -> 6; matrix products, arithmetic and copies ran while one was open for 0% -> 0% of each run, Pallas kernels for 17% -> 14%
where the time goes in v6:
time: 42.3 us; the launch traced here: 42.1 us
  Pallas kernels  14.9 us (35%)
  starting transfers between devices  14.5 us (34%)
  waiting for transfers between devices  12 us (28%)
  between operations  0.7 us (2%)
    ppermute x10, starting transfers between devices, swap(): return lax.ppermute(value, AXES, pairs)  14.5 us
    ppermute x10, waiting for transfers between devices, swap(): return lax.ppermute(value, AXES, pairs)  12 us
    pallas_call x1, Pallas kernels, gather(): pl.pallas_call(functools.partial(gather_kernel, cube, step, sorted_here),...  7.84 us
    pallas_call x1, Pallas kernels, feature_grads(): pl.pallas_call(functools.partial(feature_kernel, step, scale, cube), in_s...  6.03 us
    pallas_call x1, Pallas kernels, finish(): pl.pallas_call(functools.partial(finish_kernel, scale), in_specs=[VMEM] *...  0.88 us
  transfers between devices with their start and end apart: 10, of which 6 were waited for; matrix products, arithmetic and copies ran while one was open for 0% of the time, Pallas kernels for 14%

profile of v6, /device:TPU:0, one launch (start us, length us, event | category | flops | bytes accessed | tf_op | source)
XLA Modules:
  0.0 42.1 jit_solution(5088180424138676979)
XLA Ops:
  0.6 7.8 %gather.1 = (bf16[3072,384]{1,0:T(8,128)(2,1)}, bf16[512,256]{1,0:T(8,128)(2,1)}, f32[832,128]{1,0:T(8,128)S(1)}, f32[832,128]{1,0:T(8,128)S(1)}) custom-call(s32[1]{0:T(128)} %bitcast.where_ref, bf16[3072,512]{1,0:T(8,128)(2,1)} %bitcast.11, bf16[3072,512]{1,0:T(8,128)(2,1)} %bitcast.12, bf16[512,128]{1,0:T(8,128)(2,1)} %wr_hbm.1, ...), custom_call_target="tpu_custom_call" | custom-call | flops 3221225472 | bytes 8650752 | tf_op jit(solution)/shard_map/gather/pallas_call | solution.py:212
  8.5 0.5 %collective-permute-start = (f32[832,128]{1,0:T(8,128)S(1)}, f32[832,128]{1,0:T(8,128)S(1)}, u32[]{:S(2)}, u32[]{:S(2)}) collective-permute-start(f32[832,128]{1,0:T(8,128)S(1)} %get-tuple-element.27), channel_id=1, source_target_pairs={{0,4},{1,5},{2,6},{3,7},{4,0},{5,1},{6,2},{7,3},{8,12},{9,13},{10,... | collective-permute-start | bytes 1277960 | tf_op jit(solution)/shard_map/ppermute | solution.py:73
  9.0 1.4 %collective-permute-done.b_ref = f32[832,128]{1,0:T(8,128)S(1)} collective-permute-done((f32[832,128]{1,0:T(8,128)S(1)}, f32[832,128]{1,0:T(8,128)S(1)}, u32[]{:S(2)}, u32[]{:S(2)}) %collective-permute-start) | collective-permute-done | bytes 426016 | tf_op jit(solution)/shard_map/ppermute | solution.py:73
  10.5 2.9 %collective-permute-start.6 = (f32[384,128]{1,0:T(8,128)S(1)}, f32[384,128]{1,0:T(8,128)S(1)}, u32[]{:S(2)}, u32[]{:S(2)}) collective-permute-start(f32[384,128]{1,0:T(8,128)S(1)} %get-tuple-element.32), channel_id=1, source_target_pairs={{0,8},{1,9},{2,10},{3,11},{4,20},{5,21},{6,22},{7,23},{8,0},{9,1},... | collective-permute-start | bytes 589832 | tf_op jit(solution)/shard_map/ppermute | solution.py:73
  13.4 0.1 collective-permute-start.1
  13.5 3.9 %collective-permute-done.1.b_ref = f32[64,128]{1,0:T(8,128)S(1)} collective-permute-done((f32[64,128]{1,0:T(8,128)S(1)}, f32[64,128]{1,0:T(8,128)S(1)}, u32[]{:S(2)}, u32[]{:S(2)}) %collective-permute-start.1) | collective-permute-done | bytes 32800 | tf_op jit(solution)/shard_map/ppermute | solution.py:73
  17.4 2.0 %collective-permute-start.2 = (f32[64,128]{1,0:T(8,128)S(1)}, f32[64,128]{1,0:T(8,128)S(1)}, u32[]{:S(2)}, u32[]{:S(2)}) collective-permute-start(f32[64,128]{1,0:T(8,128)S(1)} %add.14.a_ref), channel_id=1, source_target_pairs={{0,16},{1,17},{2,18},{3,19},{4,12},{5,13},{6,14},{7,15},{8,24},{9,... | collective-permute-start | bytes 98312 | tf_op jit(solution)/shard_map/ppermute | solution.py:73
  19.4 1.9 %collective-permute-done.2.b_ref = f32[64,128]{1,0:T(8,128)S(1)} collective-permute-done((f32[64,128]{1,0:T(8,128)S(1)}, f32[64,128]{1,0:T(8,128)S(1)}, u32[]{:S(2)}, u32[]{:S(2)}) %collective-permute-start.2) | collective-permute-done | bytes 32800 | tf_op jit(solution)/shard_map/ppermute | solution.py:73
  21.3 0.0 collective-permute-done.6.b_ref
  21.4 2.1 %collective-permute-start.7 = (f32[192,128]{1,0:T(8,128)S(1)}, f32[192,128]{1,0:T(8,128)S(1)}, u32[]{:S(2)}, u32[]{:S(2)}) collective-permute-start(f32[192,128]{1,0:T(8,128)S(1)} %get-tuple-element.34), channel_id=1, source_target_pairs={{0,16},{1,17},{2,18},{3,19},{4,12},{5,13},{6,14},{7,15},{8,24},{9,... | collective-permute-start | bytes 294920 | tf_op jit(solution)/shard_map/ppermute | solution.py:73
  23.5 1.6 %collective-permute-start.3 = (f32[64,128]{1,0:T(8,128)S(1)}, f32[64,128]{1,0:T(8,128)S(1)}, u32[]{:S(2)}, u32[]{:S(2)}) collective-permute-start(f32[64,128]{1,0:T(8,128)S(1)} %add.15.a_ref._), channel_id=1, source_target_pairs={{0,1},{1,0},{2,3},{3,2},{4,5},{5,4},{6,7},{7,6},{8,9},{9,8},{10,11... | collective-permute-start | bytes 98312 | tf_op jit(solution)/shard_map/ppermute | solution.py:73
  25.0 2.3 %collective-permute-done.3.b_ref = f32[64,128]{1,0:T(8,128)S(1)} collective-permute-done((f32[64,128]{1,0:T(8,128)S(1)}, f32[64,128]{1,0:T(8,128)S(1)}, u32[]{:S(2)}, u32[]{:S(2)}) %collective-permute-start.3) | collective-permute-done | bytes 32800 | tf_op jit(solution)/shard_map/ppermute | solution.py:73
  27.4 2.9 %collective-permute-start.4 = (f32[64,128]{1,0:T(8,128)S(1)}, f32[64,128]{1,0:T(8,128)S(1)}, u32[]{:S(2)}, u32[]{:S(2)}) collective-permute-start(f32[64,128]{1,0:T(8,128)S(1)} %add.16.a_ref._), channel_id=1, source_target_pairs={{0,2},{1,3},{2,0},{3,1},{4,6},{5,7},{6,4},{7,5},{8,10},{9,11},{10,... | collective-permute-start | bytes 98312 | tf_op jit(solution)/shard_map/ppermute | solution.py:73
  30.2 0.0 collective-permute-done.7.b_ref
  30.3 1.7 %collective-permute-start.8 = (f32[96,128]{1,0:T(8,128)S(1)}, f32[96,128]{1,0:T(8,128)S(1)}, u32[]{:S(2)}, u32[]{:S(2)}) collective-permute-start(f32[96,128]{1,0:T(8,128)S(1)} %get-tuple-element.36), channel_id=1, source_target_pairs={{0,1},{1,0},{2,3},{3,2},{4,5},{5,4},{6,7},{7,6},{8,9},{9,8},{10,11... | collective-permute-start | bytes 147464 | tf_op jit(solution)/shard_map/ppermute | solution.py:73
  31.9 0.3 collective-permute-done.4.b_ref
  32.2 0.0 collective-permute-start.5
  32.2 2.2 %collective-permute-done.8.b_ref = f32[96,128]{1,0:T(8,128)S(1)} collective-permute-done((f32[96,128]{1,0:T(8,128)S(1)}, f32[96,128]{1,0:T(8,128)S(1)}, u32[]{:S(2)}, u32[]{:S(2)}) %collective-permute-start.8) | collective-permute-done | bytes 49184 | tf_op jit(solution)/shard_map/ppermute | solution.py:73
  34.4 0.8 %collective-permute-start.9 = (f32[48,128]{1,0:T(8,128)S(1)}, f32[48,128]{1,0:T(8,128)S(1)}, u32[]{:S(2)}, u32[]{:S(2)}) collective-permute-start(f32[48,128]{1,0:T(8,128)S(1)} %get-tuple-element.38), channel_id=1, source_target_pairs={{0,2},{1,3},{2,0},{3,1},{4,6},{5,7},{6,4},{7,5},{8,10},{9,11},{10,... | collective-permute-start | bytes 73736 | tf_op jit(solution)/shard_map/ppermute | solution.py:73
  35.2 0.0 collective-permute-done.5.other_ref
  35.2 6.0 %feature_grads.1 = (bf16[3072,512]{1,0:T(8,128)(2,1)}, f32[64,64]{1,0:T(8,128)}, f32[128,128]{1,0:T(8,128)}, f32[64,128]{1,0:T(8,128)S(1)}, f32[64,128]{1,0:T(8,128)S(1)}) custom-call(s32[1]{0:T(128)} %bitcast.where_ref, f32[64,128]{1,0:T(8,128)S(1)} %add.17.mine_ref._, f32[64,128]{1,0:T(8,128)S(1)} %collective-permute-done.5.other_ref, f32[64,64]{1,0:T(8,128)} %adj_hbm.1, ...), custom_call_target="tpu_custom_call" | custom-call | flops 1610612736 | bytes 8650752 | tf_op jit(solution)/shard_map/feature_grads/pallas_call | solution.py:334
  41.2 0.0 collective-permute-done.9.got_ref
  41.2 0.9 %finish.1 = (f32[16,128]{1,0:T(8,128)}, f32[16,64]{1,0:T(8,128)}, f32[16,128]{1,0:T(8,128)}) custom-call(f32[48,128]{1,0:T(8,128)S(1)} %get-tuple-element.37.kept_ref, f32[48,128]{1,0:T(8,128)S(1)} %collective-permute-done.9.got_ref, f32[64,128]{1,0:T(8,128)S(1)} %get-tuple-element.39.no_ref, f32[64,128]{1,0:T(8,128)S(1)} %get-tuple-element.40.dn_ref), custom_call_target="tpu_custom_call" | custom-call | bytes 65536 | tf_op jit(solution)/shard_map/finish/pallas_call | solution.py:374
  (9 shorter events, 0.1 us)
Async XLA Ops:
  8.5 1.9 %collective-permute-start = (f32[832,128]{1,0:T(8,128)S(1)}, f32[832,128]{1,0:T(8,128)S(1)}, u32[]{:S(2)}, u32[]{:S(2)}) collective-permute-start(f32[832,128]{1,0:T(8,128)S(1)} %get-tuple-element.27), channel_id=1, source_target_pairs={{0,4},{1,5},{2,6},{3,7},{4,0},{5,1},{6,2},{7,3},{8,12},{9,13},{10,... | collective-permute-start | bytes 1277960 | tf_op jit(solution)/shard_map/ppermute | solution.py:73
  10.5 10.9 %collective-permute-start.6 = (f32[384,128]{1,0:T(8,128)S(1)}, f32[384,128]{1,0:T(8,128)S(1)}, u32[]{:S(2)}, u32[]{:S(2)}) collective-permute-start(f32[384,128]{1,0:T(8,128)S(1)} %get-tuple-element.32), channel_id=1, source_target_pairs={{0,8},{1,9},{2,10},{3,11},{4,20},{5,21},{6,22},{7,23},{8,0},{9,1},... | collective-permute-start | bytes 589832 | tf_op jit(solution)/shard_map/ppermute | solution.py:73
  13.4 4.0 %collective-permute-start.1 = (f32[64,128]{1,0:T(8,128)S(1)}, f32[64,128]{1,0:T(8,128)S(1)}, u32[]{:S(2)}, u32[]{:S(2)}) collective-permute-start(f32[64,128]{1,0:T(8,128)S(1)} %add.13.a_ref._), channel_id=1, source_target_pairs={{0,8},{1,9},{2,10},{3,11},{4,20},{5,21},{6,22},{7,23},{8,0},{9,1},... | collective-permute-start | bytes 98312 | tf_op jit(solution)/shard_map/ppermute | solution.py:73
  17.4 3.9 %collective-permute-start.2 = (f32[64,128]{1,0:T(8,128)S(1)}, f32[64,128]{1,0:T(8,128)S(1)}, u32[]{:S(2)}, u32[]{:S(2)}) collective-permute-start(f32[64,128]{1,0:T(8,128)S(1)} %add.14.a_ref), channel_id=1, source_target_pairs={{0,16},{1,17},{2,18},{3,19},{4,12},{5,13},{6,14},{7,15},{8,24},{9,... | collective-permute-start | bytes 98312 | tf_op jit(solution)/shard_map/ppermute | solution.py:73
  21.4 8.9 %collective-permute-start.7 = (f32[192,128]{1,0:T(8,128)S(1)}, f32[192,128]{1,0:T(8,128)S(1)}, u32[]{:S(2)}, u32[]{:S(2)}) collective-permute-start(f32[192,128]{1,0:T(8,128)S(1)} %get-tuple-element.34), channel_id=1, source_target_pairs={{0,16},{1,17},{2,18},{3,19},{4,12},{5,13},{6,14},{7,15},{8,24},{9,... | collective-permute-start | bytes 294920 | tf_op jit(solution)/shard_map/ppermute | solution.py:73
  23.5 3.9 %collective-permute-start.3 = (f32[64,128]{1,0:T(8,128)S(1)}, f32[64,128]{1,0:T(8,128)S(1)}, u32[]{:S(2)}, u32[]{:S(2)}) collective-permute-start(f32[64,128]{1,0:T(8,128)S(1)} %add.15.a_ref._), channel_id=1, source_target_pairs={{0,1},{1,0},{2,3},{3,2},{4,5},{5,4},{6,7},{7,6},{8,9},{9,8},{10,11... | collective-permute-start | bytes 98312 | tf_op jit(solution)/shard_map/ppermute | solution.py:73
  27.4 4.8 %collective-permute-start.4 = (f32[64,128]{1,0:T(8,128)S(1)}, f32[64,128]{1,0:T(8,128)S(1)}, u32[]{:S(2)}, u32[]{:S(2)}) collective-permute-start(f32[64,128]{1,0:T(8,128)S(1)} %add.16.a_ref._), channel_id=1, source_target_pairs={{0,2},{1,3},{2,0},{3,1},{4,6},{5,7},{6,4},{7,5},{8,10},{9,11},{10,... | collective-permute-start | bytes 98312 | tf_op jit(solution)/shard_map/ppermute | solution.py:73
  30.3 4.2 %collective-permute-start.8 = (f32[96,128]{1,0:T(8,128)S(1)}, f32[96,128]{1,0:T(8,128)S(1)}, u32[]{:S(2)}, u32[]{:S(2)}) collective-permute-start(f32[96,128]{1,0:T(8,128)S(1)} %get-tuple-element.36), channel_id=1, source_target_pairs={{0,1},{1,0},{2,3},{3,2},{4,5},{5,4},{6,7},{7,6},{8,9},{9,8},{10,11... | collective-permute-start | bytes 147464 | tf_op jit(solution)/shard_map/ppermute | solution.py:73
  32.2 3.0 %collective-permute-start.5 = (f32[64,128]{1,0:T(8,128)S(1)}, f32[64,128]{1,0:T(8,128)S(1)}, u32[]{:S(2)}, u32[]{:S(2)}) collective-permute-start(f32[64,128]{1,0:T(8,128)S(1)} %add.17.mine_ref._), channel_id=1, source_target_pairs={{0,4},{1,5},{2,6},{3,7},{4,0},{5,1},{6,2},{7,3},{8,12},{9,13},{10,... | collective-permute-start | bytes 98312 | tf_op jit(solution)/shard_map/ppermute | solution.py:73
  34.4 6.8 %collective-permute-start.9 = (f32[48,128]{1,0:T(8,128)S(1)}, f32[48,128]{1,0:T(8,128)S(1)}, u32[]{:S(2)}, u32[]{:S(2)}) collective-permute-start(f32[48,128]{1,0:T(8,128)S(1)} %get-tuple-element.38), channel_id=1, source_target_pairs={{0,2},{1,3},{2,0},{3,1},{4,6},{5,7},{6,4},{7,5},{8,10},{9,11},{10,... | collective-permute-start | bytes 73736 | tf_op jit(solution)/shard_map/ppermute | solution.py:73

commit v7 on v6

v7 whole, which is shorter than its diff:
```python
import functools
import math

import jax
import jax.numpy as jnp
from jax import lax
from jax.experimental import pallas as pl
from jax.experimental.pallas import tpu as pltpu
from jax.sharding import PartitionSpec as P

AXES = ("gx", "gy", "gz")
F32 = jnp.float32
BF16 = jnp.bfloat16
HBM = pl.BlockSpec(memory_space=pltpu.HBM)
VMEM = pl.BlockSpec(memory_space=pltpu.VMEM)
SMEM = pl.BlockSpec(memory_space=pltpu.SMEM)
VMEM_LIMIT = 24 * 1024 * 1024


def exact(a, b, dims=((1,), (0,))):
    return lax.dot_general(
        a, b, (dims, ((), ())), precision=lax.Precision.HIGHEST, preferred_element_type=F32
    )


def mxu(a, b, dims=((1,), (0,))):
    return lax.dot_general(a, b, (dims, ((), ())), preferred_element_type=F32)


def params():
    return pltpu.CompilerParams(vmem_limit_bytes=VMEM_LIMIT)


def cost(flops, nbytes):
    return pl.CostEstimate(flops=flops, bytes_accessed=nbytes, transcendentals=0)


def in_hbm(*values):
    return [pltpu.with_memory_space_constraint(value, pltpu.HBM) for value in values]


def row_block(total):
    for size in (768, 512, 384, 256, 128, 64, 32, 16):
        if total % size == 0:
            return size
    return total


class Plan:
    def __init__(self, mesh):
        size = {axis: mesh.shape[axis] for axis in AXES}
        self.count = math.prod(size.values())
        stride = {"gx": size["gy"] * size["gz"], "gy": size["gz"], "gz": 1}
        self.core = stride["gy"]
        spans = ((size["gx"], stride["gx"]), (size["gy"] // 2, 2 * stride["gy"]), (size["gz"], stride["gz"]))
        self.groups = [[k * step for k in range(n)] for n, step in spans if n > 1]
        self.masks = [0]
        for group in self.groups:
            self.masks = [mask | bits for mask in self.masks for bits in group]

    def side(self, device):
        return lax.bitwise_and(lax.div(device, jnp.int32(self.core)), jnp.int32(1))

    def swap(self, value, mask):
        return lax.ppermute(value, AXES, [(d, d ^ mask) for d in range(self.count)])


def gather_kernel(
    plan, step, sorted_here, where_ref, x_hbm, g_hbm, wr_hbm, wpt_hbm, we_hbm, rdp_hbm, wcat_hbm, *rest
):
    if sorted_here:
        kept_ref, sent_ref, turned_ref, *rest = rest
    else:
        keep_ref, send_ref, turned_ref, *rest = rest
    x_ref, g_ref, rdp_ref, cat_ref, wpt_ref, we_ref, sums_ref, term_ref, small_sem, in_sem, out_sem = rest
    rows = x_ref.shape[0]
    cr = we_ref.shape[1]
    nodes = wpt_ref.shape[0]
    wide = 2 * cr
    count = rows // step
    move = pltpu.make_async_copy
    small = [
        move(wr_hbm, cat_ref.at[:, pl.ds(0, cr)], small_sem.at[0]),
        move(wpt_hbm, wpt_ref, small_sem.at[1]),
        move(we_hbm, we_ref, small_sem.at[2]),
    ]
    load_cuts = sorted({0, min(1, count), min(2, count), count})
    store_cuts = sorted({0, max(count - 2, 0), max(count - 1, 0), count})
    span = lambda cuts, i: pl.ds(cuts[i] * step, (cuts[i + 1] - cuts[i]) * step)
    loads = [
        (
            move(x_hbm.at[span(load_cuts, i)], x_ref.at[span(load_cuts, i)], in_sem.at[0, i]),
            move(g_hbm.at[span(load_cuts, i)], g_ref.at[span(load_cuts, i)], in_sem.at[1, i]),
        )
        for i in range(len(load_cuts) - 1)
    ]
    stores = [
        move(rdp_ref.at[span(store_cuts, i)], rdp_hbm.at[span(store_cuts, i)], out_sem.at[i])
        for i in range(len(store_cuts) - 1)
    ]
    for copy in (*small, *loads[0]):
        copy.start()
    sums_ref[...] = jnp.zeros_like(sums_ref)
    term_ref[...] = jnp.zeros_like(term_ref)
    small[0].wait()
    small[1].wait()
    padded = jnp.concatenate([wpt_ref[...], jnp.zeros_like(wpt_ref)], axis=0)
    cat_ref[:, cr:] = padded.T
    keep_weights = move(cat_ref, wcat_hbm, small_sem.at[3])
    keep_weights.start()
    small[2].wait()

    @pl.loop(0, count)
    def _(i):
        for k, pair in enumerate(loads):
            @pl.when(i == load_cuts[k])
            def _():
                for copy in pair:
                    copy.wait()
                if k + 1 < len(loads):
                    for copy in loads[k + 1]:
                        copy.start()

        c = pl.ds(pl.multiple_of(i * step, step), step)
        x, g = x_ref[c], g_ref[c]
        both = mxu(x, cat_ref[...]).astype(BF16)
        mapped = mxu(g, we_ref[...]).astype(BF16)
        rdp = jnp.concatenate([both[:, :cr], mapped, both[:, cr:]], axis=1)
        rdp_ref[c] = rdp
        turned = rdp.T
        proj = turned[wide : wide + nodes]
        sums_ref[: wide + nodes] += mxu(turned[: wide + nodes], x)
        sums_ref[wide + nodes :] += mxu(proj, g)
        term = mxu(proj, rdp[:, :wide])
        term_ref[0] += term[:, :cr]
        term_ref[1] += term[:, cr:]
        for k, copy in enumerate(stores):
            pl.when(i == store_cuts[k + 1] - 1)(copy.start)

    me = where_ref[0]
    side = plan.side(me)
    turned_ref[...] = sums_ref[...].T
    if not sorted_here:
        keep_ref[...] = term_ref[side]
        send_ref[...] = term_ref[1 - side]
    else:
        kept_ref[:nodes] = term_ref[side]
        sent_ref[:nodes] = term_ref[1 - side]
        size = turned_ref.shape[0] // plan.count
        for base, out_ref in ((me, kept_ref), (me ^ plan.core, sent_ref)):
            to = nodes
            for mask in plan.masks:
                at = pl.multiple_of((base ^ mask) * size, size)
                block = turned_ref[pl.ds(at, size), :]
                for lane in range(0, block.shape[1], cr):
                    out_ref[to : to + size] = block[:, lane : lane + cr]
                    to += size
    for copy in (keep_weights, *stores):
        copy.wait()


def gather(plan, where, x, g, wr, wpt, we):
    rows, chan = x.shape
    cr, nodes = wr.shape[1], wpt.shape[0]
    step = row_block(rows)
    width = 2 * cr + 2 * nodes
    half = plan.count // 2
    size = chan // plan.count
    sorted_here = size % 8 == 0
    outs = [
        (HBM, pltpu.HBM((rows, width), BF16)),
        (HBM, pltpu.HBM((chan, cr + 2 * nodes), BF16)),
    ]
    scratch = []
    if sorted_here:
        outs += [(VMEM, pltpu.VMEM((nodes + half * size * width // cr, cr), F32))] * 2
        scratch += [pltpu.VMEM((chan, width), F32)]
    else:
        outs += [(VMEM, jax.ShapeDtypeStruct((nodes, cr), F32))] * 2
        outs += [(VMEM, jax.ShapeDtypeStruct((chan, width), F32))]
    scratch += [
        pltpu.VMEM((rows, chan), BF16),
        pltpu.VMEM((rows, chan), BF16),
        pltpu.VMEM((rows, width), BF16),
        pltpu.VMEM((chan, cr + 2 * nodes), BF16),
        pltpu.VMEM(wpt.shape, BF16),
        pltpu.VMEM(we.shape, BF16),
        pltpu.VMEM((width, chan), F32),
        pltpu.VMEM((2, nodes, cr), F32),
        pltpu.SemaphoreType.DMA((4,)),
        pltpu.SemaphoreType.DMA((2, 3)),
        pltpu.SemaphoreType.DMA((3,)),
    ]
    rdp, wcat, kept, sent, *sums = pl.pallas_call(
        functools.partial(gather_kernel, plan, step, sorted_here),
        in_specs=[SMEM] + [HBM] * 5,
        out_specs=[spec for spec, _ in outs],
        out_shape=[shape for _, shape in outs],
        scratch_shapes=scratch,
        compiler_params=params(),
        cost_estimate=cost(2 * rows * chan * 1024, rows * chan * 4 + rows * 768),
        name="gather",
    )(where, *in_hbm(x, g, wr, wpt, we))
    if not sorted_here:
        table = jnp.array(plan.masks, jnp.int32)
        cut = sums[0].reshape(plan.count, size, width // cr, cr).transpose(0, 2, 1, 3)
        lay = lambda head, index: jnp.concatenate([head, cut[index].reshape(-1, cr)])
        kept = lay(kept, where[0] ^ table)
        sent = lay(sent, where[0] ^ plan.core ^ table)
    return rdp, wcat, kept, sent


def step_kernel(head, ins, parts, *refs):
    terms, outs = refs[:ins], refs[ins:]

    def total(start, size):
        value = terms[0][start : start + size]
        for ref in terms[1:]:
            value = value + ref[start : start + size]
        return value

    nodes = total(0, head)
    rest = terms[0].shape[0] - head
    if parts == 1:
        outs[0][...] = nodes
        outs[1][...] = total(head, rest)
        return
    size = rest // parts
    for k, ref in enumerate(outs):
        ref[:head] = nodes
        ref[head:] = total(head + k * size, size)


def step(head, parts, terms):
    rest, lanes = terms[0].shape[0] - head, terms[0].shape[1]
    shapes = (head, rest) if parts == 1 else (head + rest // parts,) * parts
    return pl.pallas_call(
        functools.partial(step_kernel, head, len(terms), parts),
        in_specs=[VMEM] * len(terms),
        out_specs=[VMEM] * len(shapes),
        out_shape=[pltpu.VMEM((size, lanes), F32) for size in shapes],
        compiler_params=params(),
        cost_estimate=cost(terms[0].size, 12 * terms[0].size),
        name="step",
    )(*terms)


def feature_kernel(
    step, scale, plan, where_ref, mine_ref, other_ref, sums_ref, adj_hbm, nw_hbm, wcat_hbm, rdp_hbm, g_hbm,
    out_hbm, gr_ref, gp_ref, ge_ref, ga_ref, gn_ref,
    adj_ref, nw_ref, wcat_ref, rdp_ref, g_ref, out_ref, mix_ref, dnb_ref, in_sem, out_sem,
):
    nodes_n, cr = mine_ref.shape
    rows = g_ref.shape[0]
    wide = 2 * cr
    move = pltpu.make_async_copy
    pairs = (
        (adj_hbm, adj_ref), (nw_hbm, nw_ref), (rdp_hbm, rdp_ref), (wcat_hbm, wcat_ref), (g_hbm, g_ref)
    )
    loads = [move(src, dst, in_sem.at[k]) for k, (src, dst) in enumerate(pairs)]
    for copy in loads:
        copy.start()
    first = plan.side(where_ref[0]) == 0
    mine, other = mine_ref[...], other_ref[...]
    nodes = scale * jnp.where(first, mine, other)
    d_node_out = jnp.where(first, other, mine)
    loads[0].wait()
    loads[1].wait()
    adj, nw = adj_ref[...], nw_ref[...]
    hidden = nodes - exact(adj, nodes)
    pre = exact(hidden, nw)
    node_out = jnp.maximum(pre, 0.0).astype(BF16)
    d_pre = jnp.where(pre > 0.0, d_node_out, 0.0)
    d_hidden = exact(d_pre, nw, ((1,), (1,)))
    d_nodes = d_hidden - exact(adj, d_hidden, ((0,), (0,)))
    dn = d_nodes.astype(BF16)
    no_f, dn_f = node_out.astype(F32), dn.astype(F32)
    dnb_ref[:nodes_n] = dn
    dnb_ref[nodes_n:] = jnp.zeros((nodes_n, cr), BF16)
    blank = jnp.zeros((cr, cr), BF16)
    zero = jnp.zeros((nodes_n, cr), F32)
    mix_ref[:cr, :cr] = jnp.concatenate([dn_f, zero], axis=0).T.astype(BF16)
    mix_ref[cr:, :cr] = blank
    mix_ref[:cr, cr:] = blank
    mix_ref[cr:, cr:] = jnp.concatenate([no_f, zero], axis=0).T.astype(BF16)
    for copy in loads[2:]:
        copy.wait()
    copies = []
    for i, start in enumerate(range(0, rows, step)):
        c = pl.ds(start, step)
        rdp = rdp_ref[c]
        mixed = mxu(rdp[:, :wide], mix_ref[...])
        d_proj = (mixed[:, cr:] + scale * mixed[:, :cr]).astype(BF16)
        d_red = (scale * mxu(rdp[:, wide:], dnb_ref[...])).astype(BF16)
        both = jnp.concatenate([d_red, d_proj], axis=1)
        out = g_ref[c].astype(F32) + mxu(both, wcat_ref[...], ((1,), (1,)))
        out_ref[c] = out.astype(BF16)
        copies.append(move(out_ref.at[c], out_hbm.at[c], out_sem.at[i]))
        copies[-1].start()
    gn_ref[...] = scale * exact(hidden, d_pre, ((0,), (0,)))
    ga_ref[...] = -scale * exact(d_hidden, nodes, ((1,), (1,)))
    size = gr_ref.shape[0]
    x_red, x_dm, with_proj = (sums_ref[k * size : (k + 1) * size] for k in range(3))
    gr_ref[...] = scale * scale * exact(with_proj[:, :nodes_n], dn_f)
    gp_ref[...] = scale * exact(x_dm, no_f, ((1,), (1,))) + scale * scale * exact(
        x_red, dn_f, ((1,), (1,))
    )
    ge_ref[...] = scale * exact(with_proj[:, nodes_n:], no_f)
    for copy in copies:
        copy.wait()


def feature_grads(plan, where, mine, other, sums, adjacency, node_weight, wcat, rdp, g, scale):
    rows, chan = g.shape
    nodes, cr = adjacency.shape[0], node_weight.shape[0]
    step = row_block(rows)
    size = chan // plan.count
    loaded = (adjacency, node_weight, wcat, rdp, g)
    return pl.pallas_call(
        functools.partial(feature_kernel, step, scale, plan),
        in_specs=[SMEM, VMEM, VMEM, VMEM] + [HBM] * len(loaded),
        out_specs=[HBM] + [VMEM] * 5,
        out_shape=[
            pltpu.HBM((rows, chan), BF16),
            jax.ShapeDtypeStruct((size, cr), F32),
            jax.ShapeDtypeStruct((size, nodes), F32),
            jax.ShapeDtypeStruct((size, cr), F32),
            jax.ShapeDtypeStruct((nodes, nodes), F32),
            jax.ShapeDtypeStruct((cr, cr), F32),
        ],
        scratch_shapes=[pltpu.VMEM(value.shape, value.dtype) for value in loaded]
        + [
            pltpu.VMEM((rows, chan), BF16),
            pltpu.VMEM((2 * cr, 2 * cr), BF16),
            pltpu.VMEM((2 * nodes, cr), BF16),
            pltpu.SemaphoreType.DMA((len(loaded),)),
            pltpu.SemaphoreType.DMA((rows // step,)),
        ],
        compiler_params=params(),
        cost_estimate=cost(2 * rows * 4 * 65536, rows * chan * 4 + rows * 768),
        name="feature_grads",
    )(where, mine, other, sums, *in_hbm(*loaded))


def on_device(
    plan, features, cotangent, reduce_weight, project_weight, expand_weight, adjacency, node_weight
):
    size_x, size_y, size_z, chan = features.shape
    local = size_x * size_y * size_z
    scale = 1.0 / math.sqrt(local * plan.count)
    flat_x = features.transpose(0, 2, 1, 3).reshape(local, chan)
    flat_g = cotangent.transpose(0, 2, 1, 3).reshape(local, chan)
    me = lax.axis_index(AXES).astype(jnp.int32)
    where = me.reshape(1)

    rdp, wcat, kept, sent = gather(
        plan, where, flat_x, flat_g, reduce_weight, project_weight.T, expand_weight
    )
    head = adjacency.shape[0]
    terms = [kept, plan.swap(sent, plan.core)]
    for group in plan.groups:
        parts = step(head, len(group), terms)
        terms = [plan.swap(part, mask) if mask else part for part, mask in zip(parts, group)]
    mine, sums = step(head, 1, terms)
    other = plan.swap(mine, plan.core)

    flat_out, grad_reduce, grad_project, grad_expand, grad_adjacency, grad_node = feature_grads(
        plan, where, mine, other, sums, adjacency, node_weight, wcat, rdp, flat_g, scale
    )
    grad_features = flat_out.reshape(size_x, size_z, size_y, chan).transpose(0, 2, 1, 3)
    return (grad_features, grad_reduce, grad_project, grad_expand, grad_adjacency, grad_node)


def solution(mesh):
    return jax.shard_map(
        functools.partial(on_device, Plan(mesh)),
        mesh=mesh,
        in_specs=(P("gx", "gy", "gz", None), P("gx", "gy", "gz", None), P(), P(), P(), P(), P()),
        out_specs=(
            P("gx", "gy", "gz", None),
            P(AXES, None),
            P(AXES, None),
            P(AXES, None),
            P(),
            P(),
        ),
        check_vma=False,
    )
```

time: 42.3 us -> 39.2 us (0.927)
  starting transfers between devices: 14.5 us -> 9.51 us
  waiting for transfers between devices: 12 us -> 14.9 us
  Pallas kernels: 14.9 us -> 13.9 us
    ppermute x10 -> x8, starting transfers between devices: 14.5 us -> 9.51 us  [swap(): return lax.ppermute(value, AXES, [(d, d ^ mask) for d in range(self.count)])]
    ppermute x10 -> x8, waiting for transfers between devices: 12 us -> 14.9 us  [swap(): return lax.ppermute(value, AXES, [(d, d ^ mask) for d in range(self.count)])]
    pallas_call x12 -> x5, Pallas kernels: 14.9 us -> 13.9 us  [the longest x1 7.82 us: gather(): pl.pallas_call(functools.partial(gather_kernel, plan, step, sorted_here),...]
  transfers between devices with their start and end apart: 10 -> 8, of which waited for: 6 -> 7; matrix products, arithmetic and copies ran while one was open for 0% -> 0% of each run, Pallas kernels for 14% -> 0%
where the time goes in v7:
time: 39.2 us; the launch traced here: 39 us
  waiting for transfers between devices  14.9 us (38%)
  Pallas kernels  13.9 us (35%)
  starting transfers between devices  9.51 us (24%)
  between operations  0.67 us (2%)
    ppermute x8, waiting for transfers between devices, swap(): return lax.ppermute(value, AXES, [(d, d ^ mask) for d in range(self.count)])  14.9 us
    ppermute x8, starting transfers between devices, swap(): return lax.ppermute(value, AXES, [(d, d ^ mask) for d in range(self.count)])  9.51 us
    pallas_call x1, Pallas kernels, gather(): pl.pallas_call(functools.partial(gather_kernel, plan, step, sorted_here),...  7.82 us
    pallas_call x1, Pallas kernels, feature_grads(): pl.pallas_call(functools.partial(feature_kernel, step, scale, plan), in_s...  6 us
  transfers between devices with their start and end apart: 8, of which 7 were waited for; matrix products, arithmetic and copies ran while one was open for 0% of the time, Pallas kernels for 0%

profile of v7, /device:TPU:0, one launch (start us, length us, event | category | flops | bytes accessed | tf_op | source)
XLA Modules:
  0.0 39.0 jit_solution(17625526300714353150)
XLA Ops:
  0.6 7.8 %gather.1 = (bf16[3072,384]{1,0:T(8,128)(2,1)}, bf16[512,256]{1,0:T(8,128)(2,1)}, f32[832,128]{1,0:T(8,128)S(1)}, f32[832,128]{1,0:T(8,128)S(1)}) custom-call(s32[1]{0:T(128)} %bitcast.where_ref, bf16[3072,512]{1,0:T(8,128)(2,1)} %bitcast.11, bf16[3072,512]{1,0:T(8,128)(2,1)} %bitcast.12, bf16[512,128]{1,0:T(8,128)(2,1)} %wr_hbm.1, ...), custom_call_target="tpu_custom_call" | custom-call | flops 3221225472 | bytes 8650752 | tf_op jit(solution)/shard_map/gather/pallas_call | solution.py:194
  8.5 0.5 %collective-permute-start = (f32[832,128]{1,0:T(8,128)S(1)}, f32[832,128]{1,0:T(8,128)S(1)}, u32[]{:S(2)}, u32[]{:S(2)}) collective-permute-start(f32[832,128]{1,0:T(8,128)S(1)} %get-tuple-element.27), channel_id=1, source_target_pairs={{0,4},{1,5},{2,6},{3,7},{4,0},{5,1},{6,2},{7,3},{8,12},{9,13},{10,... | collective-permute-start | bytes 1277960 | tf_op jit(solution)/shard_map/ppermute | solution.py:65
  9.0 1.4 %collective-permute-done.refs_1_ = f32[832,128]{1,0:T(8,128)S(1)} collective-permute-done((f32[832,128]{1,0:T(8,128)S(1)}, f32[832,128]{1,0:T(8,128)S(1)}, u32[]{:S(2)}, u32[]{:S(2)}) %collective-permute-start) | collective-permute-done | bytes 426016 | tf_op jit(solution)/shard_map/ppermute | solution.py:65
  10.4 2.9 %collective-permute-start.1 = (f32[256,128]{1,0:T(8,128)S(1)}, f32[256,128]{1,0:T(8,128)S(1)}, u32[]{:S(2)}, u32[]{:S(2)}) collective-permute-start(f32[256,128]{1,0:T(8,128)S(1)} %get-tuple-element.29), channel_id=1, source_target_pairs={{0,8},{1,9},{2,10},{3,11},{4,12},{5,13},{6,14},{7,15},{8,0},{9,1},... | collective-permute-start | bytes 393224 | tf_op jit(solution)/shard_map/ppermute | solution.py:65
  13.4 1.5 %collective-permute-start.2 = (f32[256,128]{1,0:T(8,128)S(1)}, f32[256,128]{1,0:T(8,128)S(1)}, u32[]{:S(2)}, u32[]{:S(2)}) collective-permute-start(f32[256,128]{1,0:T(8,128)S(1)} %get-tuple-element.30), channel_id=1, source_target_pairs={{0,16},{1,17},{2,18},{3,19},{4,20},{5,21},{6,22},{7,23},{8,24},{9,... | collective-permute-start | bytes 393224 | tf_op jit(solution)/shard_map/ppermute | solution.py:65
  14.9 0.0 collective-permute-start.3
  14.9 2.4 %collective-permute-done.1.refs_1_ = f32[256,128]{1,0:T(8,128)S(1)} collective-permute-done((f32[256,128]{1,0:T(8,128)S(1)}, f32[256,128]{1,0:T(8,128)S(1)}, u32[]{:S(2)}, u32[]{:S(2)}) %collective-permute-start.1) | collective-permute-done | bytes 131104 | tf_op jit(solution)/shard_map/ppermute | solution.py:65
  17.3 4.2 %collective-permute-done.2.refs_2_ = f32[256,128]{1,0:T(8,128)S(1)} collective-permute-done((f32[256,128]{1,0:T(8,128)S(1)}, f32[256,128]{1,0:T(8,128)S(1)}, u32[]{:S(2)}, u32[]{:S(2)}) %collective-permute-start.2) | collective-permute-done | bytes 131104 | tf_op jit(solution)/shard_map/ppermute | solution.py:65
  21.4 0.0 collective-permute-done.3.refs_3_
  21.5 1.6 %collective-permute-start.4 = (f32[112,128]{1,0:T(8,128)S(1)}, f32[112,128]{1,0:T(8,128)S(1)}, u32[]{:S(2)}, u32[]{:S(2)}) collective-permute-start(f32[112,128]{1,0:T(8,128)S(1)} %get-tuple-element.33), channel_id=1, source_target_pairs={{0,1},{1,0},{2,3},{3,2},{4,5},{5,4},{6,7},{7,6},{8,9},{9,8},{10,11... | collective-permute-start | bytes 172040 | tf_op jit(solution)/shard_map/ppermute | solution.py:65
  23.1 2.6 %collective-permute-start.5 = (f32[112,128]{1,0:T(8,128)S(1)}, f32[112,128]{1,0:T(8,128)S(1)}, u32[]{:S(2)}, u32[]{:S(2)}) collective-permute-start(f32[112,128]{1,0:T(8,128)S(1)} %get-tuple-element.34), channel_id=1, source_target_pairs={{0,2},{1,3},{2,0},{3,1},{4,6},{5,7},{6,4},{7,5},{8,10},{9,11},{10,... | collective-permute-start | bytes 172040 | tf_op jit(solution)/shard_map/ppermute | solution.py:65
  25.7 0.2 collective-permute-start.6
  25.9 0.4 collective-permute-done.4.refs_1_
  26.3 3.1 %collective-permute-done.5.refs_2_ = f32[112,128]{1,0:T(8,128)S(1)} collective-permute-done((f32[112,128]{1,0:T(8,128)S(1)}, f32[112,128]{1,0:T(8,128)S(1)}, u32[]{:S(2)}, u32[]{:S(2)}) %collective-permute-start.5) | collective-permute-done | bytes 57376 | tf_op jit(solution)/shard_map/ppermute | solution.py:65
  29.4 2.3 %collective-permute-done.6.refs_3_ = f32[112,128]{1,0:T(8,128)S(1)} collective-permute-done((f32[112,128]{1,0:T(8,128)S(1)}, f32[112,128]{1,0:T(8,128)S(1)}, u32[]{:S(2)}, u32[]{:S(2)}) %collective-permute-start.6) | collective-permute-done | bytes 57376 | tf_op jit(solution)/shard_map/ppermute | solution.py:65
  31.7 0.1 collective-permute-start.7
  31.8 1.2 %collective-permute-done.7.other_ref = f32[64,128]{1,0:T(8,128)S(1)} collective-permute-done((f32[64,128]{1,0:T(8,128)S(1)}, f32[64,128]{1,0:T(8,128)S(1)}, u32[]{:S(2)}, u32[]{:S(2)}) %collective-permute-start.7) | collective-permute-done | bytes 32800 | tf_op jit(solution)/shard_map/ppermute | solution.py:65
  33.0 6.0 %feature_grads.1 = (bf16[3072,512]{1,0:T(8,128)(2,1)}, f32[16,128]{1,0:T(8,128)}, f32[16,64]{1,0:T(8,128)}, f32[16,128]{1,0:T(8,128)}, f32[64,64]{1,0:T(8,128)}, /*index=5*/f32[128,128]{1,0:T(8,128)}) custom-call(s32[1]{0:T(128)} %bitcast.where_ref, f32[64,128]{1,0:T(8,128)S(1)} %get-tuple-element.36.mine_ref, ...), custom_call_target="tpu_custom_call" | custom-call | flops 1610612736 | bytes 8650752 | tf_op jit(solution)/shard_map/feature_grads/pallas_call | solution.py:319
  (3 shorter events, 0.1 us)
Async XLA Ops:
  8.5 1.9 %collective-permute-start = (f32[832,128]{1,0:T(8,128)S(1)}, f32[832,128]{1,0:T(8,128)S(1)}, u32[]{:S(2)}, u32[]{:S(2)}) collective-permute-start(f32[832,128]{1,0:T(8,128)S(1)} %get-tuple-element.27), channel_id=1, source_target_pairs={{0,4},{1,5},{2,6},{3,7},{4,0},{5,1},{6,2},{7,3},{8,12},{9,13},{10,... | collective-permute-start | bytes 1277960 | tf_op jit(solution)/shard_map/ppermute | solution.py:65
  10.4 6.8 %collective-permute-start.1 = (f32[256,128]{1,0:T(8,128)S(1)}, f32[256,128]{1,0:T(8,128)S(1)}, u32[]{:S(2)}, u32[]{:S(2)}) collective-permute-start(f32[256,128]{1,0:T(8,128)S(1)} %get-tuple-element.29), channel_id=1, source_target_pairs={{0,8},{1,9},{2,10},{3,11},{4,12},{5,13},{6,14},{7,15},{8,0},{9,1},... | collective-permute-start | bytes 393224 | tf_op jit(solution)/shard_map/ppermute | solution.py:65
  13.4 8.1 %collective-permute-start.2 = (f32[256,128]{1,0:T(8,128)S(1)}, f32[256,128]{1,0:T(8,128)S(1)}, u32[]{:S(2)}, u32[]{:S(2)}) collective-permute-start(f32[256,128]{1,0:T(8,128)S(1)} %get-tuple-element.30), channel_id=1, source_target_pairs={{0,16},{1,17},{2,18},{3,19},{4,20},{5,21},{6,22},{7,23},{8,24},{9,... | collective-permute-start | bytes 393224 | tf_op jit(solution)/shard_map/ppermute | solution.py:65
  14.9 6.5 %collective-permute-start.3 = (f32[256,128]{1,0:T(8,128)S(1)}, f32[256,128]{1,0:T(8,128)S(1)}, u32[]{:S(2)}, u32[]{:S(2)}) collective-permute-start(f32[256,128]{1,0:T(8,128)S(1)} %get-tuple-element.31), channel_id=1, source_target_pairs={{0,24},{1,25},{2,26},{3,27},{4,28},{5,29},{6,30},{7,31},{8,16},{9,... | collective-permute-start | bytes 393224 | tf_op jit(solution)/shard_map/ppermute | solution.py:65
  21.5 4.8 %collective-permute-start.4 = (f32[112,128]{1,0:T(8,128)S(1)}, f32[112,128]{1,0:T(8,128)S(1)}, u32[]{:S(2)}, u32[]{:S(2)}) collective-permute-start(f32[112,128]{1,0:T(8,128)S(1)} %get-tuple-element.33), channel_id=1, source_target_pairs={{0,1},{1,0},{2,3},{3,2},{4,5},{5,4},{6,7},{7,6},{8,9},{9,8},{10,11... | collective-permute-start | bytes 172040 | tf_op jit(solution)/shard_map/ppermute | solution.py:65
  23.1 6.3 %collective-permute-start.5 = (f32[112,128]{1,0:T(8,128)S(1)}, f32[112,128]{1,0:T(8,128)S(1)}, u32[]{:S(2)}, u32[]{:S(2)}) collective-permute-start(f32[112,128]{1,0:T(8,128)S(1)} %get-tuple-element.34), channel_id=1, source_target_pairs={{0,2},{1,3},{2,0},{3,1},{4,6},{5,7},{6,4},{7,5},{8,10},{9,11},{10,... | collective-permute-start | bytes 172040 | tf_op jit(solution)/shard_map/ppermute | solution.py:65
  25.7 6.0 %collective-permute-start.6 = (f32[112,128]{1,0:T(8,128)S(1)}, f32[112,128]{1,0:T(8,128)S(1)}, u32[]{:S(2)}, u32[]{:S(2)}) collective-permute-start(f32[112,128]{1,0:T(8,128)S(1)} %get-tuple-element.35), channel_id=1, source_target_pairs={{0,3},{1,2},{2,1},{3,0},{4,7},{5,6},{6,5},{7,4},{8,11},{9,10},{10,... | collective-permute-start | bytes 172040 | tf_op jit(solution)/shard_map/ppermute | solution.py:65
  31.7 1.3 %collective-permute-start.7 = (f32[64,128]{1,0:T(8,128)S(1)}, f32[64,128]{1,0:T(8,128)S(1)}, u32[]{:S(2)}, u32[]{:S(2)}) collective-permute-start(f32[64,128]{1,0:T(8,128)S(1)} %get-tuple-element.36.mine_ref), channel_id=1, source_target_pairs={{0,4},{1,5},{2,6},{3,7},{4,0},{5,1},{6,2},{7,3},{8,12},{9,13},{10,... | collective-permute-start | bytes 98312 | tf_op jit(solution)/shard_map/ppermute | solution.py:65

commit v8 on v7

--- a/solution.py
+++ b/solution.py
@@ -15,6 +15,7 @@
 VMEM = pl.BlockSpec(memory_space=pltpu.VMEM)
 SMEM = pl.BlockSpec(memory_space=pltpu.SMEM)
 VMEM_LIMIT = 24 * 1024 * 1024
+SMALL_LIMIT = 4 * 1024 * 1024
 
 
 def exact(a, b, dims=((1,), (0,))):
@@ -27,8 +28,8 @@
     return lax.dot_general(a, b, (dims, ((), ())), preferred_element_type=F32)
 
 
-def params():
-    return pltpu.CompilerParams(vmem_limit_bytes=VMEM_LIMIT)
+def params(limit=VMEM_LIMIT):
+    return pltpu.CompilerParams(vmem_limit_bytes=limit)
 
 
 def cost(flops, nbytes):
@@ -40,7 +41,7 @@
 
 
 def row_block(total):
-    for size in (768, 512, 384, 256, 128, 64, 32, 16):
+    for size in (1024, 768, 512, 384, 256, 128, 64, 32, 16):
         if total % size == 0:
             return size
     return total
@@ -239,33 +240,49 @@
         in_specs=[VMEM] * len(terms),
         out_specs=[VMEM] * len(shapes),
         out_shape=[pltpu.VMEM((size, lanes), F32) for size in shapes],
-        compiler_params=params(),
+        compiler_params=params(SMALL_LIMIT),
         cost_estimate=cost(terms[0].size, 12 * terms[0].size),
         name="step",
     )(*terms)
 
 
+def fetch_kernel(_, *refs):
+    sems = refs[-1]
+    count = len(refs) // 2
+    copies = [
+        pltpu.make_async_copy(src, dst, sems.at[k])
+        for k, (src, dst) in enumerate(zip(refs[:count], refs[count:-1]))
+    ]
+    for copy in copies:
+        copy.start()
+    for copy in copies:
+        copy.wait()
+
+
+def fetch(after, *values):
+    return pl.pallas_call(
+        fetch_kernel,
+        in_specs=[pl.BlockSpec(memory_space=pl.ANY)] + [HBM] * len(values),
+        out_specs=[VMEM] * len(values),
+        out_shape=[pltpu.VMEM(value.shape, value.dtype) for value in values],
+        scratch_shapes=[pltpu.SemaphoreType.DMA((len(values),))],
+        compiler_params=params(SMALL_LIMIT),
+        cost_estimate=cost(0, sum(value.size * value.dtype.itemsize for value in values)),
+        name="fetch",
+    )(after, *in_hbm(*values))
+
+
 def feature_kernel(
-    step, scale, plan, where_ref, mine_ref, other_ref, sums_ref, adj_hbm, nw_hbm, wcat_hbm, rdp_hbm, g_hbm,
-    out_hbm, gr_ref, gp_ref, ge_ref, ga_ref, gn_ref,
-    adj_ref, nw_ref, wcat_ref, rdp_ref, g_ref, out_ref, mix_ref, dnb_ref, in_sem, out_sem,
+    step, scale, plan, where_ref, mine_ref, other_ref, sums_ref, adj_ref, nw_ref, wcat_ref, rdp_ref, g_ref,
+    out_hbm, gr_ref, gp_ref, ge_ref, ga_ref, gn_ref, out_ref, mix_ref, dnb_ref, out_sem,
 ):
     nodes_n, cr = mine_ref.shape
     rows = g_ref.shape[0]
     wide = 2 * cr
-    move = pltpu.make_async_copy
-    pairs = (
-        (adj_hbm, adj_ref), (nw_hbm, nw_ref), (rdp_hbm, rdp_ref), (wcat_hbm, wcat_ref), (g_hbm, g_ref)
-    )
-    loads = [move(src, dst, in_sem.at[k]) for k, (src, dst) in enumerate(pairs)]
-    for copy in loads:
-        copy.start()
     first = plan.side(where_ref[0]) == 0
     mine, other = mine_ref[...], other_ref[...]
     nodes = scale * jnp.where(first, mine, other)
     d_node_out = jnp.where(first, other, mine)
-    loads[0].wait()
-    loads[1].wait()
     adj, nw = adj_ref[...], nw_ref[...]
     hidden = nodes - exact(adj, nodes)
     pre = exact(hidden, nw)
@@ -283,8 +300,6 @@
     mix_ref[cr:, :cr] = blank
     mix_ref[:cr, cr:] = blank
     mix_ref[cr:, cr:] = jnp.concatenate([no_f, zero], axis=0).T.astype(BF16)
-    for copy in loads[2:]:
-        copy.wait()
     copies = []
     for i, start in enumerate(range(0, rows, step)):
         c = pl.ds(start, step)
@@ -295,7 +310,7 @@
         both = jnp.concatenate([d_red, d_proj], axis=1)
         out = g_ref[c].astype(F32) + mxu(both, wcat_ref[...], ((1,), (1,)))
         out_ref[c] = out.astype(BF16)
-        copies.append(move(out_ref.at[c], out_hbm.at[c], out_sem.at[i]))
+        copies.append(pltpu.make_async_copy(out_ref.at[c], out_hbm.at[c], out_sem.at[i]))
         copies[-1].start()
     gn_ref[...] = scale * exact(hidden, d_pre, ((0,), (0,)))
     ga_ref[...] = -scale * exact(d_hidden, nodes, ((1,), (1,)))
@@ -313,12 +328,15 @@
 def feature_grads(plan, where, mine, other, sums, adjacency, node_weight, wcat, rdp, g, scale):
     rows, chan = g.shape
     nodes, cr = adjacency.shape[0], node_weight.shape[0]
-    step = row_block(rows)
+    step = row_block(rows // 2)
     size = chan // plan.count
-    loaded = (adjacency, node_weight, wcat, rdp, g)
+    there = [
+        pltpu.with_memory_space_constraint(value, pltpu.VMEM)
+        for value in (mine, other, sums, adjacency, node_weight, wcat, rdp, g)
+    ]
     return pl.pallas_call(
         functools.partial(feature_kernel, step, scale, plan),
-        in_specs=[SMEM, VMEM, VMEM, VMEM] + [HBM] * len(loaded),
+        in_specs=[SMEM] + [VMEM] * len(there),
         out_specs=[HBM] + [VMEM] * 5,
         out_shape=[
             pltpu.HBM((rows, chan), BF16),
@@ -328,18 +346,16 @@
             jax.ShapeDtypeStruct((nodes, nodes), F32),
             jax.ShapeDtypeStruct((cr, cr), F32),
         ],
-        scratch_shapes=[pltpu.VMEM(value.shape, value.dtype) for value in loaded]
-        + [
+        scratch_shapes=[
             pltpu.VMEM((rows, chan), BF16),
             pltpu.VMEM((2 * cr, 2 * cr), BF16),
             pltpu.VMEM((2 * nodes, cr), BF16),
-            pltpu.SemaphoreType.DMA((len(loaded),)),
             pltpu.SemaphoreType.DMA((rows // step,)),
         ],
         compiler_params=params(),
         cost_estimate=cost(2 * rows * 4 * 65536, rows * chan * 4 + rows * 768),
         name="feature_grads",
-    )(where, mine, other, sums, *in_hbm(*loaded))
+    )(where, *there)
 
 
 def on_device(
@@ -361,11 +377,12 @@
     for group in plan.groups:
         parts = step(head, len(group), terms)
         terms = [plan.swap(part, mask) if mask else part for part, mask in zip(parts, group)]
+    ready = fetch(terms[1], adjacency, node_weight, wcat, rdp, flat_g)
     mine, sums = step(head, 1, terms)
     other = plan.swap(mine, plan.core)
 
     flat_out, grad_reduce, grad_project, grad_expand, grad_adjacency, grad_node = feature_grads(
-        plan, where, mine, other, sums, adjacency, node_weight, wcat, rdp, flat_g, scale
+        plan, where, mine, other, sums, *ready, scale
     )
     grad_features = flat_out.reshape(size_x, size_z, size_y, chan).transpose(0, 2, 1, 3)
     return (grad_features, grad_reduce, grad_project, grad_expand, grad_adjacency, grad_node)

time: 39.2 us -> 37.7 us (0.962)
  waiting for transfers between devices: 14.9 us -> 13.7 us
    pallas_call x0 -> x1, Pallas kernels: none -> 2.8 us  [fetch(): pl.pallas_call(fetch_kernel, in_specs=[pl.BlockSpec(memory_space=pl.ANY)]...]
    pallas_call x1, Pallas kernels: 6 us -> 4.13 us  [feature_grads(): pl.pallas_call(functools.partial(feature_kernel, step, scale, plan), in_s...]
    pallas_call x1, Pallas kernels: 7.82 us -> 6.56 us  [gather(): pl.pallas_call(functools.partial(gather_kernel, plan, step, sorted_here),...]
    ppermute x8, waiting for transfers between devices: 14.9 us -> 13.7 us  [swap(): return lax.ppermute(value, AXES, [(d, d ^ mask) for d in range(self.count)])]
  transfers between devices with their start and end apart: 8 -> 8, of which waited for: 7 -> 6; matrix products, arithmetic and copies ran while one was open for 0% -> 0% of each run, Pallas kernels for 0% -> 7%
where the time goes in v8:
time: 37.7 us; the launch traced here: 37.5 us
  waiting for transfers between devices  13.7 us (36%)
  Pallas kernels  13.6 us (36%)
  starting transfers between devices  9.5 us (25%)
  between operations  0.69 us (2%)
    ppermute x8, waiting for transfers between devices, swap(): return lax.ppermute(value, AXES, [(d, d ^ mask) for d in range(self.count)])  13.7 us
    ppermute x8, starting transfers between devices, swap(): return lax.ppermute(value, AXES, [(d, d ^ mask) for d in range(self.count)])  9.5 us
    pallas_call x1, Pallas kernels, gather(): pl.pallas_call(functools.partial(gather_kernel, plan, step, sorted_here),...  6.56 us
    pallas_call x1, Pallas kernels, feature_grads(): pl.pallas_call(functools.partial(feature_kernel, step, scale, plan), in_s...  4.13 us
    pallas_call x1, Pallas kernels, fetch(): pl.pallas_call(fetch_kernel, in_specs=[pl.BlockSpec(memory_space=pl.ANY)]...  2.8 us
  transfers between devices with their start and end apart: 8, of which 6 were waited for; matrix products, arithmetic and copies ran while one was open for 0% of the time, Pallas kernels for 7%

profile of v8, /device:TPU:0, one launch (start us, length us, event | category | flops | bytes accessed | tf_op | source)
XLA Modules:
  0.0 37.5 jit_solution(2661489287315960363)
XLA Ops:
  0.6 6.6 %gather.1 = (bf16[3072,384]{1,0:T(8,128)(2,1)}, bf16[512,256]{1,0:T(8,128)(2,1)}, f32[832,128]{1,0:T(8,128)S(1)}, f32[832,128]{1,0:T(8,128)S(1)}) custom-call(s32[1]{0:T(128)} %bitcast.where_ref, bf16[3072,512]{1,0:T(8,128)(2,1)} %bitcast.13, bf16[3072,512]{1,0:T(8,128)(2,1)} %bitcast.11, bf16[512,128]{1,0:T(8,128)(2,1)} %wr_hbm.1, ...), custom_call_target="tpu_custom_call" | custom-call | flops 3221225472 | bytes 8650752 | tf_op jit(solution)/shard_map/gather/pallas_call | solution.py:195
  7.2 0.5 %collective-permute-start = (f32[832,128]{1,0:T(8,128)S(1)}, f32[832,128]{1,0:T(8,128)S(1)}, u32[]{:S(2)}, u32[]{:S(2)}) collective-permute-start(f32[832,128]{1,0:T(8,128)S(1)} %get-tuple-element.32), channel_id=1, source_target_pairs={{0,4},{1,5},{2,6},{3,7},{4,0},{5,1},{6,2},{7,3},{8,12},{9,13},{10,... | collective-permute-start | bytes 1277960 | tf_op jit(solution)/shard_map/ppermute | solution.py:66
  7.7 1.4 %collective-permute-done.refs_1_ = f32[832,128]{1,0:T(8,128)S(1)} collective-permute-done((f32[832,128]{1,0:T(8,128)S(1)}, f32[832,128]{1,0:T(8,128)S(1)}, u32[]{:S(2)}, u32[]{:S(2)}) %collective-permute-start) | collective-permute-done | bytes 426016 | tf_op jit(solution)/shard_map/ppermute | solution.py:66
  9.2 2.9 %collective-permute-start.1 = (f32[256,128]{1,0:T(8,128)S(1)}, f32[256,128]{1,0:T(8,128)S(1)}, u32[]{:S(2)}, u32[]{:S(2)}) collective-permute-start(f32[256,128]{1,0:T(8,128)S(1)} %get-tuple-element.34), channel_id=1, source_target_pairs={{0,8},{1,9},{2,10},{3,11},{4,12},{5,13},{6,14},{7,15},{8,0},{9,1},... | collective-permute-start | bytes 393224 | tf_op jit(solution)/shard_map/ppermute | solution.py:66
  12.1 1.5 %collective-permute-start.2 = (f32[256,128]{1,0:T(8,128)S(1)}, f32[256,128]{1,0:T(8,128)S(1)}, u32[]{:S(2)}, u32[]{:S(2)}) collective-permute-start(f32[256,128]{1,0:T(8,128)S(1)} %get-tuple-element.35), channel_id=1, source_target_pairs={{0,16},{1,17},{2,18},{3,19},{4,20},{5,21},{6,22},{7,23},{8,24},{9,... | collective-permute-start | bytes 393224 | tf_op jit(solution)/shard_map/ppermute | solution.py:66
  13.6 0.0 collective-permute-start.3
  13.6 2.4 %collective-permute-done.1.refs_1_ = f32[256,128]{1,0:T(8,128)S(1)} collective-permute-done((f32[256,128]{1,0:T(8,128)S(1)}, f32[256,128]{1,0:T(8,128)S(1)}, u32[]{:S(2)}, u32[]{:S(2)}) %collective-permute-start.1) | collective-permute-done | bytes 131104 | tf_op jit(solution)/shard_map/ppermute | solution.py:66
  16.0 4.2 %collective-permute-done.2.refs_2_ = f32[256,128]{1,0:T(8,128)S(1)} collective-permute-done((f32[256,128]{1,0:T(8,128)S(1)}, f32[256,128]{1,0:T(8,128)S(1)}, u32[]{:S(2)}, u32[]{:S(2)}) %collective-permute-start.2) | collective-permute-done | bytes 131104 | tf_op jit(solution)/shard_map/ppermute | solution.py:66
  20.2 0.0 collective-permute-done.3.refs_3_
  20.2 1.6 %collective-permute-start.4 = (f32[112,128]{1,0:T(8,128)S(1)}, f32[112,128]{1,0:T(8,128)S(1)}, u32[]{:S(2)}, u32[]{:S(2)}) collective-permute-start(f32[112,128]{1,0:T(8,128)S(1)} %get-tuple-element.38), channel_id=1, source_target_pairs={{0,1},{1,0},{2,3},{3,2},{4,5},{5,4},{6,7},{7,6},{8,9},{9,8},{10,11... | collective-permute-start | bytes 172040 | tf_op jit(solution)/shard_map/ppermute | solution.py:66
  21.8 2.6 %collective-permute-start.5 = (f32[112,128]{1,0:T(8,128)S(1)}, f32[112,128]{1,0:T(8,128)S(1)}, u32[]{:S(2)}, u32[]{:S(2)}) collective-permute-start(f32[112,128]{1,0:T(8,128)S(1)} %get-tuple-element.39), channel_id=1, source_target_pairs={{0,2},{1,3},{2,0},{3,1},{4,6},{5,7},{6,4},{7,5},{8,10},{9,11},{10,... | collective-permute-start | bytes 172040 | tf_op jit(solution)/shard_map/ppermute | solution.py:66
  24.4 0.2 collective-permute-start.6
  24.7 0.3 collective-permute-done.4.refs_1_._
  25.0 3.2 %collective-permute-done.5.refs_2_ = f32[112,128]{1,0:T(8,128)S(1)} collective-permute-done((f32[112,128]{1,0:T(8,128)S(1)}, f32[112,128]{1,0:T(8,128)S(1)}, u32[]{:S(2)}, u32[]{:S(2)}) %collective-permute-start.5) | collective-permute-done | bytes 57376 | tf_op jit(solution)/shard_map/ppermute | solution.py:66
  28.1 2.3 %collective-permute-done.6.refs_3_ = f32[112,128]{1,0:T(8,128)S(1)} collective-permute-done((f32[112,128]{1,0:T(8,128)S(1)}, f32[112,128]{1,0:T(8,128)S(1)}, u32[]{:S(2)}, u32[]{:S(2)}) %collective-permute-start.6) | collective-permute-done | bytes 57376 | tf_op jit(solution)/shard_map/ppermute | solution.py:66
  30.4 0.1 collective-permute-start.7
  30.5 2.8 %fetch.1 = (f32[64,64]{1,0:T(8,128)S(1)}, f32[128,128]{1,0:T(8,128)S(1)}, bf16[512,256]{1,0:T(8,128)(2,1)S(1)}, bf16[3072,384]{1,0:T(8,128)(2,1)S(1)}, bf16[3072,512]{1,0:T(8,128)(2,1)S(1)}) custom-call(f32[112,128]{1,0:T(8,128)S(1)} %collective-permute-done.4.refs_1_._, f32[64,64]{1,0:T(8,128)} %refs_0_.1, f32[128,128]{1,0:T(8,128)} %refs_1_.1, ...), custom_call_target="tpu_custom_call" | custom-call | bytes 5849088 | tf_op jit(solution)/shard_map/fetch/pallas_call | solution.py:263
  33.3 0.0 collective-permute-done.7.other_ref
  33.3 4.1 %feature_grads.1 = (bf16[3072,512]{1,0:T(8,128)(2,1)}, f32[16,128]{1,0:T(8,128)}, f32[16,64]{1,0:T(8,128)}, f32[16,128]{1,0:T(8,128)}, f32[64,64]{1,0:T(8,128)}, /*index=5*/f32[128,128]{1,0:T(8,128)}) custom-call(s32[1]{0:T(128)} %bitcast.where_ref, f32[64,128]{1,0:T(8,128)S(1)} %get-tuple-element.41.mine_ref, ...), custom_call_target="tpu_custom_call" | custom-call | flops 1610612736 | bytes 8650752 | tf_op jit(solution)/shard_map/feature_grads/pallas_call | solution.py:337
  (3 shorter events, 0.1 us)
Async XLA Ops:
  7.2 1.9 %collective-permute-start = (f32[832,128]{1,0:T(8,128)S(1)}, f32[832,128]{1,0:T(8,128)S(1)}, u32[]{:S(2)}, u32[]{:S(2)}) collective-permute-start(f32[832,128]{1,0:T(8,128)S(1)} %get-tuple-element.32), channel_id=1, source_target_pairs={{0,4},{1,5},{2,6},{3,7},{4,0},{5,1},{6,2},{7,3},{8,12},{9,13},{10,... | collective-permute-start | bytes 1277960 | tf_op jit(solution)/shard_map/ppermute | solution.py:66
  9.2 6.8 %collective-permute-start.1 = (f32[256,128]{1,0:T(8,128)S(1)}, f32[256,128]{1,0:T(8,128)S(1)}, u32[]{:S(2)}, u32[]{:S(2)}) collective-permute-start(f32[256,128]{1,0:T(8,128)S(1)} %get-tuple-element.34), channel_id=1, source_target_pairs={{0,8},{1,9},{2,10},{3,11},{4,12},{5,13},{6,14},{7,15},{8,0},{9,1},... | collective-permute-start | bytes 393224 | tf_op jit(solution)/shard_map/ppermute | solution.py:66
  12.1 8.1 %collective-permute-start.2 = (f32[256,128]{1,0:T(8,128)S(1)}, f32[256,128]{1,0:T(8,128)S(1)}, u32[]{:S(2)}, u32[]{:S(2)}) collective-permute-start(f32[256,128]{1,0:T(8,128)S(1)} %get-tuple-element.35), channel_id=1, source_target_pairs={{0,16},{1,17},{2,18},{3,19},{4,20},{5,21},{6,22},{7,23},{8,24},{9,... | collective-permute-start | bytes 393224 | tf_op jit(solution)/shard_map/ppermute | solution.py:66
  13.6 6.6 %collective-permute-start.3 = (f32[256,128]{1,0:T(8,128)S(1)}, f32[256,128]{1,0:T(8,128)S(1)}, u32[]{:S(2)}, u32[]{:S(2)}) collective-permute-start(f32[256,128]{1,0:T(8,128)S(1)} %get-tuple-element.36), channel_id=1, source_target_pairs={{0,24},{1,25},{2,26},{3,27},{4,28},{5,29},{6,30},{7,31},{8,16},{9,... | collective-permute-start | bytes 393224 | tf_op jit(solution)/shard_map/ppermute | solution.py:66
  20.2 4.8 %collective-permute-start.4 = (f32[112,128]{1,0:T(8,128)S(1)}, f32[112,128]{1,0:T(8,128)S(1)}, u32[]{:S(2)}, u32[]{:S(2)}) collective-permute-start(f32[112,128]{1,0:T(8,128)S(1)} %get-tuple-element.38), channel_id=1, source_target_pairs={{0,1},{1,0},{2,3},{3,2},{4,5},{5,4},{6,7},{7,6},{8,9},{9,8},{10,11... | collective-permute-start | bytes 172040 | tf_op jit(solution)/shard_map/ppermute | solution.py:66
  21.8 6.3 %collective-permute-start.5 = (f32[112,128]{1,0:T(8,128)S(1)}, f32[112,128]{1,0:T(8,128)S(1)}, u32[]{:S(2)}, u32[]{:S(2)}) collective-permute-start(f32[112,128]{1,0:T(8,128)S(1)} %get-tuple-element.39), channel_id=1, source_target_pairs={{0,2},{1,3},{2,0},{3,1},{4,6},{5,7},{6,4},{7,5},{8,10},{9,11},{10,... | collective-permute-start | bytes 172040 | tf_op jit(solution)/shard_map/ppermute | solution.py:66
  24.4 6.0 %collective-permute-start.6 = (f32[112,128]{1,0:T(8,128)S(1)}, f32[112,128]{1,0:T(8,128)S(1)}, u32[]{:S(2)}, u32[]{:S(2)}) collective-permute-start(f32[112,128]{1,0:T(8,128)S(1)} %get-tuple-element.40), channel_id=1, source_target_pairs={{0,3},{1,2},{2,1},{3,0},{4,7},{5,6},{6,5},{7,4},{8,11},{9,10},{10,... | collective-permute-start | bytes 172040 | tf_op jit(solution)/shard_map/ppermute | solution.py:66
  30.4 2.9 %collective-permute-start.7 = (f32[64,128]{1,0:T(8,128)S(1)}, f32[64,128]{1,0:T(8,128)S(1)}, u32[]{:S(2)}, u32[]{:S(2)}) collective-permute-start(f32[64,128]{1,0:T(8,128)S(1)} %get-tuple-element.41.mine_ref), channel_id=1, source_target_pairs={{0,4},{1,5},{2,6},{3,7},{4,0},{5,1},{6,2},{7,3},{8,12},{9,13},{10,... | collective-permute-start | bytes 98312 | tf_op jit(solution)/shard_map/ppermute | solution.py:66

commit v9 on v8

--- a/solution.py
+++ b/solution.py
@@ -53,8 +53,12 @@
         self.count = math.prod(size.values())
         stride = {"gx": size["gy"] * size["gz"], "gy": size["gz"], "gz": 1}
         self.core = stride["gy"]
-        spans = ((size["gx"], stride["gx"]), (size["gy"] // 2, 2 * stride["gy"]), (size["gz"], stride["gz"]))
-        self.groups = [[k * step for k in range(n)] for n, step in spans if n > 1]
+        spans = (
+            (range(size["gx"]), stride["gx"]),
+            (range(size["gy"] // 2), 2 * stride["gy"]),
+            ([0, *range(2, size["gz"]), 1], stride["gz"]),
+        )
+        self.groups = [[k * step for k in order] for order, step in spans if len(order) > 1]
         self.masks = [0]
         for group in self.groups:
             self.masks = [mask | bits for mask in self.masks for bits in group]
@@ -67,86 +71,68 @@
 
 
 def gather_kernel(
-    plan, step, sorted_here, where_ref, x_hbm, g_hbm, wr_hbm, wpt_hbm, we_hbm, rdp_hbm, wcat_hbm, *rest
+    plan, cuts, sorted_here, where_ref, x_hbm, g_hbm, wr_hbm, wpt_hbm, we_hbm, rdp_hbm, wcat_hbm, *rest
 ):
     if sorted_here:
         kept_ref, sent_ref, turned_ref, *rest = rest
     else:
         keep_ref, send_ref, turned_ref, *rest = rest
     x_ref, g_ref, rdp_ref, cat_ref, wpt_ref, we_ref, sums_ref, term_ref, small_sem, in_sem, out_sem = rest
-    rows = x_ref.shape[0]
     cr = we_ref.shape[1]
     nodes = wpt_ref.shape[0]
     wide = 2 * cr
-    count = rows // step
     move = pltpu.make_async_copy
     small = [
         move(wr_hbm, cat_ref.at[:, pl.ds(0, cr)], small_sem.at[0]),
         move(wpt_hbm, wpt_ref, small_sem.at[1]),
         move(we_hbm, we_ref, small_sem.at[2]),
     ]
-    load_cuts = sorted({0, min(1, count), min(2, count), count})
-    store_cuts = sorted({0, max(count - 2, 0), max(count - 1, 0), count})
-    span = lambda cuts, i: pl.ds(cuts[i] * step, (cuts[i + 1] - cuts[i]) * step)
-    loads = [
-        (
-            move(x_hbm.at[span(load_cuts, i)], x_ref.at[span(load_cuts, i)], in_sem.at[0, i]),
-            move(g_hbm.at[span(load_cuts, i)], g_ref.at[span(load_cuts, i)], in_sem.at[1, i]),
-        )
-        for i in range(len(load_cuts) - 1)
-    ]
-    stores = [
-        move(rdp_ref.at[span(store_cuts, i)], rdp_hbm.at[span(store_cuts, i)], out_sem.at[i])
-        for i in range(len(store_cuts) - 1)
-    ]
-    for copy in (*small, *loads[0]):
+    spans = [pl.ds(start, stop - start) for start, stop in zip(cuts, cuts[1:])]
+    x_loads = [move(x_hbm.at[c], x_ref.at[c], in_sem.at[0, i]) for i, c in enumerate(spans)]
+    g_loads = [move(g_hbm.at[c], g_ref.at[c], in_sem.at[1, i]) for i, c in enumerate(spans)]
+    stores = [move(rdp_ref.at[c], rdp_hbm.at[c], out_sem.at[i]) for i, c in enumerate(spans)]
+    for copy in (*small, x_loads[0], g_loads[0]):
         copy.start()
-    sums_ref[...] = jnp.zeros_like(sums_ref)
-    term_ref[...] = jnp.zeros_like(term_ref)
     small[0].wait()
     small[1].wait()
     padded = jnp.concatenate([wpt_ref[...], jnp.zeros_like(wpt_ref)], axis=0)
     cat_ref[:, cr:] = padded.T
     keep_weights = move(cat_ref, wcat_hbm, small_sem.at[3])
-    keep_weights.start()
     small[2].wait()
-
-    @pl.loop(0, count)
-    def _(i):
-        for k, pair in enumerate(loads):
-            @pl.when(i == load_cuts[k])
-            def _():
-                for copy in pair:
-                    copy.wait()
-                if k + 1 < len(loads):
-                    for copy in loads[k + 1]:
-                        copy.start()
-
-        c = pl.ds(pl.multiple_of(i * step, step), step)
-        x, g = x_ref[c], g_ref[c]
-        both = mxu(x, cat_ref[...]).astype(BF16)
-        mapped = mxu(g, we_ref[...]).astype(BF16)
+    for i, c in enumerate(spans):
+        x_loads[i].wait()
+        if i + 1 < len(spans):
+            x_loads[i + 1].start()
+        both = mxu(x_ref[c], cat_ref[...]).astype(BF16)
+        g_loads[i].wait()
+        if i + 1 < len(spans):
+            g_loads[i + 1].start()
+        mapped = mxu(g_ref[c], we_ref[...]).astype(BF16)
         rdp = jnp.concatenate([both[:, :cr], mapped, both[:, cr:]], axis=1)
         rdp_ref[c] = rdp
+        stores[i].start()
         turned = rdp.T
         proj = turned[wide : wide + nodes]
-        sums_ref[: wide + nodes] += mxu(turned[: wide + nodes], x)
-        sums_ref[wide + nodes :] += mxu(proj, g)
-        term = mxu(proj, rdp[:, :wide])
-        term_ref[0] += term[:, :cr]
-        term_ref[1] += term[:, cr:]
-        for k, copy in enumerate(stores):
-            pl.when(i == store_cuts[k + 1] - 1)(copy.start)
+        pieces = (
+            (sums_ref.at[: wide + nodes], mxu(turned[: wide + nodes], x_ref[c])),
+            (sums_ref.at[wide + nodes :], mxu(proj, g_ref[c])),
+            (term_ref, mxu(proj, rdp[:, :wide])),
+        )
+        for ref, piece in pieces:
+            ref[...] = piece if i == 0 else ref[...] + piece
+    keep_weights.start()
 
     me = where_ref[0]
     side = plan.side(me)
     turned_ref[...] = sums_ref[...].T
     if not sorted_here:
-        keep_ref[...] = term_ref[side]
-        send_ref[...] = term_ref[1 - side]
+        heads = (keep_ref, send_ref)
     else:
-        kept_ref[:nodes] = term_ref[side]
-        sent_ref[:nodes] = term_ref[1 - side]
+        heads = (kept_ref.at[:nodes], sent_ref.at[:nodes])
+    left, right = term_ref[:, :cr], term_ref[:, cr:]
+    heads[0][...] = jnp.where(side == 0, left, right)
+    heads[1][...] = jnp.where(side == 0, right, left)
+    if sorted_here:
         size = turned_ref.shape[0] // plan.count
         for base, out_ref in ((me, kept_ref), (me ^ plan.core, sent_ref)):
             to = nodes
@@ -163,7 +149,7 @@
 def gather(plan, where, x, g, wr, wpt, we):
     rows, chan = x.shape
     cr, nodes = wr.shape[1], wpt.shape[0]
-    step = row_block(rows)
+    cuts = sorted({0, rows // 6 // 16 * 16, rows // 2 // 16 * 16, rows})
     width = 2 * cr + 2 * nodes
     half = plan.count // 2
     size = chan // plan.count
@@ -187,13 +173,13 @@
         pltpu.VMEM(wpt.shape, BF16),
         pltpu.VMEM(we.shape, BF16),
         pltpu.VMEM((width, chan), F32),
-        pltpu.VMEM((2, nodes, cr), F32),
+        pltpu.VMEM((nodes, 2 * cr), F32),
         pltpu.SemaphoreType.DMA((4,)),
         pltpu.SemaphoreType.DMA((2, 3)),
         pltpu.SemaphoreType.DMA((3,)),
     ]
     rdp, wcat, kept, sent, *sums = pl.pallas_call(
-        functools.partial(gather_kernel, plan, step, sorted_here),
+        functools.partial(gather_kernel, plan, cuts, sorted_here),
         in_specs=[SMEM] + [HBM] * 5,
         out_specs=[spec for spec, _ in outs],
         out_shape=[shape for _, shape in outs],
@@ -211,8 +197,8 @@
     return rdp, wcat, kept, sent
 
 
-def step_kernel(head, ins, parts, *refs):
-    terms, outs = refs[:ins], refs[ins:]
+def step_kernel(head, ins, parts, after, *refs):
+    terms, outs = refs[:ins], refs[ins + after :]
 
     def total(start, size):
         value = terms[0][start : start + size]
@@ -232,18 +218,18 @@
         ref[head:] = total(head + k * size, size)
 
 
-def step(head, parts, terms):
+def step(head, parts, terms, after=()):
     rest, lanes = terms[0].shape[0] - head, terms[0].shape[1]
     shapes = (head, rest) if parts == 1 else (head + rest // parts,) * parts
     return pl.pallas_call(
-        functools.partial(step_kernel, head, len(terms), parts),
-        in_specs=[VMEM] * len(terms),
+        functools.partial(step_kernel, head, len(terms), parts, len(after)),
+        in_specs=[VMEM] * len(terms) + [pl.BlockSpec(memory_space=pl.ANY)] * len(after),
         out_specs=[VMEM] * len(shapes),
         out_shape=[pltpu.VMEM((size, lanes), F32) for size in shapes],
         compiler_params=params(SMALL_LIMIT),
         cost_estimate=cost(terms[0].size, 12 * terms[0].size),
         name="step",
-    )(*terms)
+    )(*terms, *after)
 
 
 def fetch_kernel(_, *refs):
@@ -378,7 +364,7 @@
         parts = step(head, len(group), terms)
         terms = [plan.swap(part, mask) if mask else part for part, mask in zip(parts, group)]
     ready = fetch(terms[1], adjacency, node_weight, wcat, rdp, flat_g)
-    mine, sums = step(head, 1, terms)
+    mine, sums = step(head, 1, terms, ready[:1])
     other = plan.swap(mine, plan.core)
 
     flat_out, grad_reduce, grad_project, grad_expand, grad_adjacency, grad_node = feature_grads(

time: 37.7 us -> 36.3 us (0.963)
  waiting for transfers between devices: 13.7 us -> 10.9 us
  Pallas kernels: 13.6 us -> 15.3 us
    ppermute x8, waiting for transfers between devices: 13.7 us -> 10.9 us  [swap(): return lax.ppermute(value, AXES, [(d, d ^ mask) for d in range(self.count)])]
    pallas_call x4, Pallas kernels: 6.65 us -> 8.37 us  [the longest x1 8.28 us: gather(): pl.pallas_call(functools.partial(gather_kernel, plan, cuts, sorted_here),...]
  transfers between devices with their start and end apart: 8 -> 8, of which waited for: 6 -> 7; matrix products, arithmetic and copies ran while one was open for 0% -> 0% of each run, Pallas kernels for 7% -> 8%
where the time goes in v9:
time: 36.3 us; the launch traced here: 36.1 us
  Pallas kernels  15.3 us (42%)
  waiting for transfers between devices  10.9 us (30%)
  starting transfers between devices  9.29 us (26%)
  between operations  0.68 us (2%)
    ppermute x8, waiting for transfers between devices, swap(): return lax.ppermute(value, AXES, [(d, d ^ mask) for d in range(self.count)])  10.9 us
    ppermute x8, starting transfers between devices, swap(): return lax.ppermute(value, AXES, [(d, d ^ mask) for d in range(self.count)])  9.29 us
    pallas_call x1, Pallas kernels, gather(): pl.pallas_call(functools.partial(gather_kernel, plan, cuts, sorted_here),...  8.28 us
    pallas_call x1, Pallas kernels, feature_grads(): pl.pallas_call(functools.partial(feature_kernel, step, scale, plan), in_s...  4.13 us
    pallas_call x1, Pallas kernels, fetch(): pl.pallas_call(fetch_kernel, in_specs=[pl.BlockSpec(memory_space=pl.ANY)]...  2.79 us
  transfers between devices with their start and end apart: 8, of which 7 were waited for; matrix products, arithmetic and copies ran while one was open for 0% of the time, Pallas kernels for 8%

profile of v9, /device:TPU:0, one launch (start us, length us, event | category | flops | bytes accessed | tf_op | source)
XLA Modules:
  0.0 36.1 jit_solution(1619587434931754725)
XLA Ops:
  0.6 8.3 %gather.1 = (bf16[3072,384]{1,0:T(8,128)(2,1)}, bf16[512,256]{1,0:T(8,128)(2,1)}, f32[832,128]{1,0:T(8,128)S(1)}, f32[832,128]{1,0:T(8,128)S(1)}) custom-call(s32[1]{0:T(128)} %bitcast.where_ref, bf16[3072,512]{1,0:T(8,128)(2,1)} %bitcast.13, bf16[3072,512]{1,0:T(8,128)(2,1)} %bitcast.11, bf16[512,128]{1,0:T(8,128)(2,1)} %wr_hbm.1, ...), custom_call_target="tpu_custom_call" | custom-call | flops 3221225472 | bytes 8650752 | tf_op jit(solution)/shard_map/gather/pallas_call | solution.py:181
  8.9 0.5 %collective-permute-start = (f32[832,128]{1,0:T(8,128)S(1)}, f32[832,128]{1,0:T(8,128)S(1)}, u32[]{:S(2)}, u32[]{:S(2)}) collective-permute-start(f32[832,128]{1,0:T(8,128)S(1)} %get-tuple-element.32), channel_id=1, source_target_pairs={{0,4},{1,5},{2,6},{3,7},{4,0},{5,1},{6,2},{7,3},{8,12},{9,13},{10,... | collective-permute-start | bytes 1277960 | tf_op jit(solution)/shard_map/ppermute | solution.py:70
  9.4 1.4 %collective-permute-done.refs_1_ = f32[832,128]{1,0:T(8,128)S(1)} collective-permute-done((f32[832,128]{1,0:T(8,128)S(1)}, f32[832,128]{1,0:T(8,128)S(1)}, u32[]{:S(2)}, u32[]{:S(2)}) %collective-permute-start) | collective-permute-done | bytes 426016 | tf_op jit(solution)/shard_map/ppermute | solution.py:70
  10.9 2.9 %collective-permute-start.1 = (f32[256,128]{1,0:T(8,128)S(1)}, f32[256,128]{1,0:T(8,128)S(1)}, u32[]{:S(2)}, u32[]{:S(2)}) collective-permute-start(f32[256,128]{1,0:T(8,128)S(1)} %get-tuple-element.34), channel_id=1, source_target_pairs={{0,8},{1,9},{2,10},{3,11},{4,12},{5,13},{6,14},{7,15},{8,0},{9,1},... | collective-permute-start | bytes 393224 | tf_op jit(solution)/shard_map/ppermute | solution.py:70
  13.8 1.5 %collective-permute-start.2 = (f32[256,128]{1,0:T(8,128)S(1)}, f32[256,128]{1,0:T(8,128)S(1)}, u32[]{:S(2)}, u32[]{:S(2)}) collective-permute-start(f32[256,128]{1,0:T(8,128)S(1)} %get-tuple-element.35), channel_id=1, source_target_pairs={{0,16},{1,17},{2,18},{3,19},{4,20},{5,21},{6,22},{7,23},{8,24},{9,... | collective-permute-start | bytes 393224 | tf_op jit(solution)/shard_map/ppermute | solution.py:70
  15.3 0.0 collective-permute-start.3
  15.4 2.4 %collective-permute-done.1.refs_1_ = f32[256,128]{1,0:T(8,128)S(1)} collective-permute-done((f32[256,128]{1,0:T(8,128)S(1)}, f32[256,128]{1,0:T(8,128)S(1)}, u32[]{:S(2)}, u32[]{:S(2)}) %collective-permute-start.1) | collective-permute-done | bytes 131104 | tf_op jit(solution)/shard_map/ppermute | solution.py:70
  17.7 4.2 %collective-permute-done.2.refs_2_ = f32[256,128]{1,0:T(8,128)S(1)} collective-permute-done((f32[256,128]{1,0:T(8,128)S(1)}, f32[256,128]{1,0:T(8,128)S(1)}, u32[]{:S(2)}, u32[]{:S(2)}) %collective-permute-start.2) | collective-permute-done | bytes 131104 | tf_op jit(solution)/shard_map/ppermute | solution.py:70
  21.9 0.0 collective-permute-done.3.refs_3_
  21.9 2.7 %collective-permute-start.4 = (f32[112,128]{1,0:T(8,128)S(1)}, f32[112,128]{1,0:T(8,128)S(1)}, u32[]{:S(2)}, u32[]{:S(2)}) collective-permute-start(f32[112,128]{1,0:T(8,128)S(1)} %get-tuple-element.38), channel_id=1, source_target_pairs={{0,2},{1,3},{2,0},{3,1},{4,6},{5,7},{6,4},{7,5},{8,10},{9,11},{10,... | collective-permute-start | bytes 172040 | tf_op jit(solution)/shard_map/ppermute | solution.py:70
  24.6 1.3 %collective-permute-start.5 = (f32[112,128]{1,0:T(8,128)S(1)}, f32[112,128]{1,0:T(8,128)S(1)}, u32[]{:S(2)}, u32[]{:S(2)}) collective-permute-start(f32[112,128]{1,0:T(8,128)S(1)} %get-tuple-element.39), channel_id=1, source_target_pairs={{0,3},{1,2},{2,1},{3,0},{4,7},{5,6},{6,5},{7,4},{8,11},{9,10},{10,... | collective-permute-start | bytes 172040 | tf_op jit(solution)/shard_map/ppermute | solution.py:70
  25.9 0.2 collective-permute-start.6
  26.2 1.2 %collective-permute-done.4._.refs_1_ = f32[112,128]{1,0:T(8,128)S(1)} collective-permute-done((f32[112,128]{1,0:T(8,128)S(1)}, f32[112,128]{1,0:T(8,128)S(1)}, u32[]{:S(2)}, u32[]{:S(2)}) %collective-permute-start.4) | collective-permute-done | bytes 57376 | tf_op jit(solution)/shard_map/ppermute | solution.py:70
  27.4 2.8 %fetch.1 = (f32[64,64]{1,0:T(8,128)S(1)}, f32[128,128]{1,0:T(8,128)S(1)}, bf16[512,256]{1,0:T(8,128)(2,1)S(1)}, bf16[3072,384]{1,0:T(8,128)(2,1)S(1)}, bf16[3072,512]{1,0:T(8,128)(2,1)S(1)}) custom-call(f32[112,128]{1,0:T(8,128)S(1)} %collective-permute-done.4._.refs_1_, f32[64,64]{1,0:T(8,128)} %refs_0_.1, f32[128,128]{1,0:T(8,128)} %refs_1_.1, ...), custom_call_target="tpu_custom_call" | custom-call | bytes 5849088 | tf_op jit(solution)/shard_map/fetch/pallas_call | solution.py:249
  30.2 0.5 %collective-permute-done.5.refs_2_ = f32[112,128]{1,0:T(8,128)S(1)} collective-permute-done((f32[112,128]{1,0:T(8,128)S(1)}, f32[112,128]{1,0:T(8,128)S(1)}, u32[]{:S(2)}, u32[]{:S(2)}) %collective-permute-start.5) | collective-permute-done | bytes 57376 | tf_op jit(solution)/shard_map/ppermute | solution.py:70
  30.7 0.1 collective-permute-done.6.refs_3_
  30.7 0.1 collective-permute-start.7
  30.8 1.2 %collective-permute-done.7.other_ref = f32[64,128]{1,0:T(8,128)S(1)} collective-permute-done((f32[64,128]{1,0:T(8,128)S(1)}, f32[64,128]{1,0:T(8,128)S(1)}, u32[]{:S(2)}, u32[]{:S(2)}) %collective-permute-start.7) | collective-permute-done | bytes 32800 | tf_op jit(solution)/shard_map/ppermute | solution.py:70
  32.0 4.1 %feature_grads.1 = (bf16[3072,512]{1,0:T(8,128)(2,1)}, f32[16,128]{1,0:T(8,128)}, f32[16,64]{1,0:T(8,128)}, f32[16,128]{1,0:T(8,128)}, f32[64,64]{1,0:T(8,128)}, /*index=5*/f32[128,128]{1,0:T(8,128)}) custom-call(s32[1]{0:T(128)} %bitcast.where_ref, f32[64,128]{1,0:T(8,128)S(1)} %get-tuple-element.44.mine_ref, ...), custom_call_target="tpu_custom_call" | custom-call | flops 1610612736 | bytes 8650752 | tf_op jit(solution)/shard_map/feature_grads/pallas_call | solution.py:323
  (3 shorter events, 0.1 us)
Async XLA Ops:
  8.9 1.9 %collective-permute-start = (f32[832,128]{1,0:T(8,128)S(1)}, f32[832,128]{1,0:T(8,128)S(1)}, u32[]{:S(2)}, u32[]{:S(2)}) collective-permute-start(f32[832,128]{1,0:T(8,128)S(1)} %get-tuple-element.32), channel_id=1, source_target_pairs={{0,4},{1,5},{2,6},{3,7},{4,0},{5,1},{6,2},{7,3},{8,12},{9,13},{10,... | collective-permute-start | bytes 1277960 | tf_op jit(solution)/shard_map/ppermute | solution.py:70
  10.9 6.8 %collective-permute-start.1 = (f32[256,128]{1,0:T(8,128)S(1)}, f32[256,128]{1,0:T(8,128)S(1)}, u32[]{:S(2)}, u32[]{:S(2)}) collective-permute-start(f32[256,128]{1,0:T(8,128)S(1)} %get-tuple-element.34), channel_id=1, source_target_pairs={{0,8},{1,9},{2,10},{3,11},{4,12},{5,13},{6,14},{7,15},{8,0},{9,1},... | collective-permute-start | bytes 393224 | tf_op jit(solution)/shard_map/ppermute | solution.py:70
  13.8 8.1 %collective-permute-start.2 = (f32[256,128]{1,0:T(8,128)S(1)}, f32[256,128]{1,0:T(8,128)S(1)}, u32[]{:S(2)}, u32[]{:S(2)}) collective-permute-start(f32[256,128]{1,0:T(8,128)S(1)} %get-tuple-element.35), channel_id=1, source_target_pairs={{0,16},{1,17},{2,18},{3,19},{4,20},{5,21},{6,22},{7,23},{8,24},{9,... | collective-permute-start | bytes 393224 | tf_op jit(solution)/shard_map/ppermute | solution.py:70
  15.3 6.6 %collective-permute-start.3 = (f32[256,128]{1,0:T(8,128)S(1)}, f32[256,128]{1,0:T(8,128)S(1)}, u32[]{:S(2)}, u32[]{:S(2)}) collective-permute-start(f32[256,128]{1,0:T(8,128)S(1)} %get-tuple-element.36), channel_id=1, source_target_pairs={{0,24},{1,25},{2,26},{3,27},{4,28},{5,29},{6,30},{7,31},{8,16},{9,... | collective-permute-start | bytes 393224 | tf_op jit(solution)/shard_map/ppermute | solution.py:70
  21.9 5.4 %collective-permute-start.4 = (f32[112,128]{1,0:T(8,128)S(1)}, f32[112,128]{1,0:T(8,128)S(1)}, u32[]{:S(2)}, u32[]{:S(2)}) collective-permute-start(f32[112,128]{1,0:T(8,128)S(1)} %get-tuple-element.38), channel_id=1, source_target_pairs={{0,2},{1,3},{2,0},{3,1},{4,6},{5,7},{6,4},{7,5},{8,10},{9,11},{10,... | collective-permute-start | bytes 172040 | tf_op jit(solution)/shard_map/ppermute | solution.py:70
  24.6 6.1 %collective-permute-start.5 = (f32[112,128]{1,0:T(8,128)S(1)}, f32[112,128]{1,0:T(8,128)S(1)}, u32[]{:S(2)}, u32[]{:S(2)}) collective-permute-start(f32[112,128]{1,0:T(8,128)S(1)} %get-tuple-element.39), channel_id=1, source_target_pairs={{0,3},{1,2},{2,1},{3,0},{4,7},{5,6},{6,5},{7,4},{8,11},{9,10},{10,... | collective-permute-start | bytes 172040 | tf_op jit(solution)/shard_map/ppermute | solution.py:70
  25.9 4.8 %collective-permute-start.6 = (f32[112,128]{1,0:T(8,128)S(1)}, f32[112,128]{1,0:T(8,128)S(1)}, u32[]{:S(2)}, u32[]{:S(2)}) collective-permute-start(f32[112,128]{1,0:T(8,128)S(1)} %get-tuple-element.40), channel_id=1, source_target_pairs={{0,1},{1,0},{2,3},{3,2},{4,5},{5,4},{6,7},{7,6},{8,9},{9,8},{10,11... | collective-permute-start | bytes 172040 | tf_op jit(solution)/shard_map/ppermute | solution.py:70
  30.7 1.3 %collective-permute-start.7 = (f32[64,128]{1,0:T(8,128)S(1)}, f32[64,128]{1,0:T(8,128)S(1)}, u32[]{:S(2)}, u32[]{:S(2)}) collective-permute-start(f32[64,128]{1,0:T(8,128)S(1)} %get-tuple-element.44.mine_ref), channel_id=1, source_target_pairs={{0,4},{1,5},{2,6},{3,7},{4,0},{5,1},{6,2},{7,3},{8,12},{9,13},{10,... | collective-permute-start | bytes 98312 | tf_op jit(solution)/shard_map/ppermute | solution.py:70

commit v10 on v8

--- a/solution.py
+++ b/solution.py
@@ -40,9 +40,9 @@
     return [pltpu.with_memory_space_constraint(value, pltpu.HBM) for value in values]
 
 
-def row_block(total):
+def row_block(total, largest):
     for size in (1024, 768, 512, 384, 256, 128, 64, 32, 16):
-        if total % size == 0:
+        if size <= largest and total % size == 0:
             return size
     return total
 
@@ -53,8 +53,12 @@
         self.count = math.prod(size.values())
         stride = {"gx": size["gy"] * size["gz"], "gy": size["gz"], "gz": 1}
         self.core = stride["gy"]
-        spans = ((size["gx"], stride["gx"]), (size["gy"] // 2, 2 * stride["gy"]), (size["gz"], stride["gz"]))
-        self.groups = [[k * step for k in range(n)] for n, step in spans if n > 1]
+        spans = (
+            ([0, *sorted(range(1, size["gx"]), key=lambda k: -k.bit_count())], stride["gx"]),
+            (range(size["gy"] // 2), 2 * stride["gy"]),
+            ([0, *range(2, size["gz"]), 1], stride["gz"]),
+        )
+        self.groups = [[k * step for k in order] for order, step in spans if len(order) > 1]
         self.masks = [0]
         for group in self.groups:
             self.masks = [mask | bits for mask in self.masks for bits in group]
@@ -132,9 +136,7 @@
         proj = turned[wide : wide + nodes]
         sums_ref[: wide + nodes] += mxu(turned[: wide + nodes], x)
         sums_ref[wide + nodes :] += mxu(proj, g)
-        term = mxu(proj, rdp[:, :wide])
-        term_ref[0] += term[:, :cr]
-        term_ref[1] += term[:, cr:]
+        term_ref[...] += mxu(proj, rdp[:, :wide])
         for k, copy in enumerate(stores):
             pl.when(i == store_cuts[k + 1] - 1)(copy.start)
 
@@ -142,11 +144,13 @@
     side = plan.side(me)
     turned_ref[...] = sums_ref[...].T
     if not sorted_here:
-        keep_ref[...] = term_ref[side]
-        send_ref[...] = term_ref[1 - side]
+        heads = (keep_ref, send_ref)
     else:
-        kept_ref[:nodes] = term_ref[side]
-        sent_ref[:nodes] = term_ref[1 - side]
+        heads = (kept_ref.at[:nodes], sent_ref.at[:nodes])
+    left, right = term_ref[:, :cr], term_ref[:, cr:]
+    heads[0][...] = jnp.where(side == 0, left, right)
+    heads[1][...] = jnp.where(side == 0, right, left)
+    if sorted_here:
         size = turned_ref.shape[0] // plan.count
         for base, out_ref in ((me, kept_ref), (me ^ plan.core, sent_ref)):
             to = nodes
@@ -163,7 +167,7 @@
 def gather(plan, where, x, g, wr, wpt, we):
     rows, chan = x.shape
     cr, nodes = wr.shape[1], wpt.shape[0]
-    step = row_block(rows)
+    step = row_block(rows, 1024)
     width = 2 * cr + 2 * nodes
     half = plan.count // 2
     size = chan // plan.count
@@ -187,7 +191,7 @@
         pltpu.VMEM(wpt.shape, BF16),
         pltpu.VMEM(we.shape, BF16),
         pltpu.VMEM((width, chan), F32),
-        pltpu.VMEM((2, nodes, cr), F32),
+        pltpu.VMEM((nodes, 2 * cr), F32),
         pltpu.SemaphoreType.DMA((4,)),
         pltpu.SemaphoreType.DMA((2, 3)),
         pltpu.SemaphoreType.DMA((3,)),
@@ -211,8 +215,8 @@
     return rdp, wcat, kept, sent
 
 
-def step_kernel(head, ins, parts, *refs):
-    terms, outs = refs[:ins], refs[ins:]
+def step_kernel(head, ins, parts, after, *refs):
+    terms, outs = refs[:ins], refs[ins + after :]
 
     def total(start, size):
         value = terms[0][start : start + size]
@@ -232,18 +236,18 @@
         ref[head:] = total(head + k * size, size)
 
 
-def step(head, parts, terms):
+def step(head, parts, terms, after=()):
     rest, lanes = terms[0].shape[0] - head, terms[0].shape[1]
     shapes = (head, rest) if parts == 1 else (head + rest // parts,) * parts
     return pl.pallas_call(
-        functools.partial(step_kernel, head, len(terms), parts),
-        in_specs=[VMEM] * len(terms),
+        functools.partial(step_kernel, head, len(terms), parts, len(after)),
+        in_specs=[VMEM] * len(terms) + [pl.BlockSpec(memory_space=pl.ANY)] * len(after),
         out_specs=[VMEM] * len(shapes),
         out_shape=[pltpu.VMEM((size, lanes), F32) for size in shapes],
         compiler_params=params(SMALL_LIMIT),
         cost_estimate=cost(terms[0].size, 12 * terms[0].size),
         name="step",
-    )(*terms)
+    )(*terms, *after)
 
 
 def fetch_kernel(_, *refs):
@@ -300,9 +304,14 @@
     mix_ref[cr:, :cr] = blank
     mix_ref[:cr, cr:] = blank
     mix_ref[cr:, cr:] = jnp.concatenate([no_f, zero], axis=0).T.astype(BF16)
-    copies = []
-    for i, start in enumerate(range(0, rows, step)):
-        c = pl.ds(start, step)
+    def store(i, at):
+        c = pl.ds(at, step)
+        return pltpu.make_async_copy(out_ref.at[c], out_hbm.at[c], out_sem.at[i])
+
+    @pl.loop(0, rows // step)
+    def _(i):
+        at = pl.multiple_of(i * step, step)
+        c = pl.ds(at, step)
         rdp = rdp_ref[c]
         mixed = mxu(rdp[:, :wide], mix_ref[...])
         d_proj = (mixed[:, cr:] + scale * mixed[:, :cr]).astype(BF16)
@@ -310,8 +319,8 @@
         both = jnp.concatenate([d_red, d_proj], axis=1)
         out = g_ref[c].astype(F32) + mxu(both, wcat_ref[...], ((1,), (1,)))
         out_ref[c] = out.astype(BF16)
-        copies.append(pltpu.make_async_copy(out_ref.at[c], out_hbm.at[c], out_sem.at[i]))
-        copies[-1].start()
+        store(i, at).start()
+
     gn_ref[...] = scale * exact(hidden, d_pre, ((0,), (0,)))
     ga_ref[...] = -scale * exact(d_hidden, nodes, ((1,), (1,)))
     size = gr_ref.shape[0]
@@ -321,14 +330,14 @@
         x_red, dn_f, ((1,), (1,))
     )
     ge_ref[...] = scale * exact(with_proj[:, nodes_n:], no_f)
-    for copy in copies:
-        copy.wait()
+    for i in range(rows // step):
+        store(i, i * step).wait()
 
 
 def feature_grads(plan, where, mine, other, sums, adjacency, node_weight, wcat, rdp, g, scale):
     rows, chan = g.shape
     nodes, cr = adjacency.shape[0], node_weight.shape[0]
-    step = row_block(rows // 2)
+    step = row_block(rows, 512)
     size = chan // plan.count
     there = [
         pltpu.with_memory_space_constraint(value, pltpu.VMEM)
@@ -374,10 +383,11 @@
     )
     head = adjacency.shape[0]
     terms = [kept, plan.swap(sent, plan.core)]
+    ready = None
     for group in plan.groups:
-        parts = step(head, len(group), terms)
+        parts = step(head, len(group), terms, ready[:1] if ready else ())
         terms = [plan.swap(part, mask) if mask else part for part, mask in zip(parts, group)]
-    ready = fetch(terms[1], adjacency, node_weight, wcat, rdp, flat_g)
+        ready = ready or fetch(terms[1], adjacency, node_weight, wcat, rdp, flat_g)
     mine, sums = step(head, 1, terms)
     other = plan.swap(mine, plan.core)
 

time: 37.7 us -> 36.2 us (0.960)
  waiting for transfers between devices: 13.7 us -> 10.8 us
  Pallas kernels: 13.6 us -> 14.6 us
    ppermute x8, waiting for transfers between devices: 13.7 us -> 10.8 us  [swap(): return lax.ppermute(value, AXES, [(d, d ^ mask) for d in range(self.count)])]
    pallas_call x1, Pallas kernels: 4.13 us -> 5.17 us  [feature_grads(): pl.pallas_call(functools.partial(feature_kernel, step, scale, plan), in_s...]
  transfers between devices with their start and end apart: 8 -> 8, of which waited for: 6 -> 6; matrix products, arithmetic and copies ran while one was open for 0% -> 0% of each run, Pallas kernels for 7% -> 8%
where the time goes in v10:
time: 36.2 us; the launch traced here: 36 us
  Pallas kernels  14.6 us (40%)
  waiting for transfers between devices  10.8 us (30%)
  starting transfers between devices  9.85 us (27%)
  between operations  0.7 us (2%)
    ppermute x8, waiting for transfers between devices, swap(): return lax.ppermute(value, AXES, [(d, d ^ mask) for d in range(self.count)])  10.8 us
    ppermute x8, starting transfers between devices, swap(): return lax.ppermute(value, AXES, [(d, d ^ mask) for d in range(self.count)])  9.85 us
    pallas_call x1, Pallas kernels, gather(): pl.pallas_call(functools.partial(gather_kernel, plan, step, sorted_here),...  6.56 us
    pallas_call x1, Pallas kernels, feature_grads(): pl.pallas_call(functools.partial(feature_kernel, step, scale, plan), in_s...  5.17 us
    pallas_call x1, Pallas kernels, fetch(): pl.pallas_call(fetch_kernel, in_specs=[pl.BlockSpec(memory_space=pl.ANY)]...  2.79 us
  transfers between devices with their start and end apart: 8, of which 6 were waited for; matrix products, arithmetic and copies ran while one was open for 0% of the time, Pallas kernels for 8%

profile of v10, /device:TPU:0, one launch (start us, length us, event | category | flops | bytes accessed | tf_op | source)
XLA Modules:
  0.0 36.0 jit_solution(1197469948083715526)
XLA Ops:
  0.6 6.6 %gather.1 = (bf16[3072,384]{1,0:T(8,128)(2,1)}, bf16[512,256]{1,0:T(8,128)(2,1)}, f32[832,128]{1,0:T(8,128)S(1)}, f32[832,128]{1,0:T(8,128)S(1)}) custom-call(s32[1]{0:T(128)} %bitcast.where_ref, bf16[3072,512]{1,0:T(8,128)(2,1)} %bitcast.13, bf16[3072,512]{1,0:T(8,128)(2,1)} %bitcast.11, bf16[512,128]{1,0:T(8,128)(2,1)} %wr_hbm.1, ...), custom_call_target="tpu_custom_call" | custom-call | flops 3221225472 | bytes 8650752 | tf_op jit(solution)/shard_map/gather/pallas_call | solution.py:199
  7.2 0.5 %collective-permute-start = (f32[832,128]{1,0:T(8,128)S(1)}, f32[832,128]{1,0:T(8,128)S(1)}, u32[]{:S(2)}, u32[]{:S(2)}) collective-permute-start(f32[832,128]{1,0:T(8,128)S(1)} %get-tuple-element.32), channel_id=1, source_target_pairs={{0,4},{1,5},{2,6},{3,7},{4,0},{5,1},{6,2},{7,3},{8,12},{9,13},{10,... | collective-permute-start | bytes 1277960 | tf_op jit(solution)/shard_map/ppermute | solution.py:70
  7.7 1.4 %collective-permute-done.refs_1_ = f32[832,128]{1,0:T(8,128)S(1)} collective-permute-done((f32[832,128]{1,0:T(8,128)S(1)}, f32[832,128]{1,0:T(8,128)S(1)}, u32[]{:S(2)}, u32[]{:S(2)}) %collective-permute-start) | collective-permute-done | bytes 426016 | tf_op jit(solution)/shard_map/ppermute | solution.py:70
  9.2 3.9 %collective-permute-start.1 = (f32[256,128]{1,0:T(8,128)S(1)}, f32[256,128]{1,0:T(8,128)S(1)}, u32[]{:S(2)}, u32[]{:S(2)}) collective-permute-start(f32[256,128]{1,0:T(8,128)S(1)} %get-tuple-element.34), channel_id=1, source_target_pairs={{0,24},{1,25},{2,26},{3,27},{4,28},{5,29},{6,30},{7,31},{8,16},{9,... | collective-permute-start | bytes 393224 | tf_op jit(solution)/shard_map/ppermute | solution.py:70
  13.1 0.5 %collective-permute-start.2 = (f32[256,128]{1,0:T(8,128)S(1)}, f32[256,128]{1,0:T(8,128)S(1)}, u32[]{:S(2)}, u32[]{:S(2)}) collective-permute-start(f32[256,128]{1,0:T(8,128)S(1)} %get-tuple-element.35), channel_id=1, source_target_pairs={{0,8},{1,9},{2,10},{3,11},{4,12},{5,13},{6,14},{7,15},{8,0},{9,1},... | collective-permute-start | bytes 393224 | tf_op jit(solution)/shard_map/ppermute | solution.py:70
  13.6 0.1 collective-permute-start.3
  13.7 3.6 %collective-permute-done.1._.refs_1_ = f32[256,128]{1,0:T(8,128)S(1)} collective-permute-done((f32[256,128]{1,0:T(8,128)S(1)}, f32[256,128]{1,0:T(8,128)S(1)}, u32[]{:S(2)}, u32[]{:S(2)}) %collective-permute-start.1) | collective-permute-done | bytes 131104 | tf_op jit(solution)/shard_map/ppermute | solution.py:70
  17.3 2.8 %fetch.1 = (f32[64,64]{1,0:T(8,128)S(1)}, f32[128,128]{1,0:T(8,128)S(1)}, bf16[512,256]{1,0:T(8,128)(2,1)S(1)}, bf16[3072,384]{1,0:T(8,128)(2,1)S(1)}, bf16[3072,512]{1,0:T(8,128)(2,1)S(1)}) custom-call(f32[256,128]{1,0:T(8,128)S(1)} %collective-permute-done.1._.refs_1_, f32[64,64]{1,0:T(8,128)} %refs_0_.1, f32[128,128]{1,0:T(8,128)} %refs_1_.1, ...), custom_call_target="tpu_custom_call" | custom-call | bytes 5849088 | tf_op jit(solution)/shard_map/fetch/pallas_call | solution.py:267
  20.1 0.0 collective-permute-done.2.refs_2_
  20.1 0.0 collective-permute-done.3.refs_3_
  20.2 3.2 %collective-permute-start.4 = (f32[112,128]{1,0:T(8,128)S(1)}, f32[112,128]{1,0:T(8,128)S(1)}, u32[]{:S(2)}, u32[]{:S(2)}) collective-permute-start(f32[112,128]{1,0:T(8,128)S(1)} %get-tuple-element.41), channel_id=1, source_target_pairs={{0,2},{1,3},{2,0},{3,1},{4,6},{5,7},{6,4},{7,5},{8,10},{9,11},{10,... | collective-permute-start | bytes 172040 | tf_op jit(solution)/shard_map/ppermute | solution.py:70
  23.4 1.3 %collective-permute-start.5 = (f32[112,128]{1,0:T(8,128)S(1)}, f32[112,128]{1,0:T(8,128)S(1)}, u32[]{:S(2)}, u32[]{:S(2)}) collective-permute-start(f32[112,128]{1,0:T(8,128)S(1)} %get-tuple-element.42), channel_id=1, source_target_pairs={{0,3},{1,2},{2,1},{3,0},{4,7},{5,6},{6,5},{7,4},{8,11},{9,10},{10,... | collective-permute-start | bytes 172040 | tf_op jit(solution)/shard_map/ppermute | solution.py:70
  24.7 0.2 collective-permute-start.6
  24.9 0.7 %collective-permute-done.4.refs_1_ = f32[112,128]{1,0:T(8,128)S(1)} collective-permute-done((f32[112,128]{1,0:T(8,128)S(1)}, f32[112,128]{1,0:T(8,128)S(1)}, u32[]{:S(2)}, u32[]{:S(2)}) %collective-permute-start.4) | collective-permute-done | bytes 57376 | tf_op jit(solution)/shard_map/ppermute | solution.py:70
  25.6 3.8 %collective-permute-done.5.refs_2_ = f32[112,128]{1,0:T(8,128)S(1)} collective-permute-done((f32[112,128]{1,0:T(8,128)S(1)}, f32[112,128]{1,0:T(8,128)S(1)}, u32[]{:S(2)}, u32[]{:S(2)}) %collective-permute-start.5) | collective-permute-done | bytes 57376 | tf_op jit(solution)/shard_map/ppermute | solution.py:70
  29.4 0.1 collective-permute-done.6.refs_3_
  29.5 0.1 collective-permute-start.7
  29.6 1.2 %collective-permute-done.7.other_ref = f32[64,128]{1,0:T(8,128)S(1)} collective-permute-done((f32[64,128]{1,0:T(8,128)S(1)}, f32[64,128]{1,0:T(8,128)S(1)}, u32[]{:S(2)}, u32[]{:S(2)}) %collective-permute-start.7) | collective-permute-done | bytes 32800 | tf_op jit(solution)/shard_map/ppermute | solution.py:70
  30.8 5.2 %feature_grads.1 = (bf16[3072,512]{1,0:T(8,128)(2,1)}, f32[16,128]{1,0:T(8,128)}, f32[16,64]{1,0:T(8,128)}, f32[16,128]{1,0:T(8,128)}, f32[64,64]{1,0:T(8,128)}, /*index=5*/f32[128,128]{1,0:T(8,128)}) custom-call(s32[1]{0:T(128)} %bitcast.where_ref, f32[64,128]{1,0:T(8,128)S(1)} %get-tuple-element.44.mine_ref, ...), custom_call_target="tpu_custom_call" | custom-call | flops 1610612736 | bytes 8650752 | tf_op jit(solution)/shard_map/feature_grads/pallas_call | solution.py:346
  (3 shorter events, 0.1 us)
Async XLA Ops:
  7.2 1.9 %collective-permute-start = (f32[832,128]{1,0:T(8,128)S(1)}, f32[832,128]{1,0:T(8,128)S(1)}, u32[]{:S(2)}, u32[]{:S(2)}) collective-permute-start(f32[832,128]{1,0:T(8,128)S(1)} %get-tuple-element.32), channel_id=1, source_target_pairs={{0,4},{1,5},{2,6},{3,7},{4,0},{5,1},{6,2},{7,3},{8,12},{9,13},{10,... | collective-permute-start | bytes 1277960 | tf_op jit(solution)/shard_map/ppermute | solution.py:70
  9.2 8.2 %collective-permute-start.1 = (f32[256,128]{1,0:T(8,128)S(1)}, f32[256,128]{1,0:T(8,128)S(1)}, u32[]{:S(2)}, u32[]{:S(2)}) collective-permute-start(f32[256,128]{1,0:T(8,128)S(1)} %get-tuple-element.34), channel_id=1, source_target_pairs={{0,24},{1,25},{2,26},{3,27},{4,28},{5,29},{6,30},{7,31},{8,16},{9,... | collective-permute-start | bytes 393224 | tf_op jit(solution)/shard_map/ppermute | solution.py:70
  13.1 7.1 %collective-permute-start.2 = (f32[256,128]{1,0:T(8,128)S(1)}, f32[256,128]{1,0:T(8,128)S(1)}, u32[]{:S(2)}, u32[]{:S(2)}) collective-permute-start(f32[256,128]{1,0:T(8,128)S(1)} %get-tuple-element.35), channel_id=1, source_target_pairs={{0,8},{1,9},{2,10},{3,11},{4,12},{5,13},{6,14},{7,15},{8,0},{9,1},... | collective-permute-start | bytes 393224 | tf_op jit(solution)/shard_map/ppermute | solution.py:70
  13.6 6.6 %collective-permute-start.3 = (f32[256,128]{1,0:T(8,128)S(1)}, f32[256,128]{1,0:T(8,128)S(1)}, u32[]{:S(2)}, u32[]{:S(2)}) collective-permute-start(f32[256,128]{1,0:T(8,128)S(1)} %get-tuple-element.36), channel_id=1, source_target_pairs={{0,16},{1,17},{2,18},{3,19},{4,20},{5,21},{6,22},{7,23},{8,24},{9,... | collective-permute-start | bytes 393224 | tf_op jit(solution)/shard_map/ppermute | solution.py:70
  20.2 5.4 %collective-permute-start.4 = (f32[112,128]{1,0:T(8,128)S(1)}, f32[112,128]{1,0:T(8,128)S(1)}, u32[]{:S(2)}, u32[]{:S(2)}) collective-permute-start(f32[112,128]{1,0:T(8,128)S(1)} %get-tuple-element.41), channel_id=1, source_target_pairs={{0,2},{1,3},{2,0},{3,1},{4,6},{5,7},{6,4},{7,5},{8,10},{9,11},{10,... | collective-permute-start | bytes 172040 | tf_op jit(solution)/shard_map/ppermute | solution.py:70
  23.4 6.1 %collective-permute-start.5 = (f32[112,128]{1,0:T(8,128)S(1)}, f32[112,128]{1,0:T(8,128)S(1)}, u32[]{:S(2)}, u32[]{:S(2)}) collective-permute-start(f32[112,128]{1,0:T(8,128)S(1)} %get-tuple-element.42), channel_id=1, source_target_pairs={{0,3},{1,2},{2,1},{3,0},{4,7},{5,6},{6,5},{7,4},{8,11},{9,10},{10,... | collective-permute-start | bytes 172040 | tf_op jit(solution)/shard_map/ppermute | solution.py:70
  24.7 4.8 %collective-permute-start.6 = (f32[112,128]{1,0:T(8,128)S(1)}, f32[112,128]{1,0:T(8,128)S(1)}, u32[]{:S(2)}, u32[]{:S(2)}) collective-permute-start(f32[112,128]{1,0:T(8,128)S(1)} %get-tuple-element.43), channel_id=1, source_target_pairs={{0,1},{1,0},{2,3},{3,2},{4,5},{5,4},{6,7},{7,6},{8,9},{9,8},{10,11... | collective-permute-start | bytes 172040 | tf_op jit(solution)/shard_map/ppermute | solution.py:70
  29.5 1.3 %collective-permute-start.7 = (f32[64,128]{1,0:T(8,128)S(1)}, f32[64,128]{1,0:T(8,128)S(1)}, u32[]{:S(2)}, u32[]{:S(2)}) collective-permute-start(f32[64,128]{1,0:T(8,128)S(1)} %get-tuple-element.44.mine_ref), channel_id=1, source_target_pairs={{0,4},{1,5},{2,6},{3,7},{4,0},{5,1},{6,2},{7,3},{8,12},{9,13},{10,... | collective-permute-start | bytes 98312 | tf_op jit(solution)/shard_map/ppermute | solution.py:70

commit v11 on v10

--- a/solution.py
+++ b/solution.py
@@ -41,7 +41,7 @@
 
 
 def row_block(total, largest):
-    for size in (1024, 768, 512, 384, 256, 128, 64, 32, 16):
+    for size in (1536, 1024, 768, 512, 384, 256, 128, 64, 32, 16):
         if size <= largest and total % size == 0:
             return size
     return total
@@ -167,7 +167,7 @@
 def gather(plan, where, x, g, wr, wpt, we):
     rows, chan = x.shape
     cr, nodes = wr.shape[1], wpt.shape[0]
-    step = row_block(rows, 1024)
+    step = row_block(rows, 1536)
     width = 2 * cr + 2 * nodes
     half = plan.count // 2
     size = chan // plan.count
@@ -277,11 +277,10 @@
 
 
 def feature_kernel(
-    step, scale, plan, where_ref, mine_ref, other_ref, sums_ref, adj_ref, nw_ref, wcat_ref, rdp_ref, g_ref,
+    cuts, scale, plan, where_ref, mine_ref, other_ref, sums_ref, adj_ref, nw_ref, wcat_ref, rdp_ref, g_ref,
     out_hbm, gr_ref, gp_ref, ge_ref, ga_ref, gn_ref, out_ref, mix_ref, dnb_ref, out_sem,
 ):
     nodes_n, cr = mine_ref.shape
-    rows = g_ref.shape[0]
     wide = 2 * cr
     first = plan.side(where_ref[0]) == 0
     mine, other = mine_ref[...], other_ref[...]
@@ -304,14 +303,9 @@
     mix_ref[cr:, :cr] = blank
     mix_ref[:cr, cr:] = blank
     mix_ref[cr:, cr:] = jnp.concatenate([no_f, zero], axis=0).T.astype(BF16)
-    def store(i, at):
-        c = pl.ds(at, step)
-        return pltpu.make_async_copy(out_ref.at[c], out_hbm.at[c], out_sem.at[i])
-
-    @pl.loop(0, rows // step)
-    def _(i):
-        at = pl.multiple_of(i * step, step)
-        c = pl.ds(at, step)
+    copies = []
+    for i, (start, stop) in enumerate(zip(cuts, cuts[1:])):
+        c = pl.ds(start, stop - start)
         rdp = rdp_ref[c]
         mixed = mxu(rdp[:, :wide], mix_ref[...])
         d_proj = (mixed[:, cr:] + scale * mixed[:, :cr]).astype(BF16)
@@ -319,8 +313,8 @@
         both = jnp.concatenate([d_red, d_proj], axis=1)
         out = g_ref[c].astype(F32) + mxu(both, wcat_ref[...], ((1,), (1,)))
         out_ref[c] = out.astype(BF16)
-        store(i, at).start()
-
+        copies.append(pltpu.make_async_copy(out_ref.at[c], out_hbm.at[c], out_sem.at[i]))
+        copies[-1].start()
     gn_ref[...] = scale * exact(hidden, d_pre, ((0,), (0,)))
     ga_ref[...] = -scale * exact(d_hidden, nodes, ((1,), (1,)))
     size = gr_ref.shape[0]
@@ -330,21 +324,22 @@
         x_red, dn_f, ((1,), (1,))
     )
     ge_ref[...] = scale * exact(with_proj[:, nodes_n:], no_f)
-    for i in range(rows // step):
-        store(i, i * step).wait()
+    for copy in copies:
+        copy.wait()
 
 
 def feature_grads(plan, where, mine, other, sums, adjacency, node_weight, wcat, rdp, g, scale):
     rows, chan = g.shape
     nodes, cr = adjacency.shape[0], node_weight.shape[0]
-    step = row_block(rows, 512)
+    unit = row_block(rows // 12, 256)
+    cuts = sorted({0, *(rows - k * unit for k in (1, 4, 8) if k * unit < rows), rows})
     size = chan // plan.count
     there = [
         pltpu.with_memory_space_constraint(value, pltpu.VMEM)
         for value in (mine, other, sums, adjacency, node_weight, wcat, rdp, g)
     ]
     return pl.pallas_call(
-        functools.partial(feature_kernel, step, scale, plan),
+        functools.partial(feature_kernel, cuts, scale, plan),
         in_specs=[SMEM] + [VMEM] * len(there),
         out_specs=[HBM] + [VMEM] * 5,
         out_shape=[
@@ -359,7 +354,7 @@
             pltpu.VMEM((rows, chan), BF16),
             pltpu.VMEM((2 * cr, 2 * cr), BF16),
             pltpu.VMEM((2 * nodes, cr), BF16),
-            pltpu.SemaphoreType.DMA((rows // step,)),
+            pltpu.SemaphoreType.DMA((len(cuts) - 1,)),
         ],
         compiler_params=params(),
         cost_estimate=cost(2 * rows * 4 * 65536, rows * chan * 4 + rows * 768),
@@ -387,7 +382,7 @@
     for group in plan.groups:
         parts = step(head, len(group), terms, ready[:1] if ready else ())
         terms = [plan.swap(part, mask) if mask else part for part, mask in zip(parts, group)]
-        ready = ready or fetch(terms[1], adjacency, node_weight, wcat, rdp, flat_g)
+        ready = ready or fetch(parts[0], adjacency, node_weight, wcat, rdp, flat_g)
     mine, sums = step(head, 1, terms)
     other = plan.swap(mine, plan.core)
 

time: 36.2 us -> 34.1 us (0.942)
  Pallas kernels: 14.6 us -> 13.3 us
  starting transfers between devices: 9.85 us -> 9.33 us
    pallas_call x1, Pallas kernels: 5.17 us -> 4.13 us  [feature_grads(): pl.pallas_call(functools.partial(feature_kernel, cuts, scale, plan), in_s...]
    ppermute x8, starting transfers between devices: 9.85 us -> 9.33 us  [swap(): return lax.ppermute(value, AXES, [(d, d ^ mask) for d in range(self.count)])]
  transfers between devices with their start and end apart: 8 -> 8, of which waited for: 6 -> 7; matrix products, arithmetic and copies ran while one was open for 0% -> 0% of each run, Pallas kernels for 8% -> 8%
where the time goes in v11:
time: 34.1 us; the launch traced here: 33.9 us
  Pallas kernels  13.3 us (39%)
  waiting for transfers between devices  10.6 us (31%)
  starting transfers between devices  9.33 us (27%)
  between operations  0.68 us (2%)
    ppermute x8, waiting for transfers between devices, swap(): return lax.ppermute(value, AXES, [(d, d ^ mask) for d in range(self.count)])  10.6 us
    ppermute x8, starting transfers between devices, swap(): return lax.ppermute(value, AXES, [(d, d ^ mask) for d in range(self.count)])  9.33 us
    pallas_call x1, Pallas kernels, gather(): pl.pallas_call(functools.partial(gather_kernel, plan, step, sorted_here),...  6.31 us
    pallas_call x1, Pallas kernels, feature_grads(): pl.pallas_call(functools.partial(feature_kernel, cuts, scale, plan), in_s...  4.13 us
    pallas_call x1, Pallas kernels, fetch(): pl.pallas_call(fetch_kernel, in_specs=[pl.BlockSpec(memory_space=pl.ANY)]...  2.79 us
  transfers between devices with their start and end apart: 8, of which 7 were waited for; matrix products, arithmetic and copies ran while one was open for 0% of the time, Pallas kernels for 8%

profile of v11, /device:TPU:0, one launch (start us, length us, event | category | flops | bytes accessed | tf_op | source)
XLA Modules:
  0.0 33.9 jit_solution(9353999273622137119)
XLA Ops:
  0.6 6.3 %gather.1 = (bf16[3072,384]{1,0:T(8,128)(2,1)}, bf16[512,256]{1,0:T(8,128)(2,1)}, f32[832,128]{1,0:T(8,128)S(1)}, f32[832,128]{1,0:T(8,128)S(1)}) custom-call(s32[1]{0:T(128)} %bitcast.where_ref, bf16[3072,512]{1,0:T(8,128)(2,1)} %bitcast.13, bf16[3072,512]{1,0:T(8,128)(2,1)} %bitcast.11, bf16[512,128]{1,0:T(8,128)(2,1)} %wr_hbm.1, ...), custom_call_target="tpu_custom_call" | custom-call | flops 3221225472 | bytes 8650752 | tf_op jit(solution)/shard_map/gather/pallas_call | solution.py:199
  7.0 0.5 %collective-permute-start = (f32[832,128]{1,0:T(8,128)S(1)}, f32[832,128]{1,0:T(8,128)S(1)}, u32[]{:S(2)}, u32[]{:S(2)}) collective-permute-start(f32[832,128]{1,0:T(8,128)S(1)} %get-tuple-element.32), channel_id=1, source_target_pairs={{0,4},{1,5},{2,6},{3,7},{4,0},{5,1},{6,2},{7,3},{8,12},{9,13},{10,... | collective-permute-start | bytes 1277960 | tf_op jit(solution)/shard_map/ppermute | solution.py:70
  7.5 1.4 %collective-permute-done.refs_1_ = f32[832,128]{1,0:T(8,128)S(1)} collective-permute-done((f32[832,128]{1,0:T(8,128)S(1)}, f32[832,128]{1,0:T(8,128)S(1)}, u32[]{:S(2)}, u32[]{:S(2)}) %collective-permute-start) | collective-permute-done | bytes 426016 | tf_op jit(solution)/shard_map/ppermute | solution.py:70
  8.9 3.9 %collective-permute-start.1 = (f32[256,128]{1,0:T(8,128)S(1)}, f32[256,128]{1,0:T(8,128)S(1)}, u32[]{:S(2)}, u32[]{:S(2)}) collective-permute-start(f32[256,128]{1,0:T(8,128)S(1)} %get-tuple-element.34), channel_id=1, source_target_pairs={{0,24},{1,25},{2,26},{3,27},{4,28},{5,29},{6,30},{7,31},{8,16},{9,... | collective-permute-start | bytes 393224 | tf_op jit(solution)/shard_map/ppermute | solution.py:70
  12.8 0.5 %collective-permute-start.2 = (f32[256,128]{1,0:T(8,128)S(1)}, f32[256,128]{1,0:T(8,128)S(1)}, u32[]{:S(2)}, u32[]{:S(2)}) collective-permute-start(f32[256,128]{1,0:T(8,128)S(1)} %get-tuple-element.35), channel_id=1, source_target_pairs={{0,8},{1,9},{2,10},{3,11},{4,12},{5,13},{6,14},{7,15},{8,0},{9,1},... | collective-permute-start | bytes 393224 | tf_op jit(solution)/shard_map/ppermute | solution.py:70
  13.3 0.1 collective-permute-start.3
  13.4 2.8 %fetch.1 = (f32[64,64]{1,0:T(8,128)S(1)}, f32[128,128]{1,0:T(8,128)S(1)}, bf16[512,256]{1,0:T(8,128)(2,1)S(1)}, bf16[3072,384]{1,0:T(8,128)(2,1)S(1)}, bf16[3072,512]{1,0:T(8,128)(2,1)S(1)}) custom-call(f32[256,128]{1,0:T(8,128)S(1)} %get-tuple-element.33._.refs_0_, f32[64,64]{1,0:T(8,128)} %refs_0_.1, f32[128,128]{1,0:T(8,128)} %refs_1_.1, ...), custom_call_target="tpu_custom_call" | custom-call | bytes 5849088 | tf_op jit(solution)/shard_map/fetch/pallas_call | solution.py:267
  16.2 0.8 %collective-permute-done.1.refs_1_ = f32[256,128]{1,0:T(8,128)S(1)} collective-permute-done((f32[256,128]{1,0:T(8,128)S(1)}, f32[256,128]{1,0:T(8,128)S(1)}, u32[]{:S(2)}, u32[]{:S(2)}) %collective-permute-start.1) | collective-permute-done | bytes 131104 | tf_op jit(solution)/shard_map/ppermute | solution.py:70
  17.1 2.6 %collective-permute-done.2.refs_2_ = f32[256,128]{1,0:T(8,128)S(1)} collective-permute-done((f32[256,128]{1,0:T(8,128)S(1)}, f32[256,128]{1,0:T(8,128)S(1)}, u32[]{:S(2)}, u32[]{:S(2)}) %collective-permute-start.2) | collective-permute-done | bytes 131104 | tf_op jit(solution)/shard_map/ppermute | solution.py:70
  19.7 0.0 collective-permute-done.3.refs_3_
  19.7 2.6 %collective-permute-start.4 = (f32[112,128]{1,0:T(8,128)S(1)}, f32[112,128]{1,0:T(8,128)S(1)}, u32[]{:S(2)}, u32[]{:S(2)}) collective-permute-start(f32[112,128]{1,0:T(8,128)S(1)} %get-tuple-element.41), channel_id=1, source_target_pairs={{0,2},{1,3},{2,0},{3,1},{4,6},{5,7},{6,4},{7,5},{8,10},{9,11},{10,... | collective-permute-start | bytes 172040 | tf_op jit(solution)/shard_map/ppermute | solution.py:70
  22.4 1.3 %collective-permute-start.5 = (f32[112,128]{1,0:T(8,128)S(1)}, f32[112,128]{1,0:T(8,128)S(1)}, u32[]{:S(2)}, u32[]{:S(2)}) collective-permute-start(f32[112,128]{1,0:T(8,128)S(1)} %get-tuple-element.42), channel_id=1, source_target_pairs={{0,3},{1,2},{2,1},{3,0},{4,7},{5,6},{6,5},{7,4},{8,11},{9,10},{10,... | collective-permute-start | bytes 172040 | tf_op jit(solution)/shard_map/ppermute | solution.py:70
  23.7 0.2 collective-permute-start.6
  23.9 1.1 %collective-permute-done.4.refs_1_ = f32[112,128]{1,0:T(8,128)S(1)} collective-permute-done((f32[112,128]{1,0:T(8,128)S(1)}, f32[112,128]{1,0:T(8,128)S(1)}, u32[]{:S(2)}, u32[]{:S(2)}) %collective-permute-start.4) | collective-permute-done | bytes 57376 | tf_op jit(solution)/shard_map/ppermute | solution.py:70
  25.0 3.4 %collective-permute-done.5.refs_2_ = f32[112,128]{1,0:T(8,128)S(1)} collective-permute-done((f32[112,128]{1,0:T(8,128)S(1)}, f32[112,128]{1,0:T(8,128)S(1)}, u32[]{:S(2)}, u32[]{:S(2)}) %collective-permute-start.5) | collective-permute-done | bytes 57376 | tf_op jit(solution)/shard_map/ppermute | solution.py:70
  28.4 0.1 collective-permute-done.6.refs_3_
  28.5 0.1 collective-permute-start.7
  28.6 1.2 %collective-permute-done.7.other_ref = f32[64,128]{1,0:T(8,128)S(1)} collective-permute-done((f32[64,128]{1,0:T(8,128)S(1)}, f32[64,128]{1,0:T(8,128)S(1)}, u32[]{:S(2)}, u32[]{:S(2)}) %collective-permute-start.7) | collective-permute-done | bytes 32800 | tf_op jit(solution)/shard_map/ppermute | solution.py:70
  29.8 4.1 %feature_grads.1 = (bf16[3072,512]{1,0:T(8,128)(2,1)}, f32[16,128]{1,0:T(8,128)}, f32[16,64]{1,0:T(8,128)}, f32[16,128]{1,0:T(8,128)}, f32[64,64]{1,0:T(8,128)}, /*index=5*/f32[128,128]{1,0:T(8,128)}) custom-call(s32[1]{0:T(128)} %bitcast.where_ref, f32[64,128]{1,0:T(8,128)S(1)} %get-tuple-element.44.mine_ref, ...), custom_call_target="tpu_custom_call" | custom-call | flops 1610612736 | bytes 8650752 | tf_op jit(solution)/shard_map/feature_grads/pallas_call | solution.py:341
  (3 shorter events, 0.1 us)
Async XLA Ops:
  7.0 1.9 %collective-permute-start = (f32[832,128]{1,0:T(8,128)S(1)}, f32[832,128]{1,0:T(8,128)S(1)}, u32[]{:S(2)}, u32[]{:S(2)}) collective-permute-start(f32[832,128]{1,0:T(8,128)S(1)} %get-tuple-element.32), channel_id=1, source_target_pairs={{0,4},{1,5},{2,6},{3,7},{4,0},{5,1},{6,2},{7,3},{8,12},{9,13},{10,... | collective-permute-start | bytes 1277960 | tf_op jit(solution)/shard_map/ppermute | solution.py:70
  8.9 8.2 %collective-permute-start.1 = (f32[256,128]{1,0:T(8,128)S(1)}, f32[256,128]{1,0:T(8,128)S(1)}, u32[]{:S(2)}, u32[]{:S(2)}) collective-permute-start(f32[256,128]{1,0:T(8,128)S(1)} %get-tuple-element.34), channel_id=1, source_target_pairs={{0,24},{1,25},{2,26},{3,27},{4,28},{5,29},{6,30},{7,31},{8,16},{9,... | collective-permute-start | bytes 393224 | tf_op jit(solution)/shard_map/ppermute | solution.py:70
  12.8 6.9 %collective-permute-start.2 = (f32[256,128]{1,0:T(8,128)S(1)}, f32[256,128]{1,0:T(8,128)S(1)}, u32[]{:S(2)}, u32[]{:S(2)}) collective-permute-start(f32[256,128]{1,0:T(8,128)S(1)} %get-tuple-element.35), channel_id=1, source_target_pairs={{0,8},{1,9},{2,10},{3,11},{4,12},{5,13},{6,14},{7,15},{8,0},{9,1},... | collective-permute-start | bytes 393224 | tf_op jit(solution)/shard_map/ppermute | solution.py:70
  13.3 6.3 %collective-permute-start.3 = (f32[256,128]{1,0:T(8,128)S(1)}, f32[256,128]{1,0:T(8,128)S(1)}, u32[]{:S(2)}, u32[]{:S(2)}) collective-permute-start(f32[256,128]{1,0:T(8,128)S(1)} %get-tuple-element.36), channel_id=1, source_target_pairs={{0,16},{1,17},{2,18},{3,19},{4,20},{5,21},{6,22},{7,23},{8,24},{9,... | collective-permute-start | bytes 393224 | tf_op jit(solution)/shard_map/ppermute | solution.py:70
  19.7 5.3 %collective-permute-start.4 = (f32[112,128]{1,0:T(8,128)S(1)}, f32[112,128]{1,0:T(8,128)S(1)}, u32[]{:S(2)}, u32[]{:S(2)}) collective-permute-start(f32[112,128]{1,0:T(8,128)S(1)} %get-tuple-element.41), channel_id=1, source_target_pairs={{0,2},{1,3},{2,0},{3,1},{4,6},{5,7},{6,4},{7,5},{8,10},{9,11},{10,... | collective-permute-start | bytes 172040 | tf_op jit(solution)/shard_map/ppermute | solution.py:70
  22.4 6.1 %collective-permute-start.5 = (f32[112,128]{1,0:T(8,128)S(1)}, f32[112,128]{1,0:T(8,128)S(1)}, u32[]{:S(2)}, u32[]{:S(2)}) collective-permute-start(f32[112,128]{1,0:T(8,128)S(1)} %get-tuple-element.42), channel_id=1, source_target_pairs={{0,3},{1,2},{2,1},{3,0},{4,7},{5,6},{6,5},{7,4},{8,11},{9,10},{10,... | collective-permute-start | bytes 172040 | tf_op jit(solution)/shard_map/ppermute | solution.py:70
  23.7 4.8 %collective-permute-start.6 = (f32[112,128]{1,0:T(8,128)S(1)}, f32[112,128]{1,0:T(8,128)S(1)}, u32[]{:S(2)}, u32[]{:S(2)}) collective-permute-start(f32[112,128]{1,0:T(8,128)S(1)} %get-tuple-element.43), channel_id=1, source_target_pairs={{0,1},{1,0},{2,3},{3,2},{4,5},{5,4},{6,7},{7,6},{8,9},{9,8},{10,11... | collective-permute-start | bytes 172040 | tf_op jit(solution)/shard_map/ppermute | solution.py:70
  28.5 1.3 %collective-permute-start.7 = (f32[64,128]{1,0:T(8,128)S(1)}, f32[64,128]{1,0:T(8,128)S(1)}, u32[]{:S(2)}, u32[]{:S(2)}) collective-permute-start(f32[64,128]{1,0:T(8,128)S(1)} %get-tuple-element.44.mine_ref), channel_id=1, source_target_pairs={{0,4},{1,5},{2,6},{3,7},{4,0},{5,1},{6,2},{7,3},{8,12},{9,13},{10,... | collective-permute-start | bytes 98312 | tf_op jit(solution)/shard_map/ppermute | solution.py:70

commit v12 on v11

--- a/solution.py
+++ b/solution.py
@@ -117,18 +117,20 @@
 
     @pl.loop(0, count)
     def _(i):
-        for k, pair in enumerate(loads):
-            @pl.when(i == load_cuts[k])
-            def _():
-                for copy in pair:
-                    copy.wait()
-                if k + 1 < len(loads):
-                    for copy in loads[k + 1]:
-                        copy.start()
+        def arrive(which):
+            for k, pair in enumerate(loads):
+                @pl.when(i == load_cuts[k])
+                def _():
+                    pair[which].wait()
+                    if k + 1 < len(loads):
+                        loads[k + 1][which].start()
 
         c = pl.ds(pl.multiple_of(i * step, step), step)
-        x, g = x_ref[c], g_ref[c]
+        arrive(0)
+        x = x_ref[c]
         both = mxu(x, cat_ref[...]).astype(BF16)
+        arrive(1)
+        g = g_ref[c]
         mapped = mxu(g, we_ref[...]).astype(BF16)
         rdp = jnp.concatenate([both[:, :cr], mapped, both[:, cr:]], axis=1)
         rdp_ref[c] = rdp
@@ -297,17 +299,14 @@
     no_f, dn_f = node_out.astype(F32), dn.astype(F32)
     dnb_ref[:nodes_n] = dn
     dnb_ref[nodes_n:] = jnp.zeros((nodes_n, cr), BF16)
-    blank = jnp.zeros((cr, cr), BF16)
-    zero = jnp.zeros((nodes_n, cr), F32)
-    mix_ref[:cr, :cr] = jnp.concatenate([dn_f, zero], axis=0).T.astype(BF16)
-    mix_ref[cr:, :cr] = blank
-    mix_ref[:cr, cr:] = blank
-    mix_ref[cr:, cr:] = jnp.concatenate([no_f, zero], axis=0).T.astype(BF16)
+    mix_ref[...] = jnp.zeros_like(mix_ref)
+    mix_ref[:nodes_n, :cr] = dn
+    mix_ref[cr : cr + nodes_n, cr:] = node_out
     copies = []
     for i, (start, stop) in enumerate(zip(cuts, cuts[1:])):
         c = pl.ds(start, stop - start)
         rdp = rdp_ref[c]
-        mixed = mxu(rdp[:, :wide], mix_ref[...])
+        mixed = mxu(rdp[:, :wide], mix_ref[...], ((1,), (1,)))
         d_proj = (mixed[:, cr:] + scale * mixed[:, :cr]).astype(BF16)
         d_red = (scale * mxu(rdp[:, wide:], dnb_ref[...])).astype(BF16)
         both = jnp.concatenate([d_red, d_proj], axis=1)

time: 34.1 us -> 35.3 us (1.035)
  Pallas kernels: 13.3 us -> 14.6 us
    pallas_call x1, Pallas kernels: 6.31 us -> 7.69 us  [gather(): pl.pallas_call(functools.partial(gather_kernel, plan, step, sorted_here),...]
where the time goes in v12:
time: 35.3 us; the launch traced here: 35.2 us
  Pallas kernels  14.6 us (41%)
  waiting for transfers between devices  10.6 us (30%)
  starting transfers between devices  9.33 us (26%)
  between operations  0.68 us (2%)
    ppermute x8, waiting for transfers between devices, swap(): return lax.ppermute(value, AXES, [(d, d ^ mask) for d in range(self.count)])  10.6 us
    ppermute x8, starting transfers between devices, swap(): return lax.ppermute(value, AXES, [(d, d ^ mask) for d in range(self.count)])  9.33 us
    pallas_call x1, Pallas kernels, gather(): pl.pallas_call(functools.partial(gather_kernel, plan, step, sorted_here),...  7.69 us
    pallas_call x1, Pallas kernels, feature_grads(): pl.pallas_call(functools.partial(feature_kernel, cuts, scale, plan), in_s...  4.03 us
    pallas_call x1, Pallas kernels, fetch(): pl.pallas_call(fetch_kernel, in_specs=[pl.BlockSpec(memory_space=pl.ANY)]...  2.79 us
  transfers between devices with their start and end apart: 8, of which 7 were waited for; matrix products, arithmetic and copies ran while one was open for 0% of the time, Pallas kernels for 8%

profile of v12, /device:TPU:0, one launch (start us, length us, event | category | flops | bytes accessed | tf_op | source)
XLA Modules:
  0.0 35.2 jit_solution(12686302184694431501)
XLA Ops:
  0.6 7.7 %gather.1 = (bf16[3072,384]{1,0:T(8,128)(2,1)}, bf16[512,256]{1,0:T(8,128)(2,1)}, f32[832,128]{1,0:T(8,128)S(1)}, f32[832,128]{1,0:T(8,128)S(1)}) custom-call(s32[1]{0:T(128)} %bitcast.where_ref, bf16[3072,512]{1,0:T(8,128)(2,1)} %bitcast.13, bf16[3072,512]{1,0:T(8,128)(2,1)} %bitcast.11, bf16[512,128]{1,0:T(8,128)(2,1)} %wr_hbm.1, ...), custom_call_target="tpu_custom_call" | custom-call | flops 3221225472 | bytes 8650752 | tf_op jit(solution)/shard_map/gather/pallas_call | solution.py:201
  8.3 0.5 %collective-permute-start = (f32[832,128]{1,0:T(8,128)S(1)}, f32[832,128]{1,0:T(8,128)S(1)}, u32[]{:S(2)}, u32[]{:S(2)}) collective-permute-start(f32[832,128]{1,0:T(8,128)S(1)} %get-tuple-element.32), channel_id=1, source_target_pairs={{0,4},{1,5},{2,6},{3,7},{4,0},{5,1},{6,2},{7,3},{8,12},{9,13},{10,... | collective-permute-start | bytes 1277960 | tf_op jit(solution)/shard_map/ppermute | solution.py:70
  8.9 1.4 %collective-permute-done.refs_1_ = f32[832,128]{1,0:T(8,128)S(1)} collective-permute-done((f32[832,128]{1,0:T(8,128)S(1)}, f32[832,128]{1,0:T(8,128)S(1)}, u32[]{:S(2)}, u32[]{:S(2)}) %collective-permute-start) | collective-permute-done | bytes 426016 | tf_op jit(solution)/shard_map/ppermute | solution.py:70
  10.3 3.9 %collective-permute-start.1 = (f32[256,128]{1,0:T(8,128)S(1)}, f32[256,128]{1,0:T(8,128)S(1)}, u32[]{:S(2)}, u32[]{:S(2)}) collective-permute-start(f32[256,128]{1,0:T(8,128)S(1)} %get-tuple-element.34), channel_id=1, source_target_pairs={{0,24},{1,25},{2,26},{3,27},{4,28},{5,29},{6,30},{7,31},{8,16},{9,... | collective-permute-start | bytes 393224 | tf_op jit(solution)/shard_map/ppermute | solution.py:70
  14.2 0.5 %collective-permute-start.2 = (f32[256,128]{1,0:T(8,128)S(1)}, f32[256,128]{1,0:T(8,128)S(1)}, u32[]{:S(2)}, u32[]{:S(2)}) collective-permute-start(f32[256,128]{1,0:T(8,128)S(1)} %get-tuple-element.35), channel_id=1, source_target_pairs={{0,8},{1,9},{2,10},{3,11},{4,12},{5,13},{6,14},{7,15},{8,0},{9,1},... | collective-permute-start | bytes 393224 | tf_op jit(solution)/shard_map/ppermute | solution.py:70
  14.7 0.1 collective-permute-start.3
  14.8 2.8 %fetch.1 = (f32[64,64]{1,0:T(8,128)S(1)}, f32[128,128]{1,0:T(8,128)S(1)}, bf16[512,256]{1,0:T(8,128)(2,1)S(1)}, bf16[3072,384]{1,0:T(8,128)(2,1)S(1)}, bf16[3072,512]{1,0:T(8,128)(2,1)S(1)}) custom-call(f32[256,128]{1,0:T(8,128)S(1)} %get-tuple-element.33._.refs_0_, f32[64,64]{1,0:T(8,128)} %refs_0_.1, f32[128,128]{1,0:T(8,128)} %refs_1_.1, ...), custom_call_target="tpu_custom_call" | custom-call | bytes 5849088 | tf_op jit(solution)/shard_map/fetch/pallas_call | solution.py:269
  17.6 0.8 %collective-permute-done.1.refs_1_ = f32[256,128]{1,0:T(8,128)S(1)} collective-permute-done((f32[256,128]{1,0:T(8,128)S(1)}, f32[256,128]{1,0:T(8,128)S(1)}, u32[]{:S(2)}, u32[]{:S(2)}) %collective-permute-start.1) | collective-permute-done | bytes 131104 | tf_op jit(solution)/shard_map/ppermute | solution.py:70
  18.5 2.6 %collective-permute-done.2.refs_2_ = f32[256,128]{1,0:T(8,128)S(1)} collective-permute-done((f32[256,128]{1,0:T(8,128)S(1)}, f32[256,128]{1,0:T(8,128)S(1)}, u32[]{:S(2)}, u32[]{:S(2)}) %collective-permute-start.2) | collective-permute-done | bytes 131104 | tf_op jit(solution)/shard_map/ppermute | solution.py:70
  21.1 0.0 collective-permute-done.3.refs_3_
  21.1 2.6 %collective-permute-start.4 = (f32[112,128]{1,0:T(8,128)S(1)}, f32[112,128]{1,0:T(8,128)S(1)}, u32[]{:S(2)}, u32[]{:S(2)}) collective-permute-start(f32[112,128]{1,0:T(8,128)S(1)} %get-tuple-element.41), channel_id=1, source_target_pairs={{0,2},{1,3},{2,0},{3,1},{4,6},{5,7},{6,4},{7,5},{8,10},{9,11},{10,... | collective-permute-start | bytes 172040 | tf_op jit(solution)/shard_map/ppermute | solution.py:70
  23.7 1.3 %collective-permute-start.5 = (f32[112,128]{1,0:T(8,128)S(1)}, f32[112,128]{1,0:T(8,128)S(1)}, u32[]{:S(2)}, u32[]{:S(2)}) collective-permute-start(f32[112,128]{1,0:T(8,128)S(1)} %get-tuple-element.42), channel_id=1, source_target_pairs={{0,3},{1,2},{2,1},{3,0},{4,7},{5,6},{6,5},{7,4},{8,11},{9,10},{10,... | collective-permute-start | bytes 172040 | tf_op jit(solution)/shard_map/ppermute | solution.py:70
  25.1 0.2 collective-permute-start.6
  25.3 1.1 %collective-permute-done.4.refs_1_ = f32[112,128]{1,0:T(8,128)S(1)} collective-permute-done((f32[112,128]{1,0:T(8,128)S(1)}, f32[112,128]{1,0:T(8,128)S(1)}, u32[]{:S(2)}, u32[]{:S(2)}) %collective-permute-start.4) | collective-permute-done | bytes 57376 | tf_op jit(solution)/shard_map/ppermute | solution.py:70
  26.4 3.4 %collective-permute-done.5.refs_2_ = f32[112,128]{1,0:T(8,128)S(1)} collective-permute-done((f32[112,128]{1,0:T(8,128)S(1)}, f32[112,128]{1,0:T(8,128)S(1)}, u32[]{:S(2)}, u32[]{:S(2)}) %collective-permute-start.5) | collective-permute-done | bytes 57376 | tf_op jit(solution)/shard_map/ppermute | solution.py:70
  29.8 0.1 collective-permute-done.6.refs_3_
  29.9 0.1 collective-permute-start.7
  30.0 1.2 %collective-permute-done.7.other_ref = f32[64,128]{1,0:T(8,128)S(1)} collective-permute-done((f32[64,128]{1,0:T(8,128)S(1)}, f32[64,128]{1,0:T(8,128)S(1)}, u32[]{:S(2)}, u32[]{:S(2)}) %collective-permute-start.7) | collective-permute-done | bytes 32800 | tf_op jit(solution)/shard_map/ppermute | solution.py:70
  31.2 4.0 %feature_grads.1 = (bf16[3072,512]{1,0:T(8,128)(2,1)}, f32[16,128]{1,0:T(8,128)}, f32[16,64]{1,0:T(8,128)}, f32[16,128]{1,0:T(8,128)}, f32[64,64]{1,0:T(8,128)}, /*index=5*/f32[128,128]{1,0:T(8,128)}) custom-call(s32[1]{0:T(128)} %bitcast.where_ref, f32[64,128]{1,0:T(8,128)S(1)} %get-tuple-element.44.mine_ref, ...), custom_call_target="tpu_custom_call" | custom-call | flops 1610612736 | bytes 8650752 | tf_op jit(solution)/shard_map/feature_grads/pallas_call | solution.py:340
  (3 shorter events, 0.1 us)
Async XLA Ops:
  8.3 1.9 %collective-permute-start = (f32[832,128]{1,0:T(8,128)S(1)}, f32[832,128]{1,0:T(8,128)S(1)}, u32[]{:S(2)}, u32[]{:S(2)}) collective-permute-start(f32[832,128]{1,0:T(8,128)S(1)} %get-tuple-element.32), channel_id=1, source_target_pairs={{0,4},{1,5},{2,6},{3,7},{4,0},{5,1},{6,2},{7,3},{8,12},{9,13},{10,... | collective-permute-start | bytes 1277960 | tf_op jit(solution)/shard_map/ppermute | solution.py:70
  10.3 8.2 %collective-permute-start.1 = (f32[256,128]{1,0:T(8,128)S(1)}, f32[256,128]{1,0:T(8,128)S(1)}, u32[]{:S(2)}, u32[]{:S(2)}) collective-permute-start(f32[256,128]{1,0:T(8,128)S(1)} %get-tuple-element.34), channel_id=1, source_target_pairs={{0,24},{1,25},{2,26},{3,27},{4,28},{5,29},{6,30},{7,31},{8,16},{9,... | collective-permute-start | bytes 393224 | tf_op jit(solution)/shard_map/ppermute | solution.py:70
  14.2 6.9 %collective-permute-start.2 = (f32[256,128]{1,0:T(8,128)S(1)}, f32[256,128]{1,0:T(8,128)S(1)}, u32[]{:S(2)}, u32[]{:S(2)}) collective-permute-start(f32[256,128]{1,0:T(8,128)S(1)} %get-tuple-element.35), channel_id=1, source_target_pairs={{0,8},{1,9},{2,10},{3,11},{4,12},{5,13},{6,14},{7,15},{8,0},{9,1},... | collective-permute-start | bytes 393224 | tf_op jit(solution)/shard_map/ppermute | solution.py:70
  14.7 6.3 %collective-permute-start.3 = (f32[256,128]{1,0:T(8,128)S(1)}, f32[256,128]{1,0:T(8,128)S(1)}, u32[]{:S(2)}, u32[]{:S(2)}) collective-permute-start(f32[256,128]{1,0:T(8,128)S(1)} %get-tuple-element.36), channel_id=1, source_target_pairs={{0,16},{1,17},{2,18},{3,19},{4,20},{5,21},{6,22},{7,23},{8,24},{9,... | collective-permute-start | bytes 393224 | tf_op jit(solution)/shard_map/ppermute | solution.py:70
  21.1 5.3 %collective-permute-start.4 = (f32[112,128]{1,0:T(8,128)S(1)}, f32[112,128]{1,0:T(8,128)S(1)}, u32[]{:S(2)}, u32[]{:S(2)}) collective-permute-start(f32[112,128]{1,0:T(8,128)S(1)} %get-tuple-element.41), channel_id=1, source_target_pairs={{0,2},{1,3},{2,0},{3,1},{4,6},{5,7},{6,4},{7,5},{8,10},{9,11},{10,... | collective-permute-start | bytes 172040 | tf_op jit(solution)/shard_map/ppermute | solution.py:70
  23.7 6.1 %collective-permute-start.5 = (f32[112,128]{1,0:T(8,128)S(1)}, f32[112,128]{1,0:T(8,128)S(1)}, u32[]{:S(2)}, u32[]{:S(2)}) collective-permute-start(f32[112,128]{1,0:T(8,128)S(1)} %get-tuple-element.42), channel_id=1, source_target_pairs={{0,3},{1,2},{2,1},{3,0},{4,7},{5,6},{6,5},{7,4},{8,11},{9,10},{10,... | collective-permute-start | bytes 172040 | tf_op jit(solution)/shard_map/ppermute | solution.py:70
  25.1 4.8 %collective-permute-start.6 = (f32[112,128]{1,0:T(8,128)S(1)}, f32[112,128]{1,0:T(8,128)S(1)}, u32[]{:S(2)}, u32[]{:S(2)}) collective-permute-start(f32[112,128]{1,0:T(8,128)S(1)} %get-tuple-element.43), channel_id=1, source_target_pairs={{0,1},{1,0},{2,3},{3,2},{4,5},{5,4},{6,7},{7,6},{8,9},{9,8},{10,11... | collective-permute-start | bytes 172040 | tf_op jit(solution)/shard_map/ppermute | solution.py:70
  29.9 1.3 %collective-permute-start.7 = (f32[64,128]{1,0:T(8,128)S(1)}, f32[64,128]{1,0:T(8,128)S(1)}, u32[]{:S(2)}, u32[]{:S(2)}) collective-permute-start(f32[64,128]{1,0:T(8,128)S(1)} %get-tuple-element.44.mine_ref), channel_id=1, source_target_pairs={{0,4},{1,5},{2,6},{3,7},{4,0},{5,1},{6,2},{7,3},{8,12},{9,13},{10,... | collective-permute-start | bytes 98312 | tf_op jit(solution)/shard_map/ppermute | solution.py:70

commit v13 on v12

--- a/solution.py
+++ b/solution.py
@@ -56,7 +56,7 @@
         spans = (
             ([0, *sorted(range(1, size["gx"]), key=lambda k: -k.bit_count())], stride["gx"]),
             (range(size["gy"] // 2), 2 * stride["gy"]),
-            ([0, *range(2, size["gz"]), 1], stride["gz"]),
+            ([0, *range(size["gz"] - 1, 0, -1)], stride["gz"]),
         )
         self.groups = [[k * step for k in order] for order, step in spans if len(order) > 1]
         self.masks = [0]
@@ -89,24 +89,17 @@
         move(wpt_hbm, wpt_ref, small_sem.at[1]),
         move(we_hbm, we_ref, small_sem.at[2]),
     ]
-    load_cuts = sorted({0, min(1, count), min(2, count), count})
-    store_cuts = sorted({0, max(count - 2, 0), max(count - 1, 0), count})
-    span = lambda cuts, i: pl.ds(cuts[i] * step, (cuts[i + 1] - cuts[i]) * step)
+    spans = [pl.ds(start, step) for start in range(0, rows, step)]
     loads = [
         (
-            move(x_hbm.at[span(load_cuts, i)], x_ref.at[span(load_cuts, i)], in_sem.at[0, i]),
-            move(g_hbm.at[span(load_cuts, i)], g_ref.at[span(load_cuts, i)], in_sem.at[1, i]),
+            move(x_hbm.at[c], x_ref.at[c], in_sem.at[0, i]),
+            move(g_hbm.at[c], g_ref.at[c], in_sem.at[1, i]),
         )
-        for i in range(len(load_cuts) - 1)
-    ]
-    stores = [
-        move(rdp_ref.at[span(store_cuts, i)], rdp_hbm.at[span(store_cuts, i)], out_sem.at[i])
-        for i in range(len(store_cuts) - 1)
-    ]
+        for i, c in enumerate(spans)
+    ]
+    stores = [move(rdp_ref.at[c], rdp_hbm.at[c], out_sem.at[i]) for i, c in enumerate(spans)]
     for copy in (*small, *loads[0]):
         copy.start()
-    sums_ref[...] = jnp.zeros_like(sums_ref)
-    term_ref[...] = jnp.zeros_like(term_ref)
     small[0].wait()
     small[1].wait()
     padded = jnp.concatenate([wpt_ref[...], jnp.zeros_like(wpt_ref)], axis=0)
@@ -114,33 +107,27 @@
     keep_weights = move(cat_ref, wcat_hbm, small_sem.at[3])
     keep_weights.start()
     small[2].wait()
-
-    @pl.loop(0, count)
-    def _(i):
-        def arrive(which):
-            for k, pair in enumerate(loads):
-                @pl.when(i == load_cuts[k])
-                def _():
-                    pair[which].wait()
-                    if k + 1 < len(loads):
-                        loads[k + 1][which].start()
-
-        c = pl.ds(pl.multiple_of(i * step, step), step)
-        arrive(0)
-        x = x_ref[c]
+    for i, c in enumerate(spans):
+        for copy in loads[i]:
+            copy.wait()
+        if i + 1 < count:
+            for copy in loads[i + 1]:
+                copy.start()
+        x, g = x_ref[c], g_ref[c]
         both = mxu(x, cat_ref[...]).astype(BF16)
-        arrive(1)
-        g = g_ref[c]
         mapped = mxu(g, we_ref[...]).astype(BF16)
         rdp = jnp.concatenate([both[:, :cr], mapped, both[:, cr:]], axis=1)
         rdp_ref[c] = rdp
         turned = rdp.T
         proj = turned[wide : wide + nodes]
-        sums_ref[: wide + nodes] += mxu(turned[: wide + nodes], x)
-        sums_ref[wide + nodes :] += mxu(proj, g)
-        term_ref[...] += mxu(proj, rdp[:, :wide])
-        for k, copy in enumerate(stores):
-            pl.when(i == store_cuts[k + 1] - 1)(copy.start)
+        pieces = (
+            (sums_ref.at[: wide + nodes], mxu(turned[: wide + nodes], x)),
+            (sums_ref.at[wide + nodes :], mxu(proj, g)),
+            (term_ref, mxu(proj, rdp[:, :wide])),
+        )
+        for ref, piece in pieces:
+            ref[...] = ref[...] + piece if i else piece
+        stores[i].start()
 
     me = where_ref[0]
     side = plan.side(me)
@@ -195,8 +182,8 @@
         pltpu.VMEM((width, chan), F32),
         pltpu.VMEM((nodes, 2 * cr), F32),
         pltpu.SemaphoreType.DMA((4,)),
-        pltpu.SemaphoreType.DMA((2, 3)),
-        pltpu.SemaphoreType.DMA((3,)),
+        pltpu.SemaphoreType.DMA((2, rows // step)),
+        pltpu.SemaphoreType.DMA((rows // step,)),
     ]
     rdp, wcat, kept, sent, *sums = pl.pallas_call(
         functools.partial(gather_kernel, plan, step, sorted_here),

time: 35.3 us -> 34.7 us (0.983)
  Pallas kernels: 14.6 us -> 14 us
    pallas_call x1, Pallas kernels: 7.69 us -> 7.05 us  [gather(): pl.pallas_call(functools.partial(gather_kernel, plan, step, sorted_here),...]
  transfers between devices with their start and end apart: 8 -> 8, of which waited for: 7 -> 6; matrix products, arithmetic and copies ran while one was open for 0% -> 0% of each run, Pallas kernels for 8% -> 8%
where the time goes in v13:
time: 34.7 us; the launch traced here: 34.5 us
  Pallas kernels  14 us (40%)
  waiting for transfers between devices  10.3 us (30%)
  starting transfers between devices  9.56 us (28%)
  between operations  0.68 us (2%)
    ppermute x8, waiting for transfers between devices, swap(): return lax.ppermute(value, AXES, [(d, d ^ mask) for d in range(self.count)])  10.3 us
    ppermute x8, starting transfers between devices, swap(): return lax.ppermute(value, AXES, [(d, d ^ mask) for d in range(self.count)])  9.56 us
    pallas_call x1, Pallas kernels, gather(): pl.pallas_call(functools.partial(gather_kernel, plan, step, sorted_here),...  7.05 us
    pallas_call x1, Pallas kernels, feature_grads(): pl.pallas_call(functools.partial(feature_kernel, cuts, scale, plan), in_s...  4.03 us
    pallas_call x1, Pallas kernels, fetch(): pl.pallas_call(fetch_kernel, in_specs=[pl.BlockSpec(memory_space=pl.ANY)]...  2.79 us
  transfers between devices with their start and end apart: 8, of which 6 were waited for; matrix products, arithmetic and copies ran while one was open for 0% of the time, Pallas kernels for 8%

profile of v13, /device:TPU:0, one launch (start us, length us, event | category | flops | bytes accessed | tf_op | source)
XLA Modules:
  0.0 34.5 jit_solution(3292559310467933639)
XLA Ops:
  0.6 7.0 %gather.1 = (bf16[3072,384]{1,0:T(8,128)(2,1)}, bf16[512,256]{1,0:T(8,128)(2,1)}, f32[832,128]{1,0:T(8,128)S(1)}, f32[832,128]{1,0:T(8,128)S(1)}) custom-call(s32[1]{0:T(128)} %bitcast.where_ref, bf16[3072,512]{1,0:T(8,128)(2,1)} %bitcast.13, bf16[3072,512]{1,0:T(8,128)(2,1)} %bitcast.11, bf16[512,128]{1,0:T(8,128)(2,1)} %wr_hbm.1, ...), custom_call_target="tpu_custom_call" | custom-call | flops 3221225472 | bytes 8650752 | tf_op jit(solution)/shard_map/gather/pallas_call | solution.py:188
  7.7 0.5 %collective-permute-start = (f32[832,128]{1,0:T(8,128)S(1)}, f32[832,128]{1,0:T(8,128)S(1)}, u32[]{:S(2)}, u32[]{:S(2)}) collective-permute-start(f32[832,128]{1,0:T(8,128)S(1)} %get-tuple-element.32), channel_id=1, source_target_pairs={{0,4},{1,5},{2,6},{3,7},{4,0},{5,1},{6,2},{7,3},{8,12},{9,13},{10,... | collective-permute-start | bytes 1277960 | tf_op jit(solution)/shard_map/ppermute | solution.py:70
  8.2 1.4 %collective-permute-done.refs_1_ = f32[832,128]{1,0:T(8,128)S(1)} collective-permute-done((f32[832,128]{1,0:T(8,128)S(1)}, f32[832,128]{1,0:T(8,128)S(1)}, u32[]{:S(2)}, u32[]{:S(2)}) %collective-permute-start) | collective-permute-done | bytes 426016 | tf_op jit(solution)/shard_map/ppermute | solution.py:70
  9.7 3.9 %collective-permute-start.1 = (f32[256,128]{1,0:T(8,128)S(1)}, f32[256,128]{1,0:T(8,128)S(1)}, u32[]{:S(2)}, u32[]{:S(2)}) collective-permute-start(f32[256,128]{1,0:T(8,128)S(1)} %get-tuple-element.34), channel_id=1, source_target_pairs={{0,24},{1,25},{2,26},{3,27},{4,28},{5,29},{6,30},{7,31},{8,16},{9,... | collective-permute-start | bytes 393224 | tf_op jit(solution)/shard_map/ppermute | solution.py:70
  13.5 0.5 %collective-permute-start.2 = (f32[256,128]{1,0:T(8,128)S(1)}, f32[256,128]{1,0:T(8,128)S(1)}, u32[]{:S(2)}, u32[]{:S(2)}) collective-permute-start(f32[256,128]{1,0:T(8,128)S(1)} %get-tuple-element.35), channel_id=1, source_target_pairs={{0,8},{1,9},{2,10},{3,11},{4,12},{5,13},{6,14},{7,15},{8,0},{9,1},... | collective-permute-start | bytes 393224 | tf_op jit(solution)/shard_map/ppermute | solution.py:70
  14.1 0.1 collective-permute-start.3
  14.2 2.8 %fetch.1 = (f32[64,64]{1,0:T(8,128)S(1)}, f32[128,128]{1,0:T(8,128)S(1)}, bf16[512,256]{1,0:T(8,128)(2,1)S(1)}, bf16[3072,384]{1,0:T(8,128)(2,1)S(1)}, bf16[3072,512]{1,0:T(8,128)(2,1)S(1)}) custom-call(f32[256,128]{1,0:T(8,128)S(1)} %get-tuple-element.33._.refs_0_, f32[64,64]{1,0:T(8,128)} %refs_0_.1, f32[128,128]{1,0:T(8,128)} %refs_1_.1, ...), custom_call_target="tpu_custom_call" | custom-call | bytes 5849088 | tf_op jit(solution)/shard_map/fetch/pallas_call | solution.py:256
  17.0 0.8 %collective-permute-done.1.refs_1_ = f32[256,128]{1,0:T(8,128)S(1)} collective-permute-done((f32[256,128]{1,0:T(8,128)S(1)}, f32[256,128]{1,0:T(8,128)S(1)}, u32[]{:S(2)}, u32[]{:S(2)}) %collective-permute-start.1) | collective-permute-done | bytes 131104 | tf_op jit(solution)/shard_map/ppermute | solution.py:70
  17.8 2.6 %collective-permute-done.2.refs_2_ = f32[256,128]{1,0:T(8,128)S(1)} collective-permute-done((f32[256,128]{1,0:T(8,128)S(1)}, f32[256,128]{1,0:T(8,128)S(1)}, u32[]{:S(2)}, u32[]{:S(2)}) %collective-permute-start.2) | collective-permute-done | bytes 131104 | tf_op jit(solution)/shard_map/ppermute | solution.py:70
  20.4 0.0 collective-permute-done.3.refs_3_
  20.5 3.7 %collective-permute-start.4 = (f32[112,128]{1,0:T(8,128)S(1)}, f32[112,128]{1,0:T(8,128)S(1)}, u32[]{:S(2)}, u32[]{:S(2)}) collective-permute-start(f32[112,128]{1,0:T(8,128)S(1)} %get-tuple-element.41), channel_id=1, source_target_pairs={{0,3},{1,2},{2,1},{3,0},{4,7},{5,6},{6,5},{7,4},{8,11},{9,10},{10,... | collective-permute-start | bytes 172040 | tf_op jit(solution)/shard_map/ppermute | solution.py:70
  24.1 0.0 collective-permute-start.5
  24.1 0.8 %collective-permute-start.6 = (f32[112,128]{1,0:T(8,128)S(1)}, f32[112,128]{1,0:T(8,128)S(1)}, u32[]{:S(2)}, u32[]{:S(2)}) collective-permute-start(f32[112,128]{1,0:T(8,128)S(1)} %get-tuple-element.43), channel_id=1, source_target_pairs={{0,1},{1,0},{2,3},{3,2},{4,5},{5,4},{6,7},{7,6},{8,9},{9,8},{10,11... | collective-permute-start | bytes 172040 | tf_op jit(solution)/shard_map/ppermute | solution.py:70
  24.9 2.2 %collective-permute-done.4.refs_1_ = f32[112,128]{1,0:T(8,128)S(1)} collective-permute-done((f32[112,128]{1,0:T(8,128)S(1)}, f32[112,128]{1,0:T(8,128)S(1)}, u32[]{:S(2)}, u32[]{:S(2)}) %collective-permute-start.4) | collective-permute-done | bytes 57376 | tf_op jit(solution)/shard_map/ppermute | solution.py:70
  27.1 2.1 %collective-permute-done.5.refs_2_ = f32[112,128]{1,0:T(8,128)S(1)} collective-permute-done((f32[112,128]{1,0:T(8,128)S(1)}, f32[112,128]{1,0:T(8,128)S(1)}, u32[]{:S(2)}, u32[]{:S(2)}) %collective-permute-start.5) | collective-permute-done | bytes 57376 | tf_op jit(solution)/shard_map/ppermute | solution.py:70
  29.2 0.0 collective-permute-done.6.refs_3_
  29.2 0.1 collective-permute-start.7
  29.3 1.2 %collective-permute-done.7.other_ref = f32[64,128]{1,0:T(8,128)S(1)} collective-permute-done((f32[64,128]{1,0:T(8,128)S(1)}, f32[64,128]{1,0:T(8,128)S(1)}, u32[]{:S(2)}, u32[]{:S(2)}) %collective-permute-start.7) | collective-permute-done | bytes 32800 | tf_op jit(solution)/shard_map/ppermute | solution.py:70
  30.5 4.0 %feature_grads.1 = (bf16[3072,512]{1,0:T(8,128)(2,1)}, f32[16,128]{1,0:T(8,128)}, f32[16,64]{1,0:T(8,128)}, f32[16,128]{1,0:T(8,128)}, f32[64,64]{1,0:T(8,128)}, /*index=5*/f32[128,128]{1,0:T(8,128)}) custom-call(s32[1]{0:T(128)} %bitcast.where_ref, f32[64,128]{1,0:T(8,128)S(1)} %get-tuple-element.44.mine_ref, ...), custom_call_target="tpu_custom_call" | custom-call | flops 1610612736 | bytes 8650752 | tf_op jit(solution)/shard_map/feature_grads/pallas_call | solution.py:327
  (3 shorter events, 0.1 us)
Async XLA Ops:
  7.7 1.9 %collective-permute-start = (f32[832,128]{1,0:T(8,128)S(1)}, f32[832,128]{1,0:T(8,128)S(1)}, u32[]{:S(2)}, u32[]{:S(2)}) collective-permute-start(f32[832,128]{1,0:T(8,128)S(1)} %get-tuple-element.32), channel_id=1, source_target_pairs={{0,4},{1,5},{2,6},{3,7},{4,0},{5,1},{6,2},{7,3},{8,12},{9,13},{10,... | collective-permute-start | bytes 1277960 | tf_op jit(solution)/shard_map/ppermute | solution.py:70
  9.7 8.2 %collective-permute-start.1 = (f32[256,128]{1,0:T(8,128)S(1)}, f32[256,128]{1,0:T(8,128)S(1)}, u32[]{:S(2)}, u32[]{:S(2)}) collective-permute-start(f32[256,128]{1,0:T(8,128)S(1)} %get-tuple-element.34), channel_id=1, source_target_pairs={{0,24},{1,25},{2,26},{3,27},{4,28},{5,29},{6,30},{7,31},{8,16},{9,... | collective-permute-start | bytes 393224 | tf_op jit(solution)/shard_map/ppermute | solution.py:70
  13.5 6.9 %collective-permute-start.2 = (f32[256,128]{1,0:T(8,128)S(1)}, f32[256,128]{1,0:T(8,128)S(1)}, u32[]{:S(2)}, u32[]{:S(2)}) collective-permute-start(f32[256,128]{1,0:T(8,128)S(1)} %get-tuple-element.35), channel_id=1, source_target_pairs={{0,8},{1,9},{2,10},{3,11},{4,12},{5,13},{6,14},{7,15},{8,0},{9,1},... | collective-permute-start | bytes 393224 | tf_op jit(solution)/shard_map/ppermute | solution.py:70
  14.1 6.3 %collective-permute-start.3 = (f32[256,128]{1,0:T(8,128)S(1)}, f32[256,128]{1,0:T(8,128)S(1)}, u32[]{:S(2)}, u32[]{:S(2)}) collective-permute-start(f32[256,128]{1,0:T(8,128)S(1)} %get-tuple-element.36), channel_id=1, source_target_pairs={{0,16},{1,17},{2,18},{3,19},{4,20},{5,21},{6,22},{7,23},{8,24},{9,... | collective-permute-start | bytes 393224 | tf_op jit(solution)/shard_map/ppermute | solution.py:70
  20.5 6.7 %collective-permute-start.4 = (f32[112,128]{1,0:T(8,128)S(1)}, f32[112,128]{1,0:T(8,128)S(1)}, u32[]{:S(2)}, u32[]{:S(2)}) collective-permute-start(f32[112,128]{1,0:T(8,128)S(1)} %get-tuple-element.41), channel_id=1, source_target_pairs={{0,3},{1,2},{2,1},{3,0},{4,7},{5,6},{6,5},{7,4},{8,11},{9,10},{10,... | collective-permute-start | bytes 172040 | tf_op jit(solution)/shard_map/ppermute | solution.py:70
  24.1 5.1 %collective-permute-start.5 = (f32[112,128]{1,0:T(8,128)S(1)}, f32[112,128]{1,0:T(8,128)S(1)}, u32[]{:S(2)}, u32[]{:S(2)}) collective-permute-start(f32[112,128]{1,0:T(8,128)S(1)} %get-tuple-element.42), channel_id=1, source_target_pairs={{0,2},{1,3},{2,0},{3,1},{4,6},{5,7},{6,4},{7,5},{8,10},{9,11},{10,... | collective-permute-start | bytes 172040 | tf_op jit(solution)/shard_map/ppermute | solution.py:70
  24.1 5.1 %collective-permute-start.6 = (f32[112,128]{1,0:T(8,128)S(1)}, f32[112,128]{1,0:T(8,128)S(1)}, u32[]{:S(2)}, u32[]{:S(2)}) collective-permute-start(f32[112,128]{1,0:T(8,128)S(1)} %get-tuple-element.43), channel_id=1, source_target_pairs={{0,1},{1,0},{2,3},{3,2},{4,5},{5,4},{6,7},{7,6},{8,9},{9,8},{10,11... | collective-permute-start | bytes 172040 | tf_op jit(solution)/shard_map/ppermute | solution.py:70
  29.2 1.3 %collective-permute-start.7 = (f32[64,128]{1,0:T(8,128)S(1)}, f32[64,128]{1,0:T(8,128)S(1)}, u32[]{:S(2)}, u32[]{:S(2)}) collective-permute-start(f32[64,128]{1,0:T(8,128)S(1)} %get-tuple-element.44.mine_ref), channel_id=1, source_target_pairs={{0,4},{1,5},{2,6},{3,7},{4,0},{5,1},{6,2},{7,3},{8,12},{9,13},{10,... | collective-permute-start | bytes 98312 | tf_op jit(solution)/shard_map/ppermute | solution.py:70

commit v14 on v11

--- a/solution.py
+++ b/solution.py
@@ -16,6 +16,7 @@
 SMEM = pl.BlockSpec(memory_space=pltpu.SMEM)
 VMEM_LIMIT = 24 * 1024 * 1024
 SMALL_LIMIT = 4 * 1024 * 1024
+LAPS = 2
 
 
 def exact(a, b, dims=((1,), (0,))):
@@ -297,24 +298,29 @@
     no_f, dn_f = node_out.astype(F32), dn.astype(F32)
     dnb_ref[:nodes_n] = dn
     dnb_ref[nodes_n:] = jnp.zeros((nodes_n, cr), BF16)
-    blank = jnp.zeros((cr, cr), BF16)
-    zero = jnp.zeros((nodes_n, cr), F32)
-    mix_ref[:cr, :cr] = jnp.concatenate([dn_f, zero], axis=0).T.astype(BF16)
-    mix_ref[cr:, :cr] = blank
-    mix_ref[:cr, cr:] = blank
-    mix_ref[cr:, cr:] = jnp.concatenate([no_f, zero], axis=0).T.astype(BF16)
-    copies = []
-    for i, (start, stop) in enumerate(zip(cuts, cuts[1:])):
-        c = pl.ds(start, stop - start)
-        rdp = rdp_ref[c]
-        mixed = mxu(rdp[:, :wide], mix_ref[...])
-        d_proj = (mixed[:, cr:] + scale * mixed[:, :cr]).astype(BF16)
-        d_red = (scale * mxu(rdp[:, wide:], dnb_ref[...])).astype(BF16)
-        both = jnp.concatenate([d_red, d_proj], axis=1)
-        out = g_ref[c].astype(F32) + mxu(both, wcat_ref[...], ((1,), (1,)))
-        out_ref[c] = out.astype(BF16)
-        copies.append(pltpu.make_async_copy(out_ref.at[c], out_hbm.at[c], out_sem.at[i]))
-        copies[-1].start()
+    mix_ref[...] = jnp.zeros_like(mix_ref)
+    mix_ref[:nodes_n, :cr] = dn
+    mix_ref[cr : cr + nodes_n, cr:] = node_out
+    rows = g_ref.shape[0] // LAPS
+
+    def store(lap, part):
+        start, stop = cuts[part : part + 2]
+        c = pl.ds(pl.multiple_of(lap * rows + start, 16), stop - start)
+        return c, pltpu.make_async_copy(out_ref.at[c], out_hbm.at[c], out_sem.at[lap, part])
+
+    @pl.loop(0, LAPS)
+    def _(lap):
+        for part in range(len(cuts) - 1):
+            c, copy = store(lap, part)
+            rdp = rdp_ref[c]
+            mixed = mxu(rdp[:, :wide], mix_ref[...], ((1,), (1,)))
+            d_proj = (mixed[:, cr:] + scale * mixed[:, :cr]).astype(BF16)
+            d_red = (scale * mxu(rdp[:, wide:], dnb_ref[...])).astype(BF16)
+            both = jnp.concatenate([d_red, d_proj], axis=1)
+            out = g_ref[c].astype(F32) + mxu(both, wcat_ref[...], ((1,), (1,)))
+            out_ref[c] = out.astype(BF16)
+            copy.start()
+
     gn_ref[...] = scale * exact(hidden, d_pre, ((0,), (0,)))
     ga_ref[...] = -scale * exact(d_hidden, nodes, ((1,), (1,)))
     size = gr_ref.shape[0]
@@ -324,15 +330,16 @@
         x_red, dn_f, ((1,), (1,))
     )
     ge_ref[...] = scale * exact(with_proj[:, nodes_n:], no_f)
-    for copy in copies:
-        copy.wait()
+    for lap in range(LAPS):
+        for part in range(len(cuts) - 1):
+            store(lap, part)[1].wait()
 
 
 def feature_grads(plan, where, mine, other, sums, adjacency, node_weight, wcat, rdp, g, scale):
     rows, chan = g.shape
     nodes, cr = adjacency.shape[0], node_weight.shape[0]
-    unit = row_block(rows // 12, 256)
-    cuts = sorted({0, *(rows - k * unit for k in (1, 4, 8) if k * unit < rows), rows})
+    lap = rows // LAPS
+    cuts = sorted({0, lap - row_block(lap // 6, 256), lap})
     size = chan // plan.count
     there = [
         pltpu.with_memory_space_constraint(value, pltpu.VMEM)
@@ -354,7 +361,7 @@
             pltpu.VMEM((rows, chan), BF16),
             pltpu.VMEM((2 * cr, 2 * cr), BF16),
             pltpu.VMEM((2 * nodes, cr), BF16),
-            pltpu.SemaphoreType.DMA((len(cuts) - 1,)),
+            pltpu.SemaphoreType.DMA((LAPS, len(cuts) - 1)),
         ],
         compiler_params=params(),
         cost_estimate=cost(2 * rows * 4 * 65536, rows * chan * 4 + rows * 768),

time: 34.1 us -> 34.6 us (1.015)
  Pallas kernels: 13.3 us -> 13.8 us
    pallas_call x1, Pallas kernels: 4.13 us -> 4.63 us  [feature_grads(): pl.pallas_call(functools.partial(feature_kernel, cuts, scale, plan), in_s...]
where the time goes in v14:
time: 34.6 us; the launch traced here: 34.4 us
  Pallas kernels  13.8 us (40%)
  waiting for transfers between devices  10.6 us (31%)
  starting transfers between devices  9.33 us (27%)
  between operations  0.68 us (2%)
    ppermute x8, waiting for transfers between devices, swap(): return lax.ppermute(value, AXES, [(d, d ^ mask) for d in range(self.count)])  10.6 us
    ppermute x8, starting transfers between devices, swap(): return lax.ppermute(value, AXES, [(d, d ^ mask) for d in range(self.count)])  9.33 us
    pallas_call x1, Pallas kernels, gather(): pl.pallas_call(functools.partial(gather_kernel, plan, step, sorted_here),...  6.31 us
    pallas_call x1, Pallas kernels, feature_grads(): pl.pallas_call(functools.partial(feature_kernel, cuts, scale, plan), in_s...  4.63 us
    pallas_call x1, Pallas kernels, fetch(): pl.pallas_call(fetch_kernel, in_specs=[pl.BlockSpec(memory_space=pl.ANY)]...  2.79 us
  transfers between devices with their start and end apart: 8, of which 7 were waited for; matrix products, arithmetic and copies ran while one was open for 0% of the time, Pallas kernels for 8%

profile of v14, /device:TPU:0, one launch (start us, length us, event | category | flops | bytes accessed | tf_op | source)
XLA Modules:
  0.0 34.4 jit_solution(18073340588479184049)
XLA Ops:
  0.6 6.3 %gather.1 = (bf16[3072,384]{1,0:T(8,128)(2,1)}, bf16[512,256]{1,0:T(8,128)(2,1)}, f32[832,128]{1,0:T(8,128)S(1)}, f32[832,128]{1,0:T(8,128)S(1)}) custom-call(s32[1]{0:T(128)} %bitcast.where_ref, bf16[3072,512]{1,0:T(8,128)(2,1)} %bitcast.13, bf16[3072,512]{1,0:T(8,128)(2,1)} %bitcast.11, bf16[512,128]{1,0:T(8,128)(2,1)} %wr_hbm.1, ...), custom_call_target="tpu_custom_call" | custom-call | flops 3221225472 | bytes 8650752 | tf_op jit(solution)/shard_map/gather/pallas_call | solution.py:200
  7.0 0.5 %collective-permute-start = (f32[832,128]{1,0:T(8,128)S(1)}, f32[832,128]{1,0:T(8,128)S(1)}, u32[]{:S(2)}, u32[]{:S(2)}) collective-permute-start(f32[832,128]{1,0:T(8,128)S(1)} %get-tuple-element.32), channel_id=1, source_target_pairs={{0,4},{1,5},{2,6},{3,7},{4,0},{5,1},{6,2},{7,3},{8,12},{9,13},{10,... | collective-permute-start | bytes 1277960 | tf_op jit(solution)/shard_map/ppermute | solution.py:71
  7.5 1.4 %collective-permute-done.refs_1_ = f32[832,128]{1,0:T(8,128)S(1)} collective-permute-done((f32[832,128]{1,0:T(8,128)S(1)}, f32[832,128]{1,0:T(8,128)S(1)}, u32[]{:S(2)}, u32[]{:S(2)}) %collective-permute-start) | collective-permute-done | bytes 426016 | tf_op jit(solution)/shard_map/ppermute | solution.py:71
  8.9 3.9 %collective-permute-start.1 = (f32[256,128]{1,0:T(8,128)S(1)}, f32[256,128]{1,0:T(8,128)S(1)}, u32[]{:S(2)}, u32[]{:S(2)}) collective-permute-start(f32[256,128]{1,0:T(8,128)S(1)} %get-tuple-element.34), channel_id=1, source_target_pairs={{0,24},{1,25},{2,26},{3,27},{4,28},{5,29},{6,30},{7,31},{8,16},{9,... | collective-permute-start | bytes 393224 | tf_op jit(solution)/shard_map/ppermute | solution.py:71
  12.8 0.5 %collective-permute-start.2 = (f32[256,128]{1,0:T(8,128)S(1)}, f32[256,128]{1,0:T(8,128)S(1)}, u32[]{:S(2)}, u32[]{:S(2)}) collective-permute-start(f32[256,128]{1,0:T(8,128)S(1)} %get-tuple-element.35), channel_id=1, source_target_pairs={{0,8},{1,9},{2,10},{3,11},{4,12},{5,13},{6,14},{7,15},{8,0},{9,1},... | collective-permute-start | bytes 393224 | tf_op jit(solution)/shard_map/ppermute | solution.py:71
  13.3 0.1 collective-permute-start.3
  13.4 2.8 %fetch.1 = (f32[64,64]{1,0:T(8,128)S(1)}, f32[128,128]{1,0:T(8,128)S(1)}, bf16[512,256]{1,0:T(8,128)(2,1)S(1)}, bf16[3072,384]{1,0:T(8,128)(2,1)S(1)}, bf16[3072,512]{1,0:T(8,128)(2,1)S(1)}) custom-call(f32[256,128]{1,0:T(8,128)S(1)} %get-tuple-element.33._.refs_0_, f32[64,64]{1,0:T(8,128)} %refs_0_.1, f32[128,128]{1,0:T(8,128)} %refs_1_.1, ...), custom_call_target="tpu_custom_call" | custom-call | bytes 5849088 | tf_op jit(solution)/shard_map/fetch/pallas_call | solution.py:268
  16.2 0.8 %collective-permute-done.1.refs_1_ = f32[256,128]{1,0:T(8,128)S(1)} collective-permute-done((f32[256,128]{1,0:T(8,128)S(1)}, f32[256,128]{1,0:T(8,128)S(1)}, u32[]{:S(2)}, u32[]{:S(2)}) %collective-permute-start.1) | collective-permute-done | bytes 131104 | tf_op jit(solution)/shard_map/ppermute | solution.py:71
  17.1 2.6 %collective-permute-done.2.refs_2_ = f32[256,128]{1,0:T(8,128)S(1)} collective-permute-done((f32[256,128]{1,0:T(8,128)S(1)}, f32[256,128]{1,0:T(8,128)S(1)}, u32[]{:S(2)}, u32[]{:S(2)}) %collective-permute-start.2) | collective-permute-done | bytes 131104 | tf_op jit(solution)/shard_map/ppermute | solution.py:71
  19.7 0.0 collective-permute-done.3.refs_3_
  19.7 2.6 %collective-permute-start.4 = (f32[112,128]{1,0:T(8,128)S(1)}, f32[112,128]{1,0:T(8,128)S(1)}, u32[]{:S(2)}, u32[]{:S(2)}) collective-permute-start(f32[112,128]{1,0:T(8,128)S(1)} %get-tuple-element.41), channel_id=1, source_target_pairs={{0,2},{1,3},{2,0},{3,1},{4,6},{5,7},{6,4},{7,5},{8,10},{9,11},{10,... | collective-permute-start | bytes 172040 | tf_op jit(solution)/shard_map/ppermute | solution.py:71
  22.4 1.3 %collective-permute-start.5 = (f32[112,128]{1,0:T(8,128)S(1)}, f32[112,128]{1,0:T(8,128)S(1)}, u32[]{:S(2)}, u32[]{:S(2)}) collective-permute-start(f32[112,128]{1,0:T(8,128)S(1)} %get-tuple-element.42), channel_id=1, source_target_pairs={{0,3},{1,2},{2,1},{3,0},{4,7},{5,6},{6,5},{7,4},{8,11},{9,10},{10,... | collective-permute-start | bytes 172040 | tf_op jit(solution)/shard_map/ppermute | solution.py:71
  23.7 0.2 collective-permute-start.6
  23.9 1.1 %collective-permute-done.4.refs_1_ = f32[112,128]{1,0:T(8,128)S(1)} collective-permute-done((f32[112,128]{1,0:T(8,128)S(1)}, f32[112,128]{1,0:T(8,128)S(1)}, u32[]{:S(2)}, u32[]{:S(2)}) %collective-permute-start.4) | collective-permute-done | bytes 57376 | tf_op jit(solution)/shard_map/ppermute | solution.py:71
  25.0 3.4 %collective-permute-done.5.refs_2_ = f32[112,128]{1,0:T(8,128)S(1)} collective-permute-done((f32[112,128]{1,0:T(8,128)S(1)}, f32[112,128]{1,0:T(8,128)S(1)}, u32[]{:S(2)}, u32[]{:S(2)}) %collective-permute-start.5) | collective-permute-done | bytes 57376 | tf_op jit(solution)/shard_map/ppermute | solution.py:71
  28.4 0.1 collective-permute-done.6.refs_3_
  28.5 0.1 collective-permute-start.7
  28.6 1.2 %collective-permute-done.7.other_ref = f32[64,128]{1,0:T(8,128)S(1)} collective-permute-done((f32[64,128]{1,0:T(8,128)S(1)}, f32[64,128]{1,0:T(8,128)S(1)}, u32[]{:S(2)}, u32[]{:S(2)}) %collective-permute-start.7) | collective-permute-done | bytes 32800 | tf_op jit(solution)/shard_map/ppermute | solution.py:71
  29.8 4.6 %feature_grads.1 = (bf16[3072,512]{1,0:T(8,128)(2,1)}, f32[16,128]{1,0:T(8,128)}, f32[16,64]{1,0:T(8,128)}, f32[16,128]{1,0:T(8,128)}, f32[64,64]{1,0:T(8,128)}, /*index=5*/f32[128,128]{1,0:T(8,128)}) custom-call(s32[1]{0:T(128)} %bitcast.where_ref, f32[64,128]{1,0:T(8,128)S(1)} %get-tuple-element.44.mine_ref, ...), custom_call_target="tpu_custom_call" | custom-call | flops 1610612736 | bytes 8650752 | tf_op jit(solution)/shard_map/feature_grads/pallas_call | solution.py:348
  (3 shorter events, 0.1 us)
Async XLA Ops:
  7.0 1.9 %collective-permute-start = (f32[832,128]{1,0:T(8,128)S(1)}, f32[832,128]{1,0:T(8,128)S(1)}, u32[]{:S(2)}, u32[]{:S(2)}) collective-permute-start(f32[832,128]{1,0:T(8,128)S(1)} %get-tuple-element.32), channel_id=1, source_target_pairs={{0,4},{1,5},{2,6},{3,7},{4,0},{5,1},{6,2},{7,3},{8,12},{9,13},{10,... | collective-permute-start | bytes 1277960 | tf_op jit(solution)/shard_map/ppermute | solution.py:71
  8.9 8.2 %collective-permute-start.1 = (f32[256,128]{1,0:T(8,128)S(1)}, f32[256,128]{1,0:T(8,128)S(1)}, u32[]{:S(2)}, u32[]{:S(2)}) collective-permute-start(f32[256,128]{1,0:T(8,128)S(1)} %get-tuple-element.34), channel_id=1, source_target_pairs={{0,24},{1,25},{2,26},{3,27},{4,28},{5,29},{6,30},{7,31},{8,16},{9,... | collective-permute-start | bytes 393224 | tf_op jit(solution)/shard_map/ppermute | solution.py:71
  12.8 6.9 %collective-permute-start.2 = (f32[256,128]{1,0:T(8,128)S(1)}, f32[256,128]{1,0:T(8,128)S(1)}, u32[]{:S(2)}, u32[]{:S(2)}) collective-permute-start(f32[256,128]{1,0:T(8,128)S(1)} %get-tuple-element.35), channel_id=1, source_target_pairs={{0,8},{1,9},{2,10},{3,11},{4,12},{5,13},{6,14},{7,15},{8,0},{9,1},... | collective-permute-start | bytes 393224 | tf_op jit(solution)/shard_map/ppermute | solution.py:71
  13.3 6.3 %collective-permute-start.3 = (f32[256,128]{1,0:T(8,128)S(1)}, f32[256,128]{1,0:T(8,128)S(1)}, u32[]{:S(2)}, u32[]{:S(2)}) collective-permute-start(f32[256,128]{1,0:T(8,128)S(1)} %get-tuple-element.36), channel_id=1, source_target_pairs={{0,16},{1,17},{2,18},{3,19},{4,20},{5,21},{6,22},{7,23},{8,24},{9,... | collective-permute-start | bytes 393224 | tf_op jit(solution)/shard_map/ppermute | solution.py:71
  19.7 5.3 %collective-permute-start.4 = (f32[112,128]{1,0:T(8,128)S(1)}, f32[112,128]{1,0:T(8,128)S(1)}, u32[]{:S(2)}, u32[]{:S(2)}) collective-permute-start(f32[112,128]{1,0:T(8,128)S(1)} %get-tuple-element.41), channel_id=1, source_target_pairs={{0,2},{1,3},{2,0},{3,1},{4,6},{5,7},{6,4},{7,5},{8,10},{9,11},{10,... | collective-permute-start | bytes 172040 | tf_op jit(solution)/shard_map/ppermute | solution.py:71
  22.4 6.1 %collective-permute-start.5 = (f32[112,128]{1,0:T(8,128)S(1)}, f32[112,128]{1,0:T(8,128)S(1)}, u32[]{:S(2)}, u32[]{:S(2)}) collective-permute-start(f32[112,128]{1,0:T(8,128)S(1)} %get-tuple-element.42), channel_id=1, source_target_pairs={{0,3},{1,2},{2,1},{3,0},{4,7},{5,6},{6,5},{7,4},{8,11},{9,10},{10,... | collective-permute-start | bytes 172040 | tf_op jit(solution)/shard_map/ppermute | solution.py:71
  23.7 4.8 %collective-permute-start.6 = (f32[112,128]{1,0:T(8,128)S(1)}, f32[112,128]{1,0:T(8,128)S(1)}, u32[]{:S(2)}, u32[]{:S(2)}) collective-permute-start(f32[112,128]{1,0:T(8,128)S(1)} %get-tuple-element.43), channel_id=1, source_target_pairs={{0,1},{1,0},{2,3},{3,2},{4,5},{5,4},{6,7},{7,6},{8,9},{9,8},{10,11... | collective-permute-start | bytes 172040 | tf_op jit(solution)/shard_map/ppermute | solution.py:71
  28.5 1.3 %collective-permute-start.7 = (f32[64,128]{1,0:T(8,128)S(1)}, f32[64,128]{1,0:T(8,128)S(1)}, u32[]{:S(2)}, u32[]{:S(2)}) collective-permute-start(f32[64,128]{1,0:T(8,128)S(1)} %get-tuple-element.44.mine_ref), channel_id=1, source_target_pairs={{0,4},{1,5},{2,6},{3,7},{4,0},{5,1},{6,2},{7,3},{8,12},{9,13},{10,... | collective-permute-start | bytes 98312 | tf_op jit(solution)/shard_map/ppermute | solution.py:71

commit v15 on v11

--- a/solution.py
+++ b/solution.py
@@ -297,17 +297,14 @@
     no_f, dn_f = node_out.astype(F32), dn.astype(F32)
     dnb_ref[:nodes_n] = dn
     dnb_ref[nodes_n:] = jnp.zeros((nodes_n, cr), BF16)
-    blank = jnp.zeros((cr, cr), BF16)
-    zero = jnp.zeros((nodes_n, cr), F32)
-    mix_ref[:cr, :cr] = jnp.concatenate([dn_f, zero], axis=0).T.astype(BF16)
-    mix_ref[cr:, :cr] = blank
-    mix_ref[:cr, cr:] = blank
-    mix_ref[cr:, cr:] = jnp.concatenate([no_f, zero], axis=0).T.astype(BF16)
+    mix_ref[...] = jnp.zeros_like(mix_ref)
+    mix_ref[:nodes_n, :cr] = dn
+    mix_ref[cr : cr + nodes_n, cr:] = node_out
     copies = []
     for i, (start, stop) in enumerate(zip(cuts, cuts[1:])):
         c = pl.ds(start, stop - start)
         rdp = rdp_ref[c]
-        mixed = mxu(rdp[:, :wide], mix_ref[...])
+        mixed = mxu(rdp[:, :wide], mix_ref[...], ((1,), (1,)))
         d_proj = (mixed[:, cr:] + scale * mixed[:, :cr]).astype(BF16)
         d_red = (scale * mxu(rdp[:, wide:], dnb_ref[...])).astype(BF16)
         both = jnp.concatenate([d_red, d_proj], axis=1)

time: 34.1 us -> 34 us (level)
  no operation moved by 1% of the time
where the time goes in v15:
time: 34 us; the launch traced here: 33.8 us
  Pallas kernels  13.2 us (39%)
  waiting for transfers between devices  10.6 us (31%)
  starting transfers between devices  9.33 us (27%)
  between operations  0.68 us (2%)
    ppermute x8, waiting for transfers between devices, swap(): return lax.ppermute(value, AXES, [(d, d ^ mask) for d in range(self.count)])  10.6 us
    ppermute x8, starting transfers between devices, swap(): return lax.ppermute(value, AXES, [(d, d ^ mask) for d in range(self.count)])  9.33 us
    pallas_call x1, Pallas kernels, gather(): pl.pallas_call(functools.partial(gather_kernel, plan, step, sorted_here),...  6.31 us
    pallas_call x1, Pallas kernels, feature_grads(): pl.pallas_call(functools.partial(feature_kernel, cuts, scale, plan), in_s...  4.03 us
    pallas_call x1, Pallas kernels, fetch(): pl.pallas_call(fetch_kernel, in_specs=[pl.BlockSpec(memory_space=pl.ANY)]...  2.79 us
  transfers between devices with their start and end apart: 8, of which 7 were waited for; matrix products, arithmetic and copies ran while one was open for 0% of the time, Pallas kernels for 8%

profile of v15, /device:TPU:0, one launch (start us, length us, event | category | flops | bytes accessed | tf_op | source)
XLA Modules:
  0.0 33.8 jit_solution(10653569262018454878)
XLA Ops:
  0.6 6.3 %gather.1 = (bf16[3072,384]{1,0:T(8,128)(2,1)}, bf16[512,256]{1,0:T(8,128)(2,1)}, f32[832,128]{1,0:T(8,128)S(1)}, f32[832,128]{1,0:T(8,128)S(1)}) custom-call(s32[1]{0:T(128)} %bitcast.where_ref, bf16[3072,512]{1,0:T(8,128)(2,1)} %bitcast.13, bf16[3072,512]{1,0:T(8,128)(2,1)} %bitcast.11, bf16[512,128]{1,0:T(8,128)(2,1)} %wr_hbm.1, ...), custom_call_target="tpu_custom_call" | custom-call | flops 3221225472 | bytes 8650752 | tf_op jit(solution)/shard_map/gather/pallas_call | solution.py:199
  7.0 0.5 %collective-permute-start = (f32[832,128]{1,0:T(8,128)S(1)}, f32[832,128]{1,0:T(8,128)S(1)}, u32[]{:S(2)}, u32[]{:S(2)}) collective-permute-start(f32[832,128]{1,0:T(8,128)S(1)} %get-tuple-element.32), channel_id=1, source_target_pairs={{0,4},{1,5},{2,6},{3,7},{4,0},{5,1},{6,2},{7,3},{8,12},{9,13},{10,... | collective-permute-start | bytes 1277960 | tf_op jit(solution)/shard_map/ppermute | solution.py:70
  7.5 1.4 %collective-permute-done.refs_1_ = f32[832,128]{1,0:T(8,128)S(1)} collective-permute-done((f32[832,128]{1,0:T(8,128)S(1)}, f32[832,128]{1,0:T(8,128)S(1)}, u32[]{:S(2)}, u32[]{:S(2)}) %collective-permute-start) | collective-permute-done | bytes 426016 | tf_op jit(solution)/shard_map/ppermute | solution.py:70
  8.9 3.9 %collective-permute-start.1 = (f32[256,128]{1,0:T(8,128)S(1)}, f32[256,128]{1,0:T(8,128)S(1)}, u32[]{:S(2)}, u32[]{:S(2)}) collective-permute-start(f32[256,128]{1,0:T(8,128)S(1)} %get-tuple-element.34), channel_id=1, source_target_pairs={{0,24},{1,25},{2,26},{3,27},{4,28},{5,29},{6,30},{7,31},{8,16},{9,... | collective-permute-start | bytes 393224 | tf_op jit(solution)/shard_map/ppermute | solution.py:70
  12.8 0.5 %collective-permute-start.2 = (f32[256,128]{1,0:T(8,128)S(1)}, f32[256,128]{1,0:T(8,128)S(1)}, u32[]{:S(2)}, u32[]{:S(2)}) collective-permute-start(f32[256,128]{1,0:T(8,128)S(1)} %get-tuple-element.35), channel_id=1, source_target_pairs={{0,8},{1,9},{2,10},{3,11},{4,12},{5,13},{6,14},{7,15},{8,0},{9,1},... | collective-permute-start | bytes 393224 | tf_op jit(solution)/shard_map/ppermute | solution.py:70
  13.3 0.1 collective-permute-start.3
  13.4 2.8 %fetch.1 = (f32[64,64]{1,0:T(8,128)S(1)}, f32[128,128]{1,0:T(8,128)S(1)}, bf16[512,256]{1,0:T(8,128)(2,1)S(1)}, bf16[3072,384]{1,0:T(8,128)(2,1)S(1)}, bf16[3072,512]{1,0:T(8,128)(2,1)S(1)}) custom-call(f32[256,128]{1,0:T(8,128)S(1)} %get-tuple-element.33._.refs_0_, f32[64,64]{1,0:T(8,128)} %refs_0_.1, f32[128,128]{1,0:T(8,128)} %refs_1_.1, ...), custom_call_target="tpu_custom_call" | custom-call | bytes 5849088 | tf_op jit(solution)/shard_map/fetch/pallas_call | solution.py:267
  16.2 0.8 %collective-permute-done.1.refs_1_ = f32[256,128]{1,0:T(8,128)S(1)} collective-permute-done((f32[256,128]{1,0:T(8,128)S(1)}, f32[256,128]{1,0:T(8,128)S(1)}, u32[]{:S(2)}, u32[]{:S(2)}) %collective-permute-start.1) | collective-permute-done | bytes 131104 | tf_op jit(solution)/shard_map/ppermute | solution.py:70
  17.1 2.6 %collective-permute-done.2.refs_2_ = f32[256,128]{1,0:T(8,128)S(1)} collective-permute-done((f32[256,128]{1,0:T(8,128)S(1)}, f32[256,128]{1,0:T(8,128)S(1)}, u32[]{:S(2)}, u32[]{:S(2)}) %collective-permute-start.2) | collective-permute-done | bytes 131104 | tf_op jit(solution)/shard_map/ppermute | solution.py:70
  19.7 0.0 collective-permute-done.3.refs_3_
  19.7 2.6 %collective-permute-start.4 = (f32[112,128]{1,0:T(8,128)S(1)}, f32[112,128]{1,0:T(8,128)S(1)}, u32[]{:S(2)}, u32[]{:S(2)}) collective-permute-start(f32[112,128]{1,0:T(8,128)S(1)} %get-tuple-element.41), channel_id=1, source_target_pairs={{0,2},{1,3},{2,0},{3,1},{4,6},{5,7},{6,4},{7,5},{8,10},{9,11},{10,... | collective-permute-start | bytes 172040 | tf_op jit(solution)/shard_map/ppermute | solution.py:70
  22.4 1.3 %collective-permute-start.5 = (f32[112,128]{1,0:T(8,128)S(1)}, f32[112,128]{1,0:T(8,128)S(1)}, u32[]{:S(2)}, u32[]{:S(2)}) collective-permute-start(f32[112,128]{1,0:T(8,128)S(1)} %get-tuple-element.42), channel_id=1, source_target_pairs={{0,3},{1,2},{2,1},{3,0},{4,7},{5,6},{6,5},{7,4},{8,11},{9,10},{10,... | collective-permute-start | bytes 172040 | tf_op jit(solution)/shard_map/ppermute | solution.py:70
  23.7 0.2 collective-permute-start.6
  23.9 1.1 %collective-permute-done.4.refs_1_ = f32[112,128]{1,0:T(8,128)S(1)} collective-permute-done((f32[112,128]{1,0:T(8,128)S(1)}, f32[112,128]{1,0:T(8,128)S(1)}, u32[]{:S(2)}, u32[]{:S(2)}) %collective-permute-start.4) | collective-permute-done | bytes 57376 | tf_op jit(solution)/shard_map/ppermute | solution.py:70
  25.0 3.4 %collective-permute-done.5.refs_2_ = f32[112,128]{1,0:T(8,128)S(1)} collective-permute-done((f32[112,128]{1,0:T(8,128)S(1)}, f32[112,128]{1,0:T(8,128)S(1)}, u32[]{:S(2)}, u32[]{:S(2)}) %collective-permute-start.5) | collective-permute-done | bytes 57376 | tf_op jit(solution)/shard_map/ppermute | solution.py:70
  28.4 0.1 collective-permute-done.6.refs_3_
  28.5 0.1 collective-permute-start.7
  28.6 1.2 %collective-permute-done.7.other_ref = f32[64,128]{1,0:T(8,128)S(1)} collective-permute-done((f32[64,128]{1,0:T(8,128)S(1)}, f32[64,128]{1,0:T(8,128)S(1)}, u32[]{:S(2)}, u32[]{:S(2)}) %collective-permute-start.7) | collective-permute-done | bytes 32800 | tf_op jit(solution)/shard_map/ppermute | solution.py:70
  29.8 4.0 %feature_grads.1 = (bf16[3072,512]{1,0:T(8,128)(2,1)}, f32[16,128]{1,0:T(8,128)}, f32[16,64]{1,0:T(8,128)}, f32[16,128]{1,0:T(8,128)}, f32[64,64]{1,0:T(8,128)}, /*index=5*/f32[128,128]{1,0:T(8,128)}) custom-call(s32[1]{0:T(128)} %bitcast.where_ref, f32[64,128]{1,0:T(8,128)S(1)} %get-tuple-element.44.mine_ref, ...), custom_call_target="tpu_custom_call" | custom-call | flops 1610612736 | bytes 8650752 | tf_op jit(solution)/shard_map/feature_grads/pallas_call | solution.py:338
  (3 shorter events, 0.1 us)
Async XLA Ops:
  7.0 1.9 %collective-permute-start = (f32[832,128]{1,0:T(8,128)S(1)}, f32[832,128]{1,0:T(8,128)S(1)}, u32[]{:S(2)}, u32[]{:S(2)}) collective-permute-start(f32[832,128]{1,0:T(8,128)S(1)} %get-tuple-element.32), channel_id=1, source_target_pairs={{0,4},{1,5},{2,6},{3,7},{4,0},{5,1},{6,2},{7,3},{8,12},{9,13},{10,... | collective-permute-start | bytes 1277960 | tf_op jit(solution)/shard_map/ppermute | solution.py:70
  8.9 8.2 %collective-permute-start.1 = (f32[256,128]{1,0:T(8,128)S(1)}, f32[256,128]{1,0:T(8,128)S(1)}, u32[]{:S(2)}, u32[]{:S(2)}) collective-permute-start(f32[256,128]{1,0:T(8,128)S(1)} %get-tuple-element.34), channel_id=1, source_target_pairs={{0,24},{1,25},{2,26},{3,27},{4,28},{5,29},{6,30},{7,31},{8,16},{9,... | collective-permute-start | bytes 393224 | tf_op jit(solution)/shard_map/ppermute | solution.py:70
  12.8 6.9 %collective-permute-start.2 = (f32[256,128]{1,0:T(8,128)S(1)}, f32[256,128]{1,0:T(8,128)S(1)}, u32[]{:S(2)}, u32[]{:S(2)}) collective-permute-start(f32[256,128]{1,0:T(8,128)S(1)} %get-tuple-element.35), channel_id=1, source_target_pairs={{0,8},{1,9},{2,10},{3,11},{4,12},{5,13},{6,14},{7,15},{8,0},{9,1},... | collective-permute-start | bytes 393224 | tf_op jit(solution)/shard_map/ppermute | solution.py:70
  13.3 6.3 %collective-permute-start.3 = (f32[256,128]{1,0:T(8,128)S(1)}, f32[256,128]{1,0:T(8,128)S(1)}, u32[]{:S(2)}, u32[]{:S(2)}) collective-permute-start(f32[256,128]{1,0:T(8,128)S(1)} %get-tuple-element.36), channel_id=1, source_target_pairs={{0,16},{1,17},{2,18},{3,19},{4,20},{5,21},{6,22},{7,23},{8,24},{9,... | collective-permute-start | bytes 393224 | tf_op jit(solution)/shard_map/ppermute | solution.py:70
  19.7 5.3 %collective-permute-start.4 = (f32[112,128]{1,0:T(8,128)S(1)}, f32[112,128]{1,0:T(8,128)S(1)}, u32[]{:S(2)}, u32[]{:S(2)}) collective-permute-start(f32[112,128]{1,0:T(8,128)S(1)} %get-tuple-element.41), channel_id=1, source_target_pairs={{0,2},{1,3},{2,0},{3,1},{4,6},{5,7},{6,4},{7,5},{8,10},{9,11},{10,... | collective-permute-start | bytes 172040 | tf_op jit(solution)/shard_map/ppermute | solution.py:70
  22.4 6.1 %collective-permute-start.5 = (f32[112,128]{1,0:T(8,128)S(1)}, f32[112,128]{1,0:T(8,128)S(1)}, u32[]{:S(2)}, u32[]{:S(2)}) collective-permute-start(f32[112,128]{1,0:T(8,128)S(1)} %get-tuple-element.42), channel_id=1, source_target_pairs={{0,3},{1,2},{2,1},{3,0},{4,7},{5,6},{6,5},{7,4},{8,11},{9,10},{10,... | collective-permute-start | bytes 172040 | tf_op jit(solution)/shard_map/ppermute | solution.py:70
  23.7 4.8 %collective-permute-start.6 = (f32[112,128]{1,0:T(8,128)S(1)}, f32[112,128]{1,0:T(8,128)S(1)}, u32[]{:S(2)}, u32[]{:S(2)}) collective-permute-start(f32[112,128]{1,0:T(8,128)S(1)} %get-tuple-element.43), channel_id=1, source_target_pairs={{0,1},{1,0},{2,3},{3,2},{4,5},{5,4},{6,7},{7,6},{8,9},{9,8},{10,11... | collective-permute-start | bytes 172040 | tf_op jit(solution)/shard_map/ppermute | solution.py:70
  28.5 1.3 %collective-permute-start.7 = (f32[64,128]{1,0:T(8,128)S(1)}, f32[64,128]{1,0:T(8,128)S(1)}, u32[]{:S(2)}, u32[]{:S(2)}) collective-permute-start(f32[64,128]{1,0:T(8,128)S(1)} %get-tuple-element.44.mine_ref), channel_id=1, source_target_pairs={{0,4},{1,5},{2,6},{3,7},{4,0},{5,1},{6,2},{7,3},{8,12},{9,13},{10,... | collective-permute-start | bytes 98312 | tf_op jit(solution)/shard_map/ppermute | solution.py:70

commit v16 on v15

--- a/solution.py
+++ b/solution.py
@@ -71,13 +71,13 @@
 
 
 def gather_kernel(
-    plan, step, sorted_here, where_ref, x_hbm, g_hbm, wr_hbm, wpt_hbm, we_hbm, rdp_hbm, wcat_hbm, *rest
+    plan, step, sorted_here, where_ref, x_hbm, g_hbm, wr_hbm, wpt_hbm, we_hbm, rdp_ref, cat_ref, *rest
 ):
     if sorted_here:
         kept_ref, sent_ref, turned_ref, *rest = rest
     else:
         keep_ref, send_ref, turned_ref, *rest = rest
-    x_ref, g_ref, rdp_ref, cat_ref, wpt_ref, we_ref, sums_ref, term_ref, small_sem, in_sem, out_sem = rest
+    x_ref, g_ref, wpt_ref, we_ref, sums_ref, term_ref, small_sem, in_sem = rest
     rows = x_ref.shape[0]
     cr = we_ref.shape[1]
     nodes = wpt_ref.shape[0]
@@ -90,7 +90,6 @@
         move(we_hbm, we_ref, small_sem.at[2]),
     ]
     load_cuts = sorted({0, min(1, count), min(2, count), count})
-    store_cuts = sorted({0, max(count - 2, 0), max(count - 1, 0), count})
     span = lambda cuts, i: pl.ds(cuts[i] * step, (cuts[i + 1] - cuts[i]) * step)
     loads = [
         (
@@ -98,10 +97,6 @@
             move(g_hbm.at[span(load_cuts, i)], g_ref.at[span(load_cuts, i)], in_sem.at[1, i]),
         )
         for i in range(len(load_cuts) - 1)
-    ]
-    stores = [
-        move(rdp_ref.at[span(store_cuts, i)], rdp_hbm.at[span(store_cuts, i)], out_sem.at[i])
-        for i in range(len(store_cuts) - 1)
     ]
     for copy in (*small, *loads[0]):
         copy.start()
@@ -111,8 +106,6 @@
     small[1].wait()
     padded = jnp.concatenate([wpt_ref[...], jnp.zeros_like(wpt_ref)], axis=0)
     cat_ref[:, cr:] = padded.T
-    keep_weights = move(cat_ref, wcat_hbm, small_sem.at[3])
-    keep_weights.start()
     small[2].wait()
 
     @pl.loop(0, count)
@@ -137,8 +130,6 @@
         sums_ref[: wide + nodes] += mxu(turned[: wide + nodes], x)
         sums_ref[wide + nodes :] += mxu(proj, g)
         term_ref[...] += mxu(proj, rdp[:, :wide])
-        for k, copy in enumerate(stores):
-            pl.when(i == store_cuts[k + 1] - 1)(copy.start)
 
     me = where_ref[0]
     side = plan.side(me)
@@ -160,8 +151,6 @@
                 for lane in range(0, block.shape[1], cr):
                     out_ref[to : to + size] = block[:, lane : lane + cr]
                     to += size
-    for copy in (keep_weights, *stores):
-        copy.wait()
 
 
 def gather(plan, where, x, g, wr, wpt, we):
@@ -173,8 +162,8 @@
     size = chan // plan.count
     sorted_here = size % 8 == 0
     outs = [
-        (HBM, pltpu.HBM((rows, width), BF16)),
-        (HBM, pltpu.HBM((chan, cr + 2 * nodes), BF16)),
+        (VMEM, pltpu.VMEM((rows, width), BF16)),
+        (VMEM, pltpu.VMEM((chan, cr + 2 * nodes), BF16)),
     ]
     scratch = []
     if sorted_here:
@@ -186,15 +175,12 @@
     scratch += [
         pltpu.VMEM((rows, chan), BF16),
         pltpu.VMEM((rows, chan), BF16),
-        pltpu.VMEM((rows, width), BF16),
-        pltpu.VMEM((chan, cr + 2 * nodes), BF16),
         pltpu.VMEM(wpt.shape, BF16),
         pltpu.VMEM(we.shape, BF16),
         pltpu.VMEM((width, chan), F32),
         pltpu.VMEM((nodes, 2 * cr), F32),
-        pltpu.SemaphoreType.DMA((4,)),
+        pltpu.SemaphoreType.DMA((3,)),
         pltpu.SemaphoreType.DMA((2, 3)),
-        pltpu.SemaphoreType.DMA((3,)),
     ]
     rdp, wcat, kept, sent, *sums = pl.pallas_call(
         functools.partial(gather_kernel, plan, step, sorted_here),
@@ -379,12 +365,12 @@
     for group in plan.groups:
         parts = step(head, len(group), terms, ready[:1] if ready else ())
         terms = [plan.swap(part, mask) if mask else part for part, mask in zip(parts, group)]
-        ready = ready or fetch(parts[0], adjacency, node_weight, wcat, rdp, flat_g)
+        ready = ready or fetch(parts[0], adjacency, node_weight, flat_g)
     mine, sums = step(head, 1, terms)
     other = plan.swap(mine, plan.core)
 
     flat_out, grad_reduce, grad_project, grad_expand, grad_adjacency, grad_node = feature_grads(
-        plan, where, mine, other, sums, *ready, scale
+        plan, where, mine, other, sums, *ready[:2], wcat, rdp, ready[2], scale
     )
     grad_features = flat_out.reshape(size_x, size_z, size_y, chan).transpose(0, 2, 1, 3)
     return (grad_features, grad_reduce, grad_project, grad_expand, grad_adjacency, grad_node)

time: 34 us -> 33.8 us (level)
  Pallas kernels: 13.2 us -> 12.3 us
  waiting for transfers between devices: 10.6 us -> 11.4 us
    ppermute x8, waiting for transfers between devices: 10.6 us -> 11.4 us  [swap(): return lax.ppermute(value, AXES, [(d, d ^ mask) for d in range(self.count)])]
    pallas_call x1, Pallas kernels: 2.79 us -> 1.97 us  [fetch(): pl.pallas_call(fetch_kernel, in_specs=[pl.BlockSpec(memory_space=pl.ANY)]...]
  transfers between devices with their start and end apart: 8 -> 8, of which waited for: 7 -> 7; matrix products, arithmetic and copies ran while one was open for 0% -> 0% of each run, Pallas kernels for 8% -> 6%
where the time goes in v16:
time: 33.8 us; the launch traced here: 33.7 us
  Pallas kernels  12.3 us (36%)
  waiting for transfers between devices  11.4 us (34%)
  starting transfers between devices  9.33 us (28%)
  between operations  0.68 us (2%)
    ppermute x8, waiting for transfers between devices, swap(): return lax.ppermute(value, AXES, [(d, d ^ mask) for d in range(self.count)])  11.4 us
    ppermute x8, starting transfers between devices, swap(): return lax.ppermute(value, AXES, [(d, d ^ mask) for d in range(self.count)])  9.33 us
    pallas_call x1, Pallas kernels, gather(): pl.pallas_call(functools.partial(gather_kernel, plan, step, sorted_here),...  6.18 us
    pallas_call x1, Pallas kernels, feature_grads(): pl.pallas_call(functools.partial(feature_kernel, cuts, scale, plan), in_s...  4.03 us
    pallas_call x1, Pallas kernels, fetch(): pl.pallas_call(fetch_kernel, in_specs=[pl.BlockSpec(memory_space=pl.ANY)]...  1.97 us
  transfers between devices with their start and end apart: 8, of which 7 were waited for; matrix products, arithmetic and copies ran while one was open for 0% of the time, Pallas kernels for 6%

profile of v16, /device:TPU:0, one launch (start us, length us, event | category | flops | bytes accessed | tf_op | source)
XLA Modules:
  0.0 33.7 jit_solution(4637265998365217749)
XLA Ops:
  0.6 6.2 %gather.1 = (bf16[3072,384]{1,0:T(8,128)(2,1)S(1)}, bf16[512,256]{1,0:T(8,128)(2,1)S(1)}, f32[832,128]{1,0:T(8,128)S(1)}, f32[832,128]{1,0:T(8,128)S(1)}) custom-call(s32[1]{0:T(128)} %bitcast.where_ref, bf16[3072,512]{1,0:T(8,128)(2,1)} %bitcast.13, bf16[3072,512]{1,0:T(8,128)(2,1)} %bitcast.11, bf16[512,128]{1,0:T(8,128)(2,1)} %wr_hbm.1, ...), custom_call_target="tpu_custom_call" | custom-call | flops 3221225472 | bytes 8650752 | tf_op jit(solution)/shard_map/gather/pallas_call | solution.py:185
  6.8 0.5 %collective-permute-start = (f32[832,128]{1,0:T(8,128)S(1)}, f32[832,128]{1,0:T(8,128)S(1)}, u32[]{:S(2)}, u32[]{:S(2)}) collective-permute-start(f32[832,128]{1,0:T(8,128)S(1)} %get-tuple-element.30), channel_id=1, source_target_pairs={{0,4},{1,5},{2,6},{3,7},{4,0},{5,1},{6,2},{7,3},{8,12},{9,13},{10,... | collective-permute-start | bytes 1277960 | tf_op jit(solution)/shard_map/ppermute | solution.py:70
  7.3 1.4 %collective-permute-done.refs_1_ = f32[832,128]{1,0:T(8,128)S(1)} collective-permute-done((f32[832,128]{1,0:T(8,128)S(1)}, f32[832,128]{1,0:T(8,128)S(1)}, u32[]{:S(2)}, u32[]{:S(2)}) %collective-permute-start) | collective-permute-done | bytes 426016 | tf_op jit(solution)/shard_map/ppermute | solution.py:70
  8.8 3.9 %collective-permute-start.1 = (f32[256,128]{1,0:T(8,128)S(1)}, f32[256,128]{1,0:T(8,128)S(1)}, u32[]{:S(2)}, u32[]{:S(2)}) collective-permute-start(f32[256,128]{1,0:T(8,128)S(1)} %get-tuple-element.32), channel_id=1, source_target_pairs={{0,24},{1,25},{2,26},{3,27},{4,28},{5,29},{6,30},{7,31},{8,16},{9,... | collective-permute-start | bytes 393224 | tf_op jit(solution)/shard_map/ppermute | solution.py:70
  12.7 0.5 %collective-permute-start.2 = (f32[256,128]{1,0:T(8,128)S(1)}, f32[256,128]{1,0:T(8,128)S(1)}, u32[]{:S(2)}, u32[]{:S(2)}) collective-permute-start(f32[256,128]{1,0:T(8,128)S(1)} %get-tuple-element.33), channel_id=1, source_target_pairs={{0,8},{1,9},{2,10},{3,11},{4,12},{5,13},{6,14},{7,15},{8,0},{9,1},... | collective-permute-start | bytes 393224 | tf_op jit(solution)/shard_map/ppermute | solution.py:70
  13.2 0.1 collective-permute-start.3
  13.3 2.0 %fetch.1 = (f32[64,64]{1,0:T(8,128)S(1)}, f32[128,128]{1,0:T(8,128)S(1)}, bf16[3072,512]{1,0:T(8,128)(2,1)S(1)}) custom-call(f32[256,128]{1,0:T(8,128)S(1)} %get-tuple-element.31._.refs_0_, f32[64,64]{1,0:T(8,128)} %refs_0_.1, f32[128,128]{1,0:T(8,128)} %refs_1_.1, bf16[3072,512]{1,0:T(8,128)(2,1)} %bitcast.12), custom_call_target="tpu_custom_call" | custom-call | bytes 3227648 | tf_op jit(solution)/shard_map/fetch/pallas_call | solution.py:253
  15.3 1.7 %collective-permute-done.1.refs_1_ = f32[256,128]{1,0:T(8,128)S(1)} collective-permute-done((f32[256,128]{1,0:T(8,128)S(1)}, f32[256,128]{1,0:T(8,128)S(1)}, u32[]{:S(2)}, u32[]{:S(2)}) %collective-permute-start.1) | collective-permute-done | bytes 131104 | tf_op jit(solution)/shard_map/ppermute | solution.py:70
  17.0 2.6 %collective-permute-done.2.refs_2_ = f32[256,128]{1,0:T(8,128)S(1)} collective-permute-done((f32[256,128]{1,0:T(8,128)S(1)}, f32[256,128]{1,0:T(8,128)S(1)}, u32[]{:S(2)}, u32[]{:S(2)}) %collective-permute-start.2) | collective-permute-done | bytes 131104 | tf_op jit(solution)/shard_map/ppermute | solution.py:70
  19.5 0.0 collective-permute-done.3.refs_3_
  19.6 2.6 %collective-permute-start.4 = (f32[112,128]{1,0:T(8,128)S(1)}, f32[112,128]{1,0:T(8,128)S(1)}, u32[]{:S(2)}, u32[]{:S(2)}) collective-permute-start(f32[112,128]{1,0:T(8,128)S(1)} %get-tuple-element.37), channel_id=1, source_target_pairs={{0,2},{1,3},{2,0},{3,1},{4,6},{5,7},{6,4},{7,5},{8,10},{9,11},{10,... | collective-permute-start | bytes 172040 | tf_op jit(solution)/shard_map/ppermute | solution.py:70
  22.2 1.3 %collective-permute-start.5 = (f32[112,128]{1,0:T(8,128)S(1)}, f32[112,128]{1,0:T(8,128)S(1)}, u32[]{:S(2)}, u32[]{:S(2)}) collective-permute-start(f32[112,128]{1,0:T(8,128)S(1)} %get-tuple-element.38), channel_id=1, source_target_pairs={{0,3},{1,2},{2,1},{3,0},{4,7},{5,6},{6,5},{7,4},{8,11},{9,10},{10,... | collective-permute-start | bytes 172040 | tf_op jit(solution)/shard_map/ppermute | solution.py:70
  23.6 0.2 collective-permute-start.6
  23.8 1.1 %collective-permute-done.4.refs_1_ = f32[112,128]{1,0:T(8,128)S(1)} collective-permute-done((f32[112,128]{1,0:T(8,128)S(1)}, f32[112,128]{1,0:T(8,128)S(1)}, u32[]{:S(2)}, u32[]{:S(2)}) %collective-permute-start.4) | collective-permute-done | bytes 57376 | tf_op jit(solution)/shard_map/ppermute | solution.py:70
  24.9 3.4 %collective-permute-done.5.refs_2_ = f32[112,128]{1,0:T(8,128)S(1)} collective-permute-done((f32[112,128]{1,0:T(8,128)S(1)}, f32[112,128]{1,0:T(8,128)S(1)}, u32[]{:S(2)}, u32[]{:S(2)}) %collective-permute-start.5) | collective-permute-done | bytes 57376 | tf_op jit(solution)/shard_map/ppermute | solution.py:70
  28.3 0.1 collective-permute-done.6.refs_3_
  28.4 0.1 collective-permute-start.7
  28.5 1.2 %collective-permute-done.7.other_ref = f32[64,128]{1,0:T(8,128)S(1)} collective-permute-done((f32[64,128]{1,0:T(8,128)S(1)}, f32[64,128]{1,0:T(8,128)S(1)}, u32[]{:S(2)}, u32[]{:S(2)}) %collective-permute-start.7) | collective-permute-done | bytes 32800 | tf_op jit(solution)/shard_map/ppermute | solution.py:70
  29.7 4.0 %feature_grads.1 = (bf16[3072,512]{1,0:T(8,128)(2,1)}, f32[16,128]{1,0:T(8,128)}, f32[16,64]{1,0:T(8,128)}, f32[16,128]{1,0:T(8,128)}, f32[64,64]{1,0:T(8,128)}, /*index=5*/f32[128,128]{1,0:T(8,128)}) custom-call(s32[1]{0:T(128)} %bitcast.where_ref, f32[64,128]{1,0:T(8,128)S(1)} %get-tuple-element.40.mine_ref, ...), custom_call_target="tpu_custom_call" | custom-call | flops 1610612736 | bytes 8650752 | tf_op jit(solution)/shard_map/feature_grads/pallas_call | solution.py:324
  (3 shorter events, 0.1 us)
Async XLA Ops:
  6.8 1.9 %collective-permute-start = (f32[832,128]{1,0:T(8,128)S(1)}, f32[832,128]{1,0:T(8,128)S(1)}, u32[]{:S(2)}, u32[]{:S(2)}) collective-permute-start(f32[832,128]{1,0:T(8,128)S(1)} %get-tuple-element.30), channel_id=1, source_target_pairs={{0,4},{1,5},{2,6},{3,7},{4,0},{5,1},{6,2},{7,3},{8,12},{9,13},{10,... | collective-permute-start | bytes 1277960 | tf_op jit(solution)/shard_map/ppermute | solution.py:70
  8.8 8.2 %collective-permute-start.1 = (f32[256,128]{1,0:T(8,128)S(1)}, f32[256,128]{1,0:T(8,128)S(1)}, u32[]{:S(2)}, u32[]{:S(2)}) collective-permute-start(f32[256,128]{1,0:T(8,128)S(1)} %get-tuple-element.32), channel_id=1, source_target_pairs={{0,24},{1,25},{2,26},{3,27},{4,28},{5,29},{6,30},{7,31},{8,16},{9,... | collective-permute-start | bytes 393224 | tf_op jit(solution)/shard_map/ppermute | solution.py:70
  12.7 6.9 %collective-permute-start.2 = (f32[256,128]{1,0:T(8,128)S(1)}, f32[256,128]{1,0:T(8,128)S(1)}, u32[]{:S(2)}, u32[]{:S(2)}) collective-permute-start(f32[256,128]{1,0:T(8,128)S(1)} %get-tuple-element.33), channel_id=1, source_target_pairs={{0,8},{1,9},{2,10},{3,11},{4,12},{5,13},{6,14},{7,15},{8,0},{9,1},... | collective-permute-start | bytes 393224 | tf_op jit(solution)/shard_map/ppermute | solution.py:70
  13.2 6.3 %collective-permute-start.3 = (f32[256,128]{1,0:T(8,128)S(1)}, f32[256,128]{1,0:T(8,128)S(1)}, u32[]{:S(2)}, u32[]{:S(2)}) collective-permute-start(f32[256,128]{1,0:T(8,128)S(1)} %get-tuple-element.34), channel_id=1, source_target_pairs={{0,16},{1,17},{2,18},{3,19},{4,20},{5,21},{6,22},{7,23},{8,24},{9,... | collective-permute-start | bytes 393224 | tf_op jit(solution)/shard_map/ppermute | solution.py:70
  19.6 5.3 %collective-permute-start.4 = (f32[112,128]{1,0:T(8,128)S(1)}, f32[112,128]{1,0:T(8,128)S(1)}, u32[]{:S(2)}, u32[]{:S(2)}) collective-permute-start(f32[112,128]{1,0:T(8,128)S(1)} %get-tuple-element.37), channel_id=1, source_target_pairs={{0,2},{1,3},{2,0},{3,1},{4,6},{5,7},{6,4},{7,5},{8,10},{9,11},{10,... | collective-permute-start | bytes 172040 | tf_op jit(solution)/shard_map/ppermute | solution.py:70
  22.2 6.1 %collective-permute-start.5 = (f32[112,128]{1,0:T(8,128)S(1)}, f32[112,128]{1,0:T(8,128)S(1)}, u32[]{:S(2)}, u32[]{:S(2)}) collective-permute-start(f32[112,128]{1,0:T(8,128)S(1)} %get-tuple-element.38), channel_id=1, source_target_pairs={{0,3},{1,2},{2,1},{3,0},{4,7},{5,6},{6,5},{7,4},{8,11},{9,10},{10,... | collective-permute-start | bytes 172040 | tf_op jit(solution)/shard_map/ppermute | solution.py:70
  23.6 4.8 %collective-permute-start.6 = (f32[112,128]{1,0:T(8,128)S(1)}, f32[112,128]{1,0:T(8,128)S(1)}, u32[]{:S(2)}, u32[]{:S(2)}) collective-permute-start(f32[112,128]{1,0:T(8,128)S(1)} %get-tuple-element.39), channel_id=1, source_target_pairs={{0,1},{1,0},{2,3},{3,2},{4,5},{5,4},{6,7},{7,6},{8,9},{9,8},{10,11... | collective-permute-start | bytes 172040 | tf_op jit(solution)/shard_map/ppermute | solution.py:70
  28.4 1.3 %collective-permute-start.7 = (f32[64,128]{1,0:T(8,128)S(1)}, f32[64,128]{1,0:T(8,128)S(1)}, u32[]{:S(2)}, u32[]{:S(2)}) collective-permute-start(f32[64,128]{1,0:T(8,128)S(1)} %get-tuple-element.40.mine_ref), channel_id=1, source_target_pairs={{0,4},{1,5},{2,6},{3,7},{4,0},{5,1},{6,2},{7,3},{8,12},{9,13},{10,... | collective-permute-start | bytes 98312 | tf_op jit(solution)/shard_map/ppermute | solution.py:70

commit v17 on v16

--- a/solution.py
+++ b/solution.py
@@ -156,7 +156,7 @@
 def gather(plan, where, x, g, wr, wpt, we):
     rows, chan = x.shape
     cr, nodes = wr.shape[1], wpt.shape[0]
-    step = row_block(rows, 1536)
+    step = row_block(rows, 1024)
     width = 2 * cr + 2 * nodes
     half = plan.count // 2
     size = chan // plan.count
@@ -302,11 +302,16 @@
     ga_ref[...] = -scale * exact(d_hidden, nodes, ((1,), (1,)))
     size = gr_ref.shape[0]
     x_red, x_dm, with_proj = (sums_ref[k * size : (k + 1) * size] for k in range(3))
-    gr_ref[...] = scale * scale * exact(with_proj[:, :nodes_n], dn_f)
-    gp_ref[...] = scale * exact(x_dm, no_f, ((1,), (1,))) + scale * scale * exact(
-        x_red, dn_f, ((1,), (1,))
-    )
-    ge_ref[...] = scale * exact(with_proj[:, nodes_n:], no_f)
+    dn_s = scale * dn_f
+    beside = jnp.concatenate([no_f, dn_s], axis=1)
+    gp_ref[...] = scale * exact(jnp.concatenate([x_dm, x_red], axis=1), beside, ((1,), (1,)))
+    blank = jnp.zeros_like(no_f)
+    corners = jnp.concatenate(
+        [jnp.concatenate([dn_s, blank], axis=1), jnp.concatenate([blank, no_f], axis=1)], axis=0
+    )
+    pair = scale * exact(with_proj, corners)
+    gr_ref[...] = pair[:, :cr]
+    ge_ref[...] = pair[:, cr:]
     for copy in copies:
         copy.wait()
 

time: 33.8 us -> 34.2 us (1.012)
  no operation moved by 1% of the time
where the time goes in v17:
time: 34.2 us; the launch traced here: 34 us
  Pallas kernels  12.5 us (37%)
  waiting for transfers between devices  11.4 us (33%)
  starting transfers between devices  9.33 us (27%)
  between operations  0.68 us (2%)
    ppermute x8, waiting for transfers between devices, swap(): return lax.ppermute(value, AXES, [(d, d ^ mask) for d in range(self.count)])  11.4 us
    ppermute x8, starting transfers between devices, swap(): return lax.ppermute(value, AXES, [(d, d ^ mask) for d in range(self.count)])  9.33 us
    pallas_call x1, Pallas kernels, gather(): pl.pallas_call(functools.partial(gather_kernel, plan, step, sorted_here),...  6.45 us
    pallas_call x1, Pallas kernels, feature_grads(): pl.pallas_call(functools.partial(feature_kernel, cuts, scale, plan), in_s...  4.03 us
    pallas_call x1, Pallas kernels, fetch(): pl.pallas_call(fetch_kernel, in_specs=[pl.BlockSpec(memory_space=pl.ANY)]...  1.97 us
  transfers between devices with their start and end apart: 8, of which 7 were waited for; matrix products, arithmetic and copies ran while one was open for 0% of the time, Pallas kernels for 6%

profile of v17, /device:TPU:0, one launch (start us, length us, event | category | flops | bytes accessed | tf_op | source)
XLA Modules:
  0.0 34.0 jit_solution(562983867315620498)
XLA Ops:
  0.6 6.5 %gather.1 = (bf16[3072,384]{1,0:T(8,128)(2,1)S(1)}, bf16[512,256]{1,0:T(8,128)(2,1)S(1)}, f32[832,128]{1,0:T(8,128)S(1)}, f32[832,128]{1,0:T(8,128)S(1)}) custom-call(s32[1]{0:T(128)} %bitcast.where_ref, bf16[3072,512]{1,0:T(8,128)(2,1)} %bitcast.13, bf16[3072,512]{1,0:T(8,128)(2,1)} %bitcast.11, bf16[512,128]{1,0:T(8,128)(2,1)} %wr_hbm.1, ...), custom_call_target="tpu_custom_call" | custom-call | flops 3221225472 | bytes 8650752 | tf_op jit(solution)/shard_map/gather/pallas_call | solution.py:185
  7.1 0.5 %collective-permute-start = (f32[832,128]{1,0:T(8,128)S(1)}, f32[832,128]{1,0:T(8,128)S(1)}, u32[]{:S(2)}, u32[]{:S(2)}) collective-permute-start(f32[832,128]{1,0:T(8,128)S(1)} %get-tuple-element.30), channel_id=1, source_target_pairs={{0,4},{1,5},{2,6},{3,7},{4,0},{5,1},{6,2},{7,3},{8,12},{9,13},{10,... | collective-permute-start | bytes 1277960 | tf_op jit(solution)/shard_map/ppermute | solution.py:70
  7.6 1.4 %collective-permute-done.refs_1_ = f32[832,128]{1,0:T(8,128)S(1)} collective-permute-done((f32[832,128]{1,0:T(8,128)S(1)}, f32[832,128]{1,0:T(8,128)S(1)}, u32[]{:S(2)}, u32[]{:S(2)}) %collective-permute-start) | collective-permute-done | bytes 426016 | tf_op jit(solution)/shard_map/ppermute | solution.py:70
  9.1 3.9 %collective-permute-start.1 = (f32[256,128]{1,0:T(8,128)S(1)}, f32[256,128]{1,0:T(8,128)S(1)}, u32[]{:S(2)}, u32[]{:S(2)}) collective-permute-start(f32[256,128]{1,0:T(8,128)S(1)} %get-tuple-element.32), channel_id=1, source_target_pairs={{0,24},{1,25},{2,26},{3,27},{4,28},{5,29},{6,30},{7,31},{8,16},{9,... | collective-permute-start | bytes 393224 | tf_op jit(solution)/shard_map/ppermute | solution.py:70
  12.9 0.5 %collective-permute-start.2 = (f32[256,128]{1,0:T(8,128)S(1)}, f32[256,128]{1,0:T(8,128)S(1)}, u32[]{:S(2)}, u32[]{:S(2)}) collective-permute-start(f32[256,128]{1,0:T(8,128)S(1)} %get-tuple-element.33), channel_id=1, source_target_pairs={{0,8},{1,9},{2,10},{3,11},{4,12},{5,13},{6,14},{7,15},{8,0},{9,1},... | collective-permute-start | bytes 393224 | tf_op jit(solution)/shard_map/ppermute | solution.py:70
  13.5 0.1 collective-permute-start.3
  13.6 2.0 %fetch.1 = (f32[64,64]{1,0:T(8,128)S(1)}, f32[128,128]{1,0:T(8,128)S(1)}, bf16[3072,512]{1,0:T(8,128)(2,1)S(1)}) custom-call(f32[256,128]{1,0:T(8,128)S(1)} %get-tuple-element.31._.refs_0_, f32[64,64]{1,0:T(8,128)} %refs_0_.1, f32[128,128]{1,0:T(8,128)} %refs_1_.1, bf16[3072,512]{1,0:T(8,128)(2,1)} %bitcast.12), custom_call_target="tpu_custom_call" | custom-call | bytes 3227648 | tf_op jit(solution)/shard_map/fetch/pallas_call | solution.py:253
  15.6 1.7 %collective-permute-done.1.refs_1_ = f32[256,128]{1,0:T(8,128)S(1)} collective-permute-done((f32[256,128]{1,0:T(8,128)S(1)}, f32[256,128]{1,0:T(8,128)S(1)}, u32[]{:S(2)}, u32[]{:S(2)}) %collective-permute-start.1) | collective-permute-done | bytes 131104 | tf_op jit(solution)/shard_map/ppermute | solution.py:70
  17.2 2.6 %collective-permute-done.2.refs_2_ = f32[256,128]{1,0:T(8,128)S(1)} collective-permute-done((f32[256,128]{1,0:T(8,128)S(1)}, f32[256,128]{1,0:T(8,128)S(1)}, u32[]{:S(2)}, u32[]{:S(2)}) %collective-permute-start.2) | collective-permute-done | bytes 131104 | tf_op jit(solution)/shard_map/ppermute | solution.py:70
  19.8 0.0 collective-permute-done.3.refs_3_
  19.9 2.6 %collective-permute-start.4 = (f32[112,128]{1,0:T(8,128)S(1)}, f32[112,128]{1,0:T(8,128)S(1)}, u32[]{:S(2)}, u32[]{:S(2)}) collective-permute-start(f32[112,128]{1,0:T(8,128)S(1)} %get-tuple-element.37), channel_id=1, source_target_pairs={{0,2},{1,3},{2,0},{3,1},{4,6},{5,7},{6,4},{7,5},{8,10},{9,11},{10,... | collective-permute-start | bytes 172040 | tf_op jit(solution)/shard_map/ppermute | solution.py:70
  22.5 1.4 %collective-permute-start.5 = (f32[112,128]{1,0:T(8,128)S(1)}, f32[112,128]{1,0:T(8,128)S(1)}, u32[]{:S(2)}, u32[]{:S(2)}) collective-permute-start(f32[112,128]{1,0:T(8,128)S(1)} %get-tuple-element.38), channel_id=1, source_target_pairs={{0,3},{1,2},{2,1},{3,0},{4,7},{5,6},{6,5},{7,4},{8,11},{9,10},{10,... | collective-permute-start | bytes 172040 | tf_op jit(solution)/shard_map/ppermute | solution.py:70
  23.8 0.2 collective-permute-start.6
  24.1 1.1 %collective-permute-done.4.refs_1_ = f32[112,128]{1,0:T(8,128)S(1)} collective-permute-done((f32[112,128]{1,0:T(8,128)S(1)}, f32[112,128]{1,0:T(8,128)S(1)}, u32[]{:S(2)}, u32[]{:S(2)}) %collective-permute-start.4) | collective-permute-done | bytes 57376 | tf_op jit(solution)/shard_map/ppermute | solution.py:70
  25.2 3.4 %collective-permute-done.5.refs_2_ = f32[112,128]{1,0:T(8,128)S(1)} collective-permute-done((f32[112,128]{1,0:T(8,128)S(1)}, f32[112,128]{1,0:T(8,128)S(1)}, u32[]{:S(2)}, u32[]{:S(2)}) %collective-permute-start.5) | collective-permute-done | bytes 57376 | tf_op jit(solution)/shard_map/ppermute | solution.py:70
  28.6 0.1 collective-permute-done.6.refs_3_
  28.7 0.1 collective-permute-start.7
  28.7 1.2 %collective-permute-done.7.other_ref = f32[64,128]{1,0:T(8,128)S(1)} collective-permute-done((f32[64,128]{1,0:T(8,128)S(1)}, f32[64,128]{1,0:T(8,128)S(1)}, u32[]{:S(2)}, u32[]{:S(2)}) %collective-permute-start.7) | collective-permute-done | bytes 32800 | tf_op jit(solution)/shard_map/ppermute | solution.py:70
  29.9 4.0 %feature_grads.1 = (bf16[3072,512]{1,0:T(8,128)(2,1)}, f32[16,128]{1,0:T(8,128)}, f32[16,64]{1,0:T(8,128)}, f32[16,128]{1,0:T(8,128)}, f32[64,64]{1,0:T(8,128)}, /*index=5*/f32[128,128]{1,0:T(8,128)}) custom-call(s32[1]{0:T(128)} %bitcast.where_ref, f32[64,128]{1,0:T(8,128)S(1)} %get-tuple-element.40.mine_ref, ...), custom_call_target="tpu_custom_call" | custom-call | flops 1610612736 | bytes 8650752 | tf_op jit(solution)/shard_map/feature_grads/pallas_call | solution.py:329
  (3 shorter events, 0.1 us)
Async XLA Ops:
  7.1 1.9 %collective-permute-start = (f32[832,128]{1,0:T(8,128)S(1)}, f32[832,128]{1,0:T(8,128)S(1)}, u32[]{:S(2)}, u32[]{:S(2)}) collective-permute-start(f32[832,128]{1,0:T(8,128)S(1)} %get-tuple-element.30), channel_id=1, source_target_pairs={{0,4},{1,5},{2,6},{3,7},{4,0},{5,1},{6,2},{7,3},{8,12},{9,13},{10,... | collective-permute-start | bytes 1277960 | tf_op jit(solution)/shard_map/ppermute | solution.py:70
  9.1 8.2 %collective-permute-start.1 = (f32[256,128]{1,0:T(8,128)S(1)}, f32[256,128]{1,0:T(8,128)S(1)}, u32[]{:S(2)}, u32[]{:S(2)}) collective-permute-start(f32[256,128]{1,0:T(8,128)S(1)} %get-tuple-element.32), channel_id=1, source_target_pairs={{0,24},{1,25},{2,26},{3,27},{4,28},{5,29},{6,30},{7,31},{8,16},{9,... | collective-permute-start | bytes 393224 | tf_op jit(solution)/shard_map/ppermute | solution.py:70
  12.9 6.9 %collective-permute-start.2 = (f32[256,128]{1,0:T(8,128)S(1)}, f32[256,128]{1,0:T(8,128)S(1)}, u32[]{:S(2)}, u32[]{:S(2)}) collective-permute-start(f32[256,128]{1,0:T(8,128)S(1)} %get-tuple-element.33), channel_id=1, source_target_pairs={{0,8},{1,9},{2,10},{3,11},{4,12},{5,13},{6,14},{7,15},{8,0},{9,1},... | collective-permute-start | bytes 393224 | tf_op jit(solution)/shard_map/ppermute | solution.py:70
  13.5 6.3 %collective-permute-start.3 = (f32[256,128]{1,0:T(8,128)S(1)}, f32[256,128]{1,0:T(8,128)S(1)}, u32[]{:S(2)}, u32[]{:S(2)}) collective-permute-start(f32[256,128]{1,0:T(8,128)S(1)} %get-tuple-element.34), channel_id=1, source_target_pairs={{0,16},{1,17},{2,18},{3,19},{4,20},{5,21},{6,22},{7,23},{8,24},{9,... | collective-permute-start | bytes 393224 | tf_op jit(solution)/shard_map/ppermute | solution.py:70
  19.9 5.3 %collective-permute-start.4 = (f32[112,128]{1,0:T(8,128)S(1)}, f32[112,128]{1,0:T(8,128)S(1)}, u32[]{:S(2)}, u32[]{:S(2)}) collective-permute-start(f32[112,128]{1,0:T(8,128)S(1)} %get-tuple-element.37), channel_id=1, source_target_pairs={{0,2},{1,3},{2,0},{3,1},{4,6},{5,7},{6,4},{7,5},{8,10},{9,11},{10,... | collective-permute-start | bytes 172040 | tf_op jit(solution)/shard_map/ppermute | solution.py:70
  22.5 6.1 %collective-permute-start.5 = (f32[112,128]{1,0:T(8,128)S(1)}, f32[112,128]{1,0:T(8,128)S(1)}, u32[]{:S(2)}, u32[]{:S(2)}) collective-permute-start(f32[112,128]{1,0:T(8,128)S(1)} %get-tuple-element.38), channel_id=1, source_target_pairs={{0,3},{1,2},{2,1},{3,0},{4,7},{5,6},{6,5},{7,4},{8,11},{9,10},{10,... | collective-permute-start | bytes 172040 | tf_op jit(solution)/shard_map/ppermute | solution.py:70
  23.8 4.8 %collective-permute-start.6 = (f32[112,128]{1,0:T(8,128)S(1)}, f32[112,128]{1,0:T(8,128)S(1)}, u32[]{:S(2)}, u32[]{:S(2)}) collective-permute-start(f32[112,128]{1,0:T(8,128)S(1)} %get-tuple-element.39), channel_id=1, source_target_pairs={{0,1},{1,0},{2,3},{3,2},{4,5},{5,4},{6,7},{7,6},{8,9},{9,8},{10,11... | collective-permute-start | bytes 172040 | tf_op jit(solution)/shard_map/ppermute | solution.py:70
  28.7 1.3 %collective-permute-start.7 = (f32[64,128]{1,0:T(8,128)S(1)}, f32[64,128]{1,0:T(8,128)S(1)}, u32[]{:S(2)}, u32[]{:S(2)}) collective-permute-start(f32[64,128]{1,0:T(8,128)S(1)} %get-tuple-element.40.mine_ref), channel_id=1, source_target_pairs={{0,4},{1,5},{2,6},{3,7},{4,0},{5,1},{6,2},{7,3},{8,12},{9,13},{10,... | collective-permute-start | bytes 98312 | tf_op jit(solution)/shard_map/ppermute | solution.py:70

commit v18 on v16

--- a/solution.py
+++ b/solution.py
@@ -53,21 +53,25 @@
         self.count = math.prod(size.values())
         stride = {"gx": size["gy"] * size["gz"], "gy": size["gz"], "gz": 1}
         self.core = stride["gy"]
+        wide = [0, *sorted(range(1, size["gx"]), key=lambda k: -k.bit_count())]
+        turned = [0, *sorted(range(1, size["gx"]), key=lambda k: (-k.bit_count(), -k))]
+        rest = range(size["gy"] // 2)
+        deep = [0, *range(2, size["gz"]), 1]
         spans = (
-            ([0, *sorted(range(1, size["gx"]), key=lambda k: -k.bit_count())], stride["gx"]),
-            (range(size["gy"] // 2), 2 * stride["gy"]),
-            ([0, *range(2, size["gz"]), 1], stride["gz"]),
+            (wide, turned, stride["gx"]), (rest, rest, 2 * stride["gy"]), (deep, deep, stride["gz"])
         )
-        self.groups = [[k * step for k in order] for order, step in spans if len(order) > 1]
-        self.masks = [0]
+        self.groups = [
+            [(a * step, b * step) for a, b in zip(one, other)] for one, other, step in spans if len(one) > 1
+        ]
+        self.masks = [(0, 0)]
         for group in self.groups:
-            self.masks = [mask | bits for mask in self.masks for bits in group]
+            self.masks = [(a | x, b | y) for a, b in self.masks for x, y in group]
 
     def side(self, device):
         return lax.bitwise_and(lax.div(device, jnp.int32(self.core)), jnp.int32(1))
 
     def swap(self, value, mask):
-        return lax.ppermute(value, AXES, [(d, d ^ mask) for d in range(self.count)])
+        return lax.ppermute(value, AXES, [(d, d ^ mask[d // self.core & 1]) for d in range(self.count)])
 
 
 def gather_kernel(
@@ -143,9 +147,10 @@
     heads[1][...] = jnp.where(side == 0, right, left)
     if sorted_here:
         size = turned_ref.shape[0] // plan.count
-        for base, out_ref in ((me, kept_ref), (me ^ plan.core, sent_ref)):
+        for base, of, out_ref in ((me, side, kept_ref), (me ^ plan.core, 1 - side, sent_ref)):
             to = nodes
-            for mask in plan.masks:
+            for masks in plan.masks:
+                mask = jnp.where(of == 0, *masks)
                 at = pl.multiple_of((base ^ mask) * size, size)
                 block = turned_ref[pl.ds(at, size), :]
                 for lane in range(0, block.shape[1], cr):
@@ -196,8 +201,9 @@
         table = jnp.array(plan.masks, jnp.int32)
         cut = sums[0].reshape(plan.count, size, width // cr, cr).transpose(0, 2, 1, 3)
         lay = lambda head, index: jnp.concatenate([head, cut[index].reshape(-1, cr)])
-        kept = lay(kept, where[0] ^ table)
-        sent = lay(sent, where[0] ^ plan.core ^ table)
+        side = plan.side(where[0])
+        kept = lay(kept, where[0] ^ table[:, side])
+        sent = lay(sent, where[0] ^ plan.core ^ table[:, 1 - side])
     return rdp, wcat, kept, sent
 
 
@@ -360,14 +366,14 @@
         plan, where, flat_x, flat_g, reduce_weight, project_weight.T, expand_weight
     )
     head = adjacency.shape[0]
-    terms = [kept, plan.swap(sent, plan.core)]
+    terms = [kept, plan.swap(sent, (plan.core, plan.core))]
     ready = None
     for group in plan.groups:
         parts = step(head, len(group), terms, ready[:1] if ready else ())
-        terms = [plan.swap(part, mask) if mask else part for part, mask in zip(parts, group)]
+        terms = [plan.swap(part, mask) if any(mask) else part for part, mask in zip(parts, group)]
         ready = ready or fetch(parts[0], adjacency, node_weight, flat_g)
     mine, sums = step(head, 1, terms)
-    other = plan.swap(mine, plan.core)
+    other = plan.swap(mine, (plan.core, plan.core))
 
     flat_out, grad_reduce, grad_project, grad_expand, grad_adjacency, grad_node = feature_grads(
         plan, where, mine, other, sums, *ready[:2], wcat, rdp, ready[2], scale

time: 33.8 us -> 33.9 us (level)
  transfers between devices with their start and end apart: 8 -> 8, of which waited for: 7 -> 6; matrix products, arithmetic and copies ran while one was open for 0% -> 0% of each run, Pallas kernels for 6% -> 6%
where the time goes in v18:
time: 33.9 us; the launch traced here: 33.7 us
  Pallas kernels  12.3 us (36%)
  waiting for transfers between devices  11.4 us (34%)
  starting transfers between devices  9.34 us (28%)
  between operations  0.68 us (2%)
    ppermute x8, waiting for transfers between devices, swap(): lax.ppermute(value, AXES, [(d, d ^ mask[d // self.core & 1]) for d in ran...  11.4 us
    ppermute x8, starting transfers between devices, swap(): lax.ppermute(value, AXES, [(d, d ^ mask[d // self.core & 1]) for d in ran...  9.34 us
    pallas_call x1, Pallas kernels, gather(): pl.pallas_call(functools.partial(gather_kernel, plan, step, sorted_here),...  6.18 us
    pallas_call x1, Pallas kernels, feature_grads(): pl.pallas_call(functools.partial(feature_kernel, cuts, scale, plan), in_s...  4.03 us
    pallas_call x1, Pallas kernels, fetch(): pl.pallas_call(fetch_kernel, in_specs=[pl.BlockSpec(memory_space=pl.ANY)]...  1.97 us
  transfers between devices with their start and end apart: 8, of which 6 were waited for; matrix products, arithmetic and copies ran while one was open for 0% of the time, Pallas kernels for 6%

profile of v18, /device:TPU:0, one launch (start us, length us, event | category | flops | bytes accessed | tf_op | source)
XLA Modules:
  0.0 33.7 jit_solution(10327908161099037078)
XLA Ops:
  0.6 6.2 %gather.1 = (bf16[3072,384]{1,0:T(8,128)(2,1)S(1)}, bf16[512,256]{1,0:T(8,128)(2,1)S(1)}, f32[832,128]{1,0:T(8,128)S(1)}, f32[832,128]{1,0:T(8,128)S(1)}) custom-call(s32[1]{0:T(128)} %bitcast.where_ref, bf16[3072,512]{1,0:T(8,128)(2,1)} %bitcast.13, bf16[3072,512]{1,0:T(8,128)(2,1)} %bitcast.11, bf16[512,128]{1,0:T(8,128)(2,1)} %wr_hbm.1, ...), custom_call_target="tpu_custom_call" | custom-call | flops 3221225472 | bytes 8650752 | tf_op jit(solution)/shard_map/gather/pallas_call | solution.py:190
  6.8 0.5 %collective-permute-start = (f32[832,128]{1,0:T(8,128)S(1)}, f32[832,128]{1,0:T(8,128)S(1)}, u32[]{:S(2)}, u32[]{:S(2)}) collective-permute-start(f32[832,128]{1,0:T(8,128)S(1)} %get-tuple-element.30), channel_id=1, source_target_pairs={{0,4},{1,5},{2,6},{3,7},{4,0},{5,1},{6,2},{7,3},{8,12},{9,13},{10,... | collective-permute-start | bytes 1277960 | tf_op jit(solution)/shard_map/ppermute | solution.py:74
  7.3 1.4 %collective-permute-done.refs_1_ = f32[832,128]{1,0:T(8,128)S(1)} collective-permute-done((f32[832,128]{1,0:T(8,128)S(1)}, f32[832,128]{1,0:T(8,128)S(1)}, u32[]{:S(2)}, u32[]{:S(2)}) %collective-permute-start) | collective-permute-done | bytes 426016 | tf_op jit(solution)/shard_map/ppermute | solution.py:74
  8.8 3.9 %collective-permute-start.1 = (f32[256,128]{1,0:T(8,128)S(1)}, f32[256,128]{1,0:T(8,128)S(1)}, u32[]{:S(2)}, u32[]{:S(2)}) collective-permute-start(f32[256,128]{1,0:T(8,128)S(1)} %get-tuple-element.32), channel_id=1, source_target_pairs={{0,24},{1,25},{2,26},{3,27},{4,28},{5,29},{6,30},{7,31},{8,16},{9,... | collective-permute-start | bytes 393224 | tf_op jit(solution)/shard_map/ppermute | solution.py:74
  12.7 0.5 %collective-permute-start.2 = (f32[256,128]{1,0:T(8,128)S(1)}, f32[256,128]{1,0:T(8,128)S(1)}, u32[]{:S(2)}, u32[]{:S(2)}) collective-permute-start(f32[256,128]{1,0:T(8,128)S(1)} %get-tuple-element.33), channel_id=1, source_target_pairs={{0,8},{1,9},{2,10},{3,11},{4,20},{5,21},{6,22},{7,23},{8,0},{9,1},... | collective-permute-start | bytes 393224 | tf_op jit(solution)/shard_map/ppermute | solution.py:74
  13.2 0.1 collective-permute-start.3
  13.3 2.0 %fetch.1 = (f32[64,64]{1,0:T(8,128)S(1)}, f32[128,128]{1,0:T(8,128)S(1)}, bf16[3072,512]{1,0:T(8,128)(2,1)S(1)}) custom-call(f32[256,128]{1,0:T(8,128)S(1)} %get-tuple-element.31._.refs_0_, f32[64,64]{1,0:T(8,128)} %refs_0_.1, f32[128,128]{1,0:T(8,128)} %refs_1_.1, bf16[3072,512]{1,0:T(8,128)(2,1)} %bitcast.12), custom_call_target="tpu_custom_call" | custom-call | bytes 3227648 | tf_op jit(solution)/shard_map/fetch/pallas_call | solution.py:259
  15.3 1.3 %collective-permute-done.1.refs_1_ = f32[256,128]{1,0:T(8,128)S(1)} collective-permute-done((f32[256,128]{1,0:T(8,128)S(1)}, f32[256,128]{1,0:T(8,128)S(1)}, u32[]{:S(2)}, u32[]{:S(2)}) %collective-permute-start.1) | collective-permute-done | bytes 131104 | tf_op jit(solution)/shard_map/ppermute | solution.py:74
  16.6 3.0 %collective-permute-done.2.refs_2_ = f32[256,128]{1,0:T(8,128)S(1)} collective-permute-done((f32[256,128]{1,0:T(8,128)S(1)}, f32[256,128]{1,0:T(8,128)S(1)}, u32[]{:S(2)}, u32[]{:S(2)}) %collective-permute-start.2) | collective-permute-done | bytes 131104 | tf_op jit(solution)/shard_map/ppermute | solution.py:74
  19.6 0.0 collective-permute-done.3.refs_3_
  19.6 2.7 %collective-permute-start.4 = (f32[112,128]{1,0:T(8,128)S(1)}, f32[112,128]{1,0:T(8,128)S(1)}, u32[]{:S(2)}, u32[]{:S(2)}) collective-permute-start(f32[112,128]{1,0:T(8,128)S(1)} %get-tuple-element.37), channel_id=1, source_target_pairs={{0,2},{1,3},{2,0},{3,1},{4,6},{5,7},{6,4},{7,5},{8,10},{9,11},{10,... | collective-permute-start | bytes 172040 | tf_op jit(solution)/shard_map/ppermute | solution.py:74
  22.3 1.3 %collective-permute-start.5 = (f32[112,128]{1,0:T(8,128)S(1)}, f32[112,128]{1,0:T(8,128)S(1)}, u32[]{:S(2)}, u32[]{:S(2)}) collective-permute-start(f32[112,128]{1,0:T(8,128)S(1)} %get-tuple-element.38), channel_id=1, source_target_pairs={{0,3},{1,2},{2,1},{3,0},{4,7},{5,6},{6,5},{7,4},{8,11},{9,10},{10,... | collective-permute-start | bytes 172040 | tf_op jit(solution)/shard_map/ppermute | solution.py:74
  23.6 0.2 collective-permute-start.6
  23.8 1.4 %collective-permute-done.4.refs_1_ = f32[112,128]{1,0:T(8,128)S(1)} collective-permute-done((f32[112,128]{1,0:T(8,128)S(1)}, f32[112,128]{1,0:T(8,128)S(1)}, u32[]{:S(2)}, u32[]{:S(2)}) %collective-permute-start.4) | collective-permute-done | bytes 57376 | tf_op jit(solution)/shard_map/ppermute | solution.py:74
  25.2 3.1 %collective-permute-done.5.refs_2_ = f32[112,128]{1,0:T(8,128)S(1)} collective-permute-done((f32[112,128]{1,0:T(8,128)S(1)}, f32[112,128]{1,0:T(8,128)S(1)}, u32[]{:S(2)}, u32[]{:S(2)}) %collective-permute-start.5) | collective-permute-done | bytes 57376 | tf_op jit(solution)/shard_map/ppermute | solution.py:74
  28.4 0.0 collective-permute-done.6.refs_3_
  28.4 0.1 collective-permute-start.7
  28.5 1.2 %collective-permute-done.7.other_ref = f32[64,128]{1,0:T(8,128)S(1)} collective-permute-done((f32[64,128]{1,0:T(8,128)S(1)}, f32[64,128]{1,0:T(8,128)S(1)}, u32[]{:S(2)}, u32[]{:S(2)}) %collective-permute-start.7) | collective-permute-done | bytes 32800 | tf_op jit(solution)/shard_map/ppermute | solution.py:74
  29.7 4.0 %feature_grads.1 = (bf16[3072,512]{1,0:T(8,128)(2,1)}, f32[16,128]{1,0:T(8,128)}, f32[16,64]{1,0:T(8,128)}, f32[16,128]{1,0:T(8,128)}, f32[64,64]{1,0:T(8,128)}, /*index=5*/f32[128,128]{1,0:T(8,128)}) custom-call(s32[1]{0:T(128)} %bitcast.where_ref, f32[64,128]{1,0:T(8,128)S(1)} %get-tuple-element.40.mine_ref, ...), custom_call_target="tpu_custom_call" | custom-call | flops 1610612736 | bytes 8650752 | tf_op jit(solution)/shard_map/feature_grads/pallas_call | solution.py:330
  (3 shorter events, 0.1 us)
Async XLA Ops:
  6.8 1.9 %collective-permute-start = (f32[832,128]{1,0:T(8,128)S(1)}, f32[832,128]{1,0:T(8,128)S(1)}, u32[]{:S(2)}, u32[]{:S(2)}) collective-permute-start(f32[832,128]{1,0:T(8,128)S(1)} %get-tuple-element.30), channel_id=1, source_target_pairs={{0,4},{1,5},{2,6},{3,7},{4,0},{5,1},{6,2},{7,3},{8,12},{9,13},{10,... | collective-permute-start | bytes 1277960 | tf_op jit(solution)/shard_map/ppermute | solution.py:74
  8.8 7.8 %collective-permute-start.1 = (f32[256,128]{1,0:T(8,128)S(1)}, f32[256,128]{1,0:T(8,128)S(1)}, u32[]{:S(2)}, u32[]{:S(2)}) collective-permute-start(f32[256,128]{1,0:T(8,128)S(1)} %get-tuple-element.32), channel_id=1, source_target_pairs={{0,24},{1,25},{2,26},{3,27},{4,28},{5,29},{6,30},{7,31},{8,16},{9,... | collective-permute-start | bytes 393224 | tf_op jit(solution)/shard_map/ppermute | solution.py:74
  12.7 6.9 %collective-permute-start.2 = (f32[256,128]{1,0:T(8,128)S(1)}, f32[256,128]{1,0:T(8,128)S(1)}, u32[]{:S(2)}, u32[]{:S(2)}) collective-permute-start(f32[256,128]{1,0:T(8,128)S(1)} %get-tuple-element.33), channel_id=1, source_target_pairs={{0,8},{1,9},{2,10},{3,11},{4,20},{5,21},{6,22},{7,23},{8,0},{9,1},... | collective-permute-start | bytes 393224 | tf_op jit(solution)/shard_map/ppermute | solution.py:74
  13.2 6.4 %collective-permute-start.3 = (f32[256,128]{1,0:T(8,128)S(1)}, f32[256,128]{1,0:T(8,128)S(1)}, u32[]{:S(2)}, u32[]{:S(2)}) collective-permute-start(f32[256,128]{1,0:T(8,128)S(1)} %get-tuple-element.34), channel_id=1, source_target_pairs={{0,16},{1,17},{2,18},{3,19},{4,12},{5,13},{6,14},{7,15},{8,24},{9,... | collective-permute-start | bytes 393224 | tf_op jit(solution)/shard_map/ppermute | solution.py:74
  19.6 5.6 %collective-permute-start.4 = (f32[112,128]{1,0:T(8,128)S(1)}, f32[112,128]{1,0:T(8,128)S(1)}, u32[]{:S(2)}, u32[]{:S(2)}) collective-permute-start(f32[112,128]{1,0:T(8,128)S(1)} %get-tuple-element.37), channel_id=1, source_target_pairs={{0,2},{1,3},{2,0},{3,1},{4,6},{5,7},{6,4},{7,5},{8,10},{9,11},{10,... | collective-permute-start | bytes 172040 | tf_op jit(solution)/shard_map/ppermute | solution.py:74
  22.3 6.1 %collective-permute-start.5 = (f32[112,128]{1,0:T(8,128)S(1)}, f32[112,128]{1,0:T(8,128)S(1)}, u32[]{:S(2)}, u32[]{:S(2)}) collective-permute-start(f32[112,128]{1,0:T(8,128)S(1)} %get-tuple-element.38), channel_id=1, source_target_pairs={{0,3},{1,2},{2,1},{3,0},{4,7},{5,6},{6,5},{7,4},{8,11},{9,10},{10,... | collective-permute-start | bytes 172040 | tf_op jit(solution)/shard_map/ppermute | solution.py:74
  23.6 4.8 %collective-permute-start.6 = (f32[112,128]{1,0:T(8,128)S(1)}, f32[112,128]{1,0:T(8,128)S(1)}, u32[]{:S(2)}, u32[]{:S(2)}) collective-permute-start(f32[112,128]{1,0:T(8,128)S(1)} %get-tuple-element.39), channel_id=1, source_target_pairs={{0,1},{1,0},{2,3},{3,2},{4,5},{5,4},{6,7},{7,6},{8,9},{9,8},{10,11... | collective-permute-start | bytes 172040 | tf_op jit(solution)/shard_map/ppermute | solution.py:74
  28.4 1.3 %collective-permute-start.7 = (f32[64,128]{1,0:T(8,128)S(1)}, f32[64,128]{1,0:T(8,128)S(1)}, u32[]{:S(2)}, u32[]{:S(2)}) collective-permute-start(f32[64,128]{1,0:T(8,128)S(1)} %get-tuple-element.40.mine_ref), channel_id=1, source_target_pairs={{0,4},{1,5},{2,6},{3,7},{4,0},{5,1},{6,2},{7,3},{8,12},{9,13},{10,... | collective-permute-start | bytes 98312 | tf_op jit(solution)/shard_map/ppermute | solution.py:74
